TPU v7x, 32 devices: a whole 2x2x4 slice. The times are simulated.
32 devices in a mesh: row: 8 (over y, x, core), col: 4 (over z).
Axes of the slice: x: 2, y: 2, z: 4, core: 2. Of those that a mesh axis runs over, the one named last changes fastest.
Arguments:
- x_blocks: bfloat16 [64, 8, 256, 256], P('row', 'col'), may hold values from -0.75 to 0.75, as said below
- x_cols: int32 [64, 8], P('row', 'col'), may hold values from -1 to 63, as said below
- out_cols: int32 [64, 16], P('row', 'col'), may hold values from 0 to 63, as said below
- branch_flag: int32 [64], P('row'), may hold values from 0 to 1
Outputs:
- purified: bfloat16 [64, 16, 256, 256], P('row', 'col')
- trace: float32 [1], replicated
Inputs may be any that keep to these rules, and one draw needn't show every extreme that they name: `x_cols`: slot c * 2 + s of block row i holds -1 or a block column in c * 16 to (c + 1) * 16 - 1; the filled columns of one block row are distinct. The pattern is symmetric: block row i names column j exactly when block row j names column i. The rows of one device hold at most 13 filled slots together, and the rows of some device hold exactly 13. `x_blocks`: the stored block of position (j, i) is the transpose of the stored block of position (i, j); stored diagonal blocks are symmetric. `out_cols`: slot c * 4 + o of block row i holds a block column in c * 16 to (c + 1) * 16 - 1, distinct within one block row; column i is always among the slots of block row i. `branch_flag`: entry i is 0 where block row i takes X times X, 1 where it takes 2 X minus X times X.
All inputs are finite; a program needn't handle non-finite values.
Results may differ from a plain program's by a relative error of at most 0.001.
Values may be sent and summed in bfloat16 or wider, within the bound.
No kernel may reach another device: no remote copies, remote signals or barrier semaphores. Data moves between devices by JAX's collectives and lax.ppermute only.
A program may use at most 192 MiB of HBM per device.

v0:
```python
import jax
import jax.numpy as jnp
from jax import lax
from jax.sharding import PartitionSpec as P

PACKED = 13


def per_device(x_blocks, x_cols, out_cols, branch_flag):
    rows = x_cols.shape[0]
    slots = x_cols.shape[1]
    block = x_blocks.shape[-1]
    kept = out_cols.shape[1]
    filled = x_cols >= 0
    cleared = jnp.where(filled[:, :, None, None], x_blocks, jnp.zeros_like(x_blocks))
    flag_rows = branch_flag == 1
    base_row = lax.axis_index("row") * rows
    left_blocks, left_cols = (
        lax.all_gather(cleared, "col", axis=1, tiled=True),
        lax.all_gather(x_cols, "col", axis=1, tiled=True),
    )
    count = rows * slots
    flat_fill = filled.reshape(count).astype(jnp.int32)
    place = jnp.where(flat_fill > 0, jnp.cumsum(flat_fill) - 1, -1)
    positions = jnp.arange(count, dtype=jnp.int32)
    source = jnp.sum(
        jnp.where(
            place[None, :] == jnp.arange(PACKED, dtype=jnp.int32)[:, None], positions[None, :], 0
        ),
        axis=1,
    )
    packed = cleared.reshape(count, block, block)[source]
    packed_all, right_cols = (
        lax.all_gather(packed, "row", axis=0, tiled=True),
        lax.all_gather(x_cols, "row", axis=0, tiled=True),
    )
    row_devices = lax.axis_size("row")
    fill_all = (right_cols >= 0).reshape(row_devices, count).astype(jnp.int32)
    located = (
        jnp.cumsum(fill_all, axis=1)
        - 1
        + PACKED * jnp.arange(row_devices, dtype=jnp.int32)[:, None]
    )
    located = jnp.where(fill_all > 0, located, 0).reshape(right_cols.shape)
    right_blocks = jnp.where(
        (right_cols >= 0)[:, :, None, None], packed_all[located], jnp.zeros((), jnp.bfloat16)
    )

    def fetch(local):
        entries = left_cols[local]
        live = entries >= 0
        source_rows = jnp.where(live, entries, 0)
        fetched = right_blocks[source_rows]
        fetched_cols = jnp.where(live[:, None], right_cols[source_rows], -1)
        return (left_blocks[local], fetched, fetched_cols)

    def one_row(local):
        lhs, fetched, fetched_cols = fetch(local)
        width = fetched_cols.shape[0] * fetched_cols.shape[1]
        products = jnp.einsum("exy,esyz->esxz", lhs, fetched, preferred_element_type=jnp.float32)
        targets = out_cols[local]
        match = (
            (fetched_cols[None, :, :] == targets[:, None, None])
            .astype(jnp.float32)
            .reshape(kept, width)
        )
        square = jnp.dot(
            match, products.reshape(width, block * block), precision=lax.Precision.HIGHEST
        ).reshape(kept, block, block)
        own_match = (x_cols[local][None, :] == targets[:, None]).astype(jnp.float32)
        own_blocks = cleared[local].astype(jnp.float32).reshape(slots, block * block)
        own = jnp.dot(own_match, own_blocks, precision=lax.Precision.HIGHEST).reshape(
            kept, block, block
        )
        result = jnp.where(flag_rows[local], 2.0 * own - square, square)
        diag_here = (targets == base_row + local).astype(jnp.float32)
        part = jnp.sum(diag_here * jnp.trace(result, axis1=1, axis2=2))
        return (result.astype(jnp.bfloat16), part)

    purified, parts = lax.map(one_row, jnp.arange(rows, dtype=jnp.int32))
    trace_total = lax.psum(jnp.sum(parts), ("row", "col"))
    return (purified, trace_total.reshape(1))


def solution(mesh):
    in_specs = (P("row", "col", None, None), P("row", "col"), P("row", "col"), P("row"))
    out_specs = (P("row", "col", None, None), P())
    return jax.shard_map(
        per_device, mesh=mesh, in_specs=in_specs, out_specs=out_specs, check_vma=False
    )
```

profile of v0, /device:TPU:0, one launch (start us, length us, event | category | flops | bytes accessed | tf_op | source)
XLA Modules:
  0.0 524.1 jit_solution(10985651623465988359)
XLA Ops:
  13.3 10.3 %all-gather.2 = s32[8,8,2]{1,2,0:T(2,128)S(1)} all-gather(s32[1,8,2]{1,2,0:T(2,128)S(1)} %bitcast.120), channel_id=1, replica_groups=mesh['row'=8,'col'=4] {'row'}, dimensions={0}, use_global_device_ids=true | all-gather | bytes 576 | tf_op jit(solution)/shard_map/all_gather | solution.py:35
  24.8 11.2 %all-gather.1 = s32[4,2,8]{2,1,0:T(2,128)S(1)} all-gather(s32[1,2,8]{2,1,0:T(2,128)S(1)} %bitcast.121), channel_id=1, replica_groups=mesh['row'=8,'col'=4] {'col'}, dimensions={0}, use_global_device_ids=true | all-gather | bytes 320 | tf_op jit(solution)/shard_map/all_gather | solution.py:20
  36.2 55.7 %all-gather.8.cloned.1.call-done = bf16[104,256,256]{2,1,0:T(8,128)(2,1)} async-done(((bf16[13,256,256]{2,1,0:T(8,128)(2,1)}), bf16[104,256,256]{2,1,0:T(8,128)(2,1)}) %all-gather.8.cloned.1.call-update) | async-done | bytes 13631504 | tf_op jit(solution)/shard_map/all_gather | solution.py:34
  91.8 14.2 %gather_fusion.3 = bf16[128,256,256]{2,1,0:T(8,128)(2,1)} fusion(bf16[104,256,256]{2,1,0:T(8,128)(2,1)} %all-gather.8.cloned.1.call-done, s32[1024]{0:T(1024)S(1)} %pad_clamp_fusion.1), kind=kCustom, calls=%fused_computation.3 | custom fusion | bytes 33554944 | tf_op jit(solution)/shard_map/gather | solution.py:46
  106.1 14.2 %broadcast_select_fusion.1 = bf16[64,2,256,256]{3,2,1,0:T(8,128)(2,1)} fusion(bf16[64,2,256,256]{3,2,1,0:T(8,128)(2,1)} %bitcast.118, pred[64,2]{1,0:T(8,128)(4,1)S(1)} %copy.60), kind=kLoop, calls=%fused_computation.39 | loop fusion | flops 8388608 | bytes 33554560 | tf_op jit(solution)/shard_map/jit(_where)/select_n | solution.py:45
  120.2 122.9 %all-gather.6.cloned.1.call-done = bf16[8,8,256,256]{3,2,1,0:T(8,128)(2,1)} async-done(((bf16[8,2,256,256]{3,2,1,0:T(8,128)(2,1)}), bf16[8,8,256,256]{3,2,1,0:T(8,128)(2,1)}) %all-gather.6.cloned.1.call-update) | async-done | bytes 8388624 | tf_op jit(solution)/shard_map/all_gather | solution.py:19
  243.1 234.9 %while.12 = (s32[]{:T(128)}, bf16[8,4,256,256]{3,2,1,0:T(8,128)(2,1)}, f32[8]{0:T(128)S(1)}, s32[8]{0:T(128)S(1)}, pred[8]{0:T(512)(128)(4,1)S(1)}, /*index=5*/s...) while((s32[]{:T(128)}, ...), condition=%wide.region_6.7_spmd, body=%wide.region_3.6_spmd.sunk | while | flops 589890688 | bytes 28710492 | solution.py:80
  245.6 6.5 %gather_fusion.1 = bf16[8,2,256,256]{3,2,1,0:T(8,128)(2,1)S(1)} fusion(bf16[64,2,256,256]{3,2,1,0:T(8,128)(2,1)} %get-tuple-element.289, s32[1024]{0:T(1024)S(1)} %pad_clamp_fusion.4), kind=kCustom, calls=%fused_computation.1.clone.1 | custom fusion | bytes 4194336 | tf_op jit(solution)/shard_map/while/body/eval_jaxpr/gather | solution.py:53
  256.1 5.4 %copy.100 = f32[2,8,256,256]{3,1,2,0:T(8,128)} copy(f32[2,8,256,256]{2,3,1,0:T(8,128)} %bitcast.117) | data formatting | bytes 8388608 | tf_op jit(solution)/shard_map/while
  275.0 6.5 %gather_fusion.1 = bf16[8,2,256,256]{3,2,1,0:T(8,128)(2,1)S(1)} fusion(bf16[64,2,256,256]{3,2,1,0:T(8,128)(2,1)} %get-tuple-element.289, s32[1024]{0:T(1024)S(1)} %pad_clamp_fusion.4), kind=kCustom, calls=%fused_computation.1.clone.1 | custom fusion | bytes 4194336 | tf_op jit(solution)/shard_map/while/body/eval_jaxpr/gather | solution.py:53
  285.4 5.4 %copy.100 = f32[2,8,256,256]{3,1,2,0:T(8,128)} copy(f32[2,8,256,256]{2,3,1,0:T(8,128)} %bitcast.117) | data formatting | bytes 8388608 | tf_op jit(solution)/shard_map/while
  304.3 6.5 %gather_fusion.1 = bf16[8,2,256,256]{3,2,1,0:T(8,128)(2,1)S(1)} fusion(bf16[64,2,256,256]{3,2,1,0:T(8,128)(2,1)} %get-tuple-element.289, s32[1024]{0:T(1024)S(1)} %pad_clamp_fusion.4), kind=kCustom, calls=%fused_computation.1.clone.1 | custom fusion | bytes 4194336 | tf_op jit(solution)/shard_map/while/body/eval_jaxpr/gather | solution.py:53
  314.8 5.4 %copy.100 = f32[2,8,256,256]{3,1,2,0:T(8,128)} copy(f32[2,8,256,256]{2,3,1,0:T(8,128)} %bitcast.117) | data formatting | bytes 8388608 | tf_op jit(solution)/shard_map/while
  333.7 6.5 %gather_fusion.1 = bf16[8,2,256,256]{3,2,1,0:T(8,128)(2,1)S(1)} fusion(bf16[64,2,256,256]{3,2,1,0:T(8,128)(2,1)} %get-tuple-element.289, s32[1024]{0:T(1024)S(1)} %pad_clamp_fusion.4), kind=kCustom, calls=%fused_computation.1.clone.1 | custom fusion | bytes 4194336 | tf_op jit(solution)/shard_map/while/body/eval_jaxpr/gather | solution.py:53
  344.2 5.4 %copy.100 = f32[2,8,256,256]{3,1,2,0:T(8,128)} copy(f32[2,8,256,256]{2,3,1,0:T(8,128)} %bitcast.117) | data formatting | bytes 8388608 | tf_op jit(solution)/shard_map/while
  363.0 6.5 %gather_fusion.1 = bf16[8,2,256,256]{3,2,1,0:T(8,128)(2,1)S(1)} fusion(bf16[64,2,256,256]{3,2,1,0:T(8,128)(2,1)} %get-tuple-element.289, s32[1024]{0:T(1024)S(1)} %pad_clamp_fusion.4), kind=kCustom, calls=%fused_computation.1.clone.1 | custom fusion | bytes 4194336 | tf_op jit(solution)/shard_map/while/body/eval_jaxpr/gather | solution.py:53
  373.5 5.4 %copy.100 = f32[2,8,256,256]{3,1,2,0:T(8,128)} copy(f32[2,8,256,256]{2,3,1,0:T(8,128)} %bitcast.117) | data formatting | bytes 8388608 | tf_op jit(solution)/shard_map/while
  392.4 6.5 %gather_fusion.1 = bf16[8,2,256,256]{3,2,1,0:T(8,128)(2,1)S(1)} fusion(bf16[64,2,256,256]{3,2,1,0:T(8,128)(2,1)} %get-tuple-element.289, s32[1024]{0:T(1024)S(1)} %pad_clamp_fusion.4), kind=kCustom, calls=%fused_computation.1.clone.1 | custom fusion | bytes 4194336 | tf_op jit(solution)/shard_map/while/body/eval_jaxpr/gather | solution.py:53
  402.9 5.4 %copy.100 = f32[2,8,256,256]{3,1,2,0:T(8,128)} copy(f32[2,8,256,256]{2,3,1,0:T(8,128)} %bitcast.117) | data formatting | bytes 8388608 | tf_op jit(solution)/shard_map/while
  421.8 6.5 %gather_fusion.1 = bf16[8,2,256,256]{3,2,1,0:T(8,128)(2,1)S(1)} fusion(bf16[64,2,256,256]{3,2,1,0:T(8,128)(2,1)} %get-tuple-element.289, s32[1024]{0:T(1024)S(1)} %pad_clamp_fusion.4), kind=kCustom, calls=%fused_computation.1.clone.1 | custom fusion | bytes 4194336 | tf_op jit(solution)/shard_map/while/body/eval_jaxpr/gather | solution.py:53
  432.3 5.4 %copy.100 = f32[2,8,256,256]{3,1,2,0:T(8,128)} copy(f32[2,8,256,256]{2,3,1,0:T(8,128)} %bitcast.117) | data formatting | bytes 8388608 | tf_op jit(solution)/shard_map/while
  451.1 6.5 %gather_fusion.1 = bf16[8,2,256,256]{3,2,1,0:T(8,128)(2,1)S(1)} fusion(bf16[64,2,256,256]{3,2,1,0:T(8,128)(2,1)} %get-tuple-element.289, s32[1024]{0:T(1024)S(1)} %pad_clamp_fusion.4), kind=kCustom, calls=%fused_computation.1.clone.1 | custom fusion | bytes 4194336 | tf_op jit(solution)/shard_map/while/body/eval_jaxpr/gather | solution.py:53
  461.6 5.4 %copy.100 = f32[2,8,256,256]{3,1,2,0:T(8,128)} copy(f32[2,8,256,256]{2,3,1,0:T(8,128)} %bitcast.117) | data formatting | bytes 8388608 | tf_op jit(solution)/shard_map/while
  478.6 38.6 %psum.7 = f32[1]{0:T(128)} all-reduce(f32[1]{0:T(128)} %bitcast.27), channel_id=1, replica_groups=mesh['row'=8,'col'=4] {'row','col'}, use_global_device_ids=true, to_apply=%region_8.9 | all-reduce | flops 1 | bytes 8 | tf_op jit(solution)/shard_map/psum | solution.py:81
  (213 shorter events, 127.2 us)
Async XLA Ops:
  7.2 84.7 %all-gather.8.cloned.1.call-start = ((), (), s32[]{:S(2)}) async-start(), calls=%async_computation.1 | async-start | bytes 15335424 | tf_op jit(solution)/shard_map/all_gather | solution.py:34
  10.5 2.0 copy-start
  10.5 2.7 copy-start.1
  10.5 25.6 %copy-start.2 = (s32[8,4]{0,1:T(4,128)S(1)}, s32[8,4]{0,1:T(4,128)}, u32[]{:S(2)}) copy-start(s32[8,4]{0,1:T(4,128)} %param.8) | copy-start | bytes 388
  10.5 25.7 %copy-start.3 = (s32[8]{0:T(128)S(1)}, s32[8]{0:T(128)}, u32[]{:S(2)}) copy-start(s32[8]{0:T(128)} %param.9) | copy-start | bytes 100
  12.4 230.7 %all-gather.6.cloned.1.call-start = ((), (), s32[]{:S(2)}) async-start(), calls=%async_computation | async-start | bytes 10485760 | tf_op jit(solution)/shard_map/all_gather | solution.py:19
Sparse Core Ops, SparseCore 0:
  12.5 79.2 all-gather.7
  93.4 149.6 all-gather.5
where the time goes:
time: 527 us; the launch traced here: 524 us
  waiting for transfers between devices  179 us (34%)
  local copies, waits for them, and re-layouts  149 us (28%)
  matrix products  77.6 us (15%)
  blocking collectives  60.1 us (11%)
  other arithmetic  23.1 us (4%)
  loops' own time  20.5 us (4%)
  between operations  14.2 us (3%)
    all_gather x1, waiting for transfers between devices, per_device(): lax.all_gather(cleared, 'col', axis=1, tiled=True)  123 us
    all_gather x1, waiting for transfers between devices, per_device(): lax.all_gather(packed, 'row', axis=0, tiled=True)  55.7 us
    gather x8, local copies, waits for them, and re-layouts, fetch(): fetched = right_blocks[source_rows]  51.6 us
    while x16, local copies, waits for them, and re-layouts  51.3 us
    dot_general x8, matrix products, one_row(): jnp.dot(match, products.reshape(width, block * block), precision=lax.Prec...  40.5 us
    psum x1, blocking collectives, per_device(): trace_total = lax.psum(jnp.sum(parts), ('row', 'col'))  38.6 us
    dot_general x8, matrix products, one_row(): jnp.einsum('exy,esyz->esxz', lhs, fetched, preferred_element_type=jnp.flo...  32.2 us
    another operation x1, loops' own time, per_device(): purified, parts = lax.map(one_row, jnp.arange(rows, dtype=jnp.int32))  20.5 us
  transfers between devices with their start and end apart: 2, of which 2 were waited for; matrix products, arithmetic and copies ran while one was open for 6% of the time, Pallas kernels for 0%

commit v1 on v0

v1 whole, which is shorter than its diff:
```python
import functools

import jax
import jax.numpy as jnp
from jax import lax
from jax.experimental import pallas as pl
from jax.experimental.pallas import tpu as pltpu
from jax.sharding import PartitionSpec as P

PACKED = 13


def multiply_kernel(
    n_pieces, spans, kept, count_ref, left_ref, right_ref, own_ref, flag_ref, *refs
):
    pieces = refs[:n_pieces]
    out_ref = refs[n_pieces]
    left, right, total, done, in_sem, out_sem = refs[n_pieces + 1 :]
    copies = []
    for index, (piece, span) in enumerate(zip(pieces, spans)):
        side, first, size = span
        target = left if side == "left" else right
        copies.append(
            pltpu.make_async_copy(piece, target.at[pl.ds(first, size)], in_sem.at[index])
        )
    for copy in copies:
        copy.start()
    for copy in copies:
        copy.wait()
    outputs = out_ref.shape[0]
    depth = done.shape[0]

    def write(output, slot):
        return pltpu.make_async_copy(done.at[slot], out_ref.at[output], out_sem.at[slot])

    def one_output(output, carry):
        slot = lax.rem(output, depth)

        @pl.when(output >= depth)
        def _():
            write(output - depth, slot).wait()

        n_terms = count_ref[output]
        flag = flag_ref[output // kept]
        own = own_ref[output]
        total[...] = jnp.zeros_like(total)

        def one_term(term, carry):
            total[...] += jnp.dot(
                left[left_ref[output, term]],
                right[right_ref[output, term]],
                preferred_element_type=jnp.float32,
            )
            return carry

        lax.fori_loop(0, n_terms, one_term, 0)

        @pl.when(flag == 0)
        def _():
            done[slot] = total[...].astype(done.dtype)

        @pl.when(jnp.logical_and(flag != 0, own < 0))
        def _():
            done[slot] = (-total[...]).astype(done.dtype)

        @pl.when(jnp.logical_and(flag != 0, own >= 0))
        def _():
            mine = left[jnp.maximum(own, 0)].astype(jnp.float32)
            done[slot] = (2.0 * mine - total[...]).astype(done.dtype)

        write(output, slot).start()
        return carry

    lax.fori_loop(0, outputs, one_output, 0)
    for output in range(outputs - depth, outputs):
        write(output, output % depth).wait()


def multiply(left_pieces, right_pieces, tables, kept):
    counts, left_index, right_index, own_index, flags = tables
    outputs = counts.shape[0]
    block = left_pieces[0][1].shape[-1]
    dtype = left_pieces[0][1].dtype
    pieces = [("left", first, p) for first, p in left_pieces]
    pieces += [("right", first, p) for first, p in right_pieces]
    spans = tuple((side, first, p.shape[0]) for side, first, p in pieces)
    n_left = max(first + size for side, first, size in spans if side == "left")
    n_right = max(first + size for side, first, size in spans if side == "right")
    depth = min(4, outputs)
    smem = pl.BlockSpec(memory_space=pltpu.SMEM)
    hbm = pl.BlockSpec(memory_space=pl.ANY)
    vmem_bytes = (n_left + n_right + depth + 2) * block * block * 2 + (8 << 20)
    return pl.pallas_call(
        functools.partial(multiply_kernel, len(pieces), spans, kept),
        out_shape=jax.ShapeDtypeStruct((outputs, block, block), dtype),
        in_specs=[smem] * 5 + [hbm] * len(pieces),
        out_specs=hbm,
        scratch_shapes=[
            pltpu.VMEM((n_left, block, block), dtype),
            pltpu.VMEM((n_right, block, block), dtype),
            pltpu.VMEM((block, block), jnp.float32),
            pltpu.VMEM((depth, block, block), dtype),
            pltpu.SemaphoreType.DMA((len(pieces),)),
            pltpu.SemaphoreType.DMA((depth,)),
        ],
        compiler_params=pltpu.CompilerParams(vmem_limit_bytes=vmem_bytes),
    )(counts, left_index, right_index, own_index, flags, *[p for _, _, p in pieces])


def exchange(array, mask):
    size = lax.axis_size("row")
    return lax.ppermute(array, "row", [(i, i ^ mask) for i in range(size)])


def gather_rows(packed):
    size = lax.axis_size("row")
    half = (PACKED + 1) // 2
    whole = {0: packed}
    halves = {}
    masks = []
    mask = 2
    while mask < size:
        masks.append(mask)
        mask *= 2
    for mask in masks:
        whole[mask] = exchange(packed, mask)

    def part(delta, side):
        if delta in whole:
            return whole[delta][:half] if side == 0 else whole[delta][half:]
        return halves[delta, side]

    for delta in range(2, size, 2):
        bits = [mask for mask in masks if delta & mask]
        if len(bits) > 1:
            halves[delta, 0] = exchange(part(delta ^ bits[-1], 0), bits[-1])
            halves[delta, 1] = exchange(part(delta ^ bits[0], 1), bits[0])
    pieces = []
    for delta, array in whole.items():
        pieces.append((delta * PACKED, array))
        pieces.append(((delta ^ 1) * PACKED, exchange(array, 1)))
    for (delta, side), array in halves.items():
        first = side * half
        pieces.append((delta * PACKED + first, array))
        pieces.append(((delta ^ 1) * PACKED + first, exchange(array, 1)))
    return pieces


def running_count(fill):
    count = fill.shape[-1]
    before = jnp.arange(count)[:, None] < jnp.arange(count)[None, :]
    return jnp.sum(jnp.where(before, fill[..., :, None], 0), axis=-2)


def local_trace(x_blocks, x_cols, branch_flag, first_row):
    rows, slots, block, _ = x_blocks.shape
    own_row = first_row + jnp.arange(rows, dtype=jnp.int32)
    flag = branch_flag.astype(jnp.float32)[:, None]
    norm_weight = jnp.where(x_cols >= 0, 1.0 - 2.0 * flag, 0.0)
    diag_weight = jnp.where(x_cols == own_row[:, None], 2.0 * flag, 0.0)
    values = x_blocks.astype(jnp.float32)
    eye = jnp.eye(block, dtype=jnp.float32)
    weight = norm_weight[:, :, None, None] * values + diag_weight[:, :, None, None] * eye
    return jnp.sum(weight * values)


def per_device(x_blocks, x_cols, out_cols, branch_flag):
    rows, slots = x_cols.shape
    kept = out_cols.shape[1]
    block = x_blocks.shape[-1]
    count = rows * slots
    n_row = lax.axis_size("row")
    n_col = lax.axis_size("col")
    row = lax.axis_index("row")
    col = lax.axis_index("col")

    flat_cols = x_cols.reshape(count)
    fill = (flat_cols >= 0).astype(jnp.int32)
    place = jnp.where(fill > 0, running_count(fill), -1)
    slots_of = jnp.arange(PACKED, dtype=jnp.int32)
    source = jnp.sum(
        jnp.where(
            place[None, :] == slots_of[:, None], jnp.arange(count, dtype=jnp.int32)[None, :], 0
        ),
        axis=1,
    )
    packed = x_blocks.reshape(count, block, block)[source]

    left_all = lax.all_gather(packed, "col", axis=0, tiled=True)
    right_pieces = gather_rows(packed)

    part = local_trace(x_blocks, x_cols, branch_flag, row * rows)
    facts = jnp.concatenate([flat_cols.astype(jnp.float32), part.reshape(1)])
    facts = lax.all_gather(facts, ("row", "col"), axis=0).reshape(n_row, n_col, count + 1)
    trace = jnp.sum(facts[:, :, count])
    all_cols = facts[:, :, :count].astype(jnp.int32)
    all_fill = (all_cols >= 0).astype(jnp.int32)
    all_place = running_count(all_fill)

    own_cols = lax.dynamic_index_in_dim(all_cols, row, 0, keepdims=False)
    own_place = lax.dynamic_index_in_dim(all_place, row, 0, keepdims=False)
    own_place = own_place + PACKED * jnp.arange(n_col, dtype=jnp.int32)[:, None]
    width = n_col * slots
    left_cols = own_cols.reshape(n_col, rows, slots).transpose(1, 0, 2).reshape(rows, width)
    left_place = own_place.reshape(n_col, rows, slots).transpose(1, 0, 2).reshape(rows, width)
    right_cols = lax.dynamic_index_in_dim(all_cols, col, 1, keepdims=False)
    right_place = lax.dynamic_index_in_dim(all_place, col, 1, keepdims=False)
    delta = jnp.bitwise_xor(jnp.arange(n_row, dtype=jnp.int32), row)
    right_place = (right_place + PACKED * delta[:, None]).reshape(n_row * rows, slots)
    right_cols = right_cols.reshape(n_row * rows, slots)

    hot = left_cols[:, :, None] == jnp.arange(n_row * rows, dtype=jnp.int32)
    met_cols = jnp.sum(jnp.where(hot[..., None], right_cols + 1, 0), axis=2) - 1
    met_place = jnp.sum(jnp.where(hot[..., None], right_place, 0), axis=2)
    match = met_cols[:, None, :, :] == out_cols[:, :, None, None]
    right_at = jnp.sum(jnp.where(match, met_place[:, None], 0), axis=3)
    live = jnp.any(match, axis=3)
    term = jnp.where(live, running_count(live.astype(jnp.int32)), -1)
    pick = term[:, :, None, :] == jnp.arange(width, dtype=jnp.int32)[:, None]
    right_index = jnp.sum(jnp.where(pick, right_at[:, :, None, :], 0), axis=3)
    left_index = jnp.sum(jnp.where(pick, left_place[:, None, None, :], 0), axis=3)
    counts = jnp.sum(live.astype(jnp.int32), axis=2)
    own_match = left_cols[:, None, :] == out_cols[:, :, None]
    own_index = jnp.sum(jnp.where(own_match, left_place[:, None, :] + 1, 0), axis=2) - 1

    outputs = rows * kept
    tables = (
        counts.reshape(outputs),
        left_index.reshape(outputs, width),
        right_index.reshape(outputs, width),
        own_index.reshape(outputs),
        branch_flag,
    )
    purified = multiply([(0, left_all)], right_pieces, tables, kept)
    return purified.reshape(rows, kept, block, block), trace.reshape(1)


def solution(mesh):
    in_specs = (P("row", "col", None, None), P("row", "col"), P("row", "col"), P("row"))
    out_specs = (P("row", "col", None, None), P())
    return jax.shard_map(
        per_device, mesh=mesh, in_specs=in_specs, out_specs=out_specs, check_vma=False
    )
```

time: 527 us -> 171 us (0.32)
  waiting for transfers between devices: 179 us -> 33.4 us
  local copies, waits for them, and re-layouts: 149 us -> 11.5 us
  matrix products: 77.6 us -> 0 us
  Pallas kernels: 0 us -> 20.7 us
  loops' own time: 20.5 us -> 0 us
  other arithmetic: 23.1 us -> 9.34 us
  blocking collectives: 60.1 us -> 72.5 us
  starting transfers between devices: 0.08 us -> 8.46 us
    all_gather x2 -> x1, waiting for transfers between devices: 179 us -> 17.3 us  [per_device(): left_all = lax.all_gather(packed, 'col', axis=0, tiled=True)]
    dot_general x24 -> x0, matrix products: 77.6 us -> none  [the longest x8 40.5 us: one_row(): jnp.dot(match, products.reshape(width, block * block), precision=lax.Prec...]
    unnamed x0 -> x1, blocking collectives: none -> 72.5 us
    gather x26 -> x1, local copies, waits for them, and re-layouts: 72.8 us -> 3.48 us  [per_device(): packed = x_blocks.reshape(count, block, block)[source]]
    while x21 -> x0, local copies, waits for them, and re-layouts: 51.7 us -> none
    psum x1 -> x0, blocking collectives: 38.6 us -> none  [per_device(): trace_total = lax.psum(jnp.sum(parts), ('row', 'col'))]
    all_gather x2 -> x0, blocking collectives: 21.5 us -> none  [the longest x1 11.2 us: per_device(): lax.all_gather(x_cols, 'col', axis=1, tiled=True)]
    pallas_call x0 -> x1, Pallas kernels: none -> 20.7 us  [multiply(): pl.pallas_call(functools.partial(multiply_kernel, len(pieces), spans, kep...]
  transfers between devices with their start and end apart: 2 -> 10, of which waited for: 2 -> 3; matrix products, arithmetic and copies ran while one was open for 6% -> 8% of each run, Pallas kernels for 0% -> 0%
where the time goes in v1:
time: 171 us; the launch traced here: 170 us
  blocking collectives  72.5 us (42%)
  waiting for transfers between devices  33.4 us (20%)
  Pallas kernels  20.7 us (12%)
  between operations  14.3 us (8%)
  local copies, waits for them, and re-layouts  11.5 us (7%)
  other arithmetic  9.34 us (5%)
  starting transfers between devices  8.46 us (5%)
    unnamed x1, blocking collectives  72.5 us
    pallas_call x1, Pallas kernels, multiply(): pl.pallas_call(functools.partial(multiply_kernel, len(pieces), spans, kep...  20.7 us
    all_gather x1, waiting for transfers between devices, per_device(): left_all = lax.all_gather(packed, 'col', axis=0, tiled=True)  17.3 us
    ppermute x9, waiting for transfers between devices, exchange(): return lax.ppermute(array, 'row', [(i, i ^ mask) for i in range(size)])  16.1 us
    ppermute x9, starting transfers between devices, exchange(): return lax.ppermute(array, 'row', [(i, i ^ mask) for i in range(size)])  8.42 us
    reduce_sum x1, other arithmetic, local_trace(): return jnp.sum(weight * values)  4.01 us
    gather x1, local copies, waits for them, and re-layouts, per_device(): packed = x_blocks.reshape(count, block, block)[source]  3.48 us
  transfers between devices with their start and end apart: 10, of which 3 were waited for; matrix products, arithmetic and copies ran while one was open for 8% of the time, Pallas kernels for 0%

profile of v1, /device:TPU:0, one launch (start us, length us, event | category | flops | bytes accessed | tf_op | source)
XLA Modules:
  0.0 170.1 jit_solution(601673850596437162)
XLA Ops:
  7.2 0.7 fusion.5
  8.3 3.5 %gather_fusion = bf16[13,256,256]{2,1,0:T(8,128)(2,1)} fusion(bf16[16,256,256]{2,1,0:T(8,128)(2,1)} %bitcast.20, s32[1024]{0:T(1024)S(1)} %pad_clamp_fusion), kind=kCustom, calls=%fused_computation | custom fusion | bytes 3407924 | tf_op jit(solution)/shard_map/gather | solution.py:187
  11.8 3.0 %collective-permute-start.1 = (bf16[13,256,256]{2,1,0:T(8,128)(2,1)}, bf16[13,256,256]{2,1,0:T(8,128)(2,1)S(1)}, u32[]{:S(2)}, u32[]{:S(2)}) collective-permute-start(bf16[13,256,256]{2,1,0:T(8,128)(2,1)} %gather_fusion), channel_id=1, source_target_pairs={{0,8},{4,12},{8,0},{12,4},{16,24},{20,28},{24,16},{28,20},{1,9},{5... | collective-permute-start | bytes 5111816 | tf_op jit(solution)/shard_map/ppermute | solution.py:112
  14.8 1.5 collective-permute-start.3
  16.8 4.0 %fusion.1 = f32[]{:T(128)} fusion(bf16[8,2,256,256]{3,2,1,0:T(8,128)(2,1)} %param.4, f32[256,256]{1,0:T(8,128)S(1)} %fusion.2, f32[8,2]{1,0:T(8,128)S(1)} %copy.69, f32[8,2]{1,0:T(8,128)S(1)} %copy.68), kind=kLoop, calls=%fused_computation.4 | loop fusion | flops 6291455 | bytes 2359428 | tf_op jit(solution)/shard_map/reduce_sum | solution.py:164
  20.8 0.8 maximum_dynamic-update-slice_fusion
  21.8 72.5 %all-reduce = f32[544]{0:T(1024)S(1)} all-reduce(f32[544]{0:T(1024)S(1)} %maximum_dynamic-update-slice_fusion), channel_id=2, replica_groups=mesh['row'=8,'col'=4] {'row','col'}, use_global_device_ids=true, to_apply=%add | all-reduce | flops 544 | bytes 4352
  94.4 0.2 select_reduce_fusion
  95.0 1.0 slice.19
  96.0 2.3 %collective-permute-start.5 = (bf16[7,256,256]{2,1,0:T(8,128)(2,1)}, bf16[7,256,256]{2,1,0:T(8,128)(2,1)}, u32[]{:S(2)}, u32[]{:S(2)}) collective-permute-start(bf16[7,256,256]{2,1,0:T(8,128)(2,1)} %slice.19), channel_id=1, source_target_pairs={{0,16},{4,20},{8,24},{12,28},{16,0},{20,4},{24,8},{28,12},{1,17},{... | collective-permute-start | bytes 2752520 | tf_op jit(solution)/shard_map/ppermute | solution.py:112
  98.6 0.2 select_reduce_fusion.6
  98.8 2.1 %slice.20 = bf16[6,256,256]{2,1,0:T(8,128)(2,1)} slice(bf16[13,256,256]{2,1,0:T(8,128)(2,1)} %collective-permute-done.3.refs_5_), slice={[7:13], [0:256], [0:256]} | slice | bytes 1572864 | tf_op jit(solution)/shard_map/slice | solution.py:130
  100.9 0.6 collective-permute-start.7
  101.5 0.5 collective-permute-start.4
  102.5 0.6 select_reduce_fusion.4
  103.2 15.2 %collective-permute-done.5.refs_7_ = bf16[7,256,256]{2,1,0:T(8,128)(2,1)} collective-permute-done((bf16[7,256,256]{2,1,0:T(8,128)(2,1)}, bf16[7,256,256]{2,1,0:T(8,128)(2,1)}, u32[]{:S(2)}, u32[]{:S(2)}) %collective-permute-start.5) | collective-permute-done | bytes 917536 | tf_op jit(solution)/shard_map/ppermute | solution.py:112
  118.5 0.5 collective-permute-start.8
  119.3 0.1 copy_select_fusion
  119.6 0.7 slice_reduce_fusion
  120.3 1.2 select_reduce_fusion.1
  121.5 0.8 collective-permute-done.8.refs_10_
  122.3 17.3 %all-gather.4.cloned.1.call-done.refs_0_ = bf16[52,256,256]{2,1,0:T(8,128)(2,1)} async-done(((bf16[13,256,256]{2,1,0:T(8,128)(2,1)}), bf16[52,256,256]{2,1,0:T(8,128)(2,1)}) %all-gather.4.cloned.1.call-update) | async-done | bytes 6815760 | tf_op jit(solution)/shard_map/all_gather | solution.py:189
  139.6 2.9 %copy-done.1 = bf16[52,256,256]{2,1,0:T(8,128)(2,1)S(1)} copy-done((bf16[52,256,256]{2,1,0:T(8,128)(2,1)S(1)}, bf16[52,256,256]{2,1,0:T(8,128)(2,1)}, u32[]{:S(2)}) %copy-start.1) | copy-done | bytes 6815768
  142.6 20.7 %shard_map.59 = bf16[32,256,256]{2,1,0:T(8,128)(2,1)} custom-call(s32[32]{0:T(128)S(1)} %reshape.146.count_ref, s32[32,8]{1,0:T(8,128)S(1)} %bitcast.19, s32[32,8]{1,0:T(8,128)S(1)} %bitcast.18, s32[32]{0:T(128)S(1)} %sub.17.own_ref, s32[8]{0:T(128)S(1)} %copy-done.2, bf16[52,256,256]{2,1,0:T(8,128)(2,1)S(1)} %copy-done.1, ...), custom_call_target="tpu_custom_call" | custom-call | tf_op jit(solution)/shard_map/pallas_call | solution.py:93
  (78 shorter events, 2.9 us)
Async XLA Ops:
  7.2 132.5 %all-gather.4.cloned.1.call-start = ((), (), s32[]{:S(2)}) async-start(), calls=%async_computation | async-start | bytes 8519680 | tf_op jit(solution)/shard_map/all_gather | solution.py:189
  8.3 8.1 %copy-start.4 = (s32[8,2]{0,1:T(2,128)S(1)}, s32[8,2]{0,1:T(2,128)}, u32[]{:S(2)}) copy-start(s32[8,2]{0,1:T(2,128)} %param.5) | copy-start | bytes 196
  8.3 8.1 %copy-start.2 = (s32[8]{0:T(128)S(1)}, s32[8]{0:T(128)}, u32[]{:S(2)}) copy-start(s32[8]{0:T(128)} %flag_ref.1) | copy-start | bytes 100
  11.8 83.1 %collective-permute-start.1 = (bf16[13,256,256]{2,1,0:T(8,128)(2,1)}, bf16[13,256,256]{2,1,0:T(8,128)(2,1)S(1)}, u32[]{:S(2)}, u32[]{:S(2)}) collective-permute-start(bf16[13,256,256]{2,1,0:T(8,128)(2,1)} %gather_fusion), channel_id=1, source_target_pairs={{0,8},{4,12},{8,0},{12,4},{16,24},{20,28},{24,16},{28,20},{1,9},{5... | collective-permute-start | bytes 5111816 | tf_op jit(solution)/shard_map/ppermute | solution.py:112
  14.8 106.6 %collective-permute-start = (bf16[13,256,256]{2,1,0:T(8,128)(2,1)}, bf16[13,256,256]{2,1,0:T(8,128)(2,1)}, u32[]{:S(2)}, u32[]{:S(2)}) collective-permute-start(bf16[13,256,256]{2,1,0:T(8,128)(2,1)} %gather_fusion), channel_id=1, source_target_pairs={{0,4},{4,0},{8,12},{12,8},{16,20},{20,16},{24,28},{28,24},{1,5},{5... | collective-permute-start | bytes 5111816 | tf_op jit(solution)/shard_map/ppermute | solution.py:112
  14.8 84.0 %collective-permute-start.3 = (bf16[13,256,256]{2,1,0:T(8,128)(2,1)}, bf16[13,256,256]{2,1,0:T(8,128)(2,1)}, u32[]{:S(2)}, u32[]{:S(2)}) collective-permute-start(bf16[13,256,256]{2,1,0:T(8,128)(2,1)} %gather_fusion), channel_id=1, source_target_pairs={{0,16},{4,20},{8,24},{12,28},{16,0},{20,4},{24,8},{28,12},{1,17},{... | collective-permute-start | bytes 5111816 | tf_op jit(solution)/shard_map/ppermute | solution.py:112
  16.8 81.8 %copy-start.3 = (s32[8,4]{0,1:T(4,128)S(1)}, s32[8,4]{0,1:T(4,128)}, u32[]{:S(2)}) copy-start(s32[8,4]{0,1:T(4,128)} %param.6) | copy-start | bytes 388
  94.6 45.0 %copy-start = (bf16[13,256,256]{2,1,0:T(8,128)(2,1)S(1)}, bf16[13,256,256]{2,1,0:T(8,128)(2,1)}, u32[]{:S(2)}) copy-start(bf16[13,256,256]{2,1,0:T(8,128)(2,1)} %gather_fusion) | copy-start | bytes 5111812
  96.0 22.4 %collective-permute-start.5 = (bf16[7,256,256]{2,1,0:T(8,128)(2,1)}, bf16[7,256,256]{2,1,0:T(8,128)(2,1)}, u32[]{:S(2)}, u32[]{:S(2)}) collective-permute-start(bf16[7,256,256]{2,1,0:T(8,128)(2,1)} %slice.19), channel_id=1, source_target_pairs={{0,16},{4,20},{8,24},{12,28},{16,0},{20,4},{24,8},{28,12},{1,17},{... | collective-permute-start | bytes 2752520 | tf_op jit(solution)/shard_map/ppermute | solution.py:112
  100.9 17.6 %collective-permute-start.7 = (bf16[6,256,256]{2,1,0:T(8,128)(2,1)}, bf16[6,256,256]{2,1,0:T(8,128)(2,1)}, u32[]{:S(2)}, u32[]{:S(2)}) collective-permute-start(bf16[6,256,256]{2,1,0:T(8,128)(2,1)} %slice.20), channel_id=1, source_target_pairs={{0,8},{4,12},{8,0},{12,4},{16,24},{20,28},{24,16},{28,20},{1,9},{5... | collective-permute-start | bytes 2359304 | tf_op jit(solution)/shard_map/ppermute | solution.py:112
  101.5 20.9 %collective-permute-start.2 = (bf16[13,256,256]{2,1,0:T(8,128)(2,1)S(1)}, bf16[13,256,256]{2,1,0:T(8,128)(2,1)}, u32[]{:S(2)}, u32[]{:S(2)}) collective-permute-start(bf16[13,256,256]{2,1,0:T(8,128)(2,1)S(1)} %collective-permute-done.1.refs_3_), channel_id=1, source_target_pairs={{0,4},{4,0},{8,12},{12,8},{16,20},{20,16},{24,28},{28,24},{1,5},{5... | collective-permute-start | bytes 5111816 | tf_op jit(solution)/shard_map/ppermute | solution.py:112
  101.5 20.9 %collective-permute-start.4 = (bf16[13,256,256]{2,1,0:T(8,128)(2,1)}, bf16[13,256,256]{2,1,0:T(8,128)(2,1)}, u32[]{:S(2)}, u32[]{:S(2)}) collective-permute-start(bf16[13,256,256]{2,1,0:T(8,128)(2,1)} %collective-permute-done.3.refs_5_), channel_id=1, source_target_pairs={{0,4},{4,0},{8,12},{12,8},{16,20},{20,16},{24,28},{28,24},{1,5},{5... | collective-permute-start | bytes 5111816 | tf_op jit(solution)/shard_map/ppermute | solution.py:112
  118.4 3.9 %collective-permute-start.6 = (bf16[7,256,256]{2,1,0:T(8,128)(2,1)}, bf16[7,256,256]{2,1,0:T(8,128)(2,1)}, u32[]{:S(2)}, u32[]{:S(2)}) collective-permute-start(bf16[7,256,256]{2,1,0:T(8,128)(2,1)} %collective-permute-done.5.refs_7_), channel_id=1, source_target_pairs={{0,4},{4,0},{8,12},{12,8},{16,20},{20,16},{24,28},{28,24},{1,5},{5... | collective-permute-start | bytes 2752520 | tf_op jit(solution)/shard_map/ppermute | solution.py:112
  118.5 3.8 %collective-permute-start.8 = (bf16[6,256,256]{2,1,0:T(8,128)(2,1)}, bf16[6,256,256]{2,1,0:T(8,128)(2,1)}, u32[]{:S(2)}, u32[]{:S(2)}) collective-permute-start(bf16[6,256,256]{2,1,0:T(8,128)(2,1)} %collective-permute-done.7.refs_9_), channel_id=1, source_target_pairs={{0,4},{4,0},{8,12},{12,8},{16,20},{20,16},{24,28},{28,24},{1,5},{5... | collective-permute-start | bytes 2359304 | tf_op jit(solution)/shard_map/ppermute | solution.py:112
  139.6 2.9 %copy-start.1 = (bf16[52,256,256]{2,1,0:T(8,128)(2,1)S(1)}, bf16[52,256,256]{2,1,0:T(8,128)(2,1)}, u32[]{:S(2)}) copy-start(bf16[52,256,256]{2,1,0:T(8,128)(2,1)} %all-gather.4.cloned.1.call-done.refs_0_) | copy-start | bytes 20447236
Sparse Core Ops, SparseCore 0:
  11.9 127.6 all-gather.3

commit v2 on v0

v2 whole, which is shorter than its diff:
```python
import functools

import jax
import jax.numpy as jnp
from jax import lax
from jax.experimental import pallas as pl
from jax.experimental.pallas import tpu as pltpu
from jax.sharding import PartitionSpec as P

PACKED = 13
SPLIT = (PACKED + 1) // 2
STRIDE = 1 << (PACKED - 1).bit_length()
NOTE_ROWS = 16


def pack_kernel(first, limit, cols_ref, x_ref, note_ref, out_ref, sems):
    count, block, _ = x_ref.shape
    slots = cols_ref.shape[1]
    note = pltpu.make_async_copy(
        note_ref, out_ref.at[pl.ds((limit - first) * block, NOTE_ROWS)], sems.at[count]
    )
    note.start()
    copies = []
    place = jnp.int32(0)
    for index in range(count):
        filled = cols_ref[index // slots, index % slots] >= 0
        wanted = filled & (place >= first) & (place < limit)
        target = pl.multiple_of(jnp.where(wanted, place - first, 0) * block, block)
        copy = pltpu.make_async_copy(
            x_ref.at[index], out_ref.at[pl.ds(target, block)], sems.at[index]
        )
        pl.when(wanted)(copy.start)
        copies.append((wanted, copy))
        place = place + filled.astype(jnp.int32)
    for wanted, copy in copies:
        pl.when(wanted)(copy.wait)
    note.wait()


def pack(x_blocks, x_cols, note, first, limit):
    rows, slots, block, _ = x_blocks.shape
    count = rows * slots
    hbm = pl.BlockSpec(memory_space=pl.ANY)
    return pl.pallas_call(
        functools.partial(pack_kernel, first, limit),
        out_shape=jax.ShapeDtypeStruct(
            ((limit - first) * block + NOTE_ROWS, block), x_blocks.dtype
        ),
        in_specs=[pl.BlockSpec(memory_space=pltpu.SMEM), hbm, hbm],
        out_specs=hbm,
        scratch_shapes=[pltpu.SemaphoreType.DMA((count + 1,))],
    )(x_cols, x_blocks.reshape(count, block, block), note)


def multiply_kernel(loads, kept, counts, lefts, rights, owns, flags, place_ref, *refs):
    n_refs = 1 + max(load[0] for load in loads)
    sources = refs[:n_refs]
    out_ref = refs[n_refs]
    pool, more, done, in_sem, out_sem = refs[n_refs + 1 :]
    block = out_ref.shape[-1]
    copies = []
    for number, (which, index, entry, entries, first, size, ends) in enumerate(loads):
        rows = pl.ds(0, size * block)
        source = sources[which]
        target = pool.at[pl.ds(entry, entries), pl.ds(first * block, size * block)]
        if entries == 1:
            target = pool.at[entry, pl.ds(first * block, size * block)]
            source = source.at[rows] if index is None else source.at[index, rows]
        else:
            source = source.at[:, rows]
        copy = pltpu.make_async_copy(source, target, in_sem.at[number])
        copies.append((None if ends is None else place_ref[0] == ends, copy))
    for here, copy in copies:
        copy.start() if here is None else pl.when(here)(copy.start)
    zero_entry = pool.shape[0] - 1
    pool[zero_entry, pl.ds(0, block)] = jnp.zeros((block, block), pool.dtype)
    for here, copy in copies:
        copy.wait() if here is None else pl.when(here)(copy.wait)

    outputs = out_ref.shape[0]

    def blocks(index):
        entry = lax.shift_right_logical(index, STRIDE.bit_length() - 1)
        first = pl.multiple_of(jnp.bitwise_and(index, STRIDE - 1) * block, block)
        return pool[entry, pl.ds(first, block)]

    def product(output, term):
        return jnp.dot(
            blocks(lefts[output, term]),
            blocks(rights[output, term]),
            preferred_element_type=jnp.float32,
        )

    def write(output, slot):
        return pltpu.make_async_copy(done.at[slot], out_ref.at[output], out_sem.at[slot])

    def one_row(row, carry):
        flag = flags[row].astype(jnp.float32)
        for local in range(kept):
            output = row * kept + local

            @pl.when(counts[output] > 2)
            def _():
                more[local] = product(output, 2)

                def one_term(term, carry):
                    more[local] += product(output, term)
                    return carry

                lax.fori_loop(3, counts[output], one_term, 0)

            @pl.when(counts[output] <= 2)
            def _():
                more[local] = jnp.zeros_like(more[local])

        half = lax.rem(row, 2)

        @pl.when(row >= 2)
        def _():
            for local in range(kept):
                write((row - 2) * kept + local, half * kept + local).wait()

        for local in range(kept):
            output = row * kept + local
            square = product(output, 0) + product(output, 1) + more[local]
            own = blocks(owns[output]).astype(jnp.float32)
            result = (2.0 * flag) * own + (1.0 - 2.0 * flag) * square
            done[half * kept + local] = result.astype(done.dtype)
        for local in range(kept):
            write(row * kept + local, half * kept + local).start()
        return carry

    n_rows = outputs // kept
    lax.fori_loop(0, n_rows, one_row, 0)
    for row in range(max(n_rows - 2, 0), n_rows):
        for local in range(kept):
            write(row * kept + local, (row % 2) * kept + local).wait()


def multiply(arrays, loads, n_entries, tables, place, kept, block, dtype):
    outputs = tables[0].shape[0]
    smem = pl.BlockSpec(memory_space=pltpu.SMEM)
    hbm = pl.BlockSpec(memory_space=pl.ANY)
    pool_bytes = n_entries * PACKED * block * block * 2
    return pl.pallas_call(
        functools.partial(multiply_kernel, loads, kept),
        out_shape=jax.ShapeDtypeStruct((outputs, block, block), dtype),
        in_specs=[smem] * 6 + [hbm] * len(arrays),
        out_specs=hbm,
        scratch_shapes=[
            pltpu.VMEM((n_entries, PACKED * block, block), dtype),
            pltpu.VMEM((kept, block, block), jnp.float32),
            pltpu.VMEM((2 * kept, block, block), dtype),
            pltpu.SemaphoreType.DMA((len(loads),)),
            pltpu.SemaphoreType.DMA((2 * kept,)),
        ],
        compiler_params=pltpu.CompilerParams(vmem_limit_bytes=pool_bytes + (12 << 20)),
    )(*tables, place, *arrays)


def shift(array, pairs):
    return lax.ppermute(array, "col", pairs)


def gather_line(part):
    first = shift(part, [(0, 1), (1, 0), (2, 3), (3, 2)])
    middle = shift(part, [(1, 2), (2, 1)])
    end_two = shift(middle, [(1, 0), (2, 3)])
    middle_two = shift(first, [(1, 2), (2, 1)])
    end_three = shift(middle_two, [(1, 0), (2, 3)])
    return first, (end_two, end_three), (middle, middle_two)


def running_count(fill):
    count = fill.shape[-1]
    before = jnp.arange(count)[:, None] < jnp.arange(count)[None, :]
    return jnp.sum(jnp.where(before, fill[..., :, None], 0), axis=-2)


def places(cols):
    flat = (cols >= 0).astype(jnp.int32).reshape(cols.shape[:-2] + (-1,))
    return running_count(flat).reshape(cols.shape)


def local_trace(x_blocks, x_cols, branch_flag, first_row):
    rows, slots, block, _ = x_blocks.shape
    own_row = first_row + jnp.arange(rows, dtype=jnp.int32)
    flag = branch_flag.astype(jnp.float32)[:, None]
    norm_weight = jnp.where(x_cols >= 0, 1.0 - 2.0 * flag, 0.0)
    diag_weight = jnp.where(x_cols == own_row[:, None], 2.0 * flag, 0.0)
    values = x_blocks.astype(jnp.float32)
    eye = jnp.eye(block, dtype=jnp.float32)
    weight = norm_weight[:, :, None, None] * values + diag_weight[:, :, None, None] * eye
    return jnp.sum(weight * values)


def thirds(value):
    high = lax.reduce_precision(value, 8, 7)
    middle = lax.reduce_precision(value - high, 8, 7)
    return jnp.stack([high, middle, value - high - middle]).astype(jnp.bfloat16)


def per_device(x_blocks, x_cols, out_cols, branch_flag):
    rows, slots = x_cols.shape
    kept = out_cols.shape[1]
    block = x_blocks.shape[-1]
    dtype = x_blocks.dtype
    n_row = lax.axis_size("row")
    n_col = lax.axis_size("col")
    row = lax.axis_index("row")
    col = lax.axis_index("col")
    n_blocks = n_row * rows

    def note(values):
        pad = [(0, NOTE_ROWS - values.shape[0]), (0, block - values.shape[1])]
        return jnp.pad(values.astype(dtype), pad)

    part_a = pack(x_blocks, x_cols, note(x_cols), 0, SPLIT)
    trace_part = local_trace(x_blocks, x_cols, branch_flag, row * rows)
    part_b = pack(x_blocks, x_cols, note(thirds(trace_part)[None, :]), SPLIT, PACKED)
    parts = (part_a, part_b)

    def facts(array):
        return array[..., SPLIT * block : SPLIT * block + rows, :slots].astype(jnp.int32)

    plane = [lax.all_gather(part, "row", axis=0) for part in parts]
    spans = ((0, SPLIT), (SPLIT, PACKED - SPLIT))
    arrays = list(plane)
    loads = [(which, None, 0, n_row) + spans[which] + (None,) for which in range(2)]
    if n_col == 4:
        line = [gather_line(part) for part in parts]
        n_left = 3
        for which, (first, far, near) in enumerate(line):
            for entry, ends, array in (
                (0, None, first),
                (1, 1, far[0]),
                (1, 0, near[0]),
                (2, 1, far[1]),
                (2, 0, near[1]),
            ):
                loads.append((len(arrays), None, n_row + entry, 1) + spans[which] + (ends,))
                arrays.append(array)
        at_end = (col == 0) | (col == n_col - 1)
        first, far, near = line[0]
        left_cols = [facts(first)]
        left_cols += [jnp.where(at_end, facts(far[i]), facts(near[i])) for i in range(2)]
        left_cols = jnp.stack(left_cols + [x_cols])
        left_entries = jnp.stack([n_row + jnp.int32(i) for i in range(n_left)] + [row])
    else:
        line = [lax.all_gather(part, "col", axis=0) for part in parts]
        n_left = n_col
        for which in range(2):
            loads.append((len(arrays), None, n_row, n_col) + spans[which] + (None,))
            arrays.append(line[which])
        at_end = col == 0
        left_cols = facts(line[0])
        left_entries = n_row + jnp.arange(n_col, dtype=jnp.int32)
    n_entries = n_row + n_left + 1
    nothing = (n_entries - 1) * STRIDE

    trace = jnp.sum(plane[1][:, (PACKED - SPLIT) * block, :3].astype(jnp.float32))
    mask = 1
    while mask < n_col:
        trace = trace + shift(trace, [(i, i ^ mask) for i in range(n_col)])
        mask *= 2

    every = jnp.arange(n_blocks, dtype=jnp.int32)
    left_at = places(left_cols) + STRIDE * left_entries[:, None, None]
    hit = left_cols[..., None] == every
    left_of = jnp.sum(jnp.where(hit, left_at[..., None] + 1, 0), axis=(0, 2))
    right_cols = facts(plane[0])
    right_at = places(right_cols) + STRIDE * jnp.arange(n_row, dtype=jnp.int32)[:, None, None]
    right_cols = right_cols.reshape(n_blocks, slots)
    right_at = right_at.reshape(n_blocks, slots)
    targets = out_cols.reshape(rows * kept)
    hit = right_cols[None] == targets[:, None, None]
    right_of = jnp.sum(jnp.where(hit, right_at + 1, 0), axis=2)
    left_of = jnp.repeat(left_of, kept, axis=0)
    live = (left_of > 0) & (right_of > 0)
    width = n_col * slots
    term = jnp.where(live, running_count(live.astype(jnp.int32)), -1)
    pick = term[:, None, :] == jnp.arange(width, dtype=jnp.int32)[:, None]
    lefts = jnp.sum(jnp.where(pick, left_of[:, None, :] - 1 - nothing, 0), axis=2) + nothing
    rights = jnp.sum(jnp.where(pick, right_of[:, None, :] - 1 - nothing, 0), axis=2) + nothing
    counts = jnp.sum(live.astype(jnp.int32), axis=1)
    own_at = places(x_cols) + STRIDE * row
    hit = x_cols[:, None, :] == out_cols[:, :, None]
    owns = jnp.sum(jnp.where(hit, own_at[:, None, :] - nothing, 0), axis=2) + nothing

    tables = (counts, lefts, rights, owns.reshape(rows * kept), branch_flag)
    place = at_end.astype(jnp.int32).reshape(1)
    purified = multiply(arrays, tuple(loads), n_entries, tables, place, kept, block, dtype)
    return purified.reshape(rows, kept, block, block), trace.reshape(1)


def solution(mesh):
    in_specs = (P("row", "col", None, None), P("row", "col"), P("row", "col"), P("row"))
    out_specs = (P("row", "col", None, None), P())
    return jax.shard_map(
        per_device, mesh=mesh, in_specs=in_specs, out_specs=out_specs, check_vma=False
    )
```

time: 527 us -> 231 us (0.44)
  local copies, waits for them, and re-layouts: 149 us -> 10.1 us
  waiting for transfers between devices: 179 us -> 90.8 us
  matrix products: 77.6 us -> 0 us
  blocking collectives: 60.1 us -> 0 us
  Pallas kernels: 0 us -> 59.8 us
  starting transfers between devices: 0.08 us -> 33.8 us
  loops' own time: 20.5 us -> 0 us
  other arithmetic: 23.1 us -> 12.5 us
  between operations: 14.2 us -> 22.3 us
    all_gather x2, waiting for transfers between devices: 179 us -> 0.04 us  [per_device(): plane = [lax.all_gather(part, 'row', axis=0) for part in parts]]
    ppermute x0 -> x12, waiting for transfers between devices: none -> 90.7 us  [shift(): return lax.ppermute(array, 'col', pairs)]
    dot_general x24 -> x0, matrix products: 77.6 us -> none  [the longest x8 40.5 us: one_row(): jnp.dot(match, products.reshape(width, block * block), precision=lax.Prec...]
    gather x26 -> x0, local copies, waits for them, and re-layouts: 72.8 us -> none  [the longest x8 51.6 us: fetch(): fetched = right_blocks[source_rows]]
    pallas_call x0 -> x3, Pallas kernels: none -> 59.8 us  [the longest x2 44.3 us: pack(): pl.pallas_call(functools.partial(pack_kernel, first, limit), out_shape=ja...]
    while x21 -> x0, local copies, waits for them, and re-layouts: 51.7 us -> none
    psum x1 -> x0, blocking collectives: 38.6 us -> none  [per_device(): trace_total = lax.psum(jnp.sum(parts), ('row', 'col'))]
    ppermute x0 -> x12, starting transfers between devices: none -> 33.8 us  [shift(): return lax.ppermute(array, 'col', pairs)]
  transfers between devices with their start and end apart: 2 -> 14, of which waited for: 2 -> 6; matrix products, arithmetic and copies ran while one was open for 6% -> 4% of each run, Pallas kernels for 0% -> 13%
where the time goes in v2:
time: 231 us; the launch traced here: 229 us
  waiting for transfers between devices  90.8 us (39%)
  Pallas kernels  59.8 us (26%)
  starting transfers between devices  33.8 us (15%)
  between operations  22.3 us (10%)
  other arithmetic  12.5 us (5%)
  local copies, waits for them, and re-layouts  10.1 us (4%)
    ppermute x12, waiting for transfers between devices, shift(): return lax.ppermute(array, 'col', pairs)  90.7 us
    pallas_call x2, Pallas kernels, pack(): pl.pallas_call(functools.partial(pack_kernel, first, limit), out_shape=ja...  44.3 us
    ppermute x12, starting transfers between devices, shift(): return lax.ppermute(array, 'col', pairs)  33.8 us
    pallas_call x1, Pallas kernels, multiply(): pl.pallas_call(functools.partial(multiply_kernel, loads, kept), out_shape...  15.5 us
    unnamed x14, local copies, waits for them, and re-layouts  7.34 us
  transfers between devices with their start and end apart: 14, of which 6 were waited for; matrix products, arithmetic and copies ran while one was open for 4% of the time, Pallas kernels for 13%

profile of v2, /device:TPU:0, one launch (start us, length us, event | category | flops | bytes accessed | tf_op | source)
XLA Modules:
  0.0 229.4 jit_solution(17409332778337682397)
XLA Ops:
  7.3 1.3 copy.64.cols_ref
  10.1 4.0 %fusion.1 = f32[]{:T(128)} fusion(bf16[8,2,256,256]{3,2,1,0:T(8,128)(2,1)} %param.4, f32[256,256]{1,0:T(8,128)S(1)} %fusion.2, f32[8,2]{1,0:T(8,128)S(1)} %copy.81, f32[8,2]{1,0:T(8,128)S(1)} %copy.80), kind=kLoop, calls=%fused_computation.3 | loop fusion | flops 6291455 | bytes 2359428 | tf_op jit(solution)/shard_map/reduce_sum | solution.py:194
  19.9 14.3 %shard_map.60 = bf16[1552,256]{1,0:T(8,128)(2,1)} custom-call(s32[8,2]{1,0:T(8,128)} %copy.64.cols_ref, bf16[16,256,256]{2,1,0:T(8,128)(2,1)} %bitcast.25, bf16[16,256]{1,0:T(8,128)(2,1)} %fusion.12.note_ref), custom_call_target="tpu_custom_call" | custom-call | tf_op jit(solution)/shard_map/pallas_call | solution.py:44
  35.0 30.0 %shard_map.59 = bf16[1808,256]{1,0:T(8,128)(2,1)} custom-call(s32[8,2]{1,0:T(8,128)} %copy.64.cols_ref, bf16[16,256,256]{2,1,0:T(8,128)(2,1)} %bitcast.26, bf16[16,256]{1,0:T(8,128)(2,1)} %pad.8.note_ref), custom_call_target="tpu_custom_call" | custom-call | tf_op jit(solution)/shard_map/pallas_call | solution.py:44
  65.0 7.1 %collective-permute-start = (bf16[1808,256]{1,0:T(8,128)(2,1)}, bf16[1808,256]{1,0:T(8,128)(2,1)S(1)}, u32[]{:S(2)}, u32[]{:S(2)}) collective-permute-start(bf16[1808,256]{1,0:T(8,128)(2,1)} %shard_map.59), channel_id=1, source_target_pairs={{0,1},{1,0},{2,3},{3,2},{4,5},{5,4},{6,7},{7,6},{8,9},{9,8},{10,11... | collective-permute-start | bytes 2777096 | tf_op jit(solution)/shard_map/ppermute | solution.py:162
  72.8 13.7 %collective-permute-done.refs_2_ = bf16[1808,256]{1,0:T(8,128)(2,1)S(1)} collective-permute-done((bf16[1808,256]{1,0:T(8,128)(2,1)}, bf16[1808,256]{1,0:T(8,128)(2,1)S(1)}, u32[]{:S(2)}, u32[]{:S(2)}) %collective-permute-start) | collective-permute-done | bytes 925728 | tf_op jit(solution)/shard_map/ppermute | solution.py:162
  87.2 10.9 %collective-permute-start.5 = (bf16[1552,256]{1,0:T(8,128)(2,1)}, bf16[1552,256]{1,0:T(8,128)(2,1)}, u32[]{:S(2)}, u32[]{:S(2)}) collective-permute-start(bf16[1552,256]{1,0:T(8,128)(2,1)} %shard_map.60), channel_id=1, source_target_pairs={{0,1},{1,0},{2,3},{3,2},{4,5},{5,4},{6,7},{7,6},{8,9},{9,8},{10,11... | collective-permute-start | bytes 2383880 | tf_op jit(solution)/shard_map/ppermute | solution.py:162
  98.1 1.6 collective-permute-start.6
  100.1 1.3 collective-permute-start.2
  101.4 15.6 %collective-permute-done.5.refs_7_ = bf16[1552,256]{1,0:T(8,128)(2,1)} collective-permute-done((bf16[1552,256]{1,0:T(8,128)(2,1)}, bf16[1552,256]{1,0:T(8,128)(2,1)}, u32[]{:S(2)}, u32[]{:S(2)}) %collective-permute-start.5) | collective-permute-done | bytes 794656 | tf_op jit(solution)/shard_map/ppermute | solution.py:162
  117.0 1.5 collective-permute-start.8
  118.9 1.3 collective-permute-start.4
  120.5 1.3 collective-permute-start.7
  122.0 1.3 collective-permute-start.9
  123.3 13.5 %collective-permute-done.2.refs_3_ = bf16[1808,256]{1,0:T(8,128)(2,1)} collective-permute-done((bf16[1808,256]{1,0:T(8,128)(2,1)S(1)}, bf16[1808,256]{1,0:T(8,128)(2,1)}, u32[]{:S(2)}, u32[]{:S(2)}) %collective-permute-start.2) | collective-permute-done | bytes 925728 | tf_op jit(solution)/shard_map/ppermute | solution.py:162
  137.7 19.0 %collective-permute-done.4.refs_5_ = bf16[1808,256]{1,0:T(8,128)(2,1)} collective-permute-done((bf16[1808,256]{1,0:T(8,128)(2,1)S(1)}, bf16[1808,256]{1,0:T(8,128)(2,1)}, u32[]{:S(2)}, u32[]{:S(2)}) %collective-permute-start.4) | collective-permute-done | bytes 925728 | tf_op jit(solution)/shard_map/ppermute | solution.py:162
  158.0 1.3 fusion.13
  159.3 4.8 %collective-permute-start.10 = (f32[]{:T(128)}, f32[]{:T(128)}, u32[]{:S(2)}, u32[]{:S(2)}) collective-permute-start(f32[]{:T(128)} %fusion.13), channel_id=1, source_target_pairs={{0,1},{1,0},{2,3},{3,2},{4,5},{5,4},{6,7},{7,6},{8,9},{9,8},{10,11... | collective-permute-start | bytes 20 | tf_op jit(solution)/shard_map/ppermute | solution.py:162
  164.1 25.6 %collective-permute-done.10 = f32[]{:T(128)} collective-permute-done((f32[]{:T(128)}, f32[]{:T(128)}, u32[]{:S(2)}, u32[]{:S(2)}) %collective-permute-start.10) | collective-permute-done | bytes 36 | tf_op jit(solution)/shard_map/ppermute | solution.py:162
  191.0 1.4 collective-permute-start.11
  192.3 3.2 %collective-permute-done.11 = f32[]{:T(128)} collective-permute-done((f32[]{:T(128)}, f32[]{:T(128)}, u32[]{:S(2)}, u32[]{:S(2)}) %collective-permute-start.11) | collective-permute-done | bytes 36 | tf_op jit(solution)/shard_map/ppermute | solution.py:162
  200.0 3.1 %copy-done = bf16[14464,256]{1,0:T(8,128)(2,1)S(1)} copy-done((bf16[14464,256]{1,0:T(8,128)(2,1)S(1)}, bf16[14464,256]{1,0:T(8,128)(2,1)}, u32[]{:S(2)}) %copy-start) | copy-done | bytes 7405592
  203.1 2.8 %copy-done.1 = bf16[12416,256]{1,0:T(8,128)(2,1)S(1)} copy-done((bf16[12416,256]{1,0:T(8,128)(2,1)S(1)}, bf16[12416,256]{1,0:T(8,128)(2,1)}, u32[]{:S(2)}) %copy-start.1) | copy-done | bytes 6357016
  205.9 15.5 %shard_map.61 = bf16[32,256,256]{2,1,0:T(8,128)(2,1)} custom-call(s32[32]{0:T(128)S(1)} %get-tuple-element.7.counts, s32[32,8]{1,0:T(8,128)S(1)} %get-tuple-element.13.lefts, s32[32,8]{1,0:T(8,128)S(1)} %get-tuple-element.12.rights, s32[32]{0:T(128)S(1)} %add.139.owns, s32[8]{0:T(128)S(1)} %copy-done.2, s32[1]{0:T(128)} %bitcast.12.place_ref, ...), custom_call_target="tpu_custom_call" | custom-call | tf_op jit(solution)/shard_map/pallas_call | solution.py:145
  (91 shorter events, 11.6 us)
Async XLA Ops:
  7.2 27.1 %copy-start.4 = (s32[8,2]{0,1:T(2,128)S(1)}, s32[8,2]{0,1:T(2,128)}, u32[]{:S(2)}) copy-start(s32[8,2]{0,1:T(2,128)} %param.5) | copy-start | bytes 196
  7.2 150.8 %all-gather.7.cloned.1.call-start = ((), (), s32[]{:S(2)}) async-start(), calls=%async_computation.1 | async-start | bytes 7151616 | tf_op jit(solution)/shard_map/all_gather | solution.py:226
  14.1 87.3 %copy-start.5 = (s32[8,4]{0,1:T(4,128)S(1)}, s32[8,4]{0,1:T(4,128)}, u32[]{:S(2)}) copy-start(s32[8,4]{0,1:T(4,128)} %param.6) | copy-start | bytes 388
  14.1 104.4 %copy-start.3 = (s32[8,2]{1,0:T(8,128)S(1)}, s32[8,2]{1,0:T(8,128)}, u32[]{:S(2)}) copy-start(s32[8,2]{1,0:T(8,128)} %copy.64.cols_ref) | copy-start | bytes 196
  19.9 180.1 %copy-start.2 = (s32[8]{0:T(128)S(1)}, s32[8]{0:T(128)}, u32[]{:S(2)}) copy-start(s32[8]{0:T(128)} %flags.1) | copy-start | bytes 100
  34.2 162.0 %all-gather.5.cloned.1.call-start = ((), (), s32[]{:S(2)}) async-start(), calls=%async_computation | async-start | bytes 8331264 | tf_op jit(solution)/shard_map/all_gather | solution.py:226
  65.0 21.5 %collective-permute-start = (bf16[1808,256]{1,0:T(8,128)(2,1)}, bf16[1808,256]{1,0:T(8,128)(2,1)S(1)}, u32[]{:S(2)}, u32[]{:S(2)}) collective-permute-start(bf16[1808,256]{1,0:T(8,128)(2,1)} %shard_map.59), channel_id=1, source_target_pairs={{0,1},{1,0},{2,3},{3,2},{4,5},{5,4},{6,7},{7,6},{8,9},{9,8},{10,11... | collective-permute-start | bytes 2777096 | tf_op jit(solution)/shard_map/ppermute | solution.py:162
  72.1 28.0 %collective-permute-start.1 = (bf16[1808,256]{1,0:T(8,128)(2,1)}, bf16[1808,256]{1,0:T(8,128)(2,1)S(1)}, u32[]{:S(2)}, u32[]{:S(2)}) collective-permute-start(bf16[1808,256]{1,0:T(8,128)(2,1)} %shard_map.59), channel_id=1, source_target_pairs={{1,2},{2,1},{5,6},{6,5},{9,10},{10,9},{13,14},{14,13},{17,18},{18,... | collective-permute-start | bytes 2777096 | tf_op jit(solution)/shard_map/ppermute | solution.py:162
  86.5 32.4 %collective-permute-start.3 = (bf16[1808,256]{1,0:T(8,128)(2,1)S(1)}, bf16[1808,256]{1,0:T(8,128)(2,1)S(1)}, u32[]{:S(2)}, u32[]{:S(2)}) collective-permute-start(bf16[1808,256]{1,0:T(8,128)(2,1)S(1)} %collective-permute-done.refs_2_), channel_id=1, source_target_pairs={{1,2},{2,1},{5,6},{6,5},{9,10},{10,9},{13,14},{14,13},{17,18},{18,... | collective-permute-start | bytes 2777096 | tf_op jit(solution)/shard_map/ppermute | solution.py:162
  87.2 29.8 %collective-permute-start.5 = (bf16[1552,256]{1,0:T(8,128)(2,1)}, bf16[1552,256]{1,0:T(8,128)(2,1)}, u32[]{:S(2)}, u32[]{:S(2)}) collective-permute-start(bf16[1552,256]{1,0:T(8,128)(2,1)} %shard_map.60), channel_id=1, source_target_pairs={{0,1},{1,0},{2,3},{3,2},{4,5},{5,4},{6,7},{7,6},{8,9},{9,8},{10,11... | collective-permute-start | bytes 2383880 | tf_op jit(solution)/shard_map/ppermute | solution.py:162
  98.1 22.4 %collective-permute-start.6 = (bf16[1552,256]{1,0:T(8,128)(2,1)}, bf16[1552,256]{1,0:T(8,128)(2,1)}, u32[]{:S(2)}, u32[]{:S(2)}) collective-permute-start(bf16[1552,256]{1,0:T(8,128)(2,1)} %shard_map.60), channel_id=1, source_target_pairs={{1,2},{2,1},{5,6},{6,5},{9,10},{10,9},{13,14},{14,13},{17,18},{18,... | collective-permute-start | bytes 2383880 | tf_op jit(solution)/shard_map/ppermute | solution.py:162
  100.1 36.7 %collective-permute-start.2 = (bf16[1808,256]{1,0:T(8,128)(2,1)S(1)}, bf16[1808,256]{1,0:T(8,128)(2,1)}, u32[]{:S(2)}, u32[]{:S(2)}) collective-permute-start(bf16[1808,256]{1,0:T(8,128)(2,1)S(1)} %collective-permute-done.1.refs_4_), channel_id=1, source_target_pairs={{1,0},{2,3},{5,4},{6,7},{9,8},{10,11},{13,12},{14,15},{17,16},{18,... | collective-permute-start | bytes 2777096 | tf_op jit(solution)/shard_map/ppermute | solution.py:162
  117.0 5.0 %collective-permute-start.8 = (bf16[1552,256]{1,0:T(8,128)(2,1)}, bf16[1552,256]{1,0:T(8,128)(2,1)}, u32[]{:S(2)}, u32[]{:S(2)}) collective-permute-start(bf16[1552,256]{1,0:T(8,128)(2,1)} %collective-permute-done.5.refs_7_), channel_id=1, source_target_pairs={{1,2},{2,1},{5,6},{6,5},{9,10},{10,9},{13,14},{14,13},{17,18},{18,... | collective-permute-start | bytes 2383880 | tf_op jit(solution)/shard_map/ppermute | solution.py:162
  118.9 37.7 %collective-permute-start.4 = (bf16[1808,256]{1,0:T(8,128)(2,1)S(1)}, bf16[1808,256]{1,0:T(8,128)(2,1)}, u32[]{:S(2)}, u32[]{:S(2)}) collective-permute-start(bf16[1808,256]{1,0:T(8,128)(2,1)S(1)} %collective-permute-done.3.refs_6_), channel_id=1, source_target_pairs={{1,0},{2,3},{5,4},{6,7},{9,8},{10,11},{13,12},{14,15},{17,16},{18,... | collective-permute-start | bytes 2777096 | tf_op jit(solution)/shard_map/ppermute | solution.py:162
  120.5 79.4 %collective-permute-start.7 = (bf16[1552,256]{1,0:T(8,128)(2,1)}, bf16[1552,256]{1,0:T(8,128)(2,1)}, u32[]{:S(2)}, u32[]{:S(2)}) collective-permute-start(bf16[1552,256]{1,0:T(8,128)(2,1)} %collective-permute-done.6.refs_9_), channel_id=1, source_target_pairs={{1,0},{2,3},{5,4},{6,7},{9,8},{10,11},{13,12},{14,15},{17,16},{18,... | collective-permute-start | bytes 2383880 | tf_op jit(solution)/shard_map/ppermute | solution.py:162
  122.0 78.0 %collective-permute-start.9 = (bf16[1552,256]{1,0:T(8,128)(2,1)}, bf16[1552,256]{1,0:T(8,128)(2,1)}, u32[]{:S(2)}, u32[]{:S(2)}) collective-permute-start(bf16[1552,256]{1,0:T(8,128)(2,1)} %collective-permute-done.8.refs_11_), channel_id=1, source_target_pairs={{1,0},{2,3},{5,4},{6,7},{9,8},{10,11},{13,12},{14,15},{17,16},{18,... | collective-permute-start | bytes 2383880 | tf_op jit(solution)/shard_map/ppermute | solution.py:162
  159.3 30.4 %collective-permute-start.10 = (f32[]{:T(128)}, f32[]{:T(128)}, u32[]{:S(2)}, u32[]{:S(2)}) collective-permute-start(f32[]{:T(128)} %fusion.13), channel_id=1, source_target_pairs={{0,1},{1,0},{2,3},{3,2},{4,5},{5,4},{6,7},{7,6},{8,9},{9,8},{10,11... | collective-permute-start | bytes 20 | tf_op jit(solution)/shard_map/ppermute | solution.py:162
  191.0 4.6 %collective-permute-start.11 = (f32[]{:T(128)}, f32[]{:T(128)}, u32[]{:S(2)}, u32[]{:S(2)}) collective-permute-start(f32[]{:T(128)} %add.143), channel_id=1, source_target_pairs={{0,2},{1,3},{2,0},{3,1},{4,6},{5,7},{6,4},{7,5},{8,10},{9,11},{10,... | collective-permute-start | bytes 20 | tf_op jit(solution)/shard_map/ppermute | solution.py:162
  200.0 3.1 %copy-start = (bf16[14464,256]{1,0:T(8,128)(2,1)S(1)}, bf16[14464,256]{1,0:T(8,128)(2,1)}, u32[]{:S(2)}) copy-start(bf16[14464,256]{1,0:T(8,128)(2,1)} %all-gather.5.cloned.1.call-done) | copy-start | bytes 22216708
  203.1 2.8 %copy-start.1 = (bf16[12416,256]{1,0:T(8,128)(2,1)S(1)}, bf16[12416,256]{1,0:T(8,128)(2,1)}, u32[]{:S(2)}) copy-start(bf16[12416,256]{1,0:T(8,128)(2,1)} %all-gather.7.cloned.1.call-done) | copy-start | bytes 19070980
Sparse Core Ops, SparseCore 0:
  34.3 59.4 all-gather.6
  96.3 50.2 all-gather.4

commit v3 on v2

--- a/solution.py
+++ b/solution.py
@@ -13,43 +13,88 @@
 NOTE_ROWS = 16
 
 
-def pack_kernel(first, limit, cols_ref, x_ref, note_ref, out_ref, sems):
+def pack_kernel(cols_ref, flag_ref, first_ref, x_ref, part_a, part_b, full, note, norm, sems):
     count, block, _ = x_ref.shape
-    slots = cols_ref.shape[1]
-    note = pltpu.make_async_copy(
-        note_ref, out_ref.at[pl.ds((limit - first) * block, NOTE_ROWS)], sems.at[count]
-    )
-    note.start()
-    copies = []
+    slots = cols_ref.shape[0]
+    rows = count // slots
+    sends = []
     place = jnp.int32(0)
     for index in range(count):
-        filled = cols_ref[index // slots, index % slots] >= 0
-        wanted = filled & (place >= first) & (place < limit)
-        target = pl.multiple_of(jnp.where(wanted, place - first, 0) * block, block)
-        copy = pltpu.make_async_copy(
-            x_ref.at[index], out_ref.at[pl.ds(target, block)], sems.at[index]
+        filled = cols_ref[index % slots, index // slots] >= 0
+        targets = (
+            (full, filled, place),
+            (part_a, filled & (place < SPLIT), place),
+            (part_b, filled & (place >= SPLIT), place - SPLIT),
         )
-        pl.when(wanted)(copy.start)
-        copies.append((wanted, copy))
+        for which, (out, wanted, target) in enumerate(targets):
+            target = pl.multiple_of(jnp.where(wanted, target, 0) * block, block)
+            copy = pltpu.make_async_copy(
+                x_ref.at[index], out.at[pl.ds(target, block)], sems.at[which, index]
+            )
+            pl.when(wanted)(copy.start)
+            sends.append((wanted, copy))
         place = place + filled.astype(jnp.int32)
-    for wanted, copy in copies:
-        pl.when(wanted)(copy.wait)
-    note.wait()
-
-
-def pack(x_blocks, x_cols, note, first, limit):
+
+    norm[...] = jnp.zeros_like(norm)
+    eye_rows = lax.broadcasted_iota(jnp.int32, (block, block), 0)
+    eye = eye_rows == lax.broadcasted_iota(jnp.int32, (block, block), 1)
+    for index in range(count):
+        row = index // slots
+        col = cols_ref[index % slots, row]
+        flag = flag_ref[row]
+
+        @pl.when(col >= 0)
+        def _():
+            values = x_ref[index].astype(jnp.float32)
+            weight = (1 - 2 * flag).astype(jnp.float32)
+            norm[...] += weight * jnp.sum(values * values, axis=0, keepdims=True)
+
+        @pl.when((col == first_ref[0] + row) & (flag != 0))
+        def _():
+            values = x_ref[index].astype(jnp.float32)
+            norm[...] += 2.0 * jnp.sum(jnp.where(eye, values, 0.0), axis=0, keepdims=True)
+
+    trace = jnp.full(note.shape, jnp.sum(norm[...]), jnp.float32)
+    high = trace.astype(note.dtype).astype(jnp.float32)
+    middle = (trace - high).astype(note.dtype).astype(jnp.float32)
+    low = trace - high - middle
+    down = lax.broadcasted_iota(jnp.int32, note.shape, 0)
+    across = lax.broadcasted_iota(jnp.int32, note.shape, 1)
+    facts = jnp.where(across == 0, high, jnp.where(across == 1, middle, low))
+    facts = jnp.where((down == rows) & (across < 3), facts, 0.0)
+    for index in range(count):
+        here = (down == index // slots) & (across == index % slots)
+        facts = jnp.where(here, cols_ref[index % slots, index // slots].astype(jnp.float32), facts)
+    note[...] = facts.astype(note.dtype)
+    for which, out in enumerate((full, part_a, part_b)):
+        target = out.at[pl.ds(out.shape[0] - NOTE_ROWS, NOTE_ROWS)]
+        copy = pltpu.make_async_copy(note, target, sems.at[which, count])
+        copy.start()
+        sends.append((None, copy))
+    for wanted, copy in sends:
+        copy.wait() if wanted is None else pl.when(wanted)(copy.wait)
+
+
+def pack(x_blocks, x_cols, branch_flag, first_row):
     rows, slots, block, _ = x_blocks.shape
     count = rows * slots
-    hbm = pl.BlockSpec(memory_space=pl.ANY)
+    smem = pl.BlockSpec(memory_space=pltpu.SMEM)
+    hbm = pl.BlockSpec(memory_space=pltpu.HBM)
     return pl.pallas_call(
-        functools.partial(pack_kernel, first, limit),
-        out_shape=jax.ShapeDtypeStruct(
-            ((limit - first) * block + NOTE_ROWS, block), x_blocks.dtype
-        ),
-        in_specs=[pl.BlockSpec(memory_space=pltpu.SMEM), hbm, hbm],
-        out_specs=hbm,
-        scratch_shapes=[pltpu.SemaphoreType.DMA((count + 1,))],
-    )(x_cols, x_blocks.reshape(count, block, block), note)
+        pack_kernel,
+        out_shape=[
+            jax.ShapeDtypeStruct((size * block + NOTE_ROWS, block), x_blocks.dtype)
+            for size in (SPLIT, PACKED - SPLIT, PACKED)
+        ],
+        in_specs=[smem, smem, smem, pl.BlockSpec(memory_space=pltpu.VMEM)],
+        out_specs=[hbm] * 3,
+        scratch_shapes=[
+            pltpu.VMEM((NOTE_ROWS, block), x_blocks.dtype),
+            pltpu.VMEM((1, block), jnp.float32),
+            pltpu.SemaphoreType.DMA((3, count + 1)),
+        ],
+        compiler_params=pltpu.CompilerParams(vmem_limit_bytes=(4 * count * block * block) + (8 << 20)),
+    )(x_cols.T, branch_flag, first_row.reshape(1), x_blocks.reshape(count, block, block))
 
 
 def multiply_kernel(loads, kept, counts, lefts, rights, owns, flags, place_ref, *refs):
@@ -140,7 +185,7 @@
 def multiply(arrays, loads, n_entries, tables, place, kept, block, dtype):
     outputs = tables[0].shape[0]
     smem = pl.BlockSpec(memory_space=pltpu.SMEM)
-    hbm = pl.BlockSpec(memory_space=pl.ANY)
+    hbm = pl.BlockSpec(memory_space=pltpu.HBM)
     pool_bytes = n_entries * PACKED * block * block * 2
     return pl.pallas_call(
         functools.partial(multiply_kernel, loads, kept),
@@ -182,24 +227,6 @@
     return running_count(flat).reshape(cols.shape)
 
 
-def local_trace(x_blocks, x_cols, branch_flag, first_row):
-    rows, slots, block, _ = x_blocks.shape
-    own_row = first_row + jnp.arange(rows, dtype=jnp.int32)
-    flag = branch_flag.astype(jnp.float32)[:, None]
-    norm_weight = jnp.where(x_cols >= 0, 1.0 - 2.0 * flag, 0.0)
-    diag_weight = jnp.where(x_cols == own_row[:, None], 2.0 * flag, 0.0)
-    values = x_blocks.astype(jnp.float32)
-    eye = jnp.eye(block, dtype=jnp.float32)
-    weight = norm_weight[:, :, None, None] * values + diag_weight[:, :, None, None] * eye
-    return jnp.sum(weight * values)
-
-
-def thirds(value):
-    high = lax.reduce_precision(value, 8, 7)
-    middle = lax.reduce_precision(value - high, 8, 7)
-    return jnp.stack([high, middle, value - high - middle]).astype(jnp.bfloat16)
-
-
 def per_device(x_blocks, x_cols, out_cols, branch_flag):
     rows, slots = x_cols.shape
     kept = out_cols.shape[1]
@@ -211,22 +238,17 @@
     col = lax.axis_index("col")
     n_blocks = n_row * rows
 
-    def note(values):
-        pad = [(0, NOTE_ROWS - values.shape[0]), (0, block - values.shape[1])]
-        return jnp.pad(values.astype(dtype), pad)
-
-    part_a = pack(x_blocks, x_cols, note(x_cols), 0, SPLIT)
-    trace_part = local_trace(x_blocks, x_cols, branch_flag, row * rows)
-    part_b = pack(x_blocks, x_cols, note(thirds(trace_part)[None, :]), SPLIT, PACKED)
+    part_a, part_b, full = pack(x_blocks, x_cols, branch_flag, row * rows)
     parts = (part_a, part_b)
 
     def facts(array):
-        return array[..., SPLIT * block : SPLIT * block + rows, :slots].astype(jnp.int32)
-
-    plane = [lax.all_gather(part, "row", axis=0) for part in parts]
+        first = array.shape[-2] - NOTE_ROWS
+        return array[..., first : first + rows, :slots].astype(jnp.int32)
+
+    plane = lax.all_gather(full, "row", axis=0)
     spans = ((0, SPLIT), (SPLIT, PACKED - SPLIT))
-    arrays = list(plane)
-    loads = [(which, None, 0, n_row) + spans[which] + (None,) for which in range(2)]
+    arrays = [plane]
+    loads = [(0, None, 0, n_row, 0, PACKED, None)]
     if n_col == 4:
         line = [gather_line(part) for part in parts]
         n_left = 3
@@ -258,17 +280,19 @@
     n_entries = n_row + n_left + 1
     nothing = (n_entries - 1) * STRIDE
 
-    trace = jnp.sum(plane[1][:, (PACKED - SPLIT) * block, :3].astype(jnp.float32))
-    mask = 1
-    while mask < n_col:
-        trace = trace + shift(trace, [(i, i ^ mask) for i in range(n_col)])
-        mask *= 2
+    own_trace = jnp.sum(plane[:, PACKED * block + rows, :3].astype(jnp.float32))
+    heights = jnp.arange(n_col, dtype=jnp.int32)
+    traces = jnp.where(heights == col, own_trace, 0.0)
+    for step in range(1, n_col):
+        other = shift(own_trace, [(i, i ^ step) for i in range(n_col)])
+        traces = jnp.where(heights == jnp.bitwise_xor(col, step), other, traces)
+    trace = jnp.sum(traces)
 
     every = jnp.arange(n_blocks, dtype=jnp.int32)
     left_at = places(left_cols) + STRIDE * left_entries[:, None, None]
     hit = left_cols[..., None] == every
     left_of = jnp.sum(jnp.where(hit, left_at[..., None] + 1, 0), axis=(0, 2))
-    right_cols = facts(plane[0])
+    right_cols = facts(plane)
     right_at = places(right_cols) + STRIDE * jnp.arange(n_row, dtype=jnp.int32)[:, None, None]
     right_cols = right_cols.reshape(n_blocks, slots)
     right_at = right_at.reshape(n_blocks, slots)

time: 231 us -> 168 us (0.73)
  Pallas kernels: 59.8 us -> 18.9 us
  starting transfers between devices: 33.8 us -> 22.7 us
  between operations: 22.3 us -> 14.3 us
  waiting for transfers between devices: 90.8 us -> 85.9 us
  local copies, waits for them, and re-layouts: 10.1 us -> 13.7 us
    pallas_call x2 -> x1, Pallas kernels: 44.3 us -> 3.75 us  [pack(): pl.pallas_call(pack_kernel, out_shape=[jax.ShapeDtypeStruct((size * block...]
    ppermute x12 -> x13, starting transfers between devices: 33.8 us -> 22.6 us  [shift(): return lax.ppermute(array, 'col', pairs)]
    ppermute x12 -> x13, waiting for transfers between devices: 90.7 us -> 85.8 us  [shift(): return lax.ppermute(array, 'col', pairs)]
    unnamed x14 -> x16, local copies, waits for them, and re-layouts: 7.34 us -> 11.8 us
  transfers between devices with their start and end apart: 14 -> 14, of which waited for: 6 -> 6; matrix products, arithmetic and copies ran while one was open for 4% -> 7% of each run, Pallas kernels for 13% -> 9%
where the time goes in v3:
time: 168 us; the launch traced here: 167 us
  waiting for transfers between devices  85.9 us (51%)
  starting transfers between devices  22.7 us (14%)
  Pallas kernels  18.9 us (11%)
  between operations  14.3 us (9%)
  local copies, waits for them, and re-layouts  13.7 us (8%)
  other arithmetic  11.6 us (7%)
    ppermute x13, waiting for transfers between devices, shift(): return lax.ppermute(array, 'col', pairs)  85.8 us
    ppermute x13, starting transfers between devices, shift(): return lax.ppermute(array, 'col', pairs)  22.6 us
    pallas_call x1, Pallas kernels, multiply(): pl.pallas_call(functools.partial(multiply_kernel, loads, kept), out_shape...  15.1 us
    unnamed x16, local copies, waits for them, and re-layouts  11.8 us
    pallas_call x1, Pallas kernels, pack(): pl.pallas_call(pack_kernel, out_shape=[jax.ShapeDtypeStruct((size * block...  3.75 us
  transfers between devices with their start and end apart: 14, of which 6 were waited for; matrix products, arithmetic and copies ran while one was open for 7% of the time, Pallas kernels for 9%

profile of v3, /device:TPU:0, one launch (start us, length us, event | category | flops | bytes accessed | tf_op | source)
XLA Modules:
  0.0 167.1 jit_solution(15205206225488617655)
XLA Ops:
  7.2 1.6 copy-done.1
  10.1 3.8 %shard_map.59 = (bf16[1808,256]{1,0:T(8,128)(2,1)S(1)}, bf16[1552,256]{1,0:T(8,128)(2,1)S(1)}, bf16[3344,256]{1,0:T(8,128)(2,1)}) custom-call(s32[2,8]{1,0:T(2,128)S(1)} %bitcast.24, s32[8]{0:T(128)S(1)} %copy-done.3, s32[1]{0:T(128)} %bitcast.1.first_ref, bf16[16,256,256]{2,1,0:T(8,128)(2,1)S(1)} %bitcast.22), custom_call_target="tpu_custom_call" | custom-call | tf_op jit(solution)/shard_map/pallas_call | solution.py:83
  14.8 0.9 copy-done.6
  15.8 4.0 %collective-permute-start = (bf16[1808,256]{1,0:T(8,128)(2,1)}, bf16[1808,256]{1,0:T(8,128)(2,1)S(1)}, u32[]{:S(2)}, u32[]{:S(2)}) collective-permute-start(bf16[1808,256]{1,0:T(8,128)(2,1)} %copy-done.5), channel_id=1, source_target_pairs={{0,1},{1,0},{2,3},{3,2},{4,5},{5,4},{6,7},{7,6},{8,9},{9,8},{10,11... | collective-permute-start | bytes 2777096 | tf_op jit(solution)/shard_map/ppermute | solution.py:207
  20.5 19.6 %collective-permute-done.refs_1_ = bf16[1808,256]{1,0:T(8,128)(2,1)S(1)} collective-permute-done((bf16[1808,256]{1,0:T(8,128)(2,1)}, bf16[1808,256]{1,0:T(8,128)(2,1)S(1)}, u32[]{:S(2)}, u32[]{:S(2)}) %collective-permute-start) | collective-permute-done | bytes 925728 | tf_op jit(solution)/shard_map/ppermute | solution.py:207
  40.9 4.6 %collective-permute-start.5 = (bf16[1552,256]{1,0:T(8,128)(2,1)}, bf16[1552,256]{1,0:T(8,128)(2,1)}, u32[]{:S(2)}, u32[]{:S(2)}) collective-permute-start(bf16[1552,256]{1,0:T(8,128)(2,1)} %copy-done.6), channel_id=1, source_target_pairs={{0,1},{1,0},{2,3},{3,2},{4,5},{5,4},{6,7},{7,6},{8,9},{9,8},{10,11... | collective-permute-start | bytes 2383880 | tf_op jit(solution)/shard_map/ppermute | solution.py:207
  45.5 1.5 collective-permute-start.6
  48.1 1.3 collective-permute-start.2
  50.1 14.3 %collective-permute-done.5.refs_6_ = bf16[1552,256]{1,0:T(8,128)(2,1)} collective-permute-done((bf16[1552,256]{1,0:T(8,128)(2,1)}, bf16[1552,256]{1,0:T(8,128)(2,1)}, u32[]{:S(2)}, u32[]{:S(2)}) %collective-permute-start.5) | collective-permute-done | bytes 794656 | tf_op jit(solution)/shard_map/ppermute | solution.py:207
  64.4 1.5 collective-permute-start.8
  66.0 1.3 collective-permute-start.4
  69.4 1.3 collective-permute-start.7
  70.9 1.3 collective-permute-start.9
  72.2 12.1 %collective-permute-done.2.refs_2_ = bf16[1808,256]{1,0:T(8,128)(2,1)} collective-permute-done((bf16[1808,256]{1,0:T(8,128)(2,1)S(1)}, bf16[1808,256]{1,0:T(8,128)(2,1)}, u32[]{:S(2)}, u32[]{:S(2)}) %collective-permute-start.2) | collective-permute-done | bytes 925728 | tf_op jit(solution)/shard_map/ppermute | solution.py:207
  85.0 19.0 %collective-permute-done.4.refs_4_ = bf16[1808,256]{1,0:T(8,128)(2,1)} collective-permute-done((bf16[1808,256]{1,0:T(8,128)(2,1)S(1)}, bf16[1808,256]{1,0:T(8,128)(2,1)}, u32[]{:S(2)}, u32[]{:S(2)}) %collective-permute-start.4) | collective-permute-done | bytes 925728 | tf_op jit(solution)/shard_map/ppermute | solution.py:207
  106.1 1.4 fusion.1
  107.5 1.9 %collective-permute-start.11 = (f32[]{:T(128)}, f32[]{:T(128)}, u32[]{:S(2)}, u32[]{:S(2)}) collective-permute-start(f32[]{:T(128)} %fusion.1), channel_id=1, source_target_pairs={{0,2},{1,3},{2,0},{3,1},{4,6},{5,7},{6,4},{7,5},{8,10},{9,11},{10,... | collective-permute-start | bytes 20 | tf_op jit(solution)/shard_map/ppermute | solution.py:207
  109.4 2.5 %collective-permute-start.10 = (f32[]{:T(128)}, f32[]{:T(128)}, u32[]{:S(2)}, u32[]{:S(2)}) collective-permute-start(f32[]{:T(128)} %fusion.1), channel_id=1, source_target_pairs={{0,3},{1,2},{2,1},{3,0},{4,7},{5,6},{6,5},{7,4},{8,11},{9,10},{10,... | collective-permute-start | bytes 20 | tf_op jit(solution)/shard_map/ppermute | solution.py:207
  114.5 1.2 select_reduce_fusion.1
  115.7 5.4 %collective-permute-done.7.refs_7_ = bf16[1552,256]{1,0:T(8,128)(2,1)} collective-permute-done((bf16[1552,256]{1,0:T(8,128)(2,1)}, bf16[1552,256]{1,0:T(8,128)(2,1)}, u32[]{:S(2)}, u32[]{:S(2)}) %collective-permute-start.7) | collective-permute-done | bytes 794656 | tf_op jit(solution)/shard_map/ppermute | solution.py:207
  121.1 15.3 %collective-permute-done.9.refs_9_ = bf16[1552,256]{1,0:T(8,128)(2,1)} collective-permute-done((bf16[1552,256]{1,0:T(8,128)(2,1)}, bf16[1552,256]{1,0:T(8,128)(2,1)}, u32[]{:S(2)}, u32[]{:S(2)}) %collective-permute-start.9) | collective-permute-done | bytes 794656 | tf_op jit(solution)/shard_map/ppermute | solution.py:207
  136.4 4.9 %copy-done = bf16[26752,256]{1,0:T(8,128)(2,1)S(1)} copy-done((bf16[26752,256]{1,0:T(8,128)(2,1)S(1)}, bf16[26752,256]{1,0:T(8,128)(2,1)}, u32[]{:S(2)}) %copy-start) | copy-done | bytes 13697048
  142.0 15.1 %shard_map.60 = bf16[32,256,256]{2,1,0:T(8,128)(2,1)} custom-call(s32[32]{0:T(128)S(1)} %get-tuple-element.13.counts, s32[32,8]{1,0:T(8,128)S(1)} %get-tuple-element.15.lefts, s32[32,8]{1,0:T(8,128)S(1)} %get-tuple-element.14.rights, s32[32]{0:T(128)S(1)} %add.116.owns, s32[8]{0:T(128)S(1)} %copy-done.4, s32[1]{0:T(128)} %bitcast.14.place_ref, ...), custom_call_target="tpu_custom_call" | custom-call | tf_op jit(solution)/shard_map/pallas_call | solution.py:190
  157.1 3.1 %fusion.3 = f32[]{:T(128)} fusion(f32[]{:T(128)} %fusion.1, s32[]{:T(128)S(6)} %axis_index.25, f32[]{:T(128)} %collective-permute-done.12, s32[]{:T(128)S(6)} %xor.11, f32[]{:T(128)} %collective-permute-done.11, s32[]{:T(128)S(6)} %xor.10, f32[]{:T(128)} %collective-permute-done.10, s32[]{:T(128)S(6)} %xor.9), kind=kLoop, calls=%fused_computation.40 | loop fusion | flops 35 | bytes 36 | tf_op jit(solution)/shard_map/reduce_sum | solution.py:289
  (81 shorter events, 13.8 us)
Async XLA Ops:
  7.2 99.0 %all-gather.3.cloned.1.call-start = ((), (), s32[]{:S(2)}) async-start(), calls=%async_computation | async-start | bytes 15409152 | tf_op jit(solution)/shard_map/all_gather | solution.py:248
  7.2 1.6 copy-start.1
  8.8 0.7 copy-start.2
  9.5 0.7 copy-start.3
  13.9 0.9 copy-start.5
  14.8 0.9 copy-start.6
  15.8 24.4 %collective-permute-start = (bf16[1808,256]{1,0:T(8,128)(2,1)}, bf16[1808,256]{1,0:T(8,128)(2,1)S(1)}, u32[]{:S(2)}, u32[]{:S(2)}) collective-permute-start(bf16[1808,256]{1,0:T(8,128)(2,1)} %copy-done.5), channel_id=1, source_target_pairs={{0,1},{1,0},{2,3},{3,2},{4,5},{5,4},{6,7},{7,6},{8,9},{9,8},{10,11... | collective-permute-start | bytes 2777096 | tf_op jit(solution)/shard_map/ppermute | solution.py:207
  19.8 28.3 %collective-permute-start.1 = (bf16[1808,256]{1,0:T(8,128)(2,1)}, bf16[1808,256]{1,0:T(8,128)(2,1)S(1)}, u32[]{:S(2)}, u32[]{:S(2)}) collective-permute-start(bf16[1808,256]{1,0:T(8,128)(2,1)} %copy-done.5), channel_id=1, source_target_pairs={{1,2},{2,1},{5,6},{6,5},{9,10},{10,9},{13,14},{14,13},{17,18},{18,... | collective-permute-start | bytes 2777096 | tf_op jit(solution)/shard_map/ppermute | solution.py:207
  40.2 25.8 %collective-permute-start.3 = (bf16[1808,256]{1,0:T(8,128)(2,1)S(1)}, bf16[1808,256]{1,0:T(8,128)(2,1)S(1)}, u32[]{:S(2)}, u32[]{:S(2)}) collective-permute-start(bf16[1808,256]{1,0:T(8,128)(2,1)S(1)} %collective-permute-done.refs_1_), channel_id=1, source_target_pairs={{1,2},{2,1},{5,6},{6,5},{9,10},{10,9},{13,14},{14,13},{17,18},{18,... | collective-permute-start | bytes 2777096 | tf_op jit(solution)/shard_map/ppermute | solution.py:207
  40.9 23.5 %collective-permute-start.5 = (bf16[1552,256]{1,0:T(8,128)(2,1)}, bf16[1552,256]{1,0:T(8,128)(2,1)}, u32[]{:S(2)}, u32[]{:S(2)}) collective-permute-start(bf16[1552,256]{1,0:T(8,128)(2,1)} %copy-done.6), channel_id=1, source_target_pairs={{0,1},{1,0},{2,3},{3,2},{4,5},{5,4},{6,7},{7,6},{8,9},{9,8},{10,11... | collective-permute-start | bytes 2383880 | tf_op jit(solution)/shard_map/ppermute | solution.py:207
  45.5 23.9 %collective-permute-start.6 = (bf16[1552,256]{1,0:T(8,128)(2,1)}, bf16[1552,256]{1,0:T(8,128)(2,1)}, u32[]{:S(2)}, u32[]{:S(2)}) collective-permute-start(bf16[1552,256]{1,0:T(8,128)(2,1)} %copy-done.6), channel_id=1, source_target_pairs={{1,2},{2,1},{5,6},{6,5},{9,10},{10,9},{13,14},{14,13},{17,18},{18,... | collective-permute-start | bytes 2383880 | tf_op jit(solution)/shard_map/ppermute | solution.py:207
  48.1 36.1 %collective-permute-start.2 = (bf16[1808,256]{1,0:T(8,128)(2,1)S(1)}, bf16[1808,256]{1,0:T(8,128)(2,1)}, u32[]{:S(2)}, u32[]{:S(2)}) collective-permute-start(bf16[1808,256]{1,0:T(8,128)(2,1)S(1)} %collective-permute-done.1.refs_3_), channel_id=1, source_target_pairs={{1,0},{2,3},{5,4},{6,7},{9,8},{10,11},{13,12},{14,15},{17,16},{18,... | collective-permute-start | bytes 2777096 | tf_op jit(solution)/shard_map/ppermute | solution.py:207
  64.4 6.4 %collective-permute-start.8 = (bf16[1552,256]{1,0:T(8,128)(2,1)}, bf16[1552,256]{1,0:T(8,128)(2,1)}, u32[]{:S(2)}, u32[]{:S(2)}) collective-permute-start(bf16[1552,256]{1,0:T(8,128)(2,1)} %collective-permute-done.5.refs_6_), channel_id=1, source_target_pairs={{1,2},{2,1},{5,6},{6,5},{9,10},{10,9},{13,14},{14,13},{17,18},{18,... | collective-permute-start | bytes 2383880 | tf_op jit(solution)/shard_map/ppermute | solution.py:207
  66.0 38.1 %collective-permute-start.4 = (bf16[1808,256]{1,0:T(8,128)(2,1)S(1)}, bf16[1808,256]{1,0:T(8,128)(2,1)}, u32[]{:S(2)}, u32[]{:S(2)}) collective-permute-start(bf16[1808,256]{1,0:T(8,128)(2,1)S(1)} %collective-permute-done.3.refs_5_), channel_id=1, source_target_pairs={{1,0},{2,3},{5,4},{6,7},{9,8},{10,11},{13,12},{14,15},{17,16},{18,... | collective-permute-start | bytes 2777096 | tf_op jit(solution)/shard_map/ppermute | solution.py:207
  69.4 51.8 %collective-permute-start.7 = (bf16[1552,256]{1,0:T(8,128)(2,1)}, bf16[1552,256]{1,0:T(8,128)(2,1)}, u32[]{:S(2)}, u32[]{:S(2)}) collective-permute-start(bf16[1552,256]{1,0:T(8,128)(2,1)} %collective-permute-done.6.refs_8_), channel_id=1, source_target_pairs={{1,0},{2,3},{5,4},{6,7},{9,8},{10,11},{13,12},{14,15},{17,16},{18,... | collective-permute-start | bytes 2383880 | tf_op jit(solution)/shard_map/ppermute | solution.py:207
  70.9 65.6 %collective-permute-start.9 = (bf16[1552,256]{1,0:T(8,128)(2,1)}, bf16[1552,256]{1,0:T(8,128)(2,1)}, u32[]{:S(2)}, u32[]{:S(2)}) collective-permute-start(bf16[1552,256]{1,0:T(8,128)(2,1)} %collective-permute-done.8.refs_10_), channel_id=1, source_target_pairs={{1,0},{2,3},{5,4},{6,7},{9,8},{10,11},{13,12},{14,15},{17,16},{18,... | collective-permute-start | bytes 2383880 | tf_op jit(solution)/shard_map/ppermute | solution.py:207
  107.5 49.6 %collective-permute-start.12 = (f32[]{:T(128)}, f32[]{:T(128)}, u32[]{:S(2)}, u32[]{:S(2)}) collective-permute-start(f32[]{:T(128)} %fusion.1), channel_id=1, source_target_pairs={{0,1},{1,0},{2,3},{3,2},{4,5},{5,4},{6,7},{7,6},{8,9},{9,8},{10,11... | collective-permute-start | bytes 20 | tf_op jit(solution)/shard_map/ppermute | solution.py:207
  107.5 49.6 %collective-permute-start.11 = (f32[]{:T(128)}, f32[]{:T(128)}, u32[]{:S(2)}, u32[]{:S(2)}) collective-permute-start(f32[]{:T(128)} %fusion.1), channel_id=1, source_target_pairs={{0,2},{1,3},{2,0},{3,1},{4,6},{5,7},{6,4},{7,5},{8,10},{9,11},{10,... | collective-permute-start | bytes 20 | tf_op jit(solution)/shard_map/ppermute | solution.py:207
  109.4 47.7 %collective-permute-start.10 = (f32[]{:T(128)}, f32[]{:T(128)}, u32[]{:S(2)}, u32[]{:S(2)}) collective-permute-start(f32[]{:T(128)} %fusion.1), channel_id=1, source_target_pairs={{0,3},{1,2},{2,1},{3,0},{4,7},{5,6},{6,5},{7,4},{8,11},{9,10},{10,... | collective-permute-start | bytes 20 | tf_op jit(solution)/shard_map/ppermute | solution.py:207
  136.4 4.9 %copy-start = (bf16[26752,256]{1,0:T(8,128)(2,1)S(1)}, bf16[26752,256]{1,0:T(8,128)(2,1)}, u32[]{:S(2)}) copy-start(bf16[26752,256]{1,0:T(8,128)(2,1)} %all-gather.3.cloned.1.call-done) | copy-start | bytes 41091076
  141.3 0.7 copy-start.4
Sparse Core Ops, SparseCore 0:
  15.9 79.8 all-gather.2

commit v4 on v3

v4 whole, which is shorter than its diff:
```python
import functools

import jax
import jax.numpy as jnp
from jax import lax
from jax.experimental import pallas as pl
from jax.experimental.pallas import tpu as pltpu
from jax.sharding import PartitionSpec as P

PACKED = 13
SPLIT = (PACKED + 1) // 2
STRIDE = 1 << (PACKED - 1).bit_length()
NOTE_ROWS = 16


def pack_kernel(cols_ref, flag_ref, first_ref, x_ref, part_a, part_b, full, note, norm, sems):
    count, block, _ = x_ref.shape
    slots = cols_ref.shape[0]
    rows = count // slots
    sends = []
    place = jnp.int32(0)
    for index in range(count):
        filled = cols_ref[index % slots, index // slots] >= 0
        targets = (
            (full, filled, place),
            (part_a, filled & (place < SPLIT), place),
            (part_b, filled & (place >= SPLIT), place - SPLIT),
        )
        for which, (out, wanted, target) in enumerate(targets):
            target = pl.multiple_of(jnp.where(wanted, target, 0) * block, block)
            copy = pltpu.make_async_copy(
                x_ref.at[index], out.at[pl.ds(target, block)], sems.at[which, index]
            )
            pl.when(wanted)(copy.start)
            sends.append((wanted, copy))
        place = place + filled.astype(jnp.int32)

    norm[...] = jnp.zeros_like(norm)
    eye_rows = lax.broadcasted_iota(jnp.int32, (block, block), 0)
    eye = eye_rows == lax.broadcasted_iota(jnp.int32, (block, block), 1)
    for index in range(count):
        row = index // slots
        col = cols_ref[index % slots, row]
        flag = flag_ref[row]

        @pl.when(col >= 0)
        def _():
            values = x_ref[index].astype(jnp.float32)
            weight = (1 - 2 * flag).astype(jnp.float32)
            norm[...] += weight * jnp.sum(values * values, axis=0, keepdims=True)

        @pl.when((col == first_ref[0] + row) & (flag != 0))
        def _():
            values = x_ref[index].astype(jnp.float32)
            norm[...] += 2.0 * jnp.sum(jnp.where(eye, values, 0.0), axis=0, keepdims=True)

    trace = jnp.full(note.shape, jnp.sum(norm[...]), jnp.float32)
    high = trace.astype(note.dtype).astype(jnp.float32)
    middle = (trace - high).astype(note.dtype).astype(jnp.float32)
    low = trace - high - middle
    down = lax.broadcasted_iota(jnp.int32, note.shape, 0)
    across = lax.broadcasted_iota(jnp.int32, note.shape, 1)
    facts = jnp.where(across == 0, high, jnp.where(across == 1, middle, low))
    facts = jnp.where((down == rows) & (across < 3), facts, 0.0)
    for index in range(count):
        here = (down == index // slots) & (across == index % slots)
        facts = jnp.where(here, cols_ref[index % slots, index // slots].astype(jnp.float32), facts)
    note[...] = facts.astype(note.dtype)
    for which, out in enumerate((full, part_a, part_b)):
        target = out.at[pl.ds(out.shape[0] - NOTE_ROWS, NOTE_ROWS)]
        copy = pltpu.make_async_copy(note, target, sems.at[which, count])
        copy.start()
        sends.append((None, copy))
    for wanted, copy in sends:
        copy.wait() if wanted is None else pl.when(wanted)(copy.wait)


def pack(x_blocks, x_cols, branch_flag, first_row):
    rows, slots, block, _ = x_blocks.shape
    count = rows * slots
    smem = pl.BlockSpec(memory_space=pltpu.SMEM)
    hbm = pl.BlockSpec(memory_space=pltpu.HBM)
    return pl.pallas_call(
        pack_kernel,
        out_shape=[
            jax.ShapeDtypeStruct((size * block + NOTE_ROWS, block), x_blocks.dtype)
            for size in (SPLIT, PACKED - SPLIT, PACKED)
        ],
        in_specs=[smem, smem, smem, pl.BlockSpec(memory_space=pltpu.VMEM)],
        out_specs=[hbm] * 3,
        scratch_shapes=[
            pltpu.VMEM((NOTE_ROWS, block), x_blocks.dtype),
            pltpu.VMEM((1, block), jnp.float32),
            pltpu.SemaphoreType.DMA((3, count + 1)),
        ],
        compiler_params=pltpu.CompilerParams(vmem_limit_bytes=(4 * count * block * block) + (8 << 20)),
    )(x_cols.T, branch_flag, first_row.reshape(1), x_blocks.reshape(count, block, block))


def multiply_kernel(
    loads, kept, first_turned, control, outs, counts, lefts, rights, owns, flags, *refs
):
    n_arrays = 1 + max(load[0] for load in loads)
    plane = refs[0]
    arrays = refs[:n_arrays]
    out_ref, pool, ring, total, done, in_sem, ring_sem, out_sem = refs[-8:]
    block = out_ref.shape[-1]
    n_out = control[0]
    n_terms = control[1]
    depth = ring.shape[0]
    width = done.shape[0]

    copies = []
    for number, (which, at, entry, first, size, wanted) in enumerate(loads):
        source = arrays[which]
        if at is not None:
            source = source.at[control[at] if at >= 0 else -at - 1]
        copy = pltpu.make_async_copy(
            source.at[pl.ds(0, size * block)],
            pool.at[entry, pl.ds(first * block, size * block)],
            in_sem.at[number],
        )
        copies.append(((control[wanted] != 0) & (n_out > 0), copy))
    for here, copy in copies:
        pl.when(here)(copy.start)

    def decode(index):
        entry = lax.shift_right_logical(index, STRIDE.bit_length() - 1)
        return entry, pl.multiple_of(jnp.bitwise_and(index, STRIDE - 1) * block, block)

    def fetch(term):
        entry, first = decode(rights[term])
        slot = lax.rem(term, depth)
        return pltpu.make_async_copy(
            plane.at[entry, pl.ds(first, block)], ring.at[slot], ring_sem.at[slot]
        )

    def begin(term, carry):
        fetch(term).start()
        return carry

    lax.fori_loop(0, jnp.minimum(depth, n_terms), begin, 0)
    for here, copy in copies:
        pl.when(here)(copy.wait)

    def write(number):
        slot = lax.rem(number, width)
        return pltpu.make_async_copy(done.at[slot], out_ref.at[outs[number]], out_sem.at[slot])

    def one_output(number, term):
        output = outs[number]
        total[...] = jnp.zeros_like(total)

        def one_term(term, carry):
            entry, first = decode(lefts[term])
            fetch(term).wait()
            left = pool[entry, pl.ds(first, block)]
            right = ring[lax.rem(term, depth)]

            def add(dims):
                total[...] += lax.dot_general(
                    left, right, (dims, ((), ())), preferred_element_type=jnp.float32
                )

            if first_turned is None:
                add(((1,), (0,)))
            else:
                pl.when(entry < first_turned)(lambda: add(((1,), (0,))))
                pl.when(entry >= first_turned)(lambda: add(((0,), (0,))))

            @pl.when(term + depth < n_terms)
            def _():
                fetch(term + depth).start()

            return carry

        last = term + counts[number]
        lax.fori_loop(term, last, one_term, 0)

        @pl.when(number >= width)
        def _():
            write(number - width).wait()

        flag = flags[output // kept].astype(jnp.float32)
        own = owns[output]
        _, first = decode(jnp.maximum(own, 0))
        weight = jnp.where(own >= 0, 2.0 * flag, 0.0)
        slot = lax.rem(number, width)

        @pl.when(weight == 0.0)
        def _():
            done[slot] = ((1.0 - 2.0 * flag) * total[...]).astype(done.dtype)

        @pl.when(weight != 0.0)
        def _():
            mine = pool[0, pl.ds(first, block)].astype(jnp.float32)
            done[slot] = (2.0 * mine - total[...]).astype(done.dtype)

        write(number).start()
        return last

    lax.fori_loop(0, n_out, one_output, jnp.int32(0))
    for back in range(width):
        @pl.when(n_out > back)
        def _():
            write(n_out - 1 - back).wait()


def multiply(arrays, loads, n_entries, first_turned, control, tables, shape, before=None):
    rows, kept, block, dtype = shape
    outputs = rows * kept
    smem = pl.BlockSpec(memory_space=pltpu.SMEM)
    hbm = pl.BlockSpec(memory_space=pltpu.HBM)
    depth = 32
    vmem = (n_entries * PACKED + depth + 4 + 2) * block * block * 2 + (8 << 20)
    operands = [control, *tables, *arrays]
    in_specs = [smem] * (1 + len(tables)) + [hbm] * len(arrays)
    aliases = {}
    if before is not None:
        operands += [before[1], before[0]]
        in_specs += [smem, hbm]
        aliases = {len(operands) - 1: 0}
    return pl.pallas_call(
        functools.partial(multiply_kernel, loads, kept, first_turned),
        out_shape=jax.ShapeDtypeStruct((outputs, block, block), dtype),
        in_specs=in_specs,
        out_specs=hbm,
        scratch_shapes=[
            pltpu.VMEM((n_entries, PACKED * block, block), dtype),
            pltpu.VMEM((depth, block, block), dtype),
            pltpu.VMEM((block, block), jnp.float32),
            pltpu.VMEM((4, block, block), dtype),
            pltpu.SemaphoreType.DMA((len(loads),)),
            pltpu.SemaphoreType.DMA((depth,)),
            pltpu.SemaphoreType.DMA((4,)),
        ],
        input_output_aliases=aliases,
        compiler_params=pltpu.CompilerParams(vmem_limit_bytes=vmem),
    )(*operands)


FOUR = range(4)
PLAN = {
    "first": [((q, 3), (q, 2)) for q in FOUR] + [((q, 1), (q, 0)) for q in (0, 1, 2)],
    "middle": [((q, 2), (q, 1)) for q in (0, 2, 3)],
    "middle_two": [((q, 2), (q, 1)) for q in FOUR],
    "end_two": [((q, 1), (q, 0)) for q in (0, 2, 3)],
    "end_three": [((1, 1), (1, 0))],
    "end_last": [((3, 1), (3, 0))],
    "turn_one": [((2, 0), (1, 0))],
    "turn_two": [((3, 0), (2, 0))],
    "turn_three": [((1, 0), (3, 0))],
}
TURNED = {(0, 0): 3, (1, 0): 2, (2, 0): 3, (3, 0): 1, (1, 1): 2}


def both_ends(moves):
    mirrored = [tuple((3 - q, 3 - c) for q, c in move) for move in moves]
    return list(moves) + mirrored


def send(array, name):
    n_col = lax.axis_size("col")
    pairs = []
    for (q, c), (q_to, c_to) in both_ends(PLAN[name]):
        for core in range(2):
            pairs.append(((2 * q + core) * n_col + c, (2 * q_to + core) * n_col + c_to))
    return lax.ppermute(array, ("row", "col"), sorted(pairs))


def gather_line(part):
    got = {"first": send(part, "first"), "middle": send(part, "middle")}
    got["end_two"] = send(got["middle"], "end_two")
    got["middle_two"] = send(got["first"], "middle_two")
    got["end_three"] = send(got["middle_two"], "end_three")
    got["end_last"] = send(got["middle_two"], "end_last")
    turned = send(got["first"], "turn_one") + send(got["end_two"], "turn_two")
    turned = turned + send(got["end_three"], "turn_three")
    got["turned"] = turned
    size = lax.axis_size("row")
    got["other"] = lax.ppermute(turned, "row", [(i, i ^ 1) for i in range(size)])
    return got


def arrives(name):
    table = [[0] * 4 for _ in range(4)]
    for _, (q, c) in both_ends(PLAN[name]):
        table[q][c] = 1
    return table


def look_up(table, pair, col):
    answer = jnp.int32(0)
    for q, line in enumerate(table):
        for c, value in enumerate(line):
            if value:
                answer = jnp.where((pair == q) & (col == c), value, answer)
    return answer


def running_count(fill):
    count = fill.shape[-1]
    before = jnp.arange(count)[:, None] < jnp.arange(count)[None, :]
    return jnp.sum(jnp.where(before, fill[..., :, None], 0), axis=-2)


def places(cols):
    flat = (cols >= 0).astype(jnp.int32).reshape(cols.shape[:-2] + (-1,))
    return running_count(flat).reshape(cols.shape)


def lists(left_of, right_of, chosen, width):
    kept = right_of.shape[0] // left_of.shape[0]
    outputs = right_of.shape[0]
    left_of = jnp.repeat(left_of, kept, axis=0)
    live = (left_of > 0) & (right_of > 0) & chosen[:, None]
    counts = jnp.sum(live.astype(jnp.int32), axis=1)
    term = jnp.where(live, running_count(live.astype(jnp.int32)), -1)
    across = jnp.arange(width, dtype=jnp.int32)
    pick = term[:, None, :] == across[:, None]
    lefts = jnp.sum(jnp.where(pick, left_of[:, None, :] - 1, 0), axis=2)
    rights = jnp.sum(jnp.where(pick, right_of[:, None, :] - 1, 0), axis=2)
    flat = jnp.where(across < counts[:, None], running_count(counts)[:, None] + across, -1)
    pick = flat[None] == jnp.arange(PACKED * width, dtype=jnp.int32)[:, None, None]
    lefts = jnp.sum(jnp.where(pick, lefts, 0), axis=(1, 2))
    rights = jnp.sum(jnp.where(pick, rights, 0), axis=(1, 2))
    every = jnp.arange(outputs, dtype=jnp.int32)
    number = jnp.where(chosen, running_count(chosen.astype(jnp.int32)), -1)
    pick = number[None, :] == every[:, None]
    outs = jnp.sum(jnp.where(pick, every, 0), axis=1)
    ordered = jnp.sum(jnp.where(pick, counts, 0), axis=1)
    sizes = jnp.stack([jnp.sum(chosen.astype(jnp.int32)), jnp.sum(counts)])
    return sizes, (outs, ordered, lefts, rights)


def per_device(x_blocks, x_cols, out_cols, branch_flag):
    rows, slots = x_cols.shape
    kept = out_cols.shape[1]
    block = x_blocks.shape[-1]
    dtype = x_blocks.dtype
    n_row = lax.axis_size("row")
    n_col = lax.axis_size("col")
    row = lax.axis_index("row")
    col = lax.axis_index("col")
    n_blocks = n_row * rows
    width = n_col * slots
    shape = (rows, kept, block, dtype)

    part_a, part_b, full = pack(x_blocks, x_cols, branch_flag, row * rows)

    def facts(array):
        first = array.shape[-2] - NOTE_ROWS
        return array[..., first : first + rows, :slots].astype(jnp.int32)

    plane = lax.all_gather(full, "row", axis=0)
    plane_cols = facts(plane)

    own_trace = jnp.sum(plane[:, PACKED * block + rows, :3].astype(jnp.float32))
    heights = jnp.arange(n_col, dtype=jnp.int32)
    traces = jnp.where(heights == col, own_trace, 0.0)
    for step in range(1, n_col):
        other = lax.ppermute(own_trace, "col", [(i, i ^ step) for i in range(n_col)])
        traces = jnp.where(heights == jnp.bitwise_xor(col, step), other, traces)
    trace = jnp.sum(traces).reshape(1)

    targets = out_cols.reshape(rows * kept)
    right_at = places(plane_cols) + STRIDE * jnp.arange(n_row, dtype=jnp.int32)[:, None, None]
    hit = plane_cols.reshape(n_blocks, slots)[None] == targets[:, None, None]
    right_of = jnp.sum(jnp.where(hit, right_at.reshape(n_blocks, slots) + 1, 0), axis=2)
    hit = x_cols[:, None, :] == out_cols[:, :, None]
    owns = jnp.sum(jnp.where(hit, places(x_cols)[:, None, :] + 1, 0), axis=2) - 1
    owns = owns.reshape(rows * kept)

    every = jnp.arange(n_blocks, dtype=jnp.int32)

    def straight(cols, entries, wanted):
        at = places(cols) + STRIDE * entries[:, None, None]
        hit = (cols[..., None] == every) & (wanted[:, None, None, None] != 0)
        return jnp.sum(jnp.where(hit, at[..., None] + 1, 0), axis=(0, 2))

    def turned(cols, entries, devices, wanted):
        at = places(cols) + STRIDE * entries[:, None, None]
        own = row * rows + jnp.arange(rows, dtype=jnp.int32)
        hit = (cols[..., None] == own) & (wanted != 0)
        found = jnp.sum(jnp.where(hit, at[..., None] + 1, 0), axis=2)
        names = devices[:, None] * rows + jnp.arange(rows, dtype=jnp.int32)
        found = jnp.where(names[:, :, None, None] == every, found[..., None], 0)
        return jnp.sum(found, axis=(0, 1))

    spans = ((0, SPLIT), (SPLIT, PACKED - SPLIT))
    everything = jnp.ones((rows * kept,), bool)
    one = jnp.ones((), jnp.int32)
    if not (n_col == 4 and n_row == 8):
        line = lax.all_gather(full, "col", axis=0)
        entries = 1 + jnp.arange(n_col, dtype=jnp.int32)
        left_of = straight(facts(line), entries, jnp.ones((n_col,), jnp.int32))
        sizes, tables = lists(left_of, right_of, everything, width)
        loads = [(2, None, 0, 0, PACKED, 2)]
        loads += [(1, -1 - c, 1 + c, 0, PACKED, 2) for c in range(n_col)]
        control = jnp.concatenate([sizes, one[None]])
        tables = tables + (owns, branch_flag)
        purified = multiply(
            [plane, line, full], tuple(loads), 1 + n_col, None, control, tables, shape
        )
        return purified.reshape(rows, kept, block, block), trace

    pair = row // 2
    core = row % 2
    line = [gather_line(part) for part in (part_a, part_b)]
    has = {name: look_up(arrives(name), pair, col) for name in PLAN}
    turn_table = [[0] * n_col for _ in FOUR]
    for (q, c), t in TURNED.items():
        turn_table[q][c] = t + 1
        turn_table[3 - q][3 - c] = 4 - t
    turn = look_up(turn_table, pair, col) - 1
    diagonal = (pair == col).astype(jnp.int32)
    moved = ((turn >= 0) & (diagonal == 0)).astype(jnp.int32)
    turn_devices = 2 * jnp.maximum(turn, 0) + jnp.stack([core, 1 - core])
    turn_entries = jnp.array([4, 5], jnp.int32)

    note = {name: facts(array) for name, array in line[0].items()}
    early_cols = jnp.stack(
        [
            x_cols,
            note["first"],
            jnp.where(has["middle"] != 0, note["middle"], note["end_two"]),
            note["middle_two"],
        ]
    )
    early_has = jnp.stack(
        [one, has["first"], has["middle"] + has["end_two"], has["middle_two"]]
    )
    early = straight(early_cols, jnp.arange(4, dtype=jnp.int32), early_has)
    plane_turned = jnp.stack(
        [lax.dynamic_index_in_dim(plane_cols, turn_devices[i], 0, keepdims=False) for i in range(2)]
    )
    early = early + turned(plane_turned, turn_entries, turn_devices, diagonal)

    arrays = [plane, full]
    loads = [(1, None, 0, 0, PACKED, 4)]
    loads += [(0, 2 + i, 4 + i, 0, PACKED, 5) for i in range(2)]
    names = ["first", "middle", "end_two", "middle_two"]
    late_names = ["end_three", "end_last", "turned", "other"]
    entry_of = {"first": 1, "middle": 2, "end_two": 2, "middle_two": 3}
    entry_of.update({"end_three": 3, "end_last": 3, "turned": 4, "other": 5})
    flag_of = {name: 6 + place for place, name in enumerate(names + late_names)}

    def add(some):
        for name in some:
            for which in range(2):
                loads.append((len(arrays), None, entry_of[name]) + spans[which] + (flag_of[name],))
                arrays.append(line[which][name])

    add(names)
    has["turned"] = has["other"] = moved
    flags = [turn_devices, one[None], diagonal[None]]
    flags += [has[name][None] for name in names + late_names]

    sizes, tables = lists(early, right_of, everything, width)
    control = jnp.concatenate([sizes] + flags)
    tables = tables + (owns, branch_flag)
    purified = multiply(list(arrays), tuple(loads), 6, 4, control, tables, shape)

    late_cols = jnp.where(has["end_three"] != 0, note["end_three"], note["end_last"])[None]
    late_has = (has["end_three"] + has["end_last"])[None]
    late = straight(late_cols, jnp.array([3], jnp.int32), late_has)
    late_turned = jnp.stack([note["turned"], note["other"]])
    late = late + turned(late_turned, turn_entries, turn_devices, moved)
    meets = (jnp.repeat(late, kept, axis=0) > 0) & (right_of > 0)
    chosen = jnp.any(meets, axis=1)
    add(late_names)
    sizes, tables = lists(early + late, right_of, chosen, width)
    control = jnp.concatenate([sizes] + flags)
    tables = tables + (owns, branch_flag)
    purified = multiply(
        list(arrays), tuple(loads), 6, 4, control, tables, shape, (purified, trace)
    )
    return purified.reshape(rows, kept, block, block), trace


def solution(mesh):
    in_specs = (P("row", "col", None, None), P("row", "col"), P("row", "col"), P("row"))
    out_specs = (P("row", "col", None, None), P())
    return jax.shard_map(
        per_device, mesh=mesh, in_specs=in_specs, out_specs=out_specs, check_vma=False
    )
```

time: 168 us -> 219 us (1.30)
  starting transfers between devices: 22.7 us -> 53 us
  Pallas kernels: 18.9 us -> 30.5 us
  other arithmetic: 11.6 us -> 22.1 us
  waiting for transfers between devices: 85.9 us -> 76.1 us
  local copies, waits for them, and re-layouts: 13.7 us -> 17.8 us
  between operations: 14.3 us -> 18.4 us
    ppermute x13 -> x23, starting transfers between devices: 22.6 us -> 53 us  [the longest x18 31.2 us: send(): return lax.ppermute(array, ('row', 'col'), sorted(pairs))]
    pallas_call x1 -> x2, Pallas kernels: 15.1 us -> 28.1 us  [multiply(): pl.pallas_call(functools.partial(multiply_kernel, loads, kept, first_turn...]
    ppermute x13 -> x23, waiting for transfers between devices: 85.8 us -> 76.1 us  [the longest x18 76 us: send(): return lax.ppermute(array, ('row', 'col'), sorted(pairs))]
    add x4 -> x9, other arithmetic: 0.09 us -> 5.38 us  [the longest x2 4.48 us: gather_line(): turned = turned + send(got['end_three'], 'turn_three')]
    reduce_sum x5 -> x12, other arithmetic: 5.11 us -> 8.17 us  [the longest x1 3.04 us: per_device(): trace = jnp.sum(traces).reshape(1)]
    unnamed x16 -> x18, local copies, waits for them, and re-layouts: 11.8 us -> 12.1 us
  transfers between devices with their start and end apart: 14 -> 24, of which waited for: 6 -> 4; matrix products, arithmetic and copies ran while one was open for 7% -> 13% of each run, Pallas kernels for 9% -> 12%
where the time goes in v4:
time: 219 us; the launch traced here: 218 us
  waiting for transfers between devices  76.1 us (35%)
  starting transfers between devices  53 us (24%)
  Pallas kernels  30.5 us (14%)
  other arithmetic  22.1 us (10%)
  between operations  18.4 us (8%)
  local copies, waits for them, and re-layouts  17.8 us (8%)
    ppermute x18, waiting for transfers between devices, send(): return lax.ppermute(array, ('row', 'col'), sorted(pairs))  76 us
    ppermute x18, starting transfers between devices, send(): return lax.ppermute(array, ('row', 'col'), sorted(pairs))  31.2 us
    pallas_call x2, Pallas kernels, multiply(): pl.pallas_call(functools.partial(multiply_kernel, loads, kept, first_turn...  28.1 us
    ppermute x3, starting transfers between devices, per_device(): lax.ppermute(own_trace, 'col', [(i, i ^ step) for i in range(n_col)])  21.2 us
    unnamed x18, local copies, waits for them, and re-layouts  12.1 us
    add x2, other arithmetic, gather_line(): turned = turned + send(got['end_three'], 'turn_three')  4.48 us
  transfers between devices with their start and end apart: 24, of which 4 were waited for; matrix products, arithmetic and copies ran while one was open for 13% of the time, Pallas kernels for 12%

profile of v4, /device:TPU:0, one launch (start us, length us, event | category | flops | bytes accessed | tf_op | source)
XLA Modules:
  0.0 217.9 jit_solution(10513093955227110699)
XLA Ops:
  7.2 1.6 copy-done.3
  10.1 2.4 %shard_map.77 = (bf16[1808,256]{1,0:T(8,128)(2,1)}, bf16[1552,256]{1,0:T(8,128)(2,1)}, bf16[3344,256]{1,0:T(8,128)(2,1)}) custom-call(s32[2,8]{1,0:T(2,128)S(1)} %bitcast.44, s32[8]{0:T(128)S(1)} %copy-done.5, s32[1]{0:T(128)} %bitcast.1.first_ref, bf16[16,256,256]{2,1,0:T(8,128)(2,1)S(1)} %bitcast.42), custom_call_target="tpu_custom_call" | custom-call | tf_op jit(solution)/shard_map/pallas_call | solution.py:83
  12.6 4.9 %collective-permute-start = (bf16[1808,256]{1,0:T(8,128)(2,1)}, bf16[1808,256]{1,0:T(8,128)(2,1)S(1)}, u32[]{:S(2)}, u32[]{:S(2)}) collective-permute-start(bf16[1808,256]{1,0:T(8,128)(2,1)} %get-tuple-element.5), channel_id=1, source_target_pairs={{0,1},{1,0},{3,2},{4,5},{5,4},{7,6},{8,9},{9,8},{10,11},{11,10},{1... | collective-permute-start | bytes 2777096 | tf_op jit(solution)/shard_map/ppermute | solution.py:268
  17.5 1.6 collective-permute-start.11
  19.1 3.3 %collective-permute-start.10 = (bf16[1552,256]{1,0:T(8,128)(2,1)}, bf16[1552,256]{1,0:T(8,128)(2,1)}, u32[]{:S(2)}, u32[]{:S(2)}) collective-permute-start(bf16[1552,256]{1,0:T(8,128)(2,1)} %get-tuple-element.7), channel_id=1, source_target_pairs={{0,1},{1,0},{3,2},{4,5},{5,4},{7,6},{8,9},{9,8},{10,11},{11,10},{1... | collective-permute-start | bytes 2383880 | tf_op jit(solution)/shard_map/ppermute | solution.py:268
  24.3 14.7 %collective-permute-done.refs_2_ = bf16[1808,256]{1,0:T(8,128)(2,1)S(1)} collective-permute-done((bf16[1808,256]{1,0:T(8,128)(2,1)}, bf16[1808,256]{1,0:T(8,128)(2,1)S(1)}, u32[]{:S(2)}, u32[]{:S(2)}) %collective-permute-start) | collective-permute-done | bytes 925728 | tf_op jit(solution)/shard_map/ppermute | solution.py:268
  42.7 1.6 collective-permute-start.2
  44.3 1.6 collective-permute-start.3
  51.1 4.2 %collective-permute-done.10.refs_3_ = bf16[1552,256]{1,0:T(8,128)(2,1)} collective-permute-done((bf16[1552,256]{1,0:T(8,128)(2,1)}, bf16[1552,256]{1,0:T(8,128)(2,1)}, u32[]{:S(2)}, u32[]{:S(2)}) %collective-permute-start.10) | collective-permute-done | bytes 794656 | tf_op jit(solution)/shard_map/ppermute | solution.py:268
  57.1 23.0 %collective-permute-done.6.refs_6_ = bf16[1808,256]{1,0:T(8,128)(2,1)} collective-permute-done((bf16[1808,256]{1,0:T(8,128)(2,1)S(1)}, bf16[1808,256]{1,0:T(8,128)(2,1)}, u32[]{:S(2)}, u32[]{:S(2)}) %collective-permute-start.6) | collective-permute-done | bytes 925728 | tf_op jit(solution)/shard_map/ppermute | solution.py:268
  80.1 1.6 collective-permute-start.4
  83.4 1.6 collective-permute-start.7
  85.1 1.6 collective-permute-start.8
  91.7 34.1 %collective-permute-done.12.refs_7_ = bf16[1552,256]{1,0:T(8,128)(2,1)} collective-permute-done((bf16[1552,256]{1,0:T(8,128)(2,1)}, bf16[1552,256]{1,0:T(8,128)(2,1)}, u32[]{:S(2)}, u32[]{:S(2)}) %collective-permute-start.12) | collective-permute-done | bytes 794656 | tf_op jit(solution)/shard_map/ppermute | solution.py:268
  125.7 1.6 collective-permute-start.16
  127.3 1.6 collective-permute-start.15
  132.0 1.9 add_add_fusion.refs_14_
  134.4 2.6 %add_add_fusion.1.refs_15_ = bf16[1552,256]{1,0:T(8,128)(2,1)} fusion(bf16[1552,256]{1,0:T(8,128)(2,1)} %collective-permute-done.18, bf16[1552,256]{1,0:T(8,128)(2,1)} %collective-permute-done.16, bf16[1552,256]{1,0:T(8,128)(2,1)} %collective-permute-done.17), kind=kLoop, calls=%fused_computation.3 | loop fusion | flops 794624 | bytes 3178496 | tf_op jit(solution)/shard_map/add | solution.py:278
  139.9 21.2 %collective-permute-start.21 = (f32[]{:T(128)}, f32[]{:T(128)}, u32[]{:S(2)}, u32[]{:S(2)}) collective-permute-start(f32[]{:T(128)} %fusion.3), channel_id=1, source_target_pairs={{0,2},{1,3},{2,0},{3,1},{4,6},{5,7},{6,4},{7,5},{8,10},{9,11},{10,... | collective-permute-start | bytes 20 | tf_op jit(solution)/shard_map/ppermute | solution.py:362
  170.2 2.2 %select_reduce_fusion.3 = (s32[32,8]{1,0:T(8,128)S(1)}, s32[32,8]{1,0:T(8,128)S(1)}, s32[32,8]{1,0:T(8,128)S(1)}, s32[32,8]{1,0:T(8,128)S(1)}) fusion(s32[32,64]{1,0:T(8,128)S(1)} %broadcast_select_fusion, s32[32,64]{1,0:T(8,128)S(1)} %get-tuple-element.48, s32[32,64]{1,0:T(8,128)S(1)} %get-tuple-element.51, s32[32,64]{1,0:T(8,128)S(1)} %bitcast.46, ...), kind=kLoop, calls=%fused_computation.5 | loop fusion | flops 162816 | bytes 45056 | tf_op jit(solution)/shard_map/reduce_sum | solution.py:322
  172.8 4.9 %copy-done = bf16[26752,256]{1,0:T(8,128)(2,1)S(1)} copy-done((bf16[26752,256]{1,0:T(8,128)(2,1)S(1)}, bf16[26752,256]{1,0:T(8,128)(2,1)}, u32[]{:S(2)}) %copy-start) | copy-done | bytes 13697048
  179.5 26.3 %shard_map.78.refs_19_ = bf16[32,256,256]{2,1,0:T(8,128)(2,1)} custom-call(s32[14]{0:T(128)S(1)} %concatenate.27.control, s32[32]{0:T(128)S(1)} %get-tuple-element.28.outs, s32[32]{0:T(128)S(1)} %get-tuple-element.27.counts, s32[104]{0:T(128)S(1)} %get-tuple-element.9.lefts, s32[104]{0:T(128)S(1)} %get-tuple-element.8.rights, s32[32]{0:T(128)S(1)} %sub.37.owns, ...), custom_call_target="tpu_custom_call" | custom-call | tf_op jit(solution)/shard_map/pallas_call | solution.py:223
  206.2 3.0 %fusion.5 = f32[]{:T(128)} fusion(f32[]{:T(128)} %fusion.3, s32[]{:T(128)S(6)} %axis_index.25, f32[]{:T(128)} %collective-permute-done.22, s32[]{:T(128)S(6)} %xor.11, f32[]{:T(128)} %collective-permute-done.21, s32[]{:T(128)S(6)} %xor.10, f32[]{:T(128)} %collective-permute-done.20, s32[]{:T(128)S(6)} %xor.9), kind=kLoop, calls=%fused_computation.98 | loop fusion | flops 35 | bytes 36 | tf_op jit(solution)/shard_map/reduce_sum | solution.py:364
  209.2 1.8 shard_map.79
  (158 shorter events, 34.6 us)
Async XLA Ops:
  7.2 131.3 %all-gather.3.cloned.1.call-start = ((), (), s32[]{:S(2)}) async-start(), calls=%async_computation | async-start | bytes 15409152 | tf_op jit(solution)/shard_map/all_gather | solution.py:355
  12.6 26.5 %collective-permute-start = (bf16[1808,256]{1,0:T(8,128)(2,1)}, bf16[1808,256]{1,0:T(8,128)(2,1)S(1)}, u32[]{:S(2)}, u32[]{:S(2)}) collective-permute-start(bf16[1808,256]{1,0:T(8,128)(2,1)} %get-tuple-element.5), channel_id=1, source_target_pairs={{0,1},{1,0},{3,2},{4,5},{5,4},{7,6},{8,9},{9,8},{10,11},{11,10},{1... | collective-permute-start | bytes 2777096 | tf_op jit(solution)/shard_map/ppermute | solution.py:268
  17.5 65.9 %collective-permute-start.11 = (bf16[1552,256]{1,0:T(8,128)(2,1)}, bf16[1552,256]{1,0:T(8,128)(2,1)}, u32[]{:S(2)}, u32[]{:S(2)}) collective-permute-start(bf16[1552,256]{1,0:T(8,128)(2,1)} %get-tuple-element.7), channel_id=1, source_target_pairs={{1,2},{2,1},{5,6},{6,5},{9,10},{13,14},{18,17},{22,21},{25,26},{26... | collective-permute-start | bytes 2383880 | tf_op jit(solution)/shard_map/ppermute | solution.py:268
  19.1 36.3 %collective-permute-start.10 = (bf16[1552,256]{1,0:T(8,128)(2,1)}, bf16[1552,256]{1,0:T(8,128)(2,1)}, u32[]{:S(2)}, u32[]{:S(2)}) collective-permute-start(bf16[1552,256]{1,0:T(8,128)(2,1)} %get-tuple-element.7), channel_id=1, source_target_pairs={{0,1},{1,0},{3,2},{4,5},{5,4},{7,6},{8,9},{9,8},{10,11},{11,10},{1... | collective-permute-start | bytes 2383880 | tf_op jit(solution)/shard_map/ppermute | solution.py:268
  22.4 18.1 %collective-permute-start.5 = (bf16[1808,256]{1,0:T(8,128)(2,1)}, bf16[1808,256]{1,0:T(8,128)(2,1)S(1)}, u32[]{:S(2)}, u32[]{:S(2)}) collective-permute-start(bf16[1808,256]{1,0:T(8,128)(2,1)} %get-tuple-element.5), channel_id=1, source_target_pairs={{1,2},{2,1},{5,6},{6,5},{9,10},{13,14},{18,17},{22,21},{25,26},{26... | collective-permute-start | bytes 2777096 | tf_op jit(solution)/shard_map/ppermute | solution.py:268
  39.1 3.6 %collective-permute-start.1 = (bf16[1808,256]{1,0:T(8,128)(2,1)S(1)}, bf16[1808,256]{1,0:T(8,128)(2,1)S(1)}, u32[]{:S(2)}, u32[]{:S(2)}) collective-permute-start(bf16[1808,256]{1,0:T(8,128)(2,1)S(1)} %collective-permute-done.refs_2_), channel_id=1, source_target_pairs={{1,2},{2,1},{5,6},{6,5},{9,10},{10,9},{13,14},{14,13},{17,18},{18,... | collective-permute-start | bytes 2777096 | tf_op jit(solution)/shard_map/ppermute | solution.py:268
  40.5 39.6 %collective-permute-start.6 = (bf16[1808,256]{1,0:T(8,128)(2,1)S(1)}, bf16[1808,256]{1,0:T(8,128)(2,1)}, u32[]{:S(2)}, u32[]{:S(2)}) collective-permute-start(bf16[1808,256]{1,0:T(8,128)(2,1)S(1)} %collective-permute-done.5.refs_4_), channel_id=1, source_target_pairs={{1,0},{2,3},{5,4},{6,7},{10,11},{14,15},{17,16},{21,20},{25,24},{2... | collective-permute-start | bytes 2777096 | tf_op jit(solution)/shard_map/ppermute | solution.py:268
  42.7 42.4 %collective-permute-start.2 = (bf16[1808,256]{1,0:T(8,128)(2,1)S(1)}, bf16[1808,256]{1,0:T(8,128)(2,1)}, u32[]{:S(2)}, u32[]{:S(2)}) collective-permute-start(bf16[1808,256]{1,0:T(8,128)(2,1)S(1)} %collective-permute-done.1.refs_8_), channel_id=1, source_target_pairs={{9,8},{13,12},{18,19},{22,23}} | collective-permute-start | bytes 2777096 | tf_op jit(solution)/shard_map/ppermute | solution.py:268
  44.3 44.1 %collective-permute-start.3 = (bf16[1808,256]{1,0:T(8,128)(2,1)S(1)}, bf16[1808,256]{1,0:T(8,128)(2,1)}, u32[]{:S(2)}, u32[]{:S(2)}) collective-permute-start(bf16[1808,256]{1,0:T(8,128)(2,1)S(1)} %collective-permute-done.1.refs_8_), channel_id=1, source_target_pairs={{2,3},{6,7},{25,24},{29,28}} | collective-permute-start | bytes 2777096 | tf_op jit(solution)/shard_map/ppermute | solution.py:268
  55.4 31.7 %collective-permute-start.13 = (bf16[1552,256]{1,0:T(8,128)(2,1)}, bf16[1552,256]{1,0:T(8,128)(2,1)}, u32[]{:S(2)}, u32[]{:S(2)}) collective-permute-start(bf16[1552,256]{1,0:T(8,128)(2,1)} %collective-permute-done.10.refs_3_), channel_id=1, source_target_pairs={{1,2},{2,1},{5,6},{6,5},{9,10},{10,9},{13,14},{14,13},{17,18},{18,... | collective-permute-start | bytes 2383880 | tf_op jit(solution)/shard_map/ppermute | solution.py:268
  80.1 47.2 %collective-permute-start.4 = (bf16[1808,256]{1,0:T(8,128)(2,1)S(1)}, bf16[1808,256]{1,0:T(8,128)(2,1)}, u32[]{:S(2)}, u32[]{:S(2)}) collective-permute-start(bf16[1808,256]{1,0:T(8,128)(2,1)S(1)} %collective-permute-done.refs_2_), channel_id=1, source_target_pairs={{11,19},{15,23},{16,8},{20,12}} | collective-permute-start | bytes 2777096 | tf_op jit(solution)/shard_map/ppermute | solution.py:268
  83.4 47.1 %collective-permute-start.7 = (bf16[1808,256]{1,0:T(8,128)(2,1)}, bf16[1808,256]{1,0:T(8,128)(2,1)}, u32[]{:S(2)}, u32[]{:S(2)}) collective-permute-start(bf16[1808,256]{1,0:T(8,128)(2,1)} %collective-permute-done.6.refs_6_), channel_id=1, source_target_pairs={{3,11},{7,15},{24,16},{28,20}} | collective-permute-start | bytes 2777096 | tf_op jit(solution)/shard_map/ppermute | solution.py:268
  85.1 47.0 %collective-permute-start.8 = (bf16[1808,256]{1,0:T(8,128)(2,1)}, bf16[1808,256]{1,0:T(8,128)(2,1)}, u32[]{:S(2)}, u32[]{:S(2)}) collective-permute-start(bf16[1808,256]{1,0:T(8,128)(2,1)} %collective-permute-done.2.refs_10_), channel_id=1, source_target_pairs={{8,24},{12,28},{19,3},{23,7}} | collective-permute-start | bytes 2777096 | tf_op jit(solution)/shard_map/ppermute | solution.py:268
  87.1 38.6 %collective-permute-start.12 = (bf16[1552,256]{1,0:T(8,128)(2,1)}, bf16[1552,256]{1,0:T(8,128)(2,1)}, u32[]{:S(2)}, u32[]{:S(2)}) collective-permute-start(bf16[1552,256]{1,0:T(8,128)(2,1)} %collective-permute-done.11.refs_5_), channel_id=1, source_target_pairs={{1,0},{2,3},{5,4},{6,7},{10,11},{14,15},{17,16},{21,20},{25,24},{2... | collective-permute-start | bytes 2383880 | tf_op jit(solution)/shard_map/ppermute | solution.py:268
  88.4 40.5 %collective-permute-start.14 = (bf16[1552,256]{1,0:T(8,128)(2,1)}, bf16[1552,256]{1,0:T(8,128)(2,1)}, u32[]{:S(2)}, u32[]{:S(2)}) collective-permute-start(bf16[1552,256]{1,0:T(8,128)(2,1)} %collective-permute-done.13.refs_9_), channel_id=1, source_target_pairs={{9,8},{13,12},{18,19},{22,23}} | collective-permute-start | bytes 2383880 | tf_op jit(solution)/shard_map/ppermute | solution.py:268
  125.7 8.6 %collective-permute-start.16 = (bf16[1552,256]{1,0:T(8,128)(2,1)}, bf16[1552,256]{1,0:T(8,128)(2,1)}, u32[]{:S(2)}, u32[]{:S(2)}) collective-permute-start(bf16[1552,256]{1,0:T(8,128)(2,1)} %collective-permute-done.10.refs_3_), channel_id=1, source_target_pairs={{11,19},{15,23},{16,8},{20,12}} | collective-permute-start | bytes 2383880 | tf_op jit(solution)/shard_map/ppermute | solution.py:268
  127.3 81.9 %collective-permute-start.15 = (bf16[1552,256]{1,0:T(8,128)(2,1)}, bf16[1552,256]{1,0:T(8,128)(2,1)}, u32[]{:S(2)}, u32[]{:S(2)}) collective-permute-start(bf16[1552,256]{1,0:T(8,128)(2,1)} %collective-permute-done.13.refs_9_), channel_id=1, source_target_pairs={{2,3},{6,7},{25,24},{29,28}} | collective-permute-start | bytes 2383880 | tf_op jit(solution)/shard_map/ppermute | solution.py:268
  128.9 5.4 %collective-permute-start.17 = (bf16[1552,256]{1,0:T(8,128)(2,1)}, bf16[1552,256]{1,0:T(8,128)(2,1)}, u32[]{:S(2)}, u32[]{:S(2)}) collective-permute-start(bf16[1552,256]{1,0:T(8,128)(2,1)} %collective-permute-done.12.refs_7_), channel_id=1, source_target_pairs={{3,11},{7,15},{24,16},{28,20}} | collective-permute-start | bytes 2383880 | tf_op jit(solution)/shard_map/ppermute | solution.py:268
  130.5 3.8 %collective-permute-start.18 = (bf16[1552,256]{1,0:T(8,128)(2,1)}, bf16[1552,256]{1,0:T(8,128)(2,1)}, u32[]{:S(2)}, u32[]{:S(2)}) collective-permute-start(bf16[1552,256]{1,0:T(8,128)(2,1)} %collective-permute-done.14.refs_11_), channel_id=1, source_target_pairs={{8,24},{12,28},{19,3},{23,7}} | collective-permute-start | bytes 2383880 | tf_op jit(solution)/shard_map/ppermute | solution.py:268
  133.9 3.7 %collective-permute-start.9 = (bf16[1808,256]{1,0:T(8,128)(2,1)S(1)}, bf16[1808,256]{1,0:T(8,128)(2,1)}, u32[]{:S(2)}, u32[]{:S(2)}) collective-permute-start(bf16[1808,256]{1,0:T(8,128)(2,1)S(1)} %add_add_fusion.refs_14_), channel_id=1, source_target_pairs={{0,4},{4,0},{8,12},{12,8},{16,20},{20,16},{24,28},{28,24},{1,5},{5... | collective-permute-start | bytes 2777096 | tf_op jit(solution)/shard_map/ppermute | solution.py:281
  137.0 72.3 %collective-permute-start.19 = (bf16[1552,256]{1,0:T(8,128)(2,1)}, bf16[1552,256]{1,0:T(8,128)(2,1)}, u32[]{:S(2)}, u32[]{:S(2)}) collective-permute-start(bf16[1552,256]{1,0:T(8,128)(2,1)} %add_add_fusion.1.refs_15_), channel_id=1, source_target_pairs={{0,4},{4,0},{8,12},{12,8},{16,20},{20,16},{24,28},{28,24},{1,5},{5... | collective-permute-start | bytes 2383880 | tf_op jit(solution)/shard_map/ppermute | solution.py:281
  139.8 66.3 %collective-permute-start.22 = (f32[]{:T(128)}, f32[]{:T(128)}, u32[]{:S(2)}, u32[]{:S(2)}) collective-permute-start(f32[]{:T(128)} %fusion.3), channel_id=1, source_target_pairs={{0,1},{1,0},{2,3},{3,2},{4,5},{5,4},{6,7},{7,6},{8,9},{9,8},{10,11... | collective-permute-start | bytes 20 | tf_op jit(solution)/shard_map/ppermute | solution.py:362
  139.9 66.3 %collective-permute-start.21 = (f32[]{:T(128)}, f32[]{:T(128)}, u32[]{:S(2)}, u32[]{:S(2)}) collective-permute-start(f32[]{:T(128)} %fusion.3), channel_id=1, source_target_pairs={{0,2},{1,3},{2,0},{3,1},{4,6},{5,7},{6,4},{7,5},{8,10},{9,11},{10,... | collective-permute-start | bytes 20 | tf_op jit(solution)/shard_map/ppermute | solution.py:362
  161.0 45.1 %collective-permute-start.20 = (f32[]{:T(128)}, f32[]{:T(128)}, u32[]{:S(2)}, u32[]{:S(2)}) collective-permute-start(f32[]{:T(128)} %fusion.3), channel_id=1, source_target_pairs={{0,3},{1,2},{2,1},{3,0},{4,7},{5,6},{6,5},{7,4},{8,11},{9,10},{10,... | collective-permute-start | bytes 20 | tf_op jit(solution)/shard_map/ppermute | solution.py:362
  (8 other events, 55.6 us)
Sparse Core Ops, SparseCore 0:
  12.7 79.5 all-gather.2

commit v5 on v4

v5 whole, which is shorter than its diff:
```python
import functools

import jax
import jax.numpy as jnp
from jax import lax
from jax.experimental import pallas as pl
from jax.experimental.pallas import tpu as pltpu
from jax.sharding import PartitionSpec as P

PACKED = 13
SPLIT = (PACKED + 1) // 2
STRIDE = 1 << (PACKED - 1).bit_length()
NOTE_ROWS = 16


def pack_kernel(cols_ref, flag_ref, first_ref, x_ref, part_a, part_b, full, note, norm, sems):
    count, block, _ = x_ref.shape
    slots = cols_ref.shape[0]
    rows = count // slots
    sends = []
    place = jnp.int32(0)
    for index in range(count):
        filled = cols_ref[index % slots, index // slots] >= 0
        targets = (
            (full, filled, place),
            (part_a, filled & (place < SPLIT), place),
            (part_b, filled & (place >= SPLIT), place - SPLIT),
        )
        for which, (out, wanted, target) in enumerate(targets):
            target = pl.multiple_of(jnp.where(wanted, target, 0) * block, block)
            copy = pltpu.make_async_copy(
                x_ref.at[index], out.at[pl.ds(target, block)], sems.at[which, index]
            )
            pl.when(wanted)(copy.start)
            sends.append((wanted, copy))
        place = place + filled.astype(jnp.int32)

    norm[...] = jnp.zeros_like(norm)
    eye_rows = lax.broadcasted_iota(jnp.int32, (block, block), 0)
    eye = eye_rows == lax.broadcasted_iota(jnp.int32, (block, block), 1)
    for index in range(count):
        row = index // slots
        col = cols_ref[index % slots, row]
        flag = flag_ref[row]

        @pl.when(col >= 0)
        def _():
            values = x_ref[index].astype(jnp.float32)
            weight = (1 - 2 * flag).astype(jnp.float32)
            norm[...] += weight * jnp.sum(values * values, axis=0, keepdims=True)

        @pl.when((col == first_ref[0] + row) & (flag != 0))
        def _():
            values = x_ref[index].astype(jnp.float32)
            norm[...] += 2.0 * jnp.sum(jnp.where(eye, values, 0.0), axis=0, keepdims=True)

    trace = jnp.full(note.shape, jnp.sum(norm[...]), jnp.float32)
    high = trace.astype(note.dtype).astype(jnp.float32)
    middle = (trace - high).astype(note.dtype).astype(jnp.float32)
    low = trace - high - middle
    down = lax.broadcasted_iota(jnp.int32, note.shape, 0)
    across = lax.broadcasted_iota(jnp.int32, note.shape, 1)
    facts = jnp.where(across == 0, high, jnp.where(across == 1, middle, low))
    facts = jnp.where((down == rows) & (across < 3), facts, 0.0)
    for index in range(count):
        here = (down == index // slots) & (across == index % slots)
        facts = jnp.where(here, cols_ref[index % slots, index // slots].astype(jnp.float32), facts)
    note[...] = facts.astype(note.dtype)
    for which, out in enumerate((full, part_a, part_b)):
        target = out.at[pl.ds(out.shape[0] - NOTE_ROWS, NOTE_ROWS)]
        copy = pltpu.make_async_copy(note, target, sems.at[which, count])
        copy.start()
        sends.append((None, copy))
    for wanted, copy in sends:
        copy.wait() if wanted is None else pl.when(wanted)(copy.wait)


def pack(x_blocks, x_cols, branch_flag, first_row):
    rows, slots, block, _ = x_blocks.shape
    count = rows * slots
    smem = pl.BlockSpec(memory_space=pltpu.SMEM)
    hbm = pl.BlockSpec(memory_space=pltpu.HBM)
    return pl.pallas_call(
        pack_kernel,
        out_shape=[
            jax.ShapeDtypeStruct((size * block + NOTE_ROWS, block), x_blocks.dtype)
            for size in (SPLIT, PACKED - SPLIT, PACKED)
        ],
        in_specs=[smem, smem, smem, pl.BlockSpec(memory_space=pltpu.VMEM)],
        out_specs=[hbm] * 3,
        scratch_shapes=[
            pltpu.VMEM((NOTE_ROWS, block), x_blocks.dtype),
            pltpu.VMEM((1, block), jnp.float32),
            pltpu.SemaphoreType.DMA((3, count + 1)),
        ],
        compiler_params=pltpu.CompilerParams(vmem_limit_bytes=(4 * count * block * block) + (8 << 20)),
    )(x_cols.T, branch_flag, first_row.reshape(1), x_blocks.reshape(count, block, block))


BATCH = 4


def multiply_kernel(loads, kept, layout, table, *refs):
    n_arrays = 1 + max(load[0] for load in loads)
    plane = refs[0]
    arrays = refs[:n_arrays]
    out_ref, pool, ring, more, done, in_sem, ring_sem, out_sem = refs[-8:]
    block = out_ref.shape[-1]
    n_out = table[0]
    n_terms = table[1]
    depth = ring.shape[0] - 1
    zero_entry = pool.shape[0] - 1

    copies = []
    for number, (which, at, entry, first, size, wanted) in enumerate(loads):
        source = arrays[which] if at is None else arrays[which].at[at]
        copy = pltpu.make_async_copy(
            source.at[pl.ds(0, size * block)],
            pool.at[entry, pl.ds(first * block, size * block)],
            in_sem.at[number],
        )
        copies.append(((table[wanted] != 0) & (n_out > 0), copy))
    for here, copy in copies:
        pl.when(here)(copy.start)

    def decode(index):
        entry = lax.shift_right_logical(index, STRIDE.bit_length() - 1)
        return entry, pl.multiple_of(jnp.bitwise_and(index, STRIDE - 1) * block, block)

    def fetch(term):
        entry, first = decode(table[layout["rights"] + term])
        slot = lax.rem(term, depth)
        return pltpu.make_async_copy(
            plane.at[entry, pl.ds(first, block)], ring.at[slot], ring_sem.at[slot]
        )

    def begin(term, carry):
        fetch(term).start()
        return carry

    lax.fori_loop(0, jnp.minimum(depth, n_terms), begin, 0)
    pool[zero_entry, pl.ds(0, block)] = jnp.zeros((block, block), pool.dtype)
    ring[depth] = jnp.zeros((block, block), ring.dtype)
    for here, copy in copies:
        pl.when(here)(copy.wait)

    def product(term, live):
        entry, first = decode(
            jnp.where(live, table[layout["lefts"] + term], zero_entry * STRIDE)
        )
        slot = jnp.where(live, lax.rem(term, depth), depth)
        return jnp.dot(
            pool[entry, pl.ds(first, block)], ring[slot], preferred_element_type=jnp.float32
        )

    def write(number, slot):
        output = table[layout["outs"] + number]
        return pltpu.make_async_copy(done.at[slot], out_ref.at[output], out_sem.at[slot])

    def one_batch(batch, term):
        begins, counts = [], []
        last = term
        for local in range(BATCH):
            begins.append(last)
            counts.append(table[layout["counts"] + batch * BATCH + local])
            last = last + counts[local]

        def arrived(number, carry):
            fetch(number).wait()
            return carry

        lax.fori_loop(term, last, arrived, 0)
        half = lax.rem(batch, 2) * BATCH
        for local in range(BATCH):
            @pl.when(batch >= 2)
            def _():
                write((batch - 2) * BATCH + local, half + local).wait()

            @pl.when(counts[local] > 2)
            def _():
                more[local] = product(begins[local] + 2, True)

                def one_term(number, carry):
                    more[local] += product(number, True)
                    return carry

                lax.fori_loop(begins[local] + 3, begins[local] + counts[local], one_term, 0)

            @pl.when(counts[local] <= 2)
            def _():
                more[local] = jnp.zeros_like(more[local])

        for local in range(BATCH):
            output = table[layout["outs"] + batch * BATCH + local]
            square = more[local]
            for place in range(2):
                live = counts[local] > place
                square = square + product(jnp.where(live, begins[local] + place, 0), live)
            flag = table[layout["flags"] + output // kept].astype(jnp.float32)
            own = table[layout["owns"] + output]
            entry, first = decode(jnp.where(own >= 0, own, zero_entry * STRIDE))
            mine = pool[entry, pl.ds(first, block)].astype(jnp.float32)
            result = (2.0 * flag) * mine + (1.0 - 2.0 * flag) * square
            done[half + local] = result.astype(done.dtype)
        for local in range(BATCH):
            @pl.when(batch * BATCH + local < n_out)
            def _():
                write(batch * BATCH + local, half + local).start()

        def refill(number, carry):
            fetch(number + depth).start()
            return carry

        lax.fori_loop(term, jnp.clip(n_terms - depth, term, last), refill, 0)
        return last

    n_batches = (n_out + BATCH - 1) // BATCH
    lax.fori_loop(0, n_batches, one_batch, jnp.int32(0))
    for back in range(2):
        batch = n_batches - 1 - back
        for local in range(BATCH):
            number = jnp.maximum(batch, 0) * BATCH + local

            @pl.when((batch >= 0) & (number < n_out))
            def _():
                write(number, lax.rem(batch, 2) * BATCH + local).wait()


def multiply(arrays, loads, n_entries, layout, table, shape, before=None):
    rows, kept, block, dtype = shape
    outputs = rows * kept
    smem = pl.BlockSpec(memory_space=pltpu.SMEM)
    hbm = pl.BlockSpec(memory_space=pltpu.HBM)
    depth = 48
    vmem = ((n_entries + 1) * PACKED + depth + 5 * BATCH) * block * block * 2 + (8 << 20)
    operands = [table, *arrays]
    in_specs = [smem] + [hbm] * len(arrays)
    aliases = {}
    if before is not None:
        operands += [before[1], before[0]]
        in_specs += [smem, hbm]
        aliases = {len(operands) - 1: 0}
    return pl.pallas_call(
        functools.partial(multiply_kernel, loads, kept, layout),
        out_shape=jax.ShapeDtypeStruct((outputs, block, block), dtype),
        in_specs=in_specs,
        out_specs=hbm,
        scratch_shapes=[
            pltpu.VMEM((n_entries + 1, PACKED * block, block), dtype),
            pltpu.VMEM((depth + 1, block, block), dtype),
            pltpu.VMEM((BATCH, block, block), jnp.float32),
            pltpu.VMEM((2 * BATCH, block, block), dtype),
            pltpu.SemaphoreType.DMA((len(loads),)),
            pltpu.SemaphoreType.DMA((depth,)),
            pltpu.SemaphoreType.DMA((2 * BATCH,)),
        ],
        input_output_aliases=aliases,
        compiler_params=pltpu.CompilerParams(vmem_limit_bytes=vmem),
    )(*operands)


def shift(array, pairs):
    return lax.ppermute(array, "col", pairs)


def gather_line(part):
    first = shift(part, [(0, 1), (1, 0), (2, 3), (3, 2)])
    middle = shift(part, [(1, 2), (2, 1)])
    end_two = shift(middle, [(1, 0), (2, 3)])
    middle_two = shift(first, [(1, 2), (2, 1)])
    end_three = shift(middle_two, [(1, 0), (2, 3)])
    return {
        "first": first,
        "middle": middle,
        "end_two": end_two,
        "middle_two": middle_two,
        "end_three": end_three,
    }


def running_count(fill):
    count = fill.shape[-1]
    before = jnp.arange(count)[:, None] < jnp.arange(count)[None, :]
    return jnp.sum(jnp.where(before, fill[..., :, None], 0), axis=-2)


def places(cols):
    flat = (cols >= 0).astype(jnp.int32).reshape(cols.shape[:-2] + (-1,))
    return running_count(flat).reshape(cols.shape)


def make_table(left_of, right_of, owns, flags, chosen, width, wanted):
    kept = right_of.shape[0] // left_of.shape[0]
    outputs = right_of.shape[0]
    left_of = jnp.repeat(left_of, kept, axis=0)
    live = (left_of > 0) & (right_of > 0) & chosen[:, None]
    counts = jnp.sum(live.astype(jnp.int32), axis=1)
    term = jnp.where(live, running_count(live.astype(jnp.int32)), -1)
    across = jnp.arange(width, dtype=jnp.int32)
    pick = term[:, None, :] == across[:, None]
    lefts = jnp.sum(jnp.where(pick, left_of[:, None, :] - 1, 0), axis=2)
    rights = jnp.sum(jnp.where(pick, right_of[:, None, :] - 1, 0), axis=2)
    flat = jnp.where(across < counts[:, None], running_count(counts)[:, None] + across, -1)
    pick = flat[None] == jnp.arange(PACKED * width, dtype=jnp.int32)[:, None, None]
    lefts = jnp.sum(jnp.where(pick, lefts, 0), axis=(1, 2))
    rights = jnp.sum(jnp.where(pick, rights, 0), axis=(1, 2))
    every = jnp.arange(outputs, dtype=jnp.int32)
    number = jnp.where(chosen, running_count(chosen.astype(jnp.int32)), -1)
    pick = number[None, :] == every[:, None]
    outs = jnp.sum(jnp.where(pick, every, 0), axis=1)
    ordered = jnp.sum(jnp.where(pick, counts, 0), axis=1)
    sizes = jnp.stack([jnp.sum(chosen.astype(jnp.int32)), jnp.sum(counts)])
    spare = jnp.zeros((BATCH,), jnp.int32)
    lists = {
        "sizes": sizes,
        "wanted": wanted,
        "outs": jnp.concatenate([outs, spare]),
        "counts": jnp.concatenate([ordered, spare]),
        "lefts": lefts,
        "rights": rights,
        "owns": owns,
        "flags": flags,
    }
    layout = {}
    first = 0
    for name, values in lists.items():
        layout[name] = first
        first += values.shape[0]
    return jnp.concatenate(list(lists.values())), layout


def per_device(x_blocks, x_cols, out_cols, branch_flag):
    rows, slots = x_cols.shape
    kept = out_cols.shape[1]
    block = x_blocks.shape[-1]
    dtype = x_blocks.dtype
    n_row = lax.axis_size("row")
    n_col = lax.axis_size("col")
    row = lax.axis_index("row")
    col = lax.axis_index("col")
    n_blocks = n_row * rows
    width = n_col * slots
    shape = (rows, kept, block, dtype)

    part_a, part_b, full = pack(x_blocks, x_cols, branch_flag, row * rows)

    def facts(array):
        first = array.shape[-2] - NOTE_ROWS
        return array[..., first : first + rows, :slots].astype(jnp.int32)

    plane = lax.all_gather(full, "row", axis=0)
    plane_cols = facts(plane)

    own_trace = jnp.sum(plane[:, PACKED * block + rows, :3].astype(jnp.float32))
    heights = jnp.arange(n_col, dtype=jnp.int32)
    traces = jnp.where(heights == col, own_trace, 0.0)
    for step in range(1, n_col):
        other = shift(own_trace, [(i, i ^ step) for i in range(n_col)])
        traces = jnp.where(heights == jnp.bitwise_xor(col, step), other, traces)
    trace = jnp.sum(traces).reshape(1)

    targets = out_cols.reshape(rows * kept)
    right_at = places(plane_cols) + STRIDE * jnp.arange(n_row, dtype=jnp.int32)[:, None, None]
    hit = plane_cols.reshape(n_blocks, slots)[None] == targets[:, None, None]
    right_of = jnp.sum(jnp.where(hit, right_at.reshape(n_blocks, slots) + 1, 0), axis=2)
    hit = x_cols[:, None, :] == out_cols[:, :, None]
    owns = jnp.sum(jnp.where(hit, places(x_cols)[:, None, :] + 1, 0), axis=2) - 1
    owns = owns.reshape(rows * kept)

    every = jnp.arange(n_blocks, dtype=jnp.int32)

    def straight(cols, entries, wanted):
        at = places(cols) + STRIDE * entries[:, None, None]
        hit = (cols[..., None] == every) & (wanted[:, None, None, None] != 0)
        return jnp.sum(jnp.where(hit, at[..., None] + 1, 0), axis=(0, 2))

    everything = jnp.ones((rows * kept,), bool)
    one = jnp.ones((1,), jnp.int32)
    if n_col != 4:
        line = lax.all_gather(full, "col", axis=0)
        entries = 1 + jnp.arange(n_col, dtype=jnp.int32)
        left_of = straight(facts(line), entries, jnp.ones((n_col,), jnp.int32))
        table, layout = make_table(
            left_of, right_of, owns, branch_flag, everything, width, one
        )
        loads = [(2, None, 0, 0, PACKED, 2)]
        loads += [(1, c, 1 + c, 0, PACKED, 2) for c in range(n_col)]
        purified = multiply([plane, line, full], tuple(loads), 1 + n_col, layout, table, shape)
        return purified.reshape(rows, kept, block, block), trace

    line = [gather_line(part) for part in (part_a, part_b)]
    note = {name: facts(array) for name, array in line[0].items()}
    at_end = (col == 0) | (col == n_col - 1)
    end = at_end.astype(jnp.int32)
    wanted = jnp.stack([jnp.int32(1), end, 1 - end])
    always, at_ends, inside = 2, 3, 4

    arrays = [plane, full]
    loads = [(1, None, 0, 0, PACKED, always)]

    def add(name, entry, wanted):
        spans = ((0, SPLIT), (SPLIT, PACKED - SPLIT))
        for which in range(2):
            loads.append((len(arrays), None, entry) + spans[which] + (wanted,))
            arrays.append(line[which][name])

    early_cols = [x_cols, note["first"], jnp.where(at_end, note["end_two"], note["middle"])]
    early_cols = jnp.stack(early_cols + [note["middle_two"]])
    early_wanted = jnp.stack([jnp.int32(1)] * 3 + [1 - end])
    early = straight(early_cols, jnp.arange(4, dtype=jnp.int32), early_wanted)
    add("first", 1, always)
    add("middle", 2, inside)
    add("end_two", 2, at_ends)
    add("middle_two", 3, inside)
    table, layout = make_table(early, right_of, owns, branch_flag, everything, width, wanted)
    purified = multiply(list(arrays), tuple(loads), 4, layout, table, shape)

    late = straight(note["end_three"][None], jnp.array([3], jnp.int32), end[None])
    meets = (jnp.repeat(late, kept, axis=0) > 0) & (right_of > 0)
    chosen = jnp.any(meets, axis=1)
    add("end_three", 3, at_ends)
    table, layout = make_table(early + late, right_of, owns, branch_flag, chosen, width, wanted)
    before = (purified, trace)
    purified = multiply(list(arrays), tuple(loads), 4, layout, table, shape, before)
    return purified.reshape(rows, kept, block, block), trace


def solution(mesh):
    in_specs = (P("row", "col", None, None), P("row", "col"), P("row", "col"), P("row"))
    out_specs = (P("row", "col", None, None), P())
    return jax.shard_map(
        per_device, mesh=mesh, in_specs=in_specs, out_specs=out_specs, check_vma=False
    )
```

time: 219 us -> 209 us (0.954); the launches traced: 218 us -> 211 us
  starting transfers between devices: 53 us -> 21 us
  waiting for transfers between devices: 76.1 us -> 98 us
  Pallas kernels: 30.5 us -> 46.3 us
  other arithmetic: 22.1 us -> 16.2 us
  between operations: 18.4 us -> 14.3 us
  local copies, waits for them, and re-layouts: 17.8 us -> 15 us
    ppermute x23 -> x13, starting transfers between devices: 53 us -> 21 us  [shift(): return lax.ppermute(array, 'col', pairs)]
    ppermute x23 -> x13, waiting for transfers between devices: 76.1 us -> 98 us  [shift(): return lax.ppermute(array, 'col', pairs)]
    pallas_call x2, Pallas kernels: 28.1 us -> 42.7 us  [multiply(): pl.pallas_call(functools.partial(multiply_kernel, loads, kept, layout), o...]
    add x5 -> x0, other arithmetic: 5.3 us -> none  [the longest x2 4.48 us: gather_line(): turned = turned + send(got['end_three'], 'turn_three')]
    unnamed x18 -> x12, local copies, waits for them, and re-layouts: 12.1 us -> 9.56 us
  transfers between devices with their start and end apart: 24 -> 14, of which waited for: 4 -> 4; matrix products, arithmetic and copies ran while one was open for 13% -> 11% of each run, Pallas kernels for 12% -> 10%
where the time goes in v5:
time: 209 us; the launch traced here: 211 us
  waiting for transfers between devices  98 us (47%)
  Pallas kernels  46.3 us (22%)
  starting transfers between devices  21 us (10%)
  other arithmetic  16.2 us (8%)
  local copies, waits for them, and re-layouts  15 us (7%)
  between operations  14.3 us (7%)
    ppermute x13, waiting for transfers between devices, shift(): return lax.ppermute(array, 'col', pairs)  98 us
    pallas_call x2, Pallas kernels, multiply(): pl.pallas_call(functools.partial(multiply_kernel, loads, kept, layout), o...  42.7 us
    ppermute x13, starting transfers between devices, shift(): return lax.ppermute(array, 'col', pairs)  21 us
    unnamed x12, local copies, waits for them, and re-layouts  9.56 us
  transfers between devices with their start and end apart: 14, of which 4 were waited for; matrix products, arithmetic and copies ran while one was open for 11% of the time, Pallas kernels for 10%

profile of v5, /device:TPU:0, one launch (start us, length us, event | category | flops | bytes accessed | tf_op | source)
XLA Modules:
  0.0 210.9 jit_solution(17384439078169100841)
XLA Ops:
  7.2 1.6 copy-done.1
  10.1 3.6 %shard_map.68 = (bf16[1808,256]{1,0:T(8,128)(2,1)S(1)}, bf16[1552,256]{1,0:T(8,128)(2,1)}, bf16[3344,256]{1,0:T(8,128)(2,1)}) custom-call(s32[2,8]{1,0:T(2,128)S(1)} %bitcast.31, s32[8]{0:T(128)S(1)} %copy-done.3, s32[1]{0:T(128)} %bitcast.1.first_ref, bf16[16,256,256]{2,1,0:T(8,128)(2,1)S(1)} %bitcast.29), custom_call_target="tpu_custom_call" | custom-call | tf_op jit(solution)/shard_map/pallas_call | solution.py:83
  15.5 5.9 %collective-permute-start = (bf16[1808,256]{1,0:T(8,128)(2,1)}, bf16[1808,256]{1,0:T(8,128)(2,1)S(1)}, u32[]{:S(2)}, u32[]{:S(2)}) collective-permute-start(bf16[1808,256]{1,0:T(8,128)(2,1)} %copy-done.4), channel_id=1, source_target_pairs={{0,1},{1,0},{2,3},{3,2},{4,5},{5,4},{6,7},{7,6},{8,9},{9,8},{10,11... | collective-permute-start | bytes 2777096 | tf_op jit(solution)/shard_map/ppermute | solution.py:263
  21.4 1.6 collective-permute-start.6
  24.1 1.3 collective-permute-start.4
  25.4 17.5 %collective-permute-done.refs_2_ = bf16[1808,256]{1,0:T(8,128)(2,1)S(1)} collective-permute-done((bf16[1808,256]{1,0:T(8,128)(2,1)}, bf16[1808,256]{1,0:T(8,128)(2,1)S(1)}, u32[]{:S(2)}, u32[]{:S(2)}) %collective-permute-start) | collective-permute-done | bytes 925728 | tf_op jit(solution)/shard_map/ppermute | solution.py:263
  42.9 1.6 collective-permute-start.1
  45.5 14.5 %collective-permute-done.5.refs_3_ = bf16[1552,256]{1,0:T(8,128)(2,1)} collective-permute-done((bf16[1552,256]{1,0:T(8,128)(2,1)}, bf16[1552,256]{1,0:T(8,128)(2,1)}, u32[]{:S(2)}, u32[]{:S(2)}) %collective-permute-start.5) | collective-permute-done | bytes 794656 | tf_op jit(solution)/shard_map/ppermute | solution.py:263
  60.1 1.6 collective-permute-start.8
  62.1 1.3 collective-permute-start.7
  63.5 1.3 collective-permute-start.9
  64.8 1.3 collective-permute-start.2
  66.1 13.7 %collective-permute-done.4.refs_6_ = bf16[1808,256]{1,0:T(8,128)(2,1)S(1)} collective-permute-done((bf16[1808,256]{1,0:T(8,128)(2,1)S(1)}, bf16[1808,256]{1,0:T(8,128)(2,1)S(1)}, u32[]{:S(2)}, u32[]{:S(2)}) %collective-permute-start.4) | collective-permute-done | bytes 925728 | tf_op jit(solution)/shard_map/ppermute | solution.py:263
  82.0 52.3 %collective-permute-done.2.refs_10_ = bf16[1808,256]{1,0:T(8,128)(2,1)} collective-permute-done((bf16[1808,256]{1,0:T(8,128)(2,1)}, bf16[1808,256]{1,0:T(8,128)(2,1)}, u32[]{:S(2)}, u32[]{:S(2)}) %collective-permute-start.2) | collective-permute-done | bytes 925728 | tf_op jit(solution)/shard_map/ppermute | solution.py:263
  136.2 1.4 fusion.3
  137.6 3.0 %collective-permute-start.11 = (f32[]{:T(128)}, f32[]{:T(128)}, u32[]{:S(2)}, u32[]{:S(2)}) collective-permute-start(f32[]{:T(128)} %fusion.3), channel_id=1, source_target_pairs={{0,2},{1,3},{2,0},{3,1},{4,6},{5,7},{6,4},{7,5},{8,10},{9,11},{10,... | collective-permute-start | bytes 20 | tf_op jit(solution)/shard_map/ppermute | solution.py:263
  140.5 1.4 collective-permute-start.10
  146.6 2.2 %select_reduce_fusion.3 = (s32[32,8]{1,0:T(8,128)S(1)}, s32[32,8]{1,0:T(8,128)S(1)}, s32[32,8]{1,0:T(8,128)S(1)}, s32[32,8]{1,0:T(8,128)S(1)}) fusion(s32[32,64]{1,0:T(8,128)S(1)} %get-tuple-element.41, s32[32,64]{1,0:T(8,128)S(1)} %get-tuple-element.32, s32[32,64]{1,0:T(8,128)S(1)} %get-tuple-element.35, s32[32,64]{1,0:T(8,128)S(1)} %bitcast.34, ...), kind=kLoop, calls=%fused_computation.3 | loop fusion | flops 162816 | bytes 45056 | tf_op jit(solution)/shard_map/reduce_sum | solution.py:302
  149.0 1.3 concatenate.17.table
  151.4 2.0 concatenate.16.table
  153.4 4.9 %copy-done = bf16[26752,256]{1,0:T(8,128)(2,1)S(1)} copy-done((bf16[26752,256]{1,0:T(8,128)(2,1)S(1)}, bf16[26752,256]{1,0:T(8,128)(2,1)}, u32[]{:S(2)}) %copy-start) | copy-done | bytes 13697048
  158.2 20.6 %shard_map.69.refs_13_ = bf16[32,256,256]{2,1,0:T(8,128)(2,1)} custom-call(s32[325]{0:T(512)S(1)} %concatenate.17.table, bf16[8,3344,256]{2,1,0:T(8,128)(2,1)S(1)} %bitcast.27, bf16[3344,256]{1,0:T(8,128)(2,1)} %get-tuple-element.6.refs_1_, bf16[1808,256]{1,0:T(8,128)(2,1)S(1)} %collective-permute-done.refs_2_, ...), custom_call_target="tpu_custom_call" | custom-call | tf_op jit(solution)/shard_map/pallas_call | solution.py:243
  178.9 3.1 %fusion.5 = f32[]{:T(128)} fusion(f32[]{:T(128)} %fusion.3, s32[]{:T(128)S(6)} %axis_index.25, f32[]{:T(128)} %collective-permute-done.12, s32[]{:T(128)S(6)} %xor.11, f32[]{:T(128)} %collective-permute-done.11, s32[]{:T(128)S(6)} %xor.10, f32[]{:T(128)} %collective-permute-done.10, s32[]{:T(128)S(6)} %xor.9), kind=kLoop, calls=%fused_computation.80 | loop fusion | flops 35 | bytes 36 | tf_op jit(solution)/shard_map/reduce_sum | solution.py:360
  182.0 22.1 %shard_map.70 = bf16[32,256,256]{2,1,0:T(8,128)(2,1)} custom-call(s32[325]{0:T(512)S(1)} %concatenate.16.table, bf16[8,3344,256]{2,1,0:T(8,128)(2,1)S(1)} %bitcast.28, bf16[3344,256]{1,0:T(8,128)(2,1)} %get-tuple-element.6.refs_1_, bf16[1808,256]{1,0:T(8,128)(2,1)S(1)} %collective-permute-done.refs_2_, ...), custom_call_target="tpu_custom_call", output_to_operand_aliasing={{}: (14, {})} | custom-call | tf_op jit(solution)/shard_map/pallas_call | solution.py:243
  (105 shorter events, 15.7 us)
Async XLA Ops:
  7.2 129.0 %all-gather.3.cloned.1.call-start = ((), (), s32[]{:S(2)}) async-start(), calls=%async_computation | async-start | bytes 15409152 | tf_op jit(solution)/shard_map/all_gather | solution.py:351
  7.2 1.6 copy-start.1
  8.8 0.7 copy-start.2
  9.5 0.7 copy-start.3
  13.8 0.9 copy-start.4
  14.7 9.4 %collective-permute-start.3 = (bf16[1808,256]{1,0:T(8,128)(2,1)}, bf16[1808,256]{1,0:T(8,128)(2,1)S(1)}, u32[]{:S(2)}, u32[]{:S(2)}) collective-permute-start(bf16[1808,256]{1,0:T(8,128)(2,1)} %copy-done.4), channel_id=1, source_target_pairs={{1,2},{2,1},{5,6},{6,5},{9,10},{10,9},{13,14},{14,13},{17,18},{18,... | collective-permute-start | bytes 2777096 | tf_op jit(solution)/shard_map/ppermute | solution.py:263
  15.5 27.5 %collective-permute-start = (bf16[1808,256]{1,0:T(8,128)(2,1)}, bf16[1808,256]{1,0:T(8,128)(2,1)S(1)}, u32[]{:S(2)}, u32[]{:S(2)}) collective-permute-start(bf16[1808,256]{1,0:T(8,128)(2,1)} %copy-done.4), channel_id=1, source_target_pairs={{0,1},{1,0},{2,3},{3,2},{4,5},{5,4},{6,7},{7,6},{8,9},{9,8},{10,11... | collective-permute-start | bytes 2777096 | tf_op jit(solution)/shard_map/ppermute | solution.py:263
  21.3 38.7 %collective-permute-start.5 = (bf16[1552,256]{1,0:T(8,128)(2,1)}, bf16[1552,256]{1,0:T(8,128)(2,1)}, u32[]{:S(2)}, u32[]{:S(2)}) collective-permute-start(bf16[1552,256]{1,0:T(8,128)(2,1)} %get-tuple-element.7), channel_id=1, source_target_pairs={{0,1},{1,0},{2,3},{3,2},{4,5},{5,4},{6,7},{7,6},{8,9},{9,8},{10,11... | collective-permute-start | bytes 2383880 | tf_op jit(solution)/shard_map/ppermute | solution.py:263
  21.4 40.7 %collective-permute-start.6 = (bf16[1552,256]{1,0:T(8,128)(2,1)}, bf16[1552,256]{1,0:T(8,128)(2,1)}, u32[]{:S(2)}, u32[]{:S(2)}) collective-permute-start(bf16[1552,256]{1,0:T(8,128)(2,1)} %get-tuple-element.7), channel_id=1, source_target_pairs={{1,2},{2,1},{5,6},{6,5},{9,10},{10,9},{13,14},{14,13},{17,18},{18,... | collective-permute-start | bytes 2383880 | tf_op jit(solution)/shard_map/ppermute | solution.py:263
  24.1 55.7 %collective-permute-start.4 = (bf16[1808,256]{1,0:T(8,128)(2,1)S(1)}, bf16[1808,256]{1,0:T(8,128)(2,1)S(1)}, u32[]{:S(2)}, u32[]{:S(2)}) collective-permute-start(bf16[1808,256]{1,0:T(8,128)(2,1)S(1)} %collective-permute-done.3.refs_4_), channel_id=1, source_target_pairs={{1,0},{2,3},{5,4},{6,7},{9,8},{10,11},{13,12},{14,15},{17,16},{18,... | collective-permute-start | bytes 2777096 | tf_op jit(solution)/shard_map/ppermute | solution.py:263
  42.9 21.9 %collective-permute-start.1 = (bf16[1808,256]{1,0:T(8,128)(2,1)S(1)}, bf16[1808,256]{1,0:T(8,128)(2,1)}, u32[]{:S(2)}, u32[]{:S(2)}) collective-permute-start(bf16[1808,256]{1,0:T(8,128)(2,1)S(1)} %collective-permute-done.refs_2_), channel_id=1, source_target_pairs={{1,2},{2,1},{5,6},{6,5},{9,10},{10,9},{13,14},{14,13},{17,18},{18,... | collective-permute-start | bytes 2777096 | tf_op jit(solution)/shard_map/ppermute | solution.py:263
  60.1 3.5 %collective-permute-start.8 = (bf16[1552,256]{1,0:T(8,128)(2,1)}, bf16[1552,256]{1,0:T(8,128)(2,1)}, u32[]{:S(2)}, u32[]{:S(2)}) collective-permute-start(bf16[1552,256]{1,0:T(8,128)(2,1)} %collective-permute-done.5.refs_3_), channel_id=1, source_target_pairs={{1,2},{2,1},{5,6},{6,5},{9,10},{10,9},{13,14},{14,13},{17,18},{18,... | collective-permute-start | bytes 2383880 | tf_op jit(solution)/shard_map/ppermute | solution.py:263
  62.1 91.3 %collective-permute-start.7 = (bf16[1552,256]{1,0:T(8,128)(2,1)}, bf16[1552,256]{1,0:T(8,128)(2,1)}, u32[]{:S(2)}, u32[]{:S(2)}) collective-permute-start(bf16[1552,256]{1,0:T(8,128)(2,1)} %collective-permute-done.6.refs_5_), channel_id=1, source_target_pairs={{1,0},{2,3},{5,4},{6,7},{9,8},{10,11},{13,12},{14,15},{17,16},{18,... | collective-permute-start | bytes 2383880 | tf_op jit(solution)/shard_map/ppermute | solution.py:263
  63.5 118.4 %collective-permute-start.9 = (bf16[1552,256]{1,0:T(8,128)(2,1)}, bf16[1552,256]{1,0:T(8,128)(2,1)}, u32[]{:S(2)}, u32[]{:S(2)}) collective-permute-start(bf16[1552,256]{1,0:T(8,128)(2,1)} %collective-permute-done.8.refs_9_), channel_id=1, source_target_pairs={{1,0},{2,3},{5,4},{6,7},{9,8},{10,11},{13,12},{14,15},{17,16},{18,... | collective-permute-start | bytes 2383880 | tf_op jit(solution)/shard_map/ppermute | solution.py:263
  64.8 69.4 %collective-permute-start.2 = (bf16[1808,256]{1,0:T(8,128)(2,1)}, bf16[1808,256]{1,0:T(8,128)(2,1)}, u32[]{:S(2)}, u32[]{:S(2)}) collective-permute-start(bf16[1808,256]{1,0:T(8,128)(2,1)} %collective-permute-done.1.refs_8_), channel_id=1, source_target_pairs={{1,0},{2,3},{5,4},{6,7},{9,8},{10,11},{13,12},{14,15},{17,16},{18,... | collective-permute-start | bytes 2777096 | tf_op jit(solution)/shard_map/ppermute | solution.py:263
  137.6 41.3 %collective-permute-start.12 = (f32[]{:T(128)}, f32[]{:T(128)}, u32[]{:S(2)}, u32[]{:S(2)}) collective-permute-start(f32[]{:T(128)} %fusion.3), channel_id=1, source_target_pairs={{0,1},{1,0},{2,3},{3,2},{4,5},{5,4},{6,7},{7,6},{8,9},{9,8},{10,11... | collective-permute-start | bytes 20 | tf_op jit(solution)/shard_map/ppermute | solution.py:263
  137.6 41.3 %collective-permute-start.11 = (f32[]{:T(128)}, f32[]{:T(128)}, u32[]{:S(2)}, u32[]{:S(2)}) collective-permute-start(f32[]{:T(128)} %fusion.3), channel_id=1, source_target_pairs={{0,2},{1,3},{2,0},{3,1},{4,6},{5,7},{6,4},{7,5},{8,10},{9,11},{10,... | collective-permute-start | bytes 20 | tf_op jit(solution)/shard_map/ppermute | solution.py:263
  140.5 38.3 %collective-permute-start.10 = (f32[]{:T(128)}, f32[]{:T(128)}, u32[]{:S(2)}, u32[]{:S(2)}) collective-permute-start(f32[]{:T(128)} %fusion.3), channel_id=1, source_target_pairs={{0,3},{1,2},{2,1},{3,0},{4,7},{5,6},{6,5},{7,4},{8,11},{9,10},{10,... | collective-permute-start | bytes 20 | tf_op jit(solution)/shard_map/ppermute | solution.py:263
  153.3 4.9 %copy-start = (bf16[26752,256]{1,0:T(8,128)(2,1)S(1)}, bf16[26752,256]{1,0:T(8,128)(2,1)}, u32[]{:S(2)}) copy-start(bf16[26752,256]{1,0:T(8,128)(2,1)} %all-gather.3.cloned.1.call-done) | copy-start | bytes 41091076
Sparse Core Ops, SparseCore 0:
  14.9 79.4 all-gather.2

commit v6 on v5

--- a/solution.py
+++ b/solution.py
@@ -13,7 +13,9 @@
 NOTE_ROWS = 16
 
 
-def pack_kernel(cols_ref, flag_ref, first_ref, x_ref, part_a, part_b, full, note, norm, sems):
+def pack_kernel(
+    cols_ref, flag_ref, first_ref, x_ref, part_a, part_b, full, note, norm, zeros, sems
+):
     count, block, _ = x_ref.shape
     slots = cols_ref.shape[0]
     rows = count // slots
@@ -35,6 +37,15 @@
             sends.append((wanted, copy))
         place = place + filled.astype(jnp.int32)
 
+    blank = pltpu.make_async_copy(zeros, full.at[pl.ds(0, block)], sems.at[0, count + 1])
+
+    @pl.when(place == 0)
+    def _():
+        zeros[...] = jnp.zeros_like(zeros)
+        blank.start()
+
+    sends.append((place == 0, blank))
+
     norm[...] = jnp.zeros_like(norm)
     eye_rows = lax.broadcasted_iota(jnp.int32, (block, block), 0)
     eye = eye_rows == lax.broadcasted_iota(jnp.int32, (block, block), 1)
@@ -91,7 +102,8 @@
         scratch_shapes=[
             pltpu.VMEM((NOTE_ROWS, block), x_blocks.dtype),
             pltpu.VMEM((1, block), jnp.float32),
-            pltpu.SemaphoreType.DMA((3, count + 1)),
+            pltpu.VMEM((block, block), x_blocks.dtype),
+            pltpu.SemaphoreType.DMA((3, count + 2)),
         ],
         compiler_params=pltpu.CompilerParams(vmem_limit_bytes=(4 * count * block * block) + (8 << 20)),
     )(x_cols.T, branch_flag, first_row.reshape(1), x_blocks.reshape(count, block, block))
@@ -104,11 +116,9 @@
     n_arrays = 1 + max(load[0] for load in loads)
     plane = refs[0]
     arrays = refs[:n_arrays]
-    out_ref, pool, ring, more, done, in_sem, ring_sem, out_sem = refs[-8:]
+    out_ref, pool, more, done, in_sem, out_sem = refs[-6:]
     block = out_ref.shape[-1]
     n_out = table[0]
-    n_terms = table[1]
-    depth = ring.shape[0] - 1
     zero_entry = pool.shape[0] - 1
 
     copies = []
@@ -127,20 +137,7 @@
         entry = lax.shift_right_logical(index, STRIDE.bit_length() - 1)
         return entry, pl.multiple_of(jnp.bitwise_and(index, STRIDE - 1) * block, block)
 
-    def fetch(term):
-        entry, first = decode(table[layout["rights"] + term])
-        slot = lax.rem(term, depth)
-        return pltpu.make_async_copy(
-            plane.at[entry, pl.ds(first, block)], ring.at[slot], ring_sem.at[slot]
-        )
-
-    def begin(term, carry):
-        fetch(term).start()
-        return carry
-
-    lax.fori_loop(0, jnp.minimum(depth, n_terms), begin, 0)
     pool[zero_entry, pl.ds(0, block)] = jnp.zeros((block, block), pool.dtype)
-    ring[depth] = jnp.zeros((block, block), ring.dtype)
     for here, copy in copies:
         pl.when(here)(copy.wait)
 
@@ -148,10 +145,9 @@
         entry, first = decode(
             jnp.where(live, table[layout["lefts"] + term], zero_entry * STRIDE)
         )
-        slot = jnp.where(live, lax.rem(term, depth), depth)
-        return jnp.dot(
-            pool[entry, pl.ds(first, block)], ring[slot], preferred_element_type=jnp.float32
-        )
+        left = pool[entry, pl.ds(first, block)]
+        entry, first = decode(jnp.where(live, table[layout["rights"] + term], 0))
+        return jnp.dot(left, plane[entry, pl.ds(first, block)], preferred_element_type=jnp.float32)
 
     def write(number, slot):
         output = table[layout["outs"] + number]
@@ -165,11 +161,6 @@
             counts.append(table[layout["counts"] + batch * BATCH + local])
             last = last + counts[local]
 
-        def arrived(number, carry):
-            fetch(number).wait()
-            return carry
-
-        lax.fori_loop(term, last, arrived, 0)
         half = lax.rem(batch, 2) * BATCH
         for local in range(BATCH):
             @pl.when(batch >= 2)
@@ -207,11 +198,6 @@
             def _():
                 write(batch * BATCH + local, half + local).start()
 
-        def refill(number, carry):
-            fetch(number + depth).start()
-            return carry
-
-        lax.fori_loop(term, jnp.clip(n_terms - depth, term, last), refill, 0)
         return last
 
     n_batches = (n_out + BATCH - 1) // BATCH
@@ -231,10 +217,11 @@
     outputs = rows * kept
     smem = pl.BlockSpec(memory_space=pltpu.SMEM)
     hbm = pl.BlockSpec(memory_space=pltpu.HBM)
-    depth = 48
-    vmem = ((n_entries + 1) * PACKED + depth + 5 * BATCH) * block * block * 2 + (8 << 20)
+    blocks = (n_entries + 1 + arrays[0].shape[0]) * PACKED + 4 * BATCH
+    vmem = blocks * block * block * 2 + (6 << 20)
     operands = [table, *arrays]
-    in_specs = [smem] + [hbm] * len(arrays)
+    whole = pl.BlockSpec(memory_space=pltpu.VMEM)
+    in_specs = [smem, whole] + [hbm] * (len(arrays) - 1)
     aliases = {}
     if before is not None:
         operands += [before[1], before[0]]
@@ -247,11 +234,9 @@
         out_specs=hbm,
         scratch_shapes=[
             pltpu.VMEM((n_entries + 1, PACKED * block, block), dtype),
-            pltpu.VMEM((depth + 1, block, block), dtype),
             pltpu.VMEM((BATCH, block, block), jnp.float32),
             pltpu.VMEM((2 * BATCH, block, block), dtype),
             pltpu.SemaphoreType.DMA((len(loads),)),
-            pltpu.SemaphoreType.DMA((depth,)),
             pltpu.SemaphoreType.DMA((2 * BATCH,)),
         ],
         input_output_aliases=aliases,
@@ -415,7 +400,8 @@
     table, layout = make_table(early, right_of, owns, branch_flag, everything, width, wanted)
     purified = multiply(list(arrays), tuple(loads), 4, layout, table, shape)
 
-    late = straight(note["end_three"][None], jnp.array([3], jnp.int32), end[None])
+    farthest, purified = lax.optimization_barrier((note["end_three"], purified))
+    late = straight(farthest[None], jnp.array([3], jnp.int32), end[None])
     meets = (jnp.repeat(late, kept, axis=0) > 0) & (right_of > 0)
     chosen = jnp.any(meets, axis=1)
     add("end_three", 3, at_ends)

time: 209 us -> 193 us (0.923); the launches traced: 211 us -> 192 us
  Pallas kernels: 46.3 us -> 25.5 us
  local copies, waits for them, and re-layouts: 15 us -> 19.3 us
    pallas_call x2, Pallas kernels: 42.7 us -> 21.9 us  [multiply(): pl.pallas_call(functools.partial(multiply_kernel, loads, kept, layout), o...]
    unnamed x12 -> x16, local copies, waits for them, and re-layouts: 9.56 us -> 14.5 us
  transfers between devices with their start and end apart: 14 -> 14, of which waited for: 4 -> 4; matrix products, arithmetic and copies ran while one was open for 11% -> 11% of each run, Pallas kernels for 10% -> 6%
where the time goes in v6:
time: 193 us; the launch traced here: 192 us
  waiting for transfers between devices  96.4 us (50%)
  Pallas kernels  25.5 us (13%)
  starting transfers between devices  21 us (11%)
  local copies, waits for them, and re-layouts  19.3 us (10%)
  other arithmetic  15.6 us (8%)
  between operations  14.4 us (7%)
    ppermute x13, waiting for transfers between devices, shift(): return lax.ppermute(array, 'col', pairs)  96.4 us
    pallas_call x2, Pallas kernels, multiply(): pl.pallas_call(functools.partial(multiply_kernel, loads, kept, layout), o...  21.9 us
    ppermute x13, starting transfers between devices, shift(): return lax.ppermute(array, 'col', pairs)  20.9 us
    unnamed x16, local copies, waits for them, and re-layouts  14.5 us
  transfers between devices with their start and end apart: 14, of which 4 were waited for; matrix products, arithmetic and copies ran while one was open for 11% of the time, Pallas kernels for 6%

profile of v6, /device:TPU:0, one launch (start us, length us, event | category | flops | bytes accessed | tf_op | source)
XLA Modules:
  0.0 192.2 jit_solution(1379656385833143535)
XLA Ops:
  7.2 1.6 copy-done.2
  10.1 3.6 %shard_map.68 = (bf16[1808,256]{1,0:T(8,128)(2,1)S(1)}, bf16[1552,256]{1,0:T(8,128)(2,1)}, bf16[3344,256]{1,0:T(8,128)(2,1)}) custom-call(s32[2,8]{1,0:T(2,128)S(1)} %bitcast.31, s32[8]{0:T(128)S(1)} %copy-done.4, s32[1]{0:T(128)} %bitcast.1.first_ref, bf16[16,256,256]{2,1,0:T(8,128)(2,1)S(1)} %bitcast.29), custom_call_target="tpu_custom_call" | custom-call | tf_op jit(solution)/shard_map/pallas_call | solution.py:94
  15.5 5.8 %collective-permute-start.5 = (bf16[1552,256]{1,0:T(8,128)(2,1)}, bf16[1552,256]{1,0:T(8,128)(2,1)}, u32[]{:S(2)}, u32[]{:S(2)}) collective-permute-start(bf16[1552,256]{1,0:T(8,128)(2,1)} %get-tuple-element.9), channel_id=1, source_target_pairs={{0,1},{1,0},{2,3},{3,2},{4,5},{5,4},{6,7},{7,6},{8,9},{9,8},{10,11... | collective-permute-start | bytes 2383880 | tf_op jit(solution)/shard_map/ppermute | solution.py:248
  21.4 1.6 collective-permute-start.6
  24.1 16.1 %collective-permute-done.5.refs_3_ = bf16[1552,256]{1,0:T(8,128)(2,1)} collective-permute-done((bf16[1552,256]{1,0:T(8,128)(2,1)}, bf16[1552,256]{1,0:T(8,128)(2,1)}, u32[]{:S(2)}, u32[]{:S(2)}) %collective-permute-start.5) | collective-permute-done | bytes 794656 | tf_op jit(solution)/shard_map/ppermute | solution.py:248
  40.2 1.6 collective-permute-start.8
  41.8 1.3 collective-permute-start.4
  43.1 16.8 %collective-permute-done.refs_2_ = bf16[1808,256]{1,0:T(8,128)(2,1)S(1)} collective-permute-done((bf16[1808,256]{1,0:T(8,128)(2,1)}, bf16[1808,256]{1,0:T(8,128)(2,1)S(1)}, u32[]{:S(2)}, u32[]{:S(2)}) %collective-permute-start) | collective-permute-done | bytes 925728 | tf_op jit(solution)/shard_map/ppermute | solution.py:248
  59.9 1.6 collective-permute-start.1
  62.9 1.3 collective-permute-start.7
  64.4 1.3 collective-permute-start.9
  65.7 14.1 %collective-permute-done.4.refs_6_ = bf16[1808,256]{1,0:T(8,128)(2,1)S(1)} collective-permute-done((bf16[1808,256]{1,0:T(8,128)(2,1)S(1)}, bf16[1808,256]{1,0:T(8,128)(2,1)S(1)}, u32[]{:S(2)}, u32[]{:S(2)}) %collective-permute-start.4) | collective-permute-done | bytes 925728 | tf_op jit(solution)/shard_map/ppermute | solution.py:248
  80.6 1.3 collective-permute-start.2
  83.3 49.3 %collective-permute-done.2.refs_10_ = bf16[1808,256]{1,0:T(8,128)(2,1)} collective-permute-done((bf16[1808,256]{1,0:T(8,128)(2,1)}, bf16[1808,256]{1,0:T(8,128)(2,1)}, u32[]{:S(2)}, u32[]{:S(2)}) %collective-permute-start.2) | collective-permute-done | bytes 925728 | tf_op jit(solution)/shard_map/ppermute | solution.py:248
  133.3 1.4 fusion.3
  134.6 1.9 collective-permute-start.11
  136.5 2.5 %collective-permute-start.10 = (f32[]{:T(128)}, f32[]{:T(128)}, u32[]{:S(2)}, u32[]{:S(2)}) collective-permute-start(f32[]{:T(128)} %fusion.3), channel_id=1, source_target_pairs={{0,3},{1,2},{2,1},{3,0},{4,7},{5,6},{6,5},{7,4},{8,11},{9,10},{10,... | collective-permute-start | bytes 20 | tf_op jit(solution)/shard_map/ppermute | solution.py:248
  143.7 1.4 concatenate.16.table
  145.1 4.9 %copy-done = bf16[26752,256]{1,0:T(8,128)(2,1)S(1)} copy-done((bf16[26752,256]{1,0:T(8,128)(2,1)S(1)}, bf16[26752,256]{1,0:T(8,128)(2,1)}, u32[]{:S(2)}) %copy-start) | copy-done | bytes 13697048
  150.0 11.2 %shard_map.69.refs_13_ = bf16[32,256,256]{2,1,0:T(8,128)(2,1)} custom-call(s32[325]{0:T(512)S(1)} %concatenate.16.table, bf16[8,3344,256]{2,1,0:T(8,128)(2,1)S(1)} %bitcast.27, bf16[3344,256]{1,0:T(8,128)(2,1)} %get-tuple-element.8.refs_1_, bf16[1808,256]{1,0:T(8,128)(2,1)S(1)} %collective-permute-done.refs_2_, ...), custom_call_target="tpu_custom_call" | custom-call | tf_op jit(solution)/shard_map/pallas_call | solution.py:230
  165.3 1.2 concatenate.17.table
  166.6 3.1 %fusion.5 = f32[]{:T(128)} fusion(f32[]{:T(128)} %fusion.3, s32[]{:T(128)S(6)} %axis_index.25, f32[]{:T(128)} %collective-permute-done.12, s32[]{:T(128)S(6)} %xor.11, f32[]{:T(128)} %collective-permute-done.11, s32[]{:T(128)S(6)} %xor.10, f32[]{:T(128)} %collective-permute-done.10, s32[]{:T(128)S(6)} %xor.9), kind=kLoop, calls=%fused_computation.80 | loop fusion | flops 35 | bytes 36 | tf_op jit(solution)/shard_map/reduce_sum | solution.py:345
  169.7 4.9 %copy-done.1 = bf16[26752,256]{1,0:T(8,128)(2,1)S(1)} copy-done((bf16[26752,256]{1,0:T(8,128)(2,1)S(1)}, bf16[26752,256]{1,0:T(8,128)(2,1)}, u32[]{:S(2)}) %copy-start.1) | copy-done | bytes 13697048
  174.6 10.7 %shard_map.70 = bf16[32,256,256]{2,1,0:T(8,128)(2,1)} custom-call(s32[325]{0:T(512)S(1)} %concatenate.17.table, bf16[8,3344,256]{2,1,0:T(8,128)(2,1)S(1)} %bitcast.28, bf16[3344,256]{1,0:T(8,128)(2,1)} %get-tuple-element.8.refs_1_, bf16[1808,256]{1,0:T(8,128)(2,1)S(1)} %collective-permute-done.refs_2_, ...), custom_call_target="tpu_custom_call", output_to_operand_aliasing={{}: (14, {})} | custom-call | tf_op jit(solution)/shard_map/pallas_call | solution.py:230
  (113 shorter events, 17.3 us)
Async XLA Ops:
  7.2 126.1 %all-gather.3.cloned.1.call-start = ((), (), s32[]{:S(2)}) async-start(), calls=%async_computation | async-start | bytes 15409152 | tf_op jit(solution)/shard_map/all_gather | solution.py:336
  7.2 1.6 copy-start.2
  8.8 0.7 copy-start.3
  9.5 0.7 copy-start.4
  13.8 0.9 copy-start.6
  14.7 27.1 %collective-permute-start.3 = (bf16[1808,256]{1,0:T(8,128)(2,1)}, bf16[1808,256]{1,0:T(8,128)(2,1)S(1)}, u32[]{:S(2)}, u32[]{:S(2)}) collective-permute-start(bf16[1808,256]{1,0:T(8,128)(2,1)} %copy-done.6), channel_id=1, source_target_pairs={{1,2},{2,1},{5,6},{6,5},{9,10},{10,9},{13,14},{14,13},{17,18},{18,... | collective-permute-start | bytes 2777096 | tf_op jit(solution)/shard_map/ppermute | solution.py:248
  15.5 24.7 %collective-permute-start.5 = (bf16[1552,256]{1,0:T(8,128)(2,1)}, bf16[1552,256]{1,0:T(8,128)(2,1)}, u32[]{:S(2)}, u32[]{:S(2)}) collective-permute-start(bf16[1552,256]{1,0:T(8,128)(2,1)} %get-tuple-element.9), channel_id=1, source_target_pairs={{0,1},{1,0},{2,3},{3,2},{4,5},{5,4},{6,7},{7,6},{8,9},{9,8},{10,11... | collective-permute-start | bytes 2383880 | tf_op jit(solution)/shard_map/ppermute | solution.py:248
  21.3 38.6 %collective-permute-start = (bf16[1808,256]{1,0:T(8,128)(2,1)}, bf16[1808,256]{1,0:T(8,128)(2,1)S(1)}, u32[]{:S(2)}, u32[]{:S(2)}) collective-permute-start(bf16[1808,256]{1,0:T(8,128)(2,1)} %copy-done.6), channel_id=1, source_target_pairs={{0,1},{1,0},{2,3},{3,2},{4,5},{5,4},{6,7},{7,6},{8,9},{9,8},{10,11... | collective-permute-start | bytes 2777096 | tf_op jit(solution)/shard_map/ppermute | solution.py:248
  21.4 41.5 %collective-permute-start.6 = (bf16[1552,256]{1,0:T(8,128)(2,1)}, bf16[1552,256]{1,0:T(8,128)(2,1)}, u32[]{:S(2)}, u32[]{:S(2)}) collective-permute-start(bf16[1552,256]{1,0:T(8,128)(2,1)} %get-tuple-element.9), channel_id=1, source_target_pairs={{1,2},{2,1},{5,6},{6,5},{9,10},{10,9},{13,14},{14,13},{17,18},{18,... | collective-permute-start | bytes 2383880 | tf_op jit(solution)/shard_map/ppermute | solution.py:248
  40.2 24.2 %collective-permute-start.8 = (bf16[1552,256]{1,0:T(8,128)(2,1)}, bf16[1552,256]{1,0:T(8,128)(2,1)}, u32[]{:S(2)}, u32[]{:S(2)}) collective-permute-start(bf16[1552,256]{1,0:T(8,128)(2,1)} %collective-permute-done.5.refs_3_), channel_id=1, source_target_pairs={{1,2},{2,1},{5,6},{6,5},{9,10},{10,9},{13,14},{14,13},{17,18},{18,... | collective-permute-start | bytes 2383880 | tf_op jit(solution)/shard_map/ppermute | solution.py:248
  41.8 38.0 %collective-permute-start.4 = (bf16[1808,256]{1,0:T(8,128)(2,1)S(1)}, bf16[1808,256]{1,0:T(8,128)(2,1)S(1)}, u32[]{:S(2)}, u32[]{:S(2)}) collective-permute-start(bf16[1808,256]{1,0:T(8,128)(2,1)S(1)} %collective-permute-done.3.refs_4_), channel_id=1, source_target_pairs={{1,0},{2,3},{5,4},{6,7},{9,8},{10,11},{13,12},{14,15},{17,16},{18,... | collective-permute-start | bytes 2777096 | tf_op jit(solution)/shard_map/ppermute | solution.py:248
  59.9 19.9 %collective-permute-start.1 = (bf16[1808,256]{1,0:T(8,128)(2,1)S(1)}, bf16[1808,256]{1,0:T(8,128)(2,1)}, u32[]{:S(2)}, u32[]{:S(2)}) collective-permute-start(bf16[1808,256]{1,0:T(8,128)(2,1)S(1)} %collective-permute-done.refs_2_), channel_id=1, source_target_pairs={{1,2},{2,1},{5,6},{6,5},{9,10},{10,9},{13,14},{14,13},{17,18},{18,... | collective-permute-start | bytes 2777096 | tf_op jit(solution)/shard_map/ppermute | solution.py:248
  62.9 82.2 %collective-permute-start.7 = (bf16[1552,256]{1,0:T(8,128)(2,1)}, bf16[1552,256]{1,0:T(8,128)(2,1)}, u32[]{:S(2)}, u32[]{:S(2)}) collective-permute-start(bf16[1552,256]{1,0:T(8,128)(2,1)} %collective-permute-done.6.refs_5_), channel_id=1, source_target_pairs={{1,0},{2,3},{5,4},{6,7},{9,8},{10,11},{13,12},{14,15},{17,16},{18,... | collective-permute-start | bytes 2383880 | tf_op jit(solution)/shard_map/ppermute | solution.py:248
  64.4 105.3 %collective-permute-start.9 = (bf16[1552,256]{1,0:T(8,128)(2,1)}, bf16[1552,256]{1,0:T(8,128)(2,1)}, u32[]{:S(2)}, u32[]{:S(2)}) collective-permute-start(bf16[1552,256]{1,0:T(8,128)(2,1)} %collective-permute-done.8.refs_9_), channel_id=1, source_target_pairs={{1,0},{2,3},{5,4},{6,7},{9,8},{10,11},{13,12},{14,15},{17,16},{18,... | collective-permute-start | bytes 2383880 | tf_op jit(solution)/shard_map/ppermute | solution.py:248
  80.6 52.0 %collective-permute-start.2 = (bf16[1808,256]{1,0:T(8,128)(2,1)}, bf16[1808,256]{1,0:T(8,128)(2,1)}, u32[]{:S(2)}, u32[]{:S(2)}) collective-permute-start(bf16[1808,256]{1,0:T(8,128)(2,1)} %collective-permute-done.1.refs_8_), channel_id=1, source_target_pairs={{1,0},{2,3},{5,4},{6,7},{9,8},{10,11},{13,12},{14,15},{17,16},{18,... | collective-permute-start | bytes 2777096 | tf_op jit(solution)/shard_map/ppermute | solution.py:248
  134.6 31.9 %collective-permute-start.12 = (f32[]{:T(128)}, f32[]{:T(128)}, u32[]{:S(2)}, u32[]{:S(2)}) collective-permute-start(f32[]{:T(128)} %fusion.3), channel_id=1, source_target_pairs={{0,1},{1,0},{2,3},{3,2},{4,5},{5,4},{6,7},{7,6},{8,9},{9,8},{10,11... | collective-permute-start | bytes 20 | tf_op jit(solution)/shard_map/ppermute | solution.py:248
  134.6 32.0 %collective-permute-start.11 = (f32[]{:T(128)}, f32[]{:T(128)}, u32[]{:S(2)}, u32[]{:S(2)}) collective-permute-start(f32[]{:T(128)} %fusion.3), channel_id=1, source_target_pairs={{0,2},{1,3},{2,0},{3,1},{4,6},{5,7},{6,4},{7,5},{8,10},{9,11},{10,... | collective-permute-start | bytes 20 | tf_op jit(solution)/shard_map/ppermute | solution.py:248
  136.5 30.1 %collective-permute-start.10 = (f32[]{:T(128)}, f32[]{:T(128)}, u32[]{:S(2)}, u32[]{:S(2)}) collective-permute-start(f32[]{:T(128)} %fusion.3), channel_id=1, source_target_pairs={{0,3},{1,2},{2,1},{3,0},{4,7},{5,6},{6,5},{7,4},{8,11},{9,10},{10,... | collective-permute-start | bytes 20 | tf_op jit(solution)/shard_map/ppermute | solution.py:248
  140.8 24.5 %copy-start.5 = (s32[8]{0:T(128)S(1)}, s32[8]{0:T(128)}, u32[]{:S(2)}) copy-start(s32[8]{0:T(128)} %flag_ref.1) | copy-start | bytes 100
  145.1 4.9 %copy-start = (bf16[26752,256]{1,0:T(8,128)(2,1)S(1)}, bf16[26752,256]{1,0:T(8,128)(2,1)}, u32[]{:S(2)}) copy-start(bf16[26752,256]{1,0:T(8,128)(2,1)} %all-gather.3.cloned.1.call-done) | copy-start | bytes 41091076
  169.7 4.9 %copy-start.1 = (bf16[26752,256]{1,0:T(8,128)(2,1)S(1)}, bf16[26752,256]{1,0:T(8,128)(2,1)}, u32[]{:S(2)}) copy-start(bf16[26752,256]{1,0:T(8,128)(2,1)} %all-gather.3.cloned.1.call-done) | copy-start | bytes 41091076
Sparse Core Ops, SparseCore 0:
  14.9 79.5 all-gather.2

commit v7 on v6

--- a/solution.py
+++ b/solution.py
@@ -112,13 +112,17 @@
 BATCH = 4
 
 
-def multiply_kernel(loads, kept, layout, table, *refs):
-    n_arrays = 1 + max(load[0] for load in loads)
-    plane = refs[0]
-    arrays = refs[:n_arrays]
-    out_ref, pool, more, done, in_sem, out_sem = refs[-6:]
+def multiply_kernel(loads, kept, layout, turned, early, table, plane, *refs):
+    arrays = refs[: 1 + max(load[0] for load in loads)]
+    if early:
+        out_ref, token, pool, more, done, in_sem, out_sem = refs[-7:]
+        token[0] = 0
+    else:
+        out_ref, pool, more, done, in_sem, out_sem, ring, ring_sem = refs[-8:]
+        depth = ring.shape[0] - 1
     block = out_ref.shape[-1]
     n_out = table[0]
+    n_terms = table[1]
     zero_entry = pool.shape[0] - 1
 
     copies = []
@@ -137,7 +141,43 @@
         entry = lax.shift_right_logical(index, STRIDE.bit_length() - 1)
         return entry, pl.multiple_of(jnp.bitwise_and(index, STRIDE - 1) * block, block)
 
+    def fetch(term):
+        entry, first = decode(table[layout["rights"] + term])
+        slot = lax.rem(term, depth)
+        return pltpu.make_async_copy(
+            plane.at[entry, pl.ds(first, block)], ring.at[slot], ring_sem.at[slot]
+        )
+
+    if not early:
+        def begin(term, carry):
+            fetch(term).start()
+            return carry
+
+        lax.fori_loop(0, jnp.minimum(depth, n_terms), begin, 0)
+        ring[depth] = jnp.zeros((block, block), ring.dtype)
+
     pool[zero_entry, pl.ds(0, block)] = jnp.zeros((block, block), pool.dtype)
+
+    if turned is not None:
+        is_wanted, at, target = turned
+
+        @pl.when(table[is_wanted] != 0)
+        def _():
+            down = lax.broadcasted_iota(jnp.int32, (block, block), 0)
+            eye = down == lax.broadcasted_iota(jnp.int32, (block, block), 1)
+            eye = eye.astype(jnp.float32).astype(pool.dtype)
+
+            def turn(place, carry):
+                first = pl.multiple_of(place * block, block)
+                for entry in range(2):
+                    straight = plane[table[at] + entry, pl.ds(first, block)]
+                    pool[target + entry, pl.ds(first, block)] = lax.dot_general(
+                        eye, straight, (((1,), (1,)), ((), ())), preferred_element_type=jnp.float32
+                    ).astype(pool.dtype)
+                return carry
+
+            lax.fori_loop(0, PACKED, turn, 0)
+
     for here, copy in copies:
         pl.when(here)(copy.wait)
 
@@ -146,8 +186,12 @@
             jnp.where(live, table[layout["lefts"] + term], zero_entry * STRIDE)
         )
         left = pool[entry, pl.ds(first, block)]
-        entry, first = decode(jnp.where(live, table[layout["rights"] + term], 0))
-        return jnp.dot(left, plane[entry, pl.ds(first, block)], preferred_element_type=jnp.float32)
+        if early:
+            entry, first = decode(jnp.where(live, table[layout["rights"] + term], 0))
+            right = plane[entry, pl.ds(first, block)]
+        else:
+            right = ring[jnp.where(live, lax.rem(term, depth), depth)]
+        return jnp.dot(left, right, preferred_element_type=jnp.float32)
 
     def write(number, slot):
         output = table[layout["outs"] + number]
@@ -161,25 +205,29 @@
             counts.append(table[layout["counts"] + batch * BATCH + local])
             last = last + counts[local]
 
+        if not early:
+            def arrived(number, carry):
+                fetch(number).wait()
+                return carry
+
+            lax.fori_loop(term, last, arrived, 0)
         half = lax.rem(batch, 2) * BATCH
         for local in range(BATCH):
             @pl.when(batch >= 2)
             def _():
                 write((batch - 2) * BATCH + local, half + local).wait()
 
-            @pl.when(counts[local] > 2)
-            def _():
-                more[local] = product(begins[local] + 2, True)
-
-                def one_term(number, carry):
-                    more[local] += product(number, True)
-                    return carry
-
-                lax.fori_loop(begins[local] + 3, begins[local] + counts[local], one_term, 0)
-
-            @pl.when(counts[local] <= 2)
-            def _():
-                more[local] = jnp.zeros_like(more[local])
+            more[local] = jnp.zeros_like(more[local])
+
+            def two_terms(pair, carry):
+                number = begins[local] + 2 + 2 * pair
+                second = number + 1 < begins[local] + counts[local]
+                more[local] += product(number, True) + product(
+                    jnp.where(second, number + 1, 0), second
+                )
+                return carry
+
+            lax.fori_loop(0, (counts[local] - 1) // 2, two_terms, 0)
 
         for local in range(BATCH):
             output = table[layout["outs"] + batch * BATCH + local]
@@ -198,6 +246,12 @@
             def _():
                 write(batch * BATCH + local, half + local).start()
 
+        if not early:
+            def refill(number, carry):
+                fetch(number + depth).start()
+                return carry
+
+            lax.fori_loop(term, jnp.clip(n_terms - depth, term, last), refill, 0)
         return last
 
     n_batches = (n_out + BATCH - 1) // BATCH
@@ -212,33 +266,46 @@
                 write(number, lax.rem(batch, 2) * BATCH + local).wait()
 
 
-def multiply(arrays, loads, n_entries, layout, table, shape, before=None):
+def multiply(plane, arrays, loads, n_entries, layout, table, shape, turned=None, before=None):
     rows, kept, block, dtype = shape
     outputs = rows * kept
+    early = before is None
     smem = pl.BlockSpec(memory_space=pltpu.SMEM)
     hbm = pl.BlockSpec(memory_space=pltpu.HBM)
-    blocks = (n_entries + 1 + arrays[0].shape[0]) * PACKED + 4 * BATCH
-    vmem = blocks * block * block * 2 + (6 << 20)
-    operands = [table, *arrays]
-    whole = pl.BlockSpec(memory_space=pltpu.VMEM)
-    in_specs = [smem, whole] + [hbm] * (len(arrays) - 1)
+    scratch = [
+        pltpu.VMEM((n_entries + 1, PACKED * block, block), dtype),
+        pltpu.VMEM((BATCH, block, block), jnp.float32),
+        pltpu.VMEM((2 * BATCH, block, block), dtype),
+        pltpu.SemaphoreType.DMA((len(loads),)),
+        pltpu.SemaphoreType.DMA((2 * BATCH,)),
+    ]
+    operands = [table, plane, *arrays]
+    in_specs = [smem, pl.BlockSpec(memory_space=pltpu.VMEM)] + [hbm] * len(arrays)
+    out_shape = [jax.ShapeDtypeStruct((outputs, block, block), dtype)]
+    out_specs = [hbm]
     aliases = {}
-    if before is not None:
+    if early:
+        out_shape.append(jax.ShapeDtypeStruct((1,), jnp.int32))
+        out_specs.append(smem)
+        blocks = (n_entries + 1 + plane.shape[0]) * PACKED + 4 * BATCH
+        vmem = blocks * block * block * 2 + (6 << 20)
+    else:
+        depth = 32
+        scratch += [
+            pltpu.VMEM((depth + 1, block, block), dtype),
+            pltpu.SemaphoreType.DMA((depth,)),
+        ]
+        in_specs[1] = hbm
         operands += [before[1], before[0]]
         in_specs += [smem, hbm]
         aliases = {len(operands) - 1: 0}
+        vmem = 58 << 20
     return pl.pallas_call(
-        functools.partial(multiply_kernel, loads, kept, layout),
-        out_shape=jax.ShapeDtypeStruct((outputs, block, block), dtype),
+        functools.partial(multiply_kernel, loads, kept, layout, turned, early),
+        out_shape=out_shape,
         in_specs=in_specs,
-        out_specs=hbm,
-        scratch_shapes=[
-            pltpu.VMEM((n_entries + 1, PACKED * block, block), dtype),
-            pltpu.VMEM((BATCH, block, block), jnp.float32),
-            pltpu.VMEM((2 * BATCH, block, block), dtype),
-            pltpu.SemaphoreType.DMA((len(loads),)),
-            pltpu.SemaphoreType.DMA((2 * BATCH,)),
-        ],
+        out_specs=out_specs,
+        scratch_shapes=scratch,
         input_output_aliases=aliases,
         compiler_params=pltpu.CompilerParams(vmem_limit_bytes=vmem),
     )(*operands)
@@ -253,7 +320,10 @@
     middle = shift(part, [(1, 2), (2, 1)])
     end_two = shift(middle, [(1, 0), (2, 3)])
     middle_two = shift(first, [(1, 2), (2, 1)])
-    end_three = shift(middle_two, [(1, 0), (2, 3)])
+    pairs = []
+    for row in range(lax.axis_size("row")):
+        pairs += [(4 * row + 1, 4 * row)] * (row // 2 != 0) + [(4 * row + 2, 4 * row + 3)] * (row // 2 != 3)
+    end_three = lax.ppermute(middle_two, ("row", "col"), pairs)
     return {
         "first": first,
         "middle": middle,
@@ -359,29 +429,43 @@
         hit = (cols[..., None] == every) & (wanted[:, None, None, None] != 0)
         return jnp.sum(jnp.where(hit, at[..., None] + 1, 0), axis=(0, 2))
 
+    def turned(cols, entry, device, wanted):
+        at = places(cols) + STRIDE * (entry + jnp.arange(2, dtype=jnp.int32)[:, None, None])
+        own = row * rows + jnp.arange(rows, dtype=jnp.int32)
+        hit = (cols[..., None] == own) & wanted
+        found = jnp.sum(jnp.where(hit, at[..., None] + 1, 0), axis=2)
+        names = device * rows + jnp.arange(2 * rows, dtype=jnp.int32).reshape(2, rows)
+        found = jnp.where(names[:, :, None, None] == every, found[..., None], 0)
+        return jnp.sum(found, axis=(0, 1))
+
     everything = jnp.ones((rows * kept,), bool)
     one = jnp.ones((1,), jnp.int32)
-    if n_col != 4:
+    if not (n_col == 4 and n_row == 8):
         line = lax.all_gather(full, "col", axis=0)
         entries = 1 + jnp.arange(n_col, dtype=jnp.int32)
         left_of = straight(facts(line), entries, jnp.ones((n_col,), jnp.int32))
         table, layout = make_table(
             left_of, right_of, owns, branch_flag, everything, width, one
         )
-        loads = [(2, None, 0, 0, PACKED, 2)]
-        loads += [(1, c, 1 + c, 0, PACKED, 2) for c in range(n_col)]
-        purified = multiply([plane, line, full], tuple(loads), 1 + n_col, layout, table, shape)
+        loads = [(1, None, 0, 0, PACKED, 2)]
+        loads += [(0, c, 1 + c, 0, PACKED, 2) for c in range(n_col)]
+        purified, _ = multiply(
+            plane, [line, full], tuple(loads), 1 + n_col, layout, table, shape
+        )
         return purified.reshape(rows, kept, block, block), trace
 
     line = [gather_line(part) for part in (part_a, part_b)]
     note = {name: facts(array) for name, array in line[0].items()}
     at_end = (col == 0) | (col == n_col - 1)
+    corner = at_end & (row // 2 == col)
     end = at_end.astype(jnp.int32)
-    wanted = jnp.stack([jnp.int32(1), end, 1 - end])
-    always, at_ends, inside = 2, 3, 4
-
-    arrays = [plane, full]
-    loads = [(1, None, 0, 0, PACKED, always)]
+    turn_row = 2 * (n_col - 1 - col)
+    wanted = [jnp.int32(1), end, 1 - end, end - corner, corner, turn_row]
+    wanted = jnp.stack([value.astype(jnp.int32) for value in wanted])
+    always, at_ends, inside, at_far, at_corner, turn_at = range(2, 8)
+
+    arrays = [full]
+    loads = [(0, None, 0, 0, PACKED, always)]
 
     def add(name, entry, wanted):
         spans = ((0, SPLIT), (SPLIT, PACKED - SPLIT))
@@ -393,21 +477,26 @@
     early_cols = jnp.stack(early_cols + [note["middle_two"]])
     early_wanted = jnp.stack([jnp.int32(1)] * 3 + [1 - end])
     early = straight(early_cols, jnp.arange(4, dtype=jnp.int32), early_wanted)
+    turn_cols = lax.dynamic_slice_in_dim(plane_cols, turn_row, 2, 0)
+    early = early + turned(turn_cols, 4, turn_row, corner)
     add("first", 1, always)
     add("middle", 2, inside)
     add("end_two", 2, at_ends)
     add("middle_two", 3, inside)
     table, layout = make_table(early, right_of, owns, branch_flag, everything, width, wanted)
-    purified = multiply(list(arrays), tuple(loads), 4, layout, table, shape)
-
-    farthest, purified = lax.optimization_barrier((note["end_three"], purified))
-    late = straight(farthest[None], jnp.array([3], jnp.int32), end[None])
+    purified, token = multiply(
+        plane, list(arrays), tuple(loads), 6, layout, table, shape, (at_corner, turn_at, 4)
+    )
+
+    far_cols = (note["end_three"] + token)[None]
+    late = straight(far_cols, jnp.array([3], jnp.int32), wanted[None, at_far - 2])
     meets = (jnp.repeat(late, kept, axis=0) > 0) & (right_of > 0)
     chosen = jnp.any(meets, axis=1)
-    add("end_three", 3, at_ends)
+    add("end_three", 3, at_far)
     table, layout = make_table(early + late, right_of, owns, branch_flag, chosen, width, wanted)
-    before = (purified, trace)
-    purified = multiply(list(arrays), tuple(loads), 4, layout, table, shape, before)
+    (purified,) = multiply(
+        plane, list(arrays), tuple(loads), 4, layout, table, shape, None, (purified, trace)
+    )
     return purified.reshape(rows, kept, block, block), trace
 
 

time: 193 us -> 160 us (0.83)
  the two profiles are of different devices: /device:TPU:0 before, /device:TPU:4 now
where the time goes in v7:
time: 160 us
  waiting for transfers between devices  60.1 us (38%)
  starting transfers between devices  30.9 us (19%)
  Pallas kernels  20.5 us (13%)
  other arithmetic  18.1 us (11%)
  local copies, waits for them, and re-layouts  15.5 us (10%)
  between operations  14.4 us (9%)
    ppermute x11, waiting for transfers between devices, shift(): return lax.ppermute(array, 'col', pairs)  47.5 us
    ppermute x11, starting transfers between devices, shift(): return lax.ppermute(array, 'col', pairs)  28.3 us
    pallas_call x2, Pallas kernels, multiply(): pl.pallas_call(functools.partial(multiply_kernel, loads, kept, layout, tu...  16.9 us
    unnamed x20, local copies, waits for them, and re-layouts  9.59 us
    all_gather x1, waiting for transfers between devices, per_device(): plane = lax.all_gather(full, 'row', axis=0)  8.39 us
    ppermute x2, waiting for transfers between devices, gather_line(): end_three = lax.ppermute(middle_two, ('row', 'col'), pairs)  4.15 us
    pallas_call x1, Pallas kernels, pack(): pl.pallas_call(pack_kernel, out_shape=[jax.ShapeDtypeStruct((size * block...  3.61 us
    concatenate x2, local copies, waits for them, and re-layouts, make_table(): return (jnp.concatenate(list(lists.values())), layout)  3.42 us
  transfers between devices with their start and end apart: 14, of which 5 were waited for; matrix products, arithmetic and copies ran while one was open for 16% of the time, Pallas kernels for 6%

profile of v7, /device:TPU:4, one launch (start us, length us, event | category | flops | bytes accessed | tf_op | source)
XLA Modules:
  0.0 159.5 jit_solution(6638838061435708362)
XLA Ops:
  7.2 1.6 copy-done.4
  10.1 3.6 %shard_map.68 = (bf16[1808,256]{1,0:T(8,128)(2,1)S(1)}, bf16[1552,256]{1,0:T(8,128)(2,1)}, bf16[3344,256]{1,0:T(8,128)(2,1)}) custom-call(s32[2,8]{1,0:T(2,128)S(1)} %bitcast.35, s32[8]{0:T(128)S(1)} %copy-done.6, s32[1]{0:T(128)} %bitcast.1.first_ref, bf16[16,256,256]{2,1,0:T(8,128)(2,1)S(1)} %bitcast.33), custom_call_target="tpu_custom_call" | custom-call | tf_op jit(solution)/shard_map/pallas_call | solution.py:94
  14.7 1.6 collective-permute-start.6
  16.3 3.6 %collective-permute-start.5 = (bf16[1552,256]{1,0:T(8,128)(2,1)}, bf16[1552,256]{1,0:T(8,128)(2,1)}, u32[]{:S(2)}, u32[]{:S(2)}) collective-permute-start(bf16[1552,256]{1,0:T(8,128)(2,1)} %get-tuple-element.9), channel_id=1, source_target_pairs={{0,1},{1,0},{2,3},{3,2},{4,5},{5,4},{6,7},{7,6},{8,9},{9,8},{10,11... | collective-permute-start | bytes 2383880 | tf_op jit(solution)/shard_map/ppermute | solution.py:315
  20.5 2.5 %collective-permute-start = (bf16[1808,256]{1,0:T(8,128)(2,1)}, bf16[1808,256]{1,0:T(8,128)(2,1)S(1)}, u32[]{:S(2)}, u32[]{:S(2)}) collective-permute-start(bf16[1808,256]{1,0:T(8,128)(2,1)} %copy-done.8), channel_id=1, source_target_pairs={{0,1},{1,0},{2,3},{3,2},{4,5},{5,4},{6,7},{7,6},{8,9},{9,8},{10,11... | collective-permute-start | bytes 2777096 | tf_op jit(solution)/shard_map/ppermute | solution.py:315
  24.2 1.3 collective-permute-start.4
  25.5 13.2 %collective-permute-done.5.refs_2_ = bf16[1552,256]{1,0:T(8,128)(2,1)} collective-permute-done((bf16[1552,256]{1,0:T(8,128)(2,1)}, bf16[1552,256]{1,0:T(8,128)(2,1)}, u32[]{:S(2)}, u32[]{:S(2)}) %collective-permute-start.5) | collective-permute-done | bytes 794656 | tf_op jit(solution)/shard_map/ppermute | solution.py:315
  38.7 1.6 collective-permute-start.8
  40.3 17.0 %collective-permute-done.refs_1_ = bf16[1808,256]{1,0:T(8,128)(2,1)S(1)} collective-permute-done((bf16[1808,256]{1,0:T(8,128)(2,1)}, bf16[1808,256]{1,0:T(8,128)(2,1)S(1)}, u32[]{:S(2)}, u32[]{:S(2)}) %collective-permute-start) | collective-permute-done | bytes 925728 | tf_op jit(solution)/shard_map/ppermute | solution.py:315
  57.3 1.6 %collective-permute-start.1 = (bf16[1808,256]{1,0:T(8,128)(2,1)S(1)}, bf16[1808,256]{1,0:T(8,128)(2,1)}, u32[]{:S(2)}, u32[]{:S(2)}) collective-permute-start(bf16[1808,256]{1,0:T(8,128)(2,1)S(1)} %collective-permute-done.refs_1_), channel_id=1, source_target_pairs={{1,2},{2,1},{5,6},{6,5},{9,10},{10,9},{13,14},{14,13},{17,18},{18,... | collective-permute-start | bytes 2777096 | tf_op jit(solution)/shard_map/ppermute | solution.py:315
  63.2 17.3 %collective-permute-done.4.refs_5_ = bf16[1808,256]{1,0:T(8,128)(2,1)S(1)} collective-permute-done((bf16[1808,256]{1,0:T(8,128)(2,1)S(1)}, bf16[1808,256]{1,0:T(8,128)(2,1)S(1)}, u32[]{:S(2)}, u32[]{:S(2)}) %collective-permute-start.4) | collective-permute-done | bytes 925728 | tf_op jit(solution)/shard_map/ppermute | solution.py:315
  83.9 8.4 %all-gather.3.cloned.1.call-done = bf16[26752,256]{1,0:T(8,128)(2,1)} async-done(((bf16[3344,256]{1,0:T(8,128)(2,1)}), bf16[26752,256]{1,0:T(8,128)(2,1)}) %all-gather.3.cloned.1.call-update) | async-done | bytes 13697040 | tf_op jit(solution)/shard_map/all_gather | solution.py:406
  92.3 1.4 fusion.3
  93.7 11.7 %collective-permute-start.12 = (f32[]{:T(128)}, f32[]{:T(128)}, u32[]{:S(2)}, u32[]{:S(2)}) collective-permute-start(f32[]{:T(128)} %fusion.3), channel_id=1, source_target_pairs={{0,1},{1,0},{2,3},{3,2},{4,5},{5,4},{6,7},{7,6},{8,9},{9,8},{10,11... | collective-permute-start | bytes 20 | tf_op jit(solution)/shard_map/ppermute | solution.py:315
  111.8 1.4 concatenate.16.table
  113.2 1.5 collective-permute-start.10
  114.7 4.9 %copy-done = bf16[26752,256]{1,0:T(8,128)(2,1)S(1)} copy-done((bf16[26752,256]{1,0:T(8,128)(2,1)S(1)}, bf16[26752,256]{1,0:T(8,128)(2,1)}, u32[]{:S(2)}) %copy-start) | copy-done | bytes 13697048
  119.6 8.9 %shard_map.69 = (bf16[32,256,256]{2,1,0:T(8,128)(2,1)}, s32[1]{0:T(128)}) custom-call(s32[328]{0:T(512)S(1)} %concatenate.16.table, bf16[8,3344,256]{2,1,0:T(8,128)(2,1)S(1)} %bitcast.32, bf16[3344,256]{1,0:T(8,128)(2,1)} %get-tuple-element.8.refs_0_, bf16[1808,256]{1,0:T(8,128)(2,1)S(1)} %collective-permute-done.refs_1_, ...), custom_call_target="tpu_custom_call" | custom-call | tf_op jit(solution)/shard_map/pallas_call | solution.py:303
  128.6 4.1 %collective-permute-done.2.refs_9_ = bf16[1808,256]{1,0:T(8,128)(2,1)} collective-permute-done((bf16[1808,256]{1,0:T(8,128)(2,1)}, bf16[1808,256]{1,0:T(8,128)(2,1)}, u32[]{:S(2)}, u32[]{:S(2)}) %collective-permute-start.2) | collective-permute-done | bytes 925728 | tf_op jit(solution)/shard_map/ppermute | solution.py:326
  132.7 1.3 compare_convert_fusion.2
  134.4 1.3 convert_add_fusion
  139.5 2.0 %concatenate.17.table = s32[328]{0:T(512)} concatenate(s32[1]{0:T(128)} %bitcast.21, s32[1]{0:T(128)} %bitcast.23, s32[1]{0:T(128)} %constant.31.clone.1, s32[1]{0:T(128)} %bitcast.14, s32[1]{0:T(128)} %bitcast.7, s32[1]{0:T(128)} %bitcast.15, s32[1]{0:T(128)} %bitcast.16, s32[1]{0:T(128)} %bitcast.17, s32[32]{0:T(128)S(1)} %get-tuple-element.26, s32[4]{0:T(128)S(1)} %broadcast.425, ...), dimensions={0} | concatenate | bytes 2624 | tf_op jit(solution)/shard_map/concatenate | solution.py:384
  141.6 3.1 %fusion.5 = f32[]{:T(128)} fusion(f32[]{:T(128)} %fusion.3, s32[]{:T(128)S(6)} %axis_index.25, f32[]{:T(128)} %collective-permute-done.12, s32[]{:T(128)S(6)} %xor.11, f32[]{:T(128)} %collective-permute-done.11, s32[]{:T(128)S(6)} %xor.10, f32[]{:T(128)} %collective-permute-done.10, s32[]{:T(128)S(6)} %xor.9), kind=kLoop, calls=%fused_computation.87 | loop fusion | flops 35 | bytes 36 | tf_op jit(solution)/shard_map/reduce_sum | solution.py:415
  144.7 8.0 %shard_map.70 = bf16[32,256,256]{2,1,0:T(8,128)(2,1)} custom-call(s32[328]{0:T(512)} %concatenate.17.table, bf16[8,3344,256]{2,1,0:T(8,128)(2,1)} %bitcast.31, bf16[3344,256]{1,0:T(8,128)(2,1)} %get-tuple-element.8.refs_0_, bf16[1808,256]{1,0:T(8,128)(2,1)} %copy-done.2, ...), custom_call_target="tpu_custom_call", output_to_operand_aliasing={{}: (14, {})} | custom-call | tf_op jit(solution)/shard_map/pallas_call | solution.py:303
  (130 shorter events, 22.3 us)
Async XLA Ops:
  7.2 85.1 %all-gather.3.cloned.1.call-start = ((), (), s32[]{:S(2)}) async-start(), calls=%async_computation | async-start | bytes 15409152 | tf_op jit(solution)/shard_map/all_gather | solution.py:406
  7.2 1.6 copy-start.4
  8.8 0.7 copy-start.5
  9.5 0.7 copy-start.6
  10.1 129.4 %copy-start.7 = (s32[8]{0:T(128)S(1)}, s32[8]{0:T(128)}, u32[]{:S(2)}) copy-start(s32[8]{0:T(128)} %flag_ref.1) | copy-start | bytes 100
  13.8 0.9 copy-start.8
  14.7 45.7 %collective-permute-start.6 = (bf16[1552,256]{1,0:T(8,128)(2,1)}, bf16[1552,256]{1,0:T(8,128)(2,1)}, u32[]{:S(2)}, u32[]{:S(2)}) collective-permute-start(bf16[1552,256]{1,0:T(8,128)(2,1)} %get-tuple-element.9), channel_id=1, source_target_pairs={{1,2},{2,1},{5,6},{6,5},{9,10},{10,9},{13,14},{14,13},{17,18},{18,... | collective-permute-start | bytes 2383880 | tf_op jit(solution)/shard_map/ppermute | solution.py:315
  16.3 22.5 %collective-permute-start.5 = (bf16[1552,256]{1,0:T(8,128)(2,1)}, bf16[1552,256]{1,0:T(8,128)(2,1)}, u32[]{:S(2)}, u32[]{:S(2)}) collective-permute-start(bf16[1552,256]{1,0:T(8,128)(2,1)} %get-tuple-element.9), channel_id=1, source_target_pairs={{0,1},{1,0},{2,3},{3,2},{4,5},{5,4},{6,7},{7,6},{8,9},{9,8},{10,11... | collective-permute-start | bytes 2383880 | tf_op jit(solution)/shard_map/ppermute | solution.py:315
  19.8 4.4 %collective-permute-start.3 = (bf16[1808,256]{1,0:T(8,128)(2,1)}, bf16[1808,256]{1,0:T(8,128)(2,1)S(1)}, u32[]{:S(2)}, u32[]{:S(2)}) collective-permute-start(bf16[1808,256]{1,0:T(8,128)(2,1)} %copy-done.8), channel_id=1, source_target_pairs={{1,2},{2,1},{5,6},{6,5},{9,10},{10,9},{13,14},{14,13},{17,18},{18,... | collective-permute-start | bytes 2777096 | tf_op jit(solution)/shard_map/ppermute | solution.py:315
  20.5 36.8 %collective-permute-start = (bf16[1808,256]{1,0:T(8,128)(2,1)}, bf16[1808,256]{1,0:T(8,128)(2,1)S(1)}, u32[]{:S(2)}, u32[]{:S(2)}) collective-permute-start(bf16[1808,256]{1,0:T(8,128)(2,1)} %copy-done.8), channel_id=1, source_target_pairs={{0,1},{1,0},{2,3},{3,2},{4,5},{5,4},{6,7},{7,6},{8,9},{9,8},{10,11... | collective-permute-start | bytes 2777096 | tf_op jit(solution)/shard_map/ppermute | solution.py:315
  24.2 120.5 %copy-start.1 = (bf16[1808,256]{1,0:T(8,128)(2,1)}, bf16[1808,256]{1,0:T(8,128)(2,1)S(1)}, u32[]{:S(2)}) copy-start(bf16[1808,256]{1,0:T(8,128)(2,1)S(1)} %collective-permute-done.3.refs_3_) | copy-start | bytes 2777092
  24.2 56.2 %collective-permute-start.4 = (bf16[1808,256]{1,0:T(8,128)(2,1)S(1)}, bf16[1808,256]{1,0:T(8,128)(2,1)S(1)}, u32[]{:S(2)}, u32[]{:S(2)}) collective-permute-start(bf16[1808,256]{1,0:T(8,128)(2,1)S(1)} %collective-permute-done.3.refs_3_), channel_id=1, source_target_pairs={{1,0},{2,3},{5,4},{6,7},{9,8},{10,11},{13,12},{14,15},{17,16},{18,... | collective-permute-start | bytes 2777096 | tf_op jit(solution)/shard_map/ppermute | solution.py:315
  38.7 23.1 %collective-permute-start.8 = (bf16[1552,256]{1,0:T(8,128)(2,1)}, bf16[1552,256]{1,0:T(8,128)(2,1)}, u32[]{:S(2)}, u32[]{:S(2)}) collective-permute-start(bf16[1552,256]{1,0:T(8,128)(2,1)} %collective-permute-done.5.refs_2_), channel_id=1, source_target_pairs={{1,2},{2,1},{5,6},{6,5},{9,10},{10,9},{13,14},{14,13},{17,18},{18,... | collective-permute-start | bytes 2383880 | tf_op jit(solution)/shard_map/ppermute | solution.py:315
  57.3 87.4 %copy-start.2 = (bf16[1808,256]{1,0:T(8,128)(2,1)}, bf16[1808,256]{1,0:T(8,128)(2,1)S(1)}, u32[]{:S(2)}) copy-start(bf16[1808,256]{1,0:T(8,128)(2,1)S(1)} %collective-permute-done.refs_1_) | copy-start | bytes 2777092
  57.3 23.3 %collective-permute-start.1 = (bf16[1808,256]{1,0:T(8,128)(2,1)S(1)}, bf16[1808,256]{1,0:T(8,128)(2,1)}, u32[]{:S(2)}, u32[]{:S(2)}) collective-permute-start(bf16[1808,256]{1,0:T(8,128)(2,1)S(1)} %collective-permute-done.refs_1_), channel_id=1, source_target_pairs={{1,2},{2,1},{5,6},{6,5},{9,10},{10,9},{13,14},{14,13},{17,18},{18,... | collective-permute-start | bytes 2777096 | tf_op jit(solution)/shard_map/ppermute | solution.py:315
  60.4 52.8 %collective-permute-start.7 = (bf16[1552,256]{1,0:T(8,128)(2,1)}, bf16[1552,256]{1,0:T(8,128)(2,1)}, u32[]{:S(2)}, u32[]{:S(2)}) collective-permute-start(bf16[1552,256]{1,0:T(8,128)(2,1)} %collective-permute-done.6.refs_4_), channel_id=1, source_target_pairs={{1,0},{2,3},{5,4},{6,7},{9,8},{10,11},{13,12},{14,15},{17,16},{18,... | collective-permute-start | bytes 2383880 | tf_op jit(solution)/shard_map/ppermute | solution.py:315
  61.9 82.8 %collective-permute-start.9 = (bf16[1552,256]{1,0:T(8,128)(2,1)}, bf16[1552,256]{1,0:T(8,128)(2,1)}, u32[]{:S(2)}, u32[]{:S(2)}) collective-permute-start(bf16[1552,256]{1,0:T(8,128)(2,1)} %collective-permute-done.8.refs_8_), channel_id=1, source_target_pairs={{2,3},{6,7},{9,8},{10,11},{13,12},{14,15},{17,16},{18,19},{21,20},... | collective-permute-start | bytes 2383880 | tf_op jit(solution)/shard_map/ppermute | solution.py:326
  80.4 64.3 %copy-start.3 = (bf16[1808,256]{1,0:T(8,128)(2,1)}, bf16[1808,256]{1,0:T(8,128)(2,1)S(1)}, u32[]{:S(2)}) copy-start(bf16[1808,256]{1,0:T(8,128)(2,1)S(1)} %collective-permute-done.4.refs_5_) | copy-start | bytes 2777092
  81.8 50.9 %collective-permute-start.2 = (bf16[1808,256]{1,0:T(8,128)(2,1)}, bf16[1808,256]{1,0:T(8,128)(2,1)}, u32[]{:S(2)}, u32[]{:S(2)}) collective-permute-start(bf16[1808,256]{1,0:T(8,128)(2,1)} %collective-permute-done.1.refs_7_), channel_id=1, source_target_pairs={{2,3},{6,7},{9,8},{10,11},{13,12},{14,15},{17,16},{18,19},{21,20},... | collective-permute-start | bytes 2777096 | tf_op jit(solution)/shard_map/ppermute | solution.py:326
  93.7 47.9 %collective-permute-start.12 = (f32[]{:T(128)}, f32[]{:T(128)}, u32[]{:S(2)}, u32[]{:S(2)}) collective-permute-start(f32[]{:T(128)} %fusion.3), channel_id=1, source_target_pairs={{0,1},{1,0},{2,3},{3,2},{4,5},{5,4},{6,7},{7,6},{8,9},{9,8},{10,11... | collective-permute-start | bytes 20 | tf_op jit(solution)/shard_map/ppermute | solution.py:315
  105.4 36.2 %collective-permute-start.11 = (f32[]{:T(128)}, f32[]{:T(128)}, u32[]{:S(2)}, u32[]{:S(2)}) collective-permute-start(f32[]{:T(128)} %fusion.3), channel_id=1, source_target_pairs={{0,2},{1,3},{2,0},{3,1},{4,6},{5,7},{6,4},{7,5},{8,10},{9,11},{10,... | collective-permute-start | bytes 20 | tf_op jit(solution)/shard_map/ppermute | solution.py:315
  113.2 28.4 %collective-permute-start.10 = (f32[]{:T(128)}, f32[]{:T(128)}, u32[]{:S(2)}, u32[]{:S(2)}) collective-permute-start(f32[]{:T(128)} %fusion.3), channel_id=1, source_target_pairs={{0,3},{1,2},{2,1},{3,0},{4,7},{5,6},{6,5},{7,4},{8,11},{9,10},{10,... | collective-permute-start | bytes 20 | tf_op jit(solution)/shard_map/ppermute | solution.py:315
  114.7 4.9 %copy-start = (bf16[26752,256]{1,0:T(8,128)(2,1)S(1)}, bf16[26752,256]{1,0:T(8,128)(2,1)}, u32[]{:S(2)}) copy-start(bf16[26752,256]{1,0:T(8,128)(2,1)} %all-gather.3.cloned.1.call-done) | copy-start | bytes 41091076
Sparse Core Ops, SparseCore 0:
  14.8 77.4 all-gather.2

commit v8 on v5

v8 whole, which is shorter than its diff:
```python
import functools

import jax
import jax.numpy as jnp
from jax import lax
from jax.experimental import pallas as pl
from jax.experimental.pallas import tpu as pltpu
from jax.sharding import PartitionSpec as P

PACKED = 13
SPLIT = (PACKED + 1) // 2
STRIDE = 1 << (PACKED - 1).bit_length()
VMEM_LIMIT = 58 << 20


def pack_kernel(cols_ref, x_ref, part_a, part_b, full, held, in_sems, sems):
    count, block, _ = x_ref.shape
    slots = cols_ref.shape[0]
    moves = []
    place = jnp.int32(0)
    for index in range(count):
        filled = cols_ref[index % slots, index // slots] >= 0
        load = pltpu.make_async_copy(x_ref.at[index], held.at[index], in_sems.at[index])
        pl.when(filled)(load.start)
        moves.append((filled, place, load))
        place = place + filled.astype(jnp.int32)
    sends = []
    for index, (filled, place, load) in enumerate(moves):
        pl.when(filled)(load.wait)
        targets = (
            (full, filled, place),
            (part_a, filled & (place < SPLIT), place),
            (part_b, filled & (place >= SPLIT), place - SPLIT),
        )
        for which, (out, wanted, target) in enumerate(targets):
            target = pl.multiple_of(jnp.where(wanted, target, 0) * block, block)
            copy = pltpu.make_async_copy(
                held.at[index], out.at[pl.ds(target, block)], sems.at[which, index]
            )
            pl.when(wanted)(copy.start)
            sends.append((wanted, copy))
    for wanted, copy in sends:
        pl.when(wanted)(copy.wait)


def pack(x_blocks, x_cols):
    rows, slots, block, _ = x_blocks.shape
    count = rows * slots
    hbm = pl.BlockSpec(memory_space=pltpu.HBM)
    return pl.pallas_call(
        pack_kernel,
        out_shape=[
            jax.ShapeDtypeStruct((size * block, block), x_blocks.dtype)
            for size in (SPLIT, PACKED - SPLIT, PACKED)
        ],
        in_specs=[pl.BlockSpec(memory_space=pltpu.SMEM), hbm],
        out_specs=[hbm] * 3,
        scratch_shapes=[
            pltpu.VMEM((count, block, block), x_blocks.dtype),
            pltpu.SemaphoreType.DMA((count,)),
            pltpu.SemaphoreType.DMA((3, count)),
        ],
        compiler_params=pltpu.CompilerParams(vmem_limit_bytes=VMEM_LIMIT),
    )(x_cols.T, x_blocks.reshape(count, block, block))


BATCH = 4


def multiply_kernel(loads, kept, layout, turned, table, plane, *refs):
    arrays = refs[: 1 + max(load[0] for load in loads)]
    out_ref, pool, ring, more, done, in_sem, turn_sem, ring_sem, out_sem = refs[-9:]
    depth = ring.shape[0] - 1
    block = out_ref.shape[-1]
    n_out = table[0]
    n_terms = table[1]
    zero_entry = pool.shape[0] - 1

    copies = []
    for number, (which, at, entry, first, size, wanted) in enumerate(loads):
        source = arrays[which] if at is None else arrays[which].at[at]
        copy = pltpu.make_async_copy(
            source.at[pl.ds(0, size * block)],
            pool.at[entry, pl.ds(first * block, size * block)],
            in_sem.at[number],
        )
        copies.append(((table[wanted] != 0) & (n_out > 0), copy))
    for here, copy in copies:
        pl.when(here)(copy.start)

    def decode(index):
        entry = lax.shift_right_logical(index, STRIDE.bit_length() - 1)
        return entry, pl.multiple_of(jnp.bitwise_and(index, STRIDE - 1) * block, block)

    def fetch(term):
        entry, first = decode(table[layout["rights"] + term])
        slot = lax.rem(term, depth)
        return pltpu.make_async_copy(
            plane.at[entry, pl.ds(first, block)], ring.at[slot], ring_sem.at[slot]
        )

    def begin(term, carry):
        fetch(term).start()
        return carry

    if turned is not None:
        is_wanted, at, target = turned
        rows = pltpu.make_async_copy(
            plane.at[pl.ds(table[at], 2)], pool.at[pl.ds(target, 2)], turn_sem
        )
        pl.when(table[is_wanted] != 0)(rows.start)
    lax.fori_loop(0, jnp.minimum(depth, n_terms), begin, 0)
    ring[depth] = jnp.zeros((block, block), ring.dtype)
    pool[zero_entry, pl.ds(0, block)] = jnp.zeros((block, block), pool.dtype)

    if turned is not None:
        @pl.when(table[is_wanted] != 0)
        def _():
            down = lax.broadcasted_iota(jnp.int32, (block, block), 0)
            eye = down == lax.broadcasted_iota(jnp.int32, (block, block), 1)
            eye = eye.astype(jnp.float32).astype(pool.dtype)
            rows.wait()

            def turn(place, carry):
                first = pl.multiple_of(place * block, block)
                for entry in range(target, target + 2):
                    pool[entry, pl.ds(first, block)] = lax.dot_general(
                        eye,
                        pool[entry, pl.ds(first, block)],
                        (((1,), (1,)), ((), ())),
                        preferred_element_type=jnp.float32,
                    ).astype(pool.dtype)
                return carry

            lax.fori_loop(0, PACKED, turn, 0)

    for here, copy in copies:
        pl.when(here)(copy.wait)

    def product(term, live):
        entry, first = decode(
            jnp.where(live, table[layout["lefts"] + term], zero_entry * STRIDE)
        )
        left = pool[entry, pl.ds(first, block)]
        right = ring[jnp.where(live, lax.rem(term, depth), depth)]
        return jnp.dot(left, right, preferred_element_type=jnp.float32)

    def write(number, slot):
        output = table[layout["outs"] + number]
        return pltpu.make_async_copy(done.at[slot], out_ref.at[output], out_sem.at[slot])

    def one_batch(batch, term):
        begins, counts = [], []
        last = term
        for local in range(BATCH):
            begins.append(last)
            counts.append(table[layout["counts"] + batch * BATCH + local])
            last = last + counts[local]

        def arrived(number, carry):
            fetch(number).wait()
            return carry

        lax.fori_loop(term, last, arrived, 0)
        half = lax.rem(batch, 2) * BATCH
        for local in range(BATCH):
            @pl.when(batch >= 2)
            def _():
                write((batch - 2) * BATCH + local, half + local).wait()

            more[local] = jnp.zeros_like(more[local])

            def two_terms(pair, carry):
                number = begins[local] + 2 + 2 * pair
                second = number + 1 < begins[local] + counts[local]
                more[local] += product(number, True) + product(
                    jnp.where(second, number + 1, 0), second
                )
                return carry

            lax.fori_loop(0, (counts[local] - 1) // 2, two_terms, 0)

        for local in range(BATCH):
            output = table[layout["outs"] + batch * BATCH + local]
            square = more[local]
            for place in range(2):
                live = counts[local] > place
                square = square + product(jnp.where(live, begins[local] + place, 0), live)
            flag = table[layout["flags"] + output // kept].astype(jnp.float32)
            own = table[layout["owns"] + output]
            entry, first = decode(jnp.where(own >= 0, own, zero_entry * STRIDE))
            mine = pool[entry, pl.ds(first, block)].astype(jnp.float32)
            result = (2.0 * flag) * mine + (1.0 - 2.0 * flag) * square
            done[half + local] = result.astype(done.dtype)
        for local in range(BATCH):
            @pl.when(batch * BATCH + local < n_out)
            def _():
                write(batch * BATCH + local, half + local).start()

        def refill(number, carry):
            fetch(number + depth).start()
            return carry

        lax.fori_loop(term, jnp.clip(n_terms - depth, term, last), refill, 0)
        return last

    n_batches = (n_out + BATCH - 1) // BATCH
    lax.fori_loop(0, n_batches, one_batch, jnp.int32(0))
    for back in range(2):
        batch = n_batches - 1 - back
        for local in range(BATCH):
            number = jnp.maximum(batch, 0) * BATCH + local

            @pl.when((batch >= 0) & (number < n_out))
            def _():
                write(number, lax.rem(batch, 2) * BATCH + local).wait()


def multiply(plane, arrays, loads, n_entries, layout, table, shape, turned=None, before=None):
    rows, kept, block, dtype = shape
    outputs = rows * kept
    depth = 48
    smem = pl.BlockSpec(memory_space=pltpu.SMEM)
    hbm = pl.BlockSpec(memory_space=pltpu.HBM)
    operands = [table, plane, *arrays]
    aliases = {}
    if before is not None:
        operands.append(before)
        aliases = {len(operands) - 1: 0}
    return pl.pallas_call(
        functools.partial(multiply_kernel, loads, kept, layout, turned),
        out_shape=jax.ShapeDtypeStruct((outputs, block, block), dtype),
        in_specs=[smem] + [hbm] * (len(operands) - 1),
        out_specs=hbm,
        scratch_shapes=[
            pltpu.VMEM((n_entries + 1, PACKED * block, block), dtype),
            pltpu.VMEM((depth + 1, block, block), dtype),
            pltpu.VMEM((BATCH, block, block), jnp.float32),
            pltpu.VMEM((2 * BATCH, block, block), dtype),
            pltpu.SemaphoreType.DMA((len(loads),)),
            pltpu.SemaphoreType.DMA,
            pltpu.SemaphoreType.DMA((depth,)),
            pltpu.SemaphoreType.DMA((2 * BATCH,)),
        ],
        input_output_aliases=aliases,
        compiler_params=pltpu.CompilerParams(vmem_limit_bytes=VMEM_LIMIT),
    )(*operands)


def shift(array, pairs):
    return lax.ppermute(array, "col", pairs)


def gather_line(part):
    first = shift(part, [(0, 1), (1, 0), (2, 3), (3, 2)])
    middle = shift(part, [(1, 2), (2, 1)])
    end_two = shift(middle, [(1, 0), (2, 3)])
    middle_two = shift(first, [(1, 2), (2, 1)])
    pairs = []
    for row in range(lax.axis_size("row")):
        pairs += [(4 * row + 1, 4 * row)] * (row // 2 != 0) + [(4 * row + 2, 4 * row + 3)] * (row // 2 != 3)
    end_three = lax.ppermute(middle_two, ("row", "col"), pairs)
    return {
        "first": first,
        "middle": middle,
        "end_two": end_two,
        "middle_two": middle_two,
        "end_three": end_three,
    }


def running_count(fill):
    count = fill.shape[-1]
    before = jnp.arange(count)[:, None] < jnp.arange(count)[None, :]
    return jnp.sum(jnp.where(before, fill[..., :, None], 0), axis=-2)


def places(cols):
    flat = (cols >= 0).astype(jnp.int32).reshape(cols.shape[:-2] + (-1,))
    return running_count(flat).reshape(cols.shape)


def make_table(left_of, right_of, owns, flags, chosen, width, wanted):
    kept = right_of.shape[0] // left_of.shape[0]
    outputs = right_of.shape[0]
    left_of = jnp.repeat(left_of, kept, axis=0)
    live = (left_of > 0) & (right_of > 0) & chosen[:, None]
    counts = jnp.sum(live.astype(jnp.int32), axis=1)
    term = jnp.where(live, running_count(live.astype(jnp.int32)), -1)
    across = jnp.arange(width, dtype=jnp.int32)
    pick = term[:, None, :] == across[:, None]
    lefts = jnp.sum(jnp.where(pick, left_of[:, None, :] - 1, 0), axis=2)
    rights = jnp.sum(jnp.where(pick, right_of[:, None, :] - 1, 0), axis=2)
    flat = jnp.where(across < counts[:, None], running_count(counts)[:, None] + across, -1)
    pick = flat[None] == jnp.arange(PACKED * width, dtype=jnp.int32)[:, None, None]
    lefts = jnp.sum(jnp.where(pick, lefts, 0), axis=(1, 2))
    rights = jnp.sum(jnp.where(pick, rights, 0), axis=(1, 2))
    every = jnp.arange(outputs, dtype=jnp.int32)
    number = jnp.where(chosen, running_count(chosen.astype(jnp.int32)), -1)
    pick = number[None, :] == every[:, None]
    outs = jnp.sum(jnp.where(pick, every, 0), axis=1)
    ordered = jnp.sum(jnp.where(pick, counts, 0), axis=1)
    sizes = jnp.stack([jnp.sum(chosen.astype(jnp.int32)), jnp.sum(counts)])
    spare = jnp.zeros((BATCH,), jnp.int32)
    lists = {
        "sizes": sizes,
        "wanted": wanted,
        "outs": jnp.concatenate([outs, spare]),
        "counts": jnp.concatenate([ordered, spare]),
        "lefts": lefts,
        "rights": rights,
        "owns": owns,
        "flags": flags,
    }
    layout = {}
    first = 0
    for name, values in lists.items():
        layout[name] = first
        first += values.shape[0]
    return jnp.concatenate(list(lists.values())), layout


def local_trace(x_blocks, x_cols, branch_flag, first_row):
    rows, slots, block, _ = x_blocks.shape
    own_row = first_row + jnp.arange(rows, dtype=jnp.int32)
    flag = branch_flag.astype(jnp.float32)[:, None]
    norm_weight = jnp.where(x_cols >= 0, 1.0 - 2.0 * flag, 0.0)
    diag_weight = jnp.where(x_cols == own_row[:, None], 2.0 * flag, 0.0)
    values = x_blocks.astype(jnp.float32)
    eye = jnp.eye(block, dtype=jnp.float32)
    weight = norm_weight[:, :, None, None] * values + diag_weight[:, :, None, None] * eye
    return jnp.sum(weight * values)


def gather_facts(values):
    n_row = lax.axis_size("row")
    n_col = lax.axis_size("col")
    down, across = values.shape
    padded = jnp.pad(values.astype(jnp.float32), [(0, 0), (0, 128 - across)])
    every = lax.all_gather(padded, ("row", "col"), axis=0, tiled=True)
    return every.reshape(n_row, n_col, down, 128)[..., :across]


def per_device(x_blocks, x_cols, out_cols, branch_flag):
    rows, slots = x_cols.shape
    kept = out_cols.shape[1]
    block = x_blocks.shape[-1]
    dtype = x_blocks.dtype
    n_row = lax.axis_size("row")
    n_col = lax.axis_size("col")
    row = lax.axis_index("row")
    col = lax.axis_index("col")
    n_blocks = n_row * rows
    width = n_col * slots
    shape = (rows, kept, block, dtype)

    all_cols = gather_facts(x_cols).astype(jnp.int32)
    all_places = places(all_cols)
    part_a, part_b, full = pack(x_blocks, x_cols)
    plane = lax.all_gather(full, "row", axis=0)

    trace = local_trace(x_blocks, x_cols, branch_flag, row * rows)
    trace = jnp.sum(gather_facts(jnp.pad(trace.reshape(1, 1), [(0, 7), (0, 0)]))).reshape(1)

    plane_cols = lax.dynamic_index_in_dim(all_cols, col, 1, keepdims=False)
    plane_places = lax.dynamic_index_in_dim(all_places, col, 1, keepdims=False)
    targets = out_cols.reshape(rows * kept)
    right_at = plane_places + STRIDE * jnp.arange(n_row, dtype=jnp.int32)[:, None, None]
    hit = plane_cols.reshape(n_blocks, slots)[None] == targets[:, None, None]
    right_of = jnp.sum(jnp.where(hit, right_at.reshape(n_blocks, slots) + 1, 0), axis=2)
    hit = x_cols[:, None, :] == out_cols[:, :, None]
    owns = jnp.sum(jnp.where(hit, places(x_cols)[:, None, :] + 1, 0), axis=2) - 1
    owns = owns.reshape(rows * kept)

    every = jnp.arange(n_blocks, dtype=jnp.int32)
    line_cols = lax.dynamic_index_in_dim(all_cols, row, 0, keepdims=False)
    line_places = lax.dynamic_index_in_dim(all_places, row, 0, keepdims=False)

    def straight(entries, wanted):
        at = line_places + STRIDE * entries[:, None, None]
        hit = (line_cols[..., None] == every) & wanted[:, None, None, None]
        return jnp.sum(jnp.where(hit, at[..., None] + 1, 0), axis=(0, 2))

    def turned(entry, device, wanted):
        cols = lax.dynamic_slice_in_dim(plane_cols, device, 2, 0)
        at = lax.dynamic_slice_in_dim(plane_places, device, 2, 0)
        at = at + STRIDE * (entry + jnp.arange(2, dtype=jnp.int32)[:, None, None])
        own = row * rows + jnp.arange(rows, dtype=jnp.int32)
        hit = (cols[..., None] == own) & wanted
        found = jnp.sum(jnp.where(hit, at[..., None] + 1, 0), axis=2)
        names = device * rows + jnp.arange(2 * rows, dtype=jnp.int32).reshape(2, rows)
        found = jnp.where(names[:, :, None, None] == every, found[..., None], 0)
        return jnp.sum(found, axis=(0, 1))

    heights = jnp.arange(n_col, dtype=jnp.int32)
    if not (n_col == 4 and n_row == 8):
        line = lax.all_gather(full, "col", axis=0)
        left_of = straight(1 + heights, heights >= 0)
        everything = jnp.ones((rows * kept,), bool)
        one = jnp.ones((1,), jnp.int32)
        table, layout = make_table(left_of, right_of, owns, branch_flag, everything, width, one)
        loads = [(0, None, 0, 0, PACKED, 2)]
        loads += [(1, c, 1 + c, 0, PACKED, 2) for c in range(n_col)]
        purified = multiply(plane, [full, line], tuple(loads), 1 + n_col, layout, table, shape)
        return purified.reshape(rows, kept, block, block), trace

    line = [gather_line(part) for part in (part_a, part_b)]
    at_end = (col == 0) | (col == n_col - 1)
    corner = at_end & (row // 2 == col)
    far = at_end & ~corner
    turn_row = 2 * (n_col - 1 - col)
    wanted = [at_end | True, at_end, ~at_end, far, corner, turn_row]
    wanted = jnp.stack([value.astype(jnp.int32) for value in wanted])
    always, at_ends, inside, at_far, at_corner, turn_at = range(2, 8)

    second = jnp.where(col < 2, 2, 1)
    entries = jnp.where(heights == second, 2, 3)
    entries = jnp.where(heights == jnp.bitwise_xor(col, 1), 1, entries)
    entries = jnp.where(heights == col, 0, entries)
    early = straight(entries, (entries < 3) | ~at_end) + turned(4, turn_row, corner)
    late = straight(entries, (entries == 3) & far)
    meets = (jnp.repeat(late, kept, axis=0) > 0) & (right_of > 0)
    is_late = jnp.any(meets, axis=1)

    arrays = [full]
    loads = [(0, None, 0, 0, PACKED, always)]

    def add(name, entry, wanted):
        spans = ((0, SPLIT), (SPLIT, PACKED - SPLIT))
        for which in range(2):
            loads.append((len(arrays), None, entry) + spans[which] + (wanted,))
            arrays.append(line[which][name])

    def call(left_of, chosen, before=None):
        table, layout = make_table(left_of, right_of, owns, branch_flag, chosen, width, wanted)
        turn = (at_corner, turn_at, 4) if before is None else None
        return multiply(
            plane, list(arrays), tuple(loads), 6, layout, table, shape, turn, before
        )

    add("first", 1, always)
    add("middle", 2, inside)
    add("end_two", 2, at_ends)
    add("middle_two", 3, inside)
    purified = call(early, ~is_late)
    add("end_three", 3, at_far)
    purified = call(early + late, is_late, purified)
    return purified.reshape(rows, kept, block, block), trace


def solution(mesh):
    in_specs = (P("row", "col", None, None), P("row", "col"), P("row", "col"), P("row"))
    out_specs = (P("row", "col", None, None), P())
    return jax.shard_map(
        per_device, mesh=mesh, in_specs=in_specs, out_specs=out_specs, check_vma=False
    )
```

time: 209 us -> 283 us (1.35)
  blocking collectives: 0 us -> 206 us
  waiting for transfers between devices: 98 us -> 0.06 us
  Pallas kernels: 46.3 us -> 23.3 us
  other arithmetic: 16.2 us -> 10.4 us
  local copies, waits for them, and re-layouts: 15 us -> 9.45 us
    all_gather x0 -> x2, blocking collectives: none -> 206 us  [gather_facts(): every = lax.all_gather(padded, ('row', 'col'), axis=0, tiled=True)]
    ppermute x13 -> x8, waiting for transfers between devices: 98 us -> 0.02 us  [shift(): return lax.ppermute(array, 'col', pairs)]
    pallas_call x2, Pallas kernels: 42.7 us -> 19.6 us  [multiply(): pl.pallas_call(functools.partial(multiply_kernel, loads, kept, layout, tu...]
    unnamed x12 -> x16, local copies, waits for them, and re-layouts: 9.56 us -> 2.69 us
    ppermute x13 -> x8, starting transfers between devices: 21 us -> 15.5 us  [shift(): return lax.ppermute(array, 'col', pairs)]
    ppermute x0 -> x2, starting transfers between devices: none -> 3.25 us  [gather_line(): end_three = lax.ppermute(middle_two, ('row', 'col'), pairs)]
  transfers between devices with their start and end apart: 14 -> 11, of which waited for: 4 -> 0; matrix products, arithmetic and copies ran while one was open for 11% -> 7% of each run, Pallas kernels for 10% -> 6%
where the time goes in v8:
time: 283 us
  blocking collectives  206 us (73%)
  Pallas kernels  23.3 us (8%)
  starting transfers between devices  18.8 us (7%)
  between operations  14.4 us (5%)
  other arithmetic  10.4 us (4%)
  local copies, waits for them, and re-layouts  9.45 us (3%)
    all_gather x2, blocking collectives, gather_facts(): every = lax.all_gather(padded, ('row', 'col'), axis=0, tiled=True)  206 us
    pallas_call x2, Pallas kernels, multiply(): pl.pallas_call(functools.partial(multiply_kernel, loads, kept, layout, tu...  19.6 us
    ppermute x8, starting transfers between devices, shift(): return lax.ppermute(array, 'col', pairs)  15.5 us
  transfers between devices with their start and end apart: 11, of which 0 were waited for; matrix products, arithmetic and copies ran while one was open for 7% of the time, Pallas kernels for 6%

profile of v8, /device:TPU:0, one launch (start us, length us, event | category | flops | bytes accessed | tf_op | source)
XLA Modules:
  0.0 282.7 jit_solution(13552081975710459870)
XLA Ops:
  7.3 3.8 %shard_map.59 = (bf16[1792,256]{1,0:T(8,128)(2,1)}, bf16[1536,256]{1,0:T(8,128)(2,1)}, bf16[3328,256]{1,0:T(8,128)(2,1)}) custom-call(s32[2,8]{1,0:T(2,128)} %bitcast.54, bf16[16,256,256]{2,1,0:T(8,128)(2,1)} %bitcast.44), custom_call_target="tpu_custom_call" | custom-call | tf_op jit(solution)/shard_map/pallas_call | solution.py:50
  11.0 1.5 collective-permute-start.3
  12.6 5.3 %collective-permute-start.1 = (bf16[1536,256]{1,0:T(8,128)(2,1)}, bf16[1536,256]{1,0:T(8,128)(2,1)}, u32[]{:S(2)}, u32[]{:S(2)}) collective-permute-start(bf16[1536,256]{1,0:T(8,128)(2,1)} %get-tuple-element.7), channel_id=1, source_target_pairs={{0,1},{1,0},{2,3},{3,2},{4,5},{5,4},{6,7},{7,6},{8,9},{9,8},{10,11... | collective-permute-start | bytes 2359304 | tf_op jit(solution)/shard_map/ppermute | solution.py:251
  17.9 0.7 collective-permute-start.2
  18.6 2.2 collective-permute-start
  20.8 0.8 copy.63
  22.6 0.8 copy.72
  23.5 94.1 %all_gather.12 = f32[256,128]{1,0:T(8,128)S(1)} all-gather(f32[8,128]{1,0:T(8,128)S(1)} %pad.12), channel_id=1, replica_groups=mesh['row'=8,'col'=4] {'row','col'}, dimensions={0}, use_global_device_ids=true | all-gather | bytes 135168 | tf_op jit(solution)/shard_map/all_gather | solution.py:340
  119.9 0.8 convert_reduce_fusion
  121.7 0.7 select_reduce_fusion
  122.6 1.6 collective-permute-start.6
  124.4 1.6 collective-permute-start.7
  126.8 2.0 fusion.1
  128.8 1.3 collective-permute-start.4
  130.1 1.6 collective-permute-start.8
  131.8 1.3 collective-permute-start.5
  133.1 1.6 collective-permute-start.9
  134.7 2.2 select_reduce_fusion.4
  138.0 2.0 concatenate.9.table
  140.4 1.9 concatenate.8.table
  142.3 112.2 %all_gather.15 = f32[256,128]{1,0:T(8,128)S(1)} all-gather(f32[8,128]{1,0:T(8,128)S(1)} %pad.15), channel_id=1, replica_groups=mesh['row'=8,'col'=4] {'row','col'}, dimensions={0}, use_global_device_ids=true | all-gather | bytes 135168 | tf_op jit(solution)/shard_map/all_gather | solution.py:340
  255.2 0.8 copy-done.3
  256.3 18.2 %shard_map.60.refs_11_ = bf16[32,256,256]{2,1,0:T(8,128)(2,1)} custom-call(s32[328]{0:T(512)} %concatenate.9.table, bf16[8,3328,256]{2,1,0:T(8,128)(2,1)} %bitcast.41, bf16[3328,256]{1,0:T(8,128)(2,1)} %get-tuple-element.5.refs_0_, bf16[1792,256]{1,0:T(8,128)(2,1)} %collective-permute-done.refs_1_, bf16[1536,256]{1,0:T(8,128)(2,1)} %collective-permute-done.1.refs_2_, ...), custom_call_target="tpu_custom_call" | custom-call | tf_op jit(solution)/shard_map/pallas_call | solution.py:230
  274.5 1.4 shard_map.61
  (109 shorter events, 8.0 us)
Async XLA Ops:
  7.2 119.6 %copy-start = (bf16[8,2,256,256]{3,2,1,0:T(8,128)(2,1)S(1)}, bf16[8,2,256,256]{3,2,1,0:T(8,128)(2,1)}, u32[]{:S(2)}) copy-start(bf16[8,2,256,256]{3,2,1,0:T(8,128)(2,1)} %param.4) | copy-start | bytes 6291460
  7.2 115.4 %copy-start.4 = (s32[8,2]{0,1:T(2,128)S(1)}, s32[8,2]{0,1:T(2,128)}, u32[]{:S(2)}) copy-start(s32[8,2]{0,1:T(2,128)} %param.5) | copy-start | bytes 196
  7.2 118.8 %copy-start.5 = (s32[8,4]{0,1:T(4,128)S(1)}, s32[8,4]{0,1:T(4,128)}, u32[]{:S(2)}) copy-start(s32[8,4]{0,1:T(4,128)} %param.6) | copy-start | bytes 388
  7.2 115.2 %copy-start.6 = (s32[8]{0:T(128)S(1)}, s32[8]{0:T(128)}, u32[]{:S(2)}) copy-start(s32[8]{0:T(128)} %param.7) | copy-start | bytes 100
  7.2 247.9 %all-gather.3.cloned.1.call-start = ((), (), s32[]{:S(2)}) async-start(), calls=%async_computation | async-start | bytes 15335424 | tf_op jit(solution)/shard_map/all_gather | solution.py:360
  11.0 120.7 %collective-permute-start.3 = (bf16[1536,256]{1,0:T(8,128)(2,1)}, bf16[1536,256]{1,0:T(8,128)(2,1)}, u32[]{:S(2)}, u32[]{:S(2)}) collective-permute-start(bf16[1536,256]{1,0:T(8,128)(2,1)} %get-tuple-element.7), channel_id=1, source_target_pairs={{1,2},{2,1},{5,6},{6,5},{9,10},{10,9},{13,14},{14,13},{17,18},{18,... | collective-permute-start | bytes 2359304 | tf_op jit(solution)/shard_map/ppermute | solution.py:251
  12.6 111.8 %collective-permute-start.1 = (bf16[1536,256]{1,0:T(8,128)(2,1)}, bf16[1536,256]{1,0:T(8,128)(2,1)}, u32[]{:S(2)}, u32[]{:S(2)}) collective-permute-start(bf16[1536,256]{1,0:T(8,128)(2,1)} %get-tuple-element.7), channel_id=1, source_target_pairs={{0,1},{1,0},{2,3},{3,2},{4,5},{5,4},{6,7},{7,6},{8,9},{9,8},{10,11... | collective-permute-start | bytes 2359304 | tf_op jit(solution)/shard_map/ppermute | solution.py:251
  17.9 110.9 %collective-permute-start.2 = (bf16[1792,256]{1,0:T(8,128)(2,1)}, bf16[1792,256]{1,0:T(8,128)(2,1)S(1)}, u32[]{:S(2)}, u32[]{:S(2)}) collective-permute-start(bf16[1792,256]{1,0:T(8,128)(2,1)} %get-tuple-element.6), channel_id=1, source_target_pairs={{1,2},{2,1},{5,6},{6,5},{9,10},{10,9},{13,14},{14,13},{17,18},{18,... | collective-permute-start | bytes 2752520 | tf_op jit(solution)/shard_map/ppermute | solution.py:251
  18.6 104.0 %collective-permute-start = (bf16[1792,256]{1,0:T(8,128)(2,1)}, bf16[1792,256]{1,0:T(8,128)(2,1)}, u32[]{:S(2)}, u32[]{:S(2)}) collective-permute-start(bf16[1792,256]{1,0:T(8,128)(2,1)} %get-tuple-element.6), channel_id=1, source_target_pairs={{0,1},{1,0},{2,3},{3,2},{4,5},{5,4},{6,7},{7,6},{8,9},{9,8},{10,11... | collective-permute-start | bytes 2752520 | tf_op jit(solution)/shard_map/ppermute | solution.py:251
  122.6 7.5 %collective-permute-start.6 = (bf16[1792,256]{1,0:T(8,128)(2,1)}, bf16[1792,256]{1,0:T(8,128)(2,1)}, u32[]{:S(2)}, u32[]{:S(2)}) collective-permute-start(bf16[1792,256]{1,0:T(8,128)(2,1)} %collective-permute-done.refs_1_), channel_id=1, source_target_pairs={{1,2},{2,1},{5,6},{6,5},{9,10},{10,9},{13,14},{14,13},{17,18},{18,... | collective-permute-start | bytes 2752520 | tf_op jit(solution)/shard_map/ppermute | solution.py:251
  124.4 8.6 %collective-permute-start.7 = (bf16[1536,256]{1,0:T(8,128)(2,1)}, bf16[1536,256]{1,0:T(8,128)(2,1)}, u32[]{:S(2)}, u32[]{:S(2)}) collective-permute-start(bf16[1536,256]{1,0:T(8,128)(2,1)} %collective-permute-done.1.refs_2_), channel_id=1, source_target_pairs={{1,2},{2,1},{5,6},{6,5},{9,10},{10,9},{13,14},{14,13},{17,18},{18,... | collective-permute-start | bytes 2359304 | tf_op jit(solution)/shard_map/ppermute | solution.py:251
  128.8 126.3 %copy-start.1 = (bf16[1792,256]{1,0:T(8,128)(2,1)}, bf16[1792,256]{1,0:T(8,128)(2,1)S(1)}, u32[]{:S(2)}) copy-start(bf16[1792,256]{1,0:T(8,128)(2,1)S(1)} %collective-permute-done.2.refs_3_) | copy-start | bytes 2752516
  128.8 126.3 %collective-permute-start.4 = (bf16[1792,256]{1,0:T(8,128)(2,1)S(1)}, bf16[1792,256]{1,0:T(8,128)(2,1)S(1)}, u32[]{:S(2)}, u32[]{:S(2)}) collective-permute-start(bf16[1792,256]{1,0:T(8,128)(2,1)S(1)} %collective-permute-done.2.refs_3_), channel_id=1, source_target_pairs={{1,0},{2,3},{5,4},{6,7},{9,8},{10,11},{13,12},{14,15},{17,16},{18,... | collective-permute-start | bytes 2752520 | tf_op jit(solution)/shard_map/ppermute | solution.py:251
  130.1 144.4 %collective-permute-start.8 = (bf16[1792,256]{1,0:T(8,128)(2,1)}, bf16[1792,256]{1,0:T(8,128)(2,1)}, u32[]{:S(2)}, u32[]{:S(2)}) collective-permute-start(bf16[1792,256]{1,0:T(8,128)(2,1)} %collective-permute-done.6.refs_7_), channel_id=1, source_target_pairs={{2,3},{6,7},{9,8},{10,11},{13,12},{14,15},{17,16},{18,19},{21,20},... | collective-permute-start | bytes 2752520 | tf_op jit(solution)/shard_map/ppermute | solution.py:262
  131.8 123.3 %collective-permute-start.5 = (bf16[1536,256]{1,0:T(8,128)(2,1)}, bf16[1536,256]{1,0:T(8,128)(2,1)S(1)}, u32[]{:S(2)}, u32[]{:S(2)}) collective-permute-start(bf16[1536,256]{1,0:T(8,128)(2,1)} %collective-permute-done.3.refs_4_), channel_id=1, source_target_pairs={{1,0},{2,3},{5,4},{6,7},{9,8},{10,11},{13,12},{14,15},{17,16},{18,... | collective-permute-start | bytes 2359304 | tf_op jit(solution)/shard_map/ppermute | solution.py:251
  133.1 141.4 %collective-permute-start.9 = (bf16[1536,256]{1,0:T(8,128)(2,1)}, bf16[1536,256]{1,0:T(8,128)(2,1)}, u32[]{:S(2)}, u32[]{:S(2)}) collective-permute-start(bf16[1536,256]{1,0:T(8,128)(2,1)} %collective-permute-done.7.refs_8_), channel_id=1, source_target_pairs={{2,3},{6,7},{9,8},{10,11},{13,12},{14,15},{17,16},{18,19},{21,20},... | collective-permute-start | bytes 2359304 | tf_op jit(solution)/shard_map/ppermute | solution.py:262
  255.1 0.9 copy-start.3
  255.1 1.2 copy-start.2
Sparse Core Ops, SparseCore 0:
  11.2 79.4 all-gather.2

commit v9 on v8

--- a/solution.py
+++ b/solution.py
@@ -13,19 +13,21 @@
 VMEM_LIMIT = 58 << 20
 
 
-def pack_kernel(cols_ref, x_ref, part_a, part_b, full, held, in_sems, sems):
+def pack_kernel(
+    cols_ref, flag_ref, first_ref, x_ref, part_a, part_b, full, facts, held, norm, in_sems, sems
+):
     count, block, _ = x_ref.shape
     slots = cols_ref.shape[0]
-    moves = []
+    loads = []
     place = jnp.int32(0)
     for index in range(count):
         filled = cols_ref[index % slots, index // slots] >= 0
         load = pltpu.make_async_copy(x_ref.at[index], held.at[index], in_sems.at[index])
         pl.when(filled)(load.start)
-        moves.append((filled, place, load))
+        loads.append((filled, place, load))
         place = place + filled.astype(jnp.int32)
     sends = []
-    for index, (filled, place, load) in enumerate(moves):
+    for index, (filled, place, load) in enumerate(loads):
         pl.when(filled)(load.wait)
         targets = (
             (full, filled, place),
@@ -39,29 +41,60 @@
             )
             pl.when(wanted)(copy.start)
             sends.append((wanted, copy))
+
+    norm[...] = jnp.zeros_like(norm)
+    for index in range(count):
+        row = index // slots
+        col = cols_ref[index % slots, row]
+        flag = flag_ref[row]
+
+        @pl.when(col >= 0)
+        def _():
+            values = held[index].astype(jnp.float32)
+            weight = (1 - 2 * flag).astype(jnp.float32)
+            norm[...] += weight * jnp.sum(values * values, axis=0, keepdims=True)
+
+        @pl.when((col == first_ref[0] + row) & (flag != 0))
+        def _():
+            values = held[index].astype(jnp.float32)
+            eye = lax.broadcasted_iota(jnp.int32, (block, block), 0)
+            eye = eye == lax.broadcasted_iota(jnp.int32, (block, block), 1)
+            norm[...] += 2.0 * jnp.sum(jnp.where(eye, values, 0.0), axis=0, keepdims=True)
+
+    down = lax.broadcasted_iota(jnp.int32, facts.shape, 0)
+    across = lax.broadcasted_iota(jnp.int32, facts.shape, 1)
+    values = jnp.where((down == 0) & (across == slots), jnp.sum(norm[...]), 0.0)
+    for index in range(count):
+        here = (down == index // slots) & (across == index % slots)
+        value = cols_ref[index % slots, index // slots].astype(jnp.float32)
+        values = jnp.where(here, value, values)
+    facts[...] = values
     for wanted, copy in sends:
         pl.when(wanted)(copy.wait)
 
 
-def pack(x_blocks, x_cols):
+def pack(x_blocks, x_cols, branch_flag, first_row):
     rows, slots, block, _ = x_blocks.shape
     count = rows * slots
+    smem = pl.BlockSpec(memory_space=pltpu.SMEM)
     hbm = pl.BlockSpec(memory_space=pltpu.HBM)
+    packed = [
+        jax.ShapeDtypeStruct((size * block, block), x_blocks.dtype)
+        for size in (SPLIT, PACKED - SPLIT, PACKED)
+    ]
     return pl.pallas_call(
         pack_kernel,
-        out_shape=[
-            jax.ShapeDtypeStruct((size * block, block), x_blocks.dtype)
-            for size in (SPLIT, PACKED - SPLIT, PACKED)
-        ],
-        in_specs=[pl.BlockSpec(memory_space=pltpu.SMEM), hbm],
-        out_specs=[hbm] * 3,
+        out_shape=packed + [jax.ShapeDtypeStruct((rows, 128), jnp.float32)],
+        in_specs=[smem, smem, smem, hbm],
+        out_specs=[hbm] * 3 + [pl.BlockSpec(memory_space=pltpu.VMEM)],
         scratch_shapes=[
             pltpu.VMEM((count, block, block), x_blocks.dtype),
+            pltpu.VMEM((1, block), jnp.float32),
             pltpu.SemaphoreType.DMA((count,)),
             pltpu.SemaphoreType.DMA((3, count)),
         ],
         compiler_params=pltpu.CompilerParams(vmem_limit_bytes=VMEM_LIMIT),
-    )(x_cols.T, x_blocks.reshape(count, block, block))
+    )(x_cols.T, branch_flag, first_row.reshape(1), x_blocks.reshape(count, block, block))
 
 
 BATCH = 4
@@ -320,27 +353,6 @@
     return jnp.concatenate(list(lists.values())), layout
 
 
-def local_trace(x_blocks, x_cols, branch_flag, first_row):
-    rows, slots, block, _ = x_blocks.shape
-    own_row = first_row + jnp.arange(rows, dtype=jnp.int32)
-    flag = branch_flag.astype(jnp.float32)[:, None]
-    norm_weight = jnp.where(x_cols >= 0, 1.0 - 2.0 * flag, 0.0)
-    diag_weight = jnp.where(x_cols == own_row[:, None], 2.0 * flag, 0.0)
-    values = x_blocks.astype(jnp.float32)
-    eye = jnp.eye(block, dtype=jnp.float32)
-    weight = norm_weight[:, :, None, None] * values + diag_weight[:, :, None, None] * eye
-    return jnp.sum(weight * values)
-
-
-def gather_facts(values):
-    n_row = lax.axis_size("row")
-    n_col = lax.axis_size("col")
-    down, across = values.shape
-    padded = jnp.pad(values.astype(jnp.float32), [(0, 0), (0, 128 - across)])
-    every = lax.all_gather(padded, ("row", "col"), axis=0, tiled=True)
-    return every.reshape(n_row, n_col, down, 128)[..., :across]
-
-
 def per_device(x_blocks, x_cols, out_cols, branch_flag):
     rows, slots = x_cols.shape
     kept = out_cols.shape[1]
@@ -354,13 +366,15 @@
     width = n_col * slots
     shape = (rows, kept, block, dtype)
 
-    all_cols = gather_facts(x_cols).astype(jnp.int32)
+    *packed, facts = pack(x_blocks, x_cols, branch_flag, row * rows)
+    facts = lax.all_gather(facts, ("row", "col"), axis=0, tiled=True)
+    *packed, facts = lax.optimization_barrier((*packed, facts))
+    part_a, part_b, full = packed
+    plane = lax.all_gather(full, "row", axis=0)
+    facts = facts.reshape(n_row, n_col, rows, 128)
+    trace = jnp.sum(facts[:, :, 0, slots]).reshape(1)
+    all_cols = facts[..., :slots].astype(jnp.int32)
     all_places = places(all_cols)
-    part_a, part_b, full = pack(x_blocks, x_cols)
-    plane = lax.all_gather(full, "row", axis=0)
-
-    trace = local_trace(x_blocks, x_cols, branch_flag, row * rows)
-    trace = jnp.sum(gather_facts(jnp.pad(trace.reshape(1, 1), [(0, 7), (0, 0)]))).reshape(1)
 
     plane_cols = lax.dynamic_index_in_dim(all_cols, col, 1, keepdims=False)
     plane_places = lax.dynamic_index_in_dim(all_places, col, 1, keepdims=False)

time: 283 us -> 219 us (0.77)
  the two profiles are of different devices: /device:TPU:0 before, /device:TPU:7 now
where the time goes in v9:
time: 219 us; the launch traced here: 218 us
  waiting for transfers between devices  69.6 us (32%)
  blocking collectives  60.7 us (28%)
  other arithmetic  24.1 us (11%)
  Pallas kernels  18.6 us (8%)
  starting transfers between devices  17.5 us (8%)
  between operations  14.3 us (7%)
  local copies, waits for them, and re-layouts  12.9 us (6%)
    ppermute x8, waiting for transfers between devices, shift(): return lax.ppermute(array, 'col', pairs)  61.7 us
    all_gather x1, blocking collectives, per_device(): facts = lax.all_gather(facts, ('row', 'col'), axis=0, tiled=True)  60.7 us
    ppermute x8, starting transfers between devices, shift(): return lax.ppermute(array, 'col', pairs)  14.8 us
    pallas_call x2, Pallas kernels, multiply(): pl.pallas_call(functools.partial(multiply_kernel, loads, kept, layout, tu...  14.6 us
    ppermute x2, waiting for transfers between devices, gather_line(): end_three = lax.ppermute(middle_two, ('row', 'col'), pairs)  7.86 us
    concatenate x2, local copies, waits for them, and re-layouts, make_table(): return (jnp.concatenate(list(lists.values())), layout)  5.36 us
    reduce_sum x6, other arithmetic, running_count(): return jnp.sum(jnp.where(before, fill[..., :, None], 0), axis=-2)  4.71 us
  transfers between devices with their start and end apart: 11, of which 3 were waited for; matrix products, arithmetic and copies ran while one was open for 17% of the time, Pallas kernels for 4%

profile of v9, /device:TPU:7, one launch (start us, length us, event | category | flops | bytes accessed | tf_op | source)
XLA Modules:
  0.0 217.7 jit_solution(8182437657716108186)
XLA Ops:
  7.2 4.1 %shard_map.59 = (bf16[1792,256]{1,0:T(8,128)(2,1)}, bf16[1536,256]{1,0:T(8,128)(2,1)}, bf16[3328,256]{1,0:T(8,128)(2,1)}, f32[8,128]{1,0:T(8,128)}) custom-call(s32[2,8]{1,0:T(2,128)} %bitcast.59, s32[8]{0:T(128)} %flag_ref.1, s32[1]{0:T(128)} %bitcast.1.first_ref, bf16[16,256,256]{2,1,0:T(8,128)(2,1)} %bitcast.47), custom_call_target="tpu_custom_call" | custom-call | tf_op jit(solution)/shard_map/pallas_call | solution.py:85
  11.3 60.7 %all_gather.9 = f32[256,128]{1,0:T(8,128)S(1)} all-gather(f32[8,128]{1,0:T(8,128)} %get-tuple-element.13), channel_id=1, replica_groups=mesh['row'=8,'col'=4] {'row','col'}, dimensions={0}, use_global_device_ids=true | all-gather | bytes 135168 | tf_op jit(solution)/shard_map/all_gather | solution.py:370
  72.7 4.2 %collective-permute-start.1 = (bf16[1536,256]{1,0:T(8,128)(2,1)}, bf16[1536,256]{1,0:T(8,128)(2,1)}, u32[]{:S(2)}, u32[]{:S(2)}) collective-permute-start(bf16[1536,256]{1,0:T(8,128)(2,1)} %get-tuple-element.17), channel_id=1, source_target_pairs={{0,1},{1,0},{2,3},{3,2},{4,5},{5,4},{6,7},{7,6},{8,9},{9,8},{10,11... | collective-permute-start | bytes 2359304 | tf_op jit(solution)/shard_map/ppermute | solution.py:284
  77.7 4.4 %collective-permute-start = (bf16[1792,256]{1,0:T(8,128)(2,1)}, bf16[1792,256]{1,0:T(8,128)(2,1)S(1)}, u32[]{:S(2)}, u32[]{:S(2)}) collective-permute-start(bf16[1792,256]{1,0:T(8,128)(2,1)} %get-tuple-element.16), channel_id=1, source_target_pairs={{0,1},{1,0},{2,3},{3,2},{4,5},{5,4},{6,7},{7,6},{8,9},{9,8},{10,11... | collective-permute-start | bytes 2752520 | tf_op jit(solution)/shard_map/ppermute | solution.py:284
  90.7 22.5 %collective-permute-done.refs_1_ = bf16[1792,256]{1,0:T(8,128)(2,1)S(1)} collective-permute-done((bf16[1792,256]{1,0:T(8,128)(2,1)}, bf16[1792,256]{1,0:T(8,128)(2,1)S(1)}, u32[]{:S(2)}, u32[]{:S(2)}) %collective-permute-start) | collective-permute-done | bytes 917536 | tf_op jit(solution)/shard_map/ppermute | solution.py:284
  113.9 1.4 select_reduce_fusion
  116.5 1.3 copy.53
  117.8 1.5 select_reduce_fusion.15
  119.3 1.3 add_select_fusion
  120.7 1.5 collective-permute-start.7
  123.5 2.1 convert_reduce_fusion.2
  126.9 1.3 collective-permute-start.8
  130.2 1.3 collective-permute-start.9
  132.9 3.6 %select_reduce_fusion.4 = (s32[32,8]{1,0:T(8,128)S(1)}, s32[32,8]{1,0:T(8,128)S(1)}, s32[32,8]{1,0:T(8,128)}, s32[32,8]{1,0:T(8,128)S(1)}) fusion(s32[32,64]{1,0:T(8,128)} %get-tuple-element.62, s32[32,64]{1,0:T(8,128)} %broadcast_add_fusion, s32[32,64]{1,0:T(8,128)} %get-tuple-element.51, s32[32,64]{1,0:T(8,128)S(1)} %bitcast.54, s32[32,64]{1,0:T(8,128)S(1)} %bitcast.55), kind=kLoop, calls=%fused_computation.4 | loop fusion | flops 162816 | bytes 45056 | tf_op jit(solution)/shard_map/reduce_sum | solution.py:326
  136.5 1.4 select_reduce_fusion.3
  138.5 2.7 %concatenate.9.table = s32[328]{0:T(512)} concatenate(s32[1]{0:T(128)} %bitcast.21, s32[1]{0:T(128)} %bitcast.23, s32[1]{0:T(128)} %constant.111.clone.1, s32[1]{0:T(128)} %bitcast.14, s32[1]{0:T(128)} %bitcast.15, s32[1]{0:T(128)} %bitcast.16, s32[1]{0:T(128)} %bitcast.17, s32[1]{0:T(128)} %bitcast.18, s32[32]{0:T(128)} %get-tuple-element.36, s32[4]{0:T(128)} %broadcast_in_dim.344, ...), dimensions={0} | concatenate | bytes 2624 | tf_op jit(solution)/shard_map/concatenate | solution.py:353
  141.2 1.5 select_reduce_fusion.19
  143.5 1.4 select_reduce_fusion.7
  144.9 2.7 %concatenate.8.table = s32[328]{0:T(512)} concatenate(s32[1]{0:T(128)} %bitcast.9, s32[1]{0:T(128)} %bitcast.13, s32[1]{0:T(128)} %constant.111.clone.1, s32[1]{0:T(128)} %bitcast.14, s32[1]{0:T(128)} %bitcast.15, s32[1]{0:T(128)} %bitcast.16, s32[1]{0:T(128)} %bitcast.17, s32[1]{0:T(128)} %bitcast.18, s32[32]{0:T(128)} %get-tuple-element.41, s32[4]{0:T(128)} %broadcast_in_dim.344, ...), dimensions={0} | concatenate | bytes 2624 | tf_op jit(solution)/shard_map/concatenate | solution.py:353
  147.6 1.6 slice_reduce_fusion
  149.2 39.2 %collective-permute-done.5.refs_6_ = bf16[1536,256]{1,0:T(8,128)(2,1)} collective-permute-done((bf16[1536,256]{1,0:T(8,128)(2,1)S(1)}, bf16[1536,256]{1,0:T(8,128)(2,1)}, u32[]{:S(2)}, u32[]{:S(2)}) %collective-permute-start.5) | collective-permute-done | bytes 786464 | tf_op jit(solution)/shard_map/ppermute | solution.py:284
  188.4 8.2 %shard_map.60.refs_11_ = bf16[32,256,256]{2,1,0:T(8,128)(2,1)} custom-call(s32[328]{0:T(512)} %concatenate.9.table, bf16[8,3328,256]{2,1,0:T(8,128)(2,1)} %bitcast.44, bf16[3328,256]{1,0:T(8,128)(2,1)} %get-tuple-element.15.refs_0_, bf16[1792,256]{1,0:T(8,128)(2,1)} %copy-done.1, bf16[1536,256]{1,0:T(8,128)(2,1)} %collective-permute-done.1.refs_2_, ...), custom_call_target="tpu_custom_call" | custom-call | tf_op jit(solution)/shard_map/pallas_call | solution.py:263
  196.6 7.9 %collective-permute-done.9.refs_10_ = bf16[1536,256]{1,0:T(8,128)(2,1)} collective-permute-done((bf16[1536,256]{1,0:T(8,128)(2,1)}, bf16[1536,256]{1,0:T(8,128)(2,1)}, u32[]{:S(2)}, u32[]{:S(2)}) %collective-permute-start.9) | collective-permute-done | bytes 786464 | tf_op jit(solution)/shard_map/ppermute | solution.py:295
  204.5 6.3 %shard_map.61 = bf16[32,256,256]{2,1,0:T(8,128)(2,1)} custom-call(s32[328]{0:T(512)} %concatenate.8.table, bf16[8,3328,256]{2,1,0:T(8,128)(2,1)} %bitcast.45, bf16[3328,256]{1,0:T(8,128)(2,1)} %get-tuple-element.15.refs_0_, bf16[1792,256]{1,0:T(8,128)(2,1)} %copy-done.1, ...), custom_call_target="tpu_custom_call", output_to_operand_aliasing={{}: (13, {})} | custom-call | tf_op jit(solution)/shard_map/pallas_call | solution.py:263
  (96 shorter events, 19.1 us)
Async XLA Ops:
  7.2 181.2 %all-gather.3.cloned.1.call-start = ((), (), s32[]{:S(2)}) async-start(), calls=%async_computation | async-start | bytes 15335424 | tf_op jit(solution)/shard_map/all_gather | solution.py:373
  72.0 18.7 %copy-start.4 = (f32[256,128]{1,0:T(8,128)}, f32[256,128]{1,0:T(8,128)S(1)}, u32[]{:S(2)}) copy-start(f32[256,128]{1,0:T(8,128)S(1)} %all_gather.9) | copy-start | bytes 393220
  72.0 56.9 %collective-permute-start.3 = (bf16[1536,256]{1,0:T(8,128)(2,1)}, bf16[1536,256]{1,0:T(8,128)(2,1)S(1)}, u32[]{:S(2)}, u32[]{:S(2)}) collective-permute-start(bf16[1536,256]{1,0:T(8,128)(2,1)} %get-tuple-element.17), channel_id=1, source_target_pairs={{1,2},{2,1},{5,6},{6,5},{9,10},{10,9},{13,14},{14,13},{17,18},{18,... | collective-permute-start | bytes 2359304 | tf_op jit(solution)/shard_map/ppermute | solution.py:284
  72.7 48.0 %collective-permute-start.1 = (bf16[1536,256]{1,0:T(8,128)(2,1)}, bf16[1536,256]{1,0:T(8,128)(2,1)}, u32[]{:S(2)}, u32[]{:S(2)}) collective-permute-start(bf16[1536,256]{1,0:T(8,128)(2,1)} %get-tuple-element.17), channel_id=1, source_target_pairs={{0,1},{1,0},{2,3},{3,2},{4,5},{5,4},{6,7},{7,6},{8,9},{9,8},{10,11... | collective-permute-start | bytes 2359304 | tf_op jit(solution)/shard_map/ppermute | solution.py:284
  76.9 48.6 %collective-permute-start.2 = (bf16[1792,256]{1,0:T(8,128)(2,1)}, bf16[1792,256]{1,0:T(8,128)(2,1)S(1)}, u32[]{:S(2)}, u32[]{:S(2)}) collective-permute-start(bf16[1792,256]{1,0:T(8,128)(2,1)} %get-tuple-element.16), channel_id=1, source_target_pairs={{1,2},{2,1},{5,6},{6,5},{9,10},{10,9},{13,14},{14,13},{17,18},{18,... | collective-permute-start | bytes 2752520 | tf_op jit(solution)/shard_map/ppermute | solution.py:284
  77.7 35.5 %collective-permute-start = (bf16[1792,256]{1,0:T(8,128)(2,1)}, bf16[1792,256]{1,0:T(8,128)(2,1)S(1)}, u32[]{:S(2)}, u32[]{:S(2)}) collective-permute-start(bf16[1792,256]{1,0:T(8,128)(2,1)} %get-tuple-element.16), channel_id=1, source_target_pairs={{0,1},{1,0},{2,3},{3,2},{4,5},{5,4},{6,7},{7,6},{8,9},{9,8},{10,11... | collective-permute-start | bytes 2752520 | tf_op jit(solution)/shard_map/ppermute | solution.py:284
  87.6 3.0 %copy-start.5 = (pred[32,64]{1,0:T(8,128)(4,1)}, pred[32,64]{1,0:T(8,128)(4,1)S(1)}, u32[]{:S(2)}) copy-start(pred[32,64]{1,0:T(8,128)(4,1)S(1)} %get-tuple-element.42) | copy-start | bytes 6148
  113.2 75.2 %copy-start.1 = (bf16[1792,256]{1,0:T(8,128)(2,1)}, bf16[1792,256]{1,0:T(8,128)(2,1)S(1)}, u32[]{:S(2)}) copy-start(bf16[1792,256]{1,0:T(8,128)(2,1)S(1)} %collective-permute-done.refs_1_) | copy-start | bytes 2752516
  113.2 13.7 %collective-permute-start.6 = (bf16[1792,256]{1,0:T(8,128)(2,1)S(1)}, bf16[1792,256]{1,0:T(8,128)(2,1)S(1)}, u32[]{:S(2)}, u32[]{:S(2)}) collective-permute-start(bf16[1792,256]{1,0:T(8,128)(2,1)S(1)} %collective-permute-done.refs_1_), channel_id=1, source_target_pairs={{1,2},{2,1},{5,6},{6,5},{9,10},{10,9},{13,14},{14,13},{17,18},{18,... | collective-permute-start | bytes 2752520 | tf_op jit(solution)/shard_map/ppermute | solution.py:284
  120.7 9.6 %collective-permute-start.7 = (bf16[1536,256]{1,0:T(8,128)(2,1)}, bf16[1536,256]{1,0:T(8,128)(2,1)}, u32[]{:S(2)}, u32[]{:S(2)}) collective-permute-start(bf16[1536,256]{1,0:T(8,128)(2,1)} %collective-permute-done.1.refs_2_), channel_id=1, source_target_pairs={{1,2},{2,1},{5,6},{6,5},{9,10},{10,9},{13,14},{14,13},{17,18},{18,... | collective-permute-start | bytes 2359304 | tf_op jit(solution)/shard_map/ppermute | solution.py:284
  125.6 62.8 %copy-start = (bf16[1792,256]{1,0:T(8,128)(2,1)}, bf16[1792,256]{1,0:T(8,128)(2,1)S(1)}, u32[]{:S(2)}) copy-start(bf16[1792,256]{1,0:T(8,128)(2,1)S(1)} %collective-permute-done.2.refs_3_) | copy-start | bytes 2752516
  125.6 62.8 %collective-permute-start.4 = (bf16[1792,256]{1,0:T(8,128)(2,1)S(1)}, bf16[1792,256]{1,0:T(8,128)(2,1)}, u32[]{:S(2)}, u32[]{:S(2)}) collective-permute-start(bf16[1792,256]{1,0:T(8,128)(2,1)S(1)} %collective-permute-done.2.refs_3_), channel_id=1, source_target_pairs={{1,0},{2,3},{5,4},{6,7},{9,8},{10,11},{13,12},{14,15},{17,16},{18,... | collective-permute-start | bytes 2752520 | tf_op jit(solution)/shard_map/ppermute | solution.py:284
  126.9 61.5 %copy-start.2 = (bf16[1792,256]{1,0:T(8,128)(2,1)}, bf16[1792,256]{1,0:T(8,128)(2,1)S(1)}, u32[]{:S(2)}) copy-start(bf16[1792,256]{1,0:T(8,128)(2,1)S(1)} %collective-permute-done.6.refs_7_) | copy-start | bytes 2752516
  126.9 77.6 %collective-permute-start.8 = (bf16[1792,256]{1,0:T(8,128)(2,1)S(1)}, bf16[1792,256]{1,0:T(8,128)(2,1)}, u32[]{:S(2)}, u32[]{:S(2)}) collective-permute-start(bf16[1792,256]{1,0:T(8,128)(2,1)S(1)} %collective-permute-done.6.refs_7_), channel_id=1, source_target_pairs={{2,3},{6,7},{9,8},{10,11},{13,12},{14,15},{17,16},{18,19},{21,20},... | collective-permute-start | bytes 2752520 | tf_op jit(solution)/shard_map/ppermute | solution.py:295
  128.9 59.5 %copy-start.3 = (bf16[1536,256]{1,0:T(8,128)(2,1)}, bf16[1536,256]{1,0:T(8,128)(2,1)S(1)}, u32[]{:S(2)}) copy-start(bf16[1536,256]{1,0:T(8,128)(2,1)S(1)} %collective-permute-done.3.refs_4_) | copy-start | bytes 2359300
  128.9 59.4 %collective-permute-start.5 = (bf16[1536,256]{1,0:T(8,128)(2,1)S(1)}, bf16[1536,256]{1,0:T(8,128)(2,1)}, u32[]{:S(2)}, u32[]{:S(2)}) collective-permute-start(bf16[1536,256]{1,0:T(8,128)(2,1)S(1)} %collective-permute-done.3.refs_4_), channel_id=1, source_target_pairs={{1,0},{2,3},{5,4},{6,7},{9,8},{10,11},{13,12},{14,15},{17,16},{18,... | collective-permute-start | bytes 2359304 | tf_op jit(solution)/shard_map/ppermute | solution.py:284
  130.2 74.3 %collective-permute-start.9 = (bf16[1536,256]{1,0:T(8,128)(2,1)}, bf16[1536,256]{1,0:T(8,128)(2,1)}, u32[]{:S(2)}, u32[]{:S(2)}) collective-permute-start(bf16[1536,256]{1,0:T(8,128)(2,1)} %collective-permute-done.7.refs_8_), channel_id=1, source_target_pairs={{2,3},{6,7},{9,8},{10,11},{13,12},{14,15},{17,16},{18,19},{21,20},... | collective-permute-start | bytes 2359304 | tf_op jit(solution)/shard_map/ppermute | solution.py:295
Sparse Core Ops, SparseCore 0:
  72.1 81.3 all-gather.2

commit v10 on v9

--- a/solution.py
+++ b/solution.py
@@ -61,13 +61,11 @@
             eye = eye == lax.broadcasted_iota(jnp.int32, (block, block), 1)
             norm[...] += 2.0 * jnp.sum(jnp.where(eye, values, 0.0), axis=0, keepdims=True)
 
-    down = lax.broadcasted_iota(jnp.int32, facts.shape, 0)
     across = lax.broadcasted_iota(jnp.int32, facts.shape, 1)
-    values = jnp.where((down == 0) & (across == slots), jnp.sum(norm[...]), 0.0)
+    values = jnp.where(across == count, jnp.sum(norm[...]), 0.0)
     for index in range(count):
-        here = (down == index // slots) & (across == index % slots)
         value = cols_ref[index % slots, index // slots].astype(jnp.float32)
-        values = jnp.where(here, value, values)
+        values = jnp.where(across == index, value, values)
     facts[...] = values
     for wanted, copy in sends:
         pl.when(wanted)(copy.wait)
@@ -84,7 +82,7 @@
     ]
     return pl.pallas_call(
         pack_kernel,
-        out_shape=packed + [jax.ShapeDtypeStruct((rows, 128), jnp.float32)],
+        out_shape=packed + [jax.ShapeDtypeStruct((1, 128), jnp.float32)],
         in_specs=[smem, smem, smem, hbm],
         out_specs=[hbm] * 3 + [pl.BlockSpec(memory_space=pltpu.VMEM)],
         scratch_shapes=[
@@ -284,22 +282,26 @@
     return lax.ppermute(array, "col", pairs)
 
 
-def gather_line(part):
-    first = shift(part, [(0, 1), (1, 0), (2, 3), (3, 2)])
-    middle = shift(part, [(1, 2), (2, 1)])
-    end_two = shift(middle, [(1, 0), (2, 3)])
-    middle_two = shift(first, [(1, 2), (2, 1)])
+def gather_line(parts, facts):
+    first = [shift(part, [(0, 1), (1, 0), (2, 3), (3, 2)]) for part in parts]
+    middle = [shift(part, [(1, 2), (2, 1)]) for part in parts]
+    facts = gather_facts(facts)
+    first[0], middle[0], facts = lax.optimization_barrier((first[0], middle[0], facts))
+    end_two = [shift(part, [(1, 0), (2, 3)]) for part in middle]
+    middle_two = [shift(part, [(1, 2), (2, 1)]) for part in first]
     pairs = []
     for row in range(lax.axis_size("row")):
-        pairs += [(4 * row + 1, 4 * row)] * (row // 2 != 0) + [(4 * row + 2, 4 * row + 3)] * (row // 2 != 3)
-    end_three = lax.ppermute(middle_two, ("row", "col"), pairs)
-    return {
+        pairs += [(4 * row + 1, 4 * row)] * (row // 2 != 0)
+        pairs += [(4 * row + 2, 4 * row + 3)] * (row // 2 != 3)
+    end_three = [lax.ppermute(part, ("row", "col"), pairs) for part in middle_two]
+    line = {
         "first": first,
         "middle": middle,
         "end_two": end_two,
         "middle_two": middle_two,
         "end_three": end_three,
     }
+    return line, facts
 
 
 def running_count(fill):
@@ -353,6 +355,23 @@
     return jnp.concatenate(list(lists.values())), layout
 
 
+def gather_facts(facts):
+    n_row = lax.axis_size("row")
+    n_col = lax.axis_size("col")
+    for axis, size in (("row", n_row), ("col", n_col)):
+        mask = 1
+        while mask < size:
+            other = lax.ppermute(facts, axis, [(i, i ^ mask) for i in range(size)])
+            facts = jnp.concatenate([facts, other])
+            mask *= 2
+    step = jnp.arange(n_row * n_col, dtype=jnp.int32)
+    row = jnp.bitwise_xor(lax.axis_index("row"), step % n_row)
+    col = jnp.bitwise_xor(lax.axis_index("col"), step // n_row)
+    hit = (row * n_col + col)[None, :] == step[:, None]
+    facts = jnp.sum(jnp.where(hit[..., None], facts, 0.0), axis=1)
+    return facts.reshape(n_row, n_col, 128)
+
+
 def per_device(x_blocks, x_cols, out_cols, branch_flag):
     rows, slots = x_cols.shape
     kept = out_cols.shape[1]
@@ -366,14 +385,16 @@
     width = n_col * slots
     shape = (rows, kept, block, dtype)
 
-    *packed, facts = pack(x_blocks, x_cols, branch_flag, row * rows)
-    facts = lax.all_gather(facts, ("row", "col"), axis=0, tiled=True)
-    *packed, facts = lax.optimization_barrier((*packed, facts))
-    part_a, part_b, full = packed
+    part_a, part_b, full, facts = pack(x_blocks, x_cols, branch_flag, row * rows)
     plane = lax.all_gather(full, "row", axis=0)
-    facts = facts.reshape(n_row, n_col, rows, 128)
-    trace = jnp.sum(facts[:, :, 0, slots]).reshape(1)
-    all_cols = facts[..., :slots].astype(jnp.int32)
+    tuned = n_col == 4 and n_row == 8
+    if tuned:
+        line, facts = gather_line((part_a, part_b), facts)
+    else:
+        line = lax.all_gather(full, "col", axis=0)
+        facts = gather_facts(facts)
+    trace = jnp.sum(facts[:, :, rows * slots]).reshape(1)
+    all_cols = facts[:, :, : rows * slots].astype(jnp.int32).reshape(n_row, n_col, rows, slots)
     all_places = places(all_cols)
 
     plane_cols = lax.dynamic_index_in_dim(all_cols, col, 1, keepdims=False)
@@ -407,8 +428,7 @@
         return jnp.sum(found, axis=(0, 1))
 
     heights = jnp.arange(n_col, dtype=jnp.int32)
-    if not (n_col == 4 and n_row == 8):
-        line = lax.all_gather(full, "col", axis=0)
+    if not tuned:
         left_of = straight(1 + heights, heights >= 0)
         everything = jnp.ones((rows * kept,), bool)
         one = jnp.ones((1,), jnp.int32)
@@ -418,7 +438,6 @@
         purified = multiply(plane, [full, line], tuple(loads), 1 + n_col, layout, table, shape)
         return purified.reshape(rows, kept, block, block), trace
 
-    line = [gather_line(part) for part in (part_a, part_b)]
     at_end = (col == 0) | (col == n_col - 1)
     corner = at_end & (row // 2 == col)
     far = at_end & ~corner
@@ -443,7 +462,7 @@
         spans = ((0, SPLIT), (SPLIT, PACKED - SPLIT))
         for which in range(2):
             loads.append((len(arrays), None, entry) + spans[which] + (wanted,))
-            arrays.append(line[which][name])
+            arrays.append(line[name][which])
 
     def call(left_of, chosen, before=None):
         table, layout = make_table(left_of, right_of, owns, branch_flag, chosen, width, wanted)

time: 219 us -> 155 us (0.71)
  the two profiles are of different devices: /device:TPU:7 before, /device:TPU:6 now
where the time goes in v10:
time: 155 us; the launch traced here: 154 us
  waiting for transfers between devices  63.7 us (41%)
  other arithmetic  24.4 us (16%)
  Pallas kernels  19 us (12%)
  starting transfers between devices  17.9 us (12%)
  local copies, waits for them, and re-layouts  15 us (10%)
  between operations  14.3 us (9%)
    ppermute x2, waiting for transfers between devices, gather_line(): lax.ppermute(part, ('row', 'col'), pairs)  29 us
    ppermute x5, waiting for transfers between devices, gather_facts(): other = lax.ppermute(facts, axis, [(i, i ^ mask) for i in range(size)])  27.2 us
    pallas_call x2, Pallas kernels, multiply(): pl.pallas_call(functools.partial(multiply_kernel, loads, kept, layout, tu...  14.9 us
    ppermute x8, starting transfers between devices, shift(): return lax.ppermute(array, 'col', pairs)  12.6 us
    ppermute x8, waiting for transfers between devices, shift(): return lax.ppermute(array, 'col', pairs)  7.53 us
    concatenate x2, local copies, waits for them, and re-layouts, make_table(): return (jnp.concatenate(list(lists.values())), layout)  5.24 us
    pallas_call x1, Pallas kernels, pack(): pl.pallas_call(pack_kernel, out_shape=packed + [jax.ShapeDtypeStruct((1,...  4.06 us
    reduce_sum x7, other arithmetic, running_count(): return jnp.sum(jnp.where(before, fill[..., :, None], 0), axis=-2)  3.96 us
  transfers between devices with their start and end apart: 16, of which 5 were waited for; matrix products, arithmetic and copies ran while one was open for 26% of the time, Pallas kernels for 6%

profile of v10, /device:TPU:6, one launch (start us, length us, event | category | flops | bytes accessed | tf_op | source)
XLA Modules:
  0.0 154.3 jit_solution(17000710752217642823)
XLA Ops:
  7.2 4.1 %shard_map.59 = (bf16[1792,256]{1,0:T(8,128)(2,1)}, bf16[1536,256]{1,0:T(8,128)(2,1)}, bf16[3328,256]{1,0:T(8,128)(2,1)}, f32[1,128]{1,0:T(1,128)}) custom-call(s32[2,8]{1,0:T(2,128)} %bitcast.60, s32[8]{0:T(128)} %flag_ref.1, s32[1]{0:T(128)} %bitcast.1.first_ref, bf16[16,256,256]{2,1,0:T(8,128)(2,1)} %bitcast.44), custom_call_target="tpu_custom_call" | custom-call | tf_op jit(solution)/shard_map/pallas_call | solution.py:83
  12.0 4.4 %collective-permute-start.7 = (bf16[1536,256]{1,0:T(8,128)(2,1)}, bf16[1536,256]{1,0:T(8,128)(2,1)}, u32[]{:S(2)}, u32[]{:S(2)}) collective-permute-start(bf16[1536,256]{1,0:T(8,128)(2,1)} %get-tuple-element.14), channel_id=1, source_target_pairs={{0,1},{1,0},{2,3},{3,2},{4,5},{5,4},{6,7},{7,6},{8,9},{9,8},{10,11... | collective-permute-start | bytes 2359304 | tf_op jit(solution)/shard_map/ppermute | solution.py:282
  17.2 1.9 %collective-permute-start = (bf16[1792,256]{1,0:T(8,128)(2,1)}, bf16[1792,256]{1,0:T(8,128)(2,1)S(1)}, u32[]{:S(2)}, u32[]{:S(2)}) collective-permute-start(bf16[1792,256]{1,0:T(8,128)(2,1)} %get-tuple-element.9), channel_id=1, source_target_pairs={{0,1},{1,0},{2,3},{3,2},{4,5},{5,4},{6,7},{7,6},{8,9},{9,8},{10,11... | collective-permute-start | bytes 2752520 | tf_op jit(solution)/shard_map/ppermute | solution.py:282
  24.4 3.1 %collective-permute-done.3 = f32[2,128]{1,0:T(2,128)S(1)} collective-permute-done((f32[2,128]{1,0:T(2,128)S(1)}, f32[2,128]{1,0:T(2,128)S(1)}, u32[]{:S(2)}, u32[]{:S(2)}) %collective-permute-start.3) | collective-permute-done | bytes 1056 | tf_op jit(solution)/shard_map/ppermute | solution.py:364
  29.0 2.7 %collective-permute-done.4 = f32[4,128]{1,0:T(4,128)S(1)} collective-permute-done((f32[4,128]{1,0:T(4,128)S(1)}, f32[4,128]{1,0:T(4,128)S(1)}, u32[]{:S(2)}, u32[]{:S(2)}) %collective-permute-start.4) | collective-permute-done | bytes 2080 | tf_op jit(solution)/shard_map/ppermute | solution.py:364
  32.5 21.4 %collective-permute-done.5 = f32[8,128]{1,0:T(8,128)S(1)} collective-permute-done((f32[8,128]{1,0:T(8,128)S(1)}, f32[8,128]{1,0:T(8,128)S(1)}, u32[]{:S(2)}, u32[]{:S(2)}) %collective-permute-start.5) | collective-permute-done | bytes 4128 | tf_op jit(solution)/shard_map/ppermute | solution.py:364
  54.5 1.6 %collective-permute-start.6 = (f32[16,128]{1,0:T(8,128)S(1)}, f32[16,128]{1,0:T(8,128)S(1)}, u32[]{:S(2)}, u32[]{:S(2)}) collective-permute-start(f32[16,128]{1,0:T(8,128)S(1)} %concatenate.30), channel_id=1, source_target_pairs={{0,2},{1,3},{2,0},{3,1},{4,6},{5,7},{6,4},{7,5},{8,10},{9,11},{10,... | collective-permute-start | bytes 24584 | tf_op jit(solution)/shard_map/ppermute | solution.py:364
  60.5 1.3 collective-permute-start.10
  61.8 1.6 %collective-permute-start.12 = (bf16[1536,256]{1,0:T(8,128)(2,1)}, bf16[1536,256]{1,0:T(8,128)(2,1)}, u32[]{:S(2)}, u32[]{:S(2)}) collective-permute-start(bf16[1536,256]{1,0:T(8,128)(2,1)} %collective-permute-done.7.refs_2_), channel_id=1, source_target_pairs={{1,2},{2,1},{5,6},{6,5},{9,10},{10,9},{13,14},{14,13},{17,18},{18,... | collective-permute-start | bytes 2359304 | tf_op jit(solution)/shard_map/ppermute | solution.py:282
  72.9 0.8 select_reduce_fusion.13
  74.0 1.1 convert_reduce_fusion.4
  76.7 1.3 collective-permute-start.9
  78.0 1.4 select_reduce_fusion
  80.2 1.3 collective-permute-start.13
  81.5 1.3 collective-permute-start.14
  82.9 2.3 %select_reduce_fusion.5 = (s32[32,8]{1,0:T(8,128)S(1)}, s32[32,8]{1,0:T(8,128)}, s32[32,8]{1,0:T(8,128)}, s32[32,8]{1,0:T(8,128)S(1)}) fusion(s32[32,64]{1,0:T(8,128)S(1)} %broadcast_select_fusion, s32[32,64]{1,0:T(8,128)S(1)} %broadcast_add_fusion, s32[32,64]{1,0:T(8,128)S(1)} %get-tuple-element.49, s32[32,64]{1,0:T(8,128)S(1)} %bitcast.54, ...), kind=kLoop, calls=%fused_computation.5 | loop fusion | flops 162816 | bytes 45056 | tf_op jit(solution)/shard_map/reduce_sum | solution.py:328
  86.5 2.6 %concatenate.33.table = s32[328]{0:T(512)} concatenate(s32[1]{0:T(128)} %bitcast.21, s32[1]{0:T(128)} %bitcast.23, s32[1]{0:T(128)} %constant.138.clone.1, s32[1]{0:T(128)} %bitcast.14, s32[1]{0:T(128)} %bitcast.15, s32[1]{0:T(128)} %bitcast.16, s32[1]{0:T(128)} %bitcast.17, s32[1]{0:T(128)} %bitcast.18, s32[32]{0:T(128)} %get-tuple-element.34, s32[4]{0:T(128)} %broadcast_in_dim.357, ...), dimensions={0} | concatenate | bytes 2624 | tf_op jit(solution)/shard_map/concatenate | solution.py:355
  89.0 1.5 select_reduce_fusion.20
  91.2 1.5 select_reduce_fusion.8
  92.7 2.7 %concatenate.32.table = s32[328]{0:T(512)} concatenate(s32[1]{0:T(128)} %bitcast.9, s32[1]{0:T(128)} %bitcast.13, s32[1]{0:T(128)} %constant.138.clone.1, s32[1]{0:T(128)} %bitcast.14, s32[1]{0:T(128)} %bitcast.15, s32[1]{0:T(128)} %bitcast.16, s32[1]{0:T(128)} %bitcast.17, s32[1]{0:T(128)} %bitcast.18, s32[32]{0:T(128)} %get-tuple-element.39, s32[4]{0:T(128)} %broadcast_in_dim.357, ...), dimensions={0} | concatenate | bytes 2624 | tf_op jit(solution)/shard_map/concatenate | solution.py:355
  96.0 7.5 %collective-permute-done.9.refs_5_ = bf16[1792,256]{1,0:T(8,128)(2,1)} collective-permute-done((bf16[1792,256]{1,0:T(8,128)(2,1)S(1)}, bf16[1792,256]{1,0:T(8,128)(2,1)}, u32[]{:S(2)}, u32[]{:S(2)}) %collective-permute-start.9) | collective-permute-done | bytes 917536 | tf_op jit(solution)/shard_map/ppermute | solution.py:282
  103.6 8.7 %shard_map.60.refs_11_ = bf16[32,256,256]{2,1,0:T(8,128)(2,1)} custom-call(s32[328]{0:T(512)} %concatenate.33.table, bf16[8,3328,256]{2,1,0:T(8,128)(2,1)} %bitcast.41, bf16[3328,256]{1,0:T(8,128)(2,1)} %get-tuple-element.12.refs_0_, bf16[1792,256]{1,0:T(8,128)(2,1)} %copy-done.1, bf16[1536,256]{1,0:T(8,128)(2,1)} %collective-permute-done.7.refs_2_, ...), custom_call_target="tpu_custom_call" | custom-call | tf_op jit(solution)/shard_map/pallas_call | solution.py:261
  112.2 29.0 %collective-permute-done.14.refs_10_ = bf16[1536,256]{1,0:T(8,128)(2,1)} collective-permute-done((bf16[1536,256]{1,0:T(8,128)(2,1)}, bf16[1536,256]{1,0:T(8,128)(2,1)}, u32[]{:S(2)}, u32[]{:S(2)}) %collective-permute-start.14) | collective-permute-done | bytes 786464 | tf_op jit(solution)/shard_map/ppermute | solution.py:296
  141.2 6.2 %shard_map.61 = bf16[32,256,256]{2,1,0:T(8,128)(2,1)} custom-call(s32[328]{0:T(512)} %concatenate.32.table, bf16[8,3328,256]{2,1,0:T(8,128)(2,1)} %bitcast.42, bf16[3328,256]{1,0:T(8,128)(2,1)} %get-tuple-element.12.refs_0_, bf16[1792,256]{1,0:T(8,128)(2,1)} %copy-done.1, ...), custom_call_target="tpu_custom_call", output_to_operand_aliasing={{}: (13, {})} | custom-call | tf_op jit(solution)/shard_map/pallas_call | solution.py:261
  (109 shorter events, 28.8 us)
Async XLA Ops:
  7.2 96.4 %all-gather.3.cloned.1.call-start = ((), (), s32[]{:S(2)}) async-start(), calls=%async_computation | async-start | bytes 15335424 | tf_op jit(solution)/shard_map/all_gather | solution.py:389
  11.3 49.2 %collective-permute-start.8 = (bf16[1536,256]{1,0:T(8,128)(2,1)}, bf16[1536,256]{1,0:T(8,128)(2,1)S(1)}, u32[]{:S(2)}, u32[]{:S(2)}) collective-permute-start(bf16[1536,256]{1,0:T(8,128)(2,1)} %get-tuple-element.14), channel_id=1, source_target_pairs={{1,2},{2,1},{5,6},{6,5},{9,10},{10,9},{13,14},{14,13},{17,18},{18,... | collective-permute-start | bytes 2359304 | tf_op jit(solution)/shard_map/ppermute | solution.py:282
  12.0 49.8 %collective-permute-start.7 = (bf16[1536,256]{1,0:T(8,128)(2,1)}, bf16[1536,256]{1,0:T(8,128)(2,1)}, u32[]{:S(2)}, u32[]{:S(2)}) collective-permute-start(bf16[1536,256]{1,0:T(8,128)(2,1)} %get-tuple-element.14), channel_id=1, source_target_pairs={{0,1},{1,0},{2,3},{3,2},{4,5},{5,4},{6,7},{7,6},{8,9},{9,8},{10,11... | collective-permute-start | bytes 2359304 | tf_op jit(solution)/shard_map/ppermute | solution.py:282
  16.4 47.0 %collective-permute-start.1 = (bf16[1792,256]{1,0:T(8,128)(2,1)}, bf16[1792,256]{1,0:T(8,128)(2,1)S(1)}, u32[]{:S(2)}, u32[]{:S(2)}) collective-permute-start(bf16[1792,256]{1,0:T(8,128)(2,1)} %get-tuple-element.9), channel_id=1, source_target_pairs={{1,2},{2,1},{5,6},{6,5},{9,10},{10,9},{13,14},{14,13},{17,18},{18,... | collective-permute-start | bytes 2752520 | tf_op jit(solution)/shard_map/ppermute | solution.py:282
  17.2 46.3 %collective-permute-start = (bf16[1792,256]{1,0:T(8,128)(2,1)}, bf16[1792,256]{1,0:T(8,128)(2,1)S(1)}, u32[]{:S(2)}, u32[]{:S(2)}) collective-permute-start(bf16[1792,256]{1,0:T(8,128)(2,1)} %get-tuple-element.9), channel_id=1, source_target_pairs={{0,1},{1,0},{2,3},{3,2},{4,5},{5,4},{6,7},{7,6},{8,9},{9,8},{10,11... | collective-permute-start | bytes 2752520 | tf_op jit(solution)/shard_map/ppermute | solution.py:282
  19.1 4.2 %collective-permute-start.2 = (f32[1,128]{1,0:T(1,128)}, f32[1,128]{1,0:T(1,128)S(1)}, u32[]{:S(2)}, u32[]{:S(2)}) collective-permute-start(f32[1,128]{1,0:T(1,128)} %get-tuple-element.10), channel_id=1, source_target_pairs={{0,4},{4,0},{8,12},{12,8},{16,20},{20,16},{24,28},{28,24},{1,5},{5... | collective-permute-start | bytes 1544 | tf_op jit(solution)/shard_map/ppermute | solution.py:364
  23.9 3.6 %collective-permute-start.3 = (f32[2,128]{1,0:T(2,128)S(1)}, f32[2,128]{1,0:T(2,128)S(1)}, u32[]{:S(2)}, u32[]{:S(2)}) collective-permute-start(f32[2,128]{1,0:T(2,128)S(1)} %pad_maximum_fusion.2), channel_id=1, source_target_pairs={{0,8},{4,12},{8,0},{12,4},{16,24},{20,28},{24,16},{28,20},{1,9},{5... | collective-permute-start | bytes 3080 | tf_op jit(solution)/shard_map/ppermute | solution.py:364
  28.1 3.6 %collective-permute-start.4 = (f32[4,128]{1,0:T(4,128)S(1)}, f32[4,128]{1,0:T(4,128)S(1)}, u32[]{:S(2)}, u32[]{:S(2)}) collective-permute-start(f32[4,128]{1,0:T(4,128)S(1)} %pad_maximum_fusion.1), channel_id=1, source_target_pairs={{0,16},{4,20},{8,24},{12,28},{16,0},{20,4},{24,8},{28,12},{1,17},{... | collective-permute-start | bytes 6152 | tf_op jit(solution)/shard_map/ppermute | solution.py:364
  32.3 21.6 %collective-permute-start.5 = (f32[8,128]{1,0:T(8,128)S(1)}, f32[8,128]{1,0:T(8,128)S(1)}, u32[]{:S(2)}, u32[]{:S(2)}) collective-permute-start(f32[8,128]{1,0:T(8,128)S(1)} %pad_maximum_fusion), channel_id=1, source_target_pairs={{0,1},{1,0},{2,3},{3,2},{4,5},{5,4},{6,7},{7,6},{8,9},{9,8},{10,11... | collective-permute-start | bytes 12296 | tf_op jit(solution)/shard_map/ppermute | solution.py:364
  54.5 5.1 %collective-permute-start.6 = (f32[16,128]{1,0:T(8,128)S(1)}, f32[16,128]{1,0:T(8,128)S(1)}, u32[]{:S(2)}, u32[]{:S(2)}) collective-permute-start(f32[16,128]{1,0:T(8,128)S(1)} %concatenate.30), channel_id=1, source_target_pairs={{0,2},{1,3},{2,0},{3,1},{4,6},{5,7},{6,4},{7,5},{8,10},{9,11},{10,... | collective-permute-start | bytes 24584 | tf_op jit(solution)/shard_map/ppermute | solution.py:364
  60.5 43.0 %copy-start.3 = (bf16[1536,256]{1,0:T(8,128)(2,1)}, bf16[1536,256]{1,0:T(8,128)(2,1)S(1)}, u32[]{:S(2)}) copy-start(bf16[1536,256]{1,0:T(8,128)(2,1)S(1)} %collective-permute-done.8.refs_4_) | copy-start | bytes 2359300
  60.5 35.5 %collective-permute-start.10 = (bf16[1536,256]{1,0:T(8,128)(2,1)S(1)}, bf16[1536,256]{1,0:T(8,128)(2,1)}, u32[]{:S(2)}, u32[]{:S(2)}) collective-permute-start(bf16[1536,256]{1,0:T(8,128)(2,1)S(1)} %collective-permute-done.8.refs_4_), channel_id=1, source_target_pairs={{1,0},{2,3},{5,4},{6,7},{9,8},{10,11},{13,12},{14,15},{17,16},{18,... | collective-permute-start | bytes 2359304 | tf_op jit(solution)/shard_map/ppermute | solution.py:282
  61.8 19.7 %collective-permute-start.12 = (bf16[1536,256]{1,0:T(8,128)(2,1)}, bf16[1536,256]{1,0:T(8,128)(2,1)}, u32[]{:S(2)}, u32[]{:S(2)}) collective-permute-start(bf16[1536,256]{1,0:T(8,128)(2,1)} %collective-permute-done.7.refs_2_), channel_id=1, source_target_pairs={{1,2},{2,1},{5,6},{6,5},{9,10},{10,9},{13,14},{14,13},{17,18},{18,... | collective-permute-start | bytes 2359304 | tf_op jit(solution)/shard_map/ppermute | solution.py:282
  63.4 40.1 %copy-start = (bf16[1792,256]{1,0:T(8,128)(2,1)}, bf16[1792,256]{1,0:T(8,128)(2,1)S(1)}, u32[]{:S(2)}) copy-start(bf16[1792,256]{1,0:T(8,128)(2,1)S(1)} %collective-permute-done.1.refs_3_) | copy-start | bytes 2752516
  63.4 40.1 %copy-start.1 = (bf16[1792,256]{1,0:T(8,128)(2,1)}, bf16[1792,256]{1,0:T(8,128)(2,1)S(1)}, u32[]{:S(2)}) copy-start(bf16[1792,256]{1,0:T(8,128)(2,1)S(1)} %collective-permute-done.refs_1_) | copy-start | bytes 2752516
  68.4 11.8 %collective-permute-start.11 = (bf16[1792,256]{1,0:T(8,128)(2,1)S(1)}, bf16[1792,256]{1,0:T(8,128)(2,1)S(1)}, u32[]{:S(2)}, u32[]{:S(2)}) collective-permute-start(bf16[1792,256]{1,0:T(8,128)(2,1)S(1)} %collective-permute-done.refs_1_), channel_id=1, source_target_pairs={{1,2},{2,1},{5,6},{6,5},{9,10},{10,9},{13,14},{14,13},{17,18},{18,... | collective-permute-start | bytes 2752520 | tf_op jit(solution)/shard_map/ppermute | solution.py:282
  76.7 26.8 %collective-permute-start.9 = (bf16[1792,256]{1,0:T(8,128)(2,1)S(1)}, bf16[1792,256]{1,0:T(8,128)(2,1)}, u32[]{:S(2)}, u32[]{:S(2)}) collective-permute-start(bf16[1792,256]{1,0:T(8,128)(2,1)S(1)} %collective-permute-done.1.refs_3_), channel_id=1, source_target_pairs={{1,0},{2,3},{5,4},{6,7},{9,8},{10,11},{13,12},{14,15},{17,16},{18,... | collective-permute-start | bytes 2752520 | tf_op jit(solution)/shard_map/ppermute | solution.py:282
  80.2 23.3 %copy-start.2 = (bf16[1792,256]{1,0:T(8,128)(2,1)}, bf16[1792,256]{1,0:T(8,128)(2,1)S(1)}, u32[]{:S(2)}) copy-start(bf16[1792,256]{1,0:T(8,128)(2,1)S(1)} %collective-permute-done.11.refs_7_) | copy-start | bytes 2752516
  80.2 61.0 %collective-permute-start.13 = (bf16[1792,256]{1,0:T(8,128)(2,1)S(1)}, bf16[1792,256]{1,0:T(8,128)(2,1)}, u32[]{:S(2)}, u32[]{:S(2)}) collective-permute-start(bf16[1792,256]{1,0:T(8,128)(2,1)S(1)} %collective-permute-done.11.refs_7_), channel_id=1, source_target_pairs={{2,3},{6,7},{9,8},{10,11},{13,12},{14,15},{17,16},{18,19},{21,20},... | collective-permute-start | bytes 2752520 | tf_op jit(solution)/shard_map/ppermute | solution.py:296
  81.5 59.7 %collective-permute-start.14 = (bf16[1536,256]{1,0:T(8,128)(2,1)}, bf16[1536,256]{1,0:T(8,128)(2,1)}, u32[]{:S(2)}, u32[]{:S(2)}) collective-permute-start(bf16[1536,256]{1,0:T(8,128)(2,1)} %collective-permute-done.12.refs_8_), channel_id=1, source_target_pairs={{2,3},{6,7},{9,8},{10,11},{13,12},{14,15},{17,16},{18,19},{21,20},... | collective-permute-start | bytes 2359304 | tf_op jit(solution)/shard_map/ppermute | solution.py:296
Sparse Core Ops, SparseCore 0:
  11.4 76.9 all-gather.2

commit v11 on v10

--- a/solution.py
+++ b/solution.py
@@ -135,9 +135,9 @@
         return carry
 
     if turned is not None:
-        is_wanted, at, target = turned
+        is_wanted, at, target, n_turn = turned
         rows = pltpu.make_async_copy(
-            plane.at[pl.ds(table[at], 2)], pool.at[pl.ds(target, 2)], turn_sem
+            plane.at[pl.ds(table[at], n_turn)], pool.at[pl.ds(target, n_turn)], turn_sem
         )
         pl.when(table[is_wanted] != 0)(rows.start)
     lax.fori_loop(0, jnp.minimum(depth, n_terms), begin, 0)
@@ -154,13 +154,16 @@
 
             def turn(place, carry):
                 first = pl.multiple_of(place * block, block)
-                for entry in range(target, target + 2):
-                    pool[entry, pl.ds(first, block)] = lax.dot_general(
-                        eye,
-                        pool[entry, pl.ds(first, block)],
-                        (((1,), (1,)), ((), ())),
-                        preferred_element_type=jnp.float32,
-                    ).astype(pool.dtype)
+                for entry in range(n_turn):
+                    @pl.when(table[layout["turn"] + entry * PACKED + place] != 0)
+                    def _():
+                        pool[target + entry, pl.ds(first, block)] = lax.dot_general(
+                            eye,
+                            pool[target + entry, pl.ds(first, block)],
+                            (((1,), (1,)), ((), ())),
+                            preferred_element_type=jnp.float32,
+                        ).astype(pool.dtype)
+
                 return carry
 
             lax.fori_loop(0, PACKED, turn, 0)
@@ -282,24 +285,48 @@
     return lax.ppermute(array, "col", pairs)
 
 
+def send(array, moves):
+    pairs = []
+    for (q, c), (q_to, c_to) in list(moves):
+        for core in range(2):
+            pairs.append((4 * (2 * q + core) + c, 4 * (2 * q_to + core) + c_to))
+            pairs.append((4 * (7 - 2 * q - core) + 3 - c, 4 * (7 - 2 * q_to - core) + 3 - c_to))
+    return lax.ppermute(array, ("row", "col"), sorted(set(pairs)))
+
+
+def after(array, *others):
+    return lax.optimization_barrier((array, *others))[0]
+
+
 def gather_line(parts, facts):
-    first = [shift(part, [(0, 1), (1, 0), (2, 3), (3, 2)]) for part in parts]
-    middle = [shift(part, [(1, 2), (2, 1)]) for part in parts]
-    facts = gather_facts(facts)
-    first[0], middle[0], facts = lax.optimization_barrier((first[0], middle[0], facts))
-    end_two = [shift(part, [(1, 0), (2, 3)]) for part in middle]
-    middle_two = [shift(part, [(1, 2), (2, 1)]) for part in first]
-    pairs = []
-    for row in range(lax.axis_size("row")):
-        pairs += [(4 * row + 1, 4 * row)] * (row // 2 != 0)
-        pairs += [(4 * row + 2, 4 * row + 3)] * (row // 2 != 3)
-    end_three = [lax.ppermute(part, ("row", "col"), pairs) for part in middle_two]
+    part_a, part_b = parts
+    lines = range(4)
+    down = [((q, 3), (q, 2)) for q in lines]
+    inner = [((q, 2), (q, 1)) for q in lines]
+    ends = [((q, 1), (q, 0)) for q in lines]
+    first_a = send(part_a, down + ends)
+    middle_a = send(part_a, inner)
+    over = [send(part_b, [((q, 1), (0, 0))]) for q in (1, 2, 3)]
+    facts = gather_facts(facts, ("row",))
+    first_a, middle_a, part_b, facts = lax.optimization_barrier(
+        (first_a, middle_a, part_b, facts)
+    )
+    middle_b = send(part_b, inner)
+    first_b = send(part_b, down + ends[:1])
+    end_two_a = send(middle_a, ends[1:])
+    middle_two_a = send(after(first_a, middle_b, end_two_a), inner)
+    end_two_b = send(middle_b, ends[1:])
+    middle_two_b = send(after(first_b, middle_two_a, end_two_b), inner)
+    end_three_a = send(middle_two_a, ends[1:])
+    end_three_b = send(after(middle_two_b, end_three_a), ends[1:])
+    over = [after(array, end_two_b) for array in over]
     line = {
-        "first": first,
-        "middle": middle,
-        "end_two": end_two,
-        "middle_two": middle_two,
-        "end_three": end_three,
+        "first": (first_a, first_b),
+        "middle": (middle_a, middle_b),
+        "end_two": (end_two_a, end_two_b),
+        "middle_two": (middle_two_a, middle_two_b),
+        "end_three": (end_three_a, end_three_b),
+        "round": [send(over[q - 1], [((0, 0), (q, 0))]) for q in (1, 2, 3)],
     }
     return line, facts
 
@@ -315,7 +342,7 @@
     return running_count(flat).reshape(cols.shape)
 
 
-def make_table(left_of, right_of, owns, flags, chosen, width, wanted):
+def make_table(left_of, right_of, owns, flags, chosen, width, wanted, turn=None):
     kept = right_of.shape[0] // left_of.shape[0]
     outputs = right_of.shape[0]
     left_of = jnp.repeat(left_of, kept, axis=0)
@@ -347,6 +374,8 @@
         "owns": owns,
         "flags": flags,
     }
+    if turn is not None:
+        lists["turn"] = turn
     layout = {}
     first = 0
     for name, values in lists.items():
@@ -355,21 +384,26 @@
     return jnp.concatenate(list(lists.values())), layout
 
 
-def gather_facts(facts):
-    n_row = lax.axis_size("row")
-    n_col = lax.axis_size("col")
-    for axis, size in (("row", n_row), ("col", n_col)):
+def gather_facts(facts, axes):
+    places = jnp.zeros((1,), jnp.int32)
+    own = jnp.int32(0)
+    known = 1
+    for axis in axes:
+        size = lax.axis_size(axis)
+        own = own * size + lax.axis_index(axis)
+        known *= size
+    stride = known
+    for axis in axes:
+        size = lax.axis_size(axis)
+        stride //= size
         mask = 1
         while mask < size:
             other = lax.ppermute(facts, axis, [(i, i ^ mask) for i in range(size)])
             facts = jnp.concatenate([facts, other])
+            places = jnp.concatenate([places, places + mask * stride])
             mask *= 2
-    step = jnp.arange(n_row * n_col, dtype=jnp.int32)
-    row = jnp.bitwise_xor(lax.axis_index("row"), step % n_row)
-    col = jnp.bitwise_xor(lax.axis_index("col"), step // n_row)
-    hit = (row * n_col + col)[None, :] == step[:, None]
-    facts = jnp.sum(jnp.where(hit[..., None], facts, 0.0), axis=1)
-    return facts.reshape(n_row, n_col, 128)
+    hit = jnp.bitwise_xor(own, places)[None, :] == jnp.arange(known, dtype=jnp.int32)[:, None]
+    return jnp.sum(jnp.where(hit[..., None], facts, 0.0), axis=1)
 
 
 def per_device(x_blocks, x_cols, out_cols, branch_flag):
@@ -385,20 +419,33 @@
     width = n_col * slots
     shape = (rows, kept, block, dtype)
 
-    part_a, part_b, full, facts = pack(x_blocks, x_cols, branch_flag, row * rows)
-    plane = lax.all_gather(full, "row", axis=0)
+    count = rows * slots
     tuned = n_col == 4 and n_row == 8
     if tuned:
+        part_a, part_b, full, facts = pack(x_blocks, x_cols, branch_flag, row * rows)
+        plane = lax.all_gather(full, "row", axis=0)
+        near, far_one, far_two = [
+            shift(facts, [(i, i ^ step) for i in range(n_col)]) for step in range(1, n_col)
+        ]
+        line_cols = jnp.concatenate([facts, near, far_one, far_two])
+        total = (facts + near) + (far_one + far_two)
+        facts = jnp.where(jnp.arange(128) < count, facts, total)
         line, facts = gather_line((part_a, part_b), facts)
+        trace = jnp.sum(facts[:, count]).reshape(1)
     else:
+        part_a, part_b, full, facts = pack(x_blocks, x_cols, branch_flag, row * rows)
+        plane = lax.all_gather(full, "row", axis=0)
         line = lax.all_gather(full, "col", axis=0)
-        facts = gather_facts(facts)
-    trace = jnp.sum(facts[:, :, rows * slots]).reshape(1)
-    all_cols = facts[:, :, : rows * slots].astype(jnp.int32).reshape(n_row, n_col, rows, slots)
-    all_places = places(all_cols)
-
-    plane_cols = lax.dynamic_index_in_dim(all_cols, col, 1, keepdims=False)
-    plane_places = lax.dynamic_index_in_dim(all_places, col, 1, keepdims=False)
+        every_fact = gather_facts(facts, ("row", "col")).reshape(n_row, n_col, 128)
+        trace = jnp.sum(every_fact[:, :, count]).reshape(1)
+        facts = lax.dynamic_index_in_dim(every_fact, col, 1, keepdims=False)
+        line_cols = lax.dynamic_index_in_dim(every_fact, row, 0, keepdims=False)
+
+    def slots_of(facts):
+        cols = facts[:, :count].astype(jnp.int32).reshape(facts.shape[0], rows, slots)
+        return cols, places(cols)
+
+    plane_cols, plane_places = slots_of(facts)
     targets = out_cols.reshape(rows * kept)
     right_at = plane_places + STRIDE * jnp.arange(n_row, dtype=jnp.int32)[:, None, None]
     hit = plane_cols.reshape(n_blocks, slots)[None] == targets[:, None, None]
@@ -408,24 +455,27 @@
     owns = owns.reshape(rows * kept)
 
     every = jnp.arange(n_blocks, dtype=jnp.int32)
-    line_cols = lax.dynamic_index_in_dim(all_cols, row, 0, keepdims=False)
-    line_places = lax.dynamic_index_in_dim(all_places, row, 0, keepdims=False)
+    line_cols, line_places = slots_of(line_cols)
 
     def straight(entries, wanted):
         at = line_places + STRIDE * entries[:, None, None]
         hit = (line_cols[..., None] == every) & wanted[:, None, None, None]
         return jnp.sum(jnp.where(hit, at[..., None] + 1, 0), axis=(0, 2))
 
-    def turned(entry, device, wanted):
-        cols = lax.dynamic_slice_in_dim(plane_cols, device, 2, 0)
-        at = lax.dynamic_slice_in_dim(plane_places, device, 2, 0)
-        at = at + STRIDE * (entry + jnp.arange(2, dtype=jnp.int32)[:, None, None])
+    def turned(entry, device, size, wanted):
+        cols = lax.dynamic_slice_in_dim(plane_cols, device, size, 0)
+        place = lax.dynamic_slice_in_dim(plane_places, device, size, 0)
+        at = place + STRIDE * (entry + jnp.arange(size, dtype=jnp.int32)[:, None, None])
         own = row * rows + jnp.arange(rows, dtype=jnp.int32)
         hit = (cols[..., None] == own) & wanted
         found = jnp.sum(jnp.where(hit, at[..., None] + 1, 0), axis=2)
-        names = device * rows + jnp.arange(2 * rows, dtype=jnp.int32).reshape(2, rows)
+        names = device * rows + jnp.arange(size * rows, dtype=jnp.int32).reshape(size, rows)
         found = jnp.where(names[:, :, None, None] == every, found[..., None], 0)
-        return jnp.sum(found, axis=(0, 1))
+        marks = jnp.any(hit, axis=3)[..., None] & (
+            place[..., None] == jnp.arange(PACKED, dtype=jnp.int32)
+        )
+        marks = jnp.any(marks, axis=(1, 2)).astype(jnp.int32)
+        return jnp.sum(found, axis=(0, 1)), marks.reshape(size * PACKED)
 
     heights = jnp.arange(n_col, dtype=jnp.int32)
     if not tuned:
@@ -439,44 +489,56 @@
         return purified.reshape(rows, kept, block, block), trace
 
     at_end = (col == 0) | (col == n_col - 1)
-    corner = at_end & (row // 2 == col)
+    pair = row // 2
+    corner = at_end & (pair == col)
     far = at_end & ~corner
-    turn_row = 2 * (n_col - 1 - col)
-    wanted = [at_end | True, at_end, ~at_end, far, corner, turn_row]
+    from_corner = jnp.where(col == 0, pair, 3 - pair)
+    turn_row = jnp.where(col == 0, 4, 0)
+    wanted = [at_end | True, ~far, ~at_end, far, corner, turn_row]
+    wanted += [far & (from_corner == q) for q in (1, 2, 3)]
     wanted = jnp.stack([value.astype(jnp.int32) for value in wanted])
-    always, at_ends, inside, at_far, at_corner, turn_at = range(2, 8)
-
-    second = jnp.where(col < 2, 2, 1)
-    entries = jnp.where(heights == second, 2, 3)
-    entries = jnp.where(heights == jnp.bitwise_xor(col, 1), 1, entries)
-    entries = jnp.where(heights == col, 0, entries)
-    early = straight(entries, (entries < 3) | ~at_end) + turned(4, turn_row, corner)
+    always, not_far, inside, at_far, at_corner, turn_at = range(2, 8)
+    rounds = (8, 9, 10)
+
+    entries = jnp.where(at_end, jnp.array([0, 1, 2, 3]), jnp.array([0, 1, 3, 2]))
+    entries = entries.astype(jnp.int32)
+    early = straight(entries, (entries < 2) | ((entries == 2) & ~corner) | ~at_end)
+    from_plane, marks = turned(4, turn_row, 4, corner)
+    early = early + from_plane
     late = straight(entries, (entries == 3) & far)
     meets = (jnp.repeat(late, kept, axis=0) > 0) & (right_of > 0)
     is_late = jnp.any(meets, axis=1)
 
     arrays = [full]
     loads = [(0, None, 0, 0, PACKED, always)]
-
-    def add(name, entry, wanted):
-        spans = ((0, SPLIT), (SPLIT, PACKED - SPLIT))
+    spans = ((0, SPLIT), (SPLIT, PACKED - SPLIT))
+
+    def add(array, entry, which, wanted):
+        loads.append((len(arrays), None, entry) + spans[which] + (wanted,))
+        arrays.append(array)
+
+    def call(left_of, chosen, before=None):
+        turn = marks if before is None else None
+        table, layout = make_table(
+            left_of, right_of, owns, branch_flag, chosen, width, wanted, turn
+        )
+        turn = (at_corner, turn_at, 4, 4) if before is None else None
+        n_entries = 8 if before is None else 4
+        return multiply(
+            plane, list(arrays), tuple(loads), n_entries, layout, table, shape, turn, before
+        )
+
+    add(line["first"][0], 1, 0, always)
+    add(line["first"][1], 1, 1, not_far)
+    for array, flag in zip(line["round"], rounds):
+        add(array, 1, 1, flag)
+    for name, entry, flag in (("middle", 2, inside), ("end_two", 2, at_far), ("middle_two", 3, inside)):
         for which in range(2):
-            loads.append((len(arrays), None, entry) + spans[which] + (wanted,))
-            arrays.append(line[name][which])
-
-    def call(left_of, chosen, before=None):
-        table, layout = make_table(left_of, right_of, owns, branch_flag, chosen, width, wanted)
-        turn = (at_corner, turn_at, 4) if before is None else None
-        return multiply(
-            plane, list(arrays), tuple(loads), 6, layout, table, shape, turn, before
-        )
-
-    add("first", 1, always)
-    add("middle", 2, inside)
-    add("end_two", 2, at_ends)
-    add("middle_two", 3, inside)
+            add(line[name][which], entry, which, flag)
     purified = call(early, ~is_late)
-    add("end_three", 3, at_far)
+    for which in range(2):
+        add(line["end_three"][which], 3, which, at_far)
+    purified, trace = lax.optimization_barrier((purified, trace))
     purified = call(early + late, is_late, purified)
     return purified.reshape(rows, kept, block, block), trace
 

time: 155 us -> 229 us (1.48)
  the two profiles are of different devices: /device:TPU:6 before, /device:TPU:0 now
where the time goes in v11:
time: 229 us; the launch traced here: 228 us
  waiting for transfers between devices  89.1 us (39%)
  starting transfers between devices  53.8 us (23%)
  Pallas kernels  26.1 us (11%)
  other arithmetic  26 us (11%)
  local copies, waits for them, and re-layouts  18.6 us (8%)
  between operations  14.5 us (6%)
    ppermute x16, waiting for transfers between devices, send(): return lax.ppermute(array, ('row', 'col'), sorted(set(pairs)))  74 us
    ppermute x16, starting transfers between devices, send(): return lax.ppermute(array, ('row', 'col'), sorted(set(pairs)))  47.5 us
    pallas_call x2, Pallas kernels, multiply(): pl.pallas_call(functools.partial(multiply_kernel, loads, kept, layout, tu...  22 us
    ppermute x3, waiting for transfers between devices, gather_facts(): other = lax.ppermute(facts, axis, [(i, i ^ mask) for i in range(size)])  15.1 us
    ppermute x3, starting transfers between devices, shift(): return lax.ppermute(array, 'col', pairs)  5.85 us
    concatenate x2, local copies, waits for them, and re-layouts, make_table(): return (jnp.concatenate(list(lists.values())), layout)  5.32 us
  transfers between devices with their start and end apart: 23, of which 6 were waited for; matrix products, arithmetic and copies ran while one was open for 19% of the time, Pallas kernels for 9%

profile of v11, /device:TPU:0, one launch (start us, length us, event | category | flops | bytes accessed | tf_op | source)
XLA Modules:
  0.0 228.1 jit_solution(16164406185246512335)
XLA Ops:
  7.2 4.1 %shard_map.77 = (bf16[1792,256]{1,0:T(8,128)(2,1)}, bf16[1536,256]{1,0:T(8,128)(2,1)}, bf16[3328,256]{1,0:T(8,128)(2,1)}, f32[1,128]{1,0:T(1,128)}) custom-call(s32[2,8]{1,0:T(2,128)} %bitcast.40, s32[8]{0:T(128)} %flag_ref.1, s32[1]{0:T(128)} %bitcast.1.first_ref, bf16[16,256,256]{2,1,0:T(8,128)(2,1)} %bitcast.30), custom_call_target="tpu_custom_call" | custom-call | tf_op jit(solution)/shard_map/pallas_call | solution.py:83
  11.3 5.2 %collective-permute-start.2 = (f32[1,128]{1,0:T(1,128)}, f32[1,128]{1,0:T(1,128)S(1)}, u32[]{:S(2)}, u32[]{:S(2)}) collective-permute-start(f32[1,128]{1,0:T(1,128)} %get-tuple-element.18), channel_id=1, source_target_pairs={{0,3},{1,2},{2,1},{3,0},{4,7},{5,6},{6,5},{7,4},{8,11},{9,10},{10,... | collective-permute-start | bytes 1544 | tf_op jit(solution)/shard_map/ppermute | solution.py:285
  18.5 1.3 collective-permute-start.13
  26.4 11.0 %collective-permute-start.3 = (bf16[1792,256]{1,0:T(8,128)(2,1)}, bf16[1792,256]{1,0:T(8,128)(2,1)S(1)}, u32[]{:S(2)}, u32[]{:S(2)}) collective-permute-start(bf16[1792,256]{1,0:T(8,128)(2,1)} %get-tuple-element.19), channel_id=1, source_target_pairs={{0,1},{1,0},{2,3},{3,2},{4,5},{5,4},{6,7},{7,6},{8,9},{9,8},{10,11... | collective-permute-start | bytes 2752520 | tf_op jit(solution)/shard_map/ppermute | solution.py:294
  40.7 3.1 %collective-permute-done.6 = f32[2,128]{1,0:T(2,128)S(1)} collective-permute-done((f32[2,128]{1,0:T(2,128)S(1)}, f32[2,128]{1,0:T(2,128)S(1)}, u32[]{:S(2)}, u32[]{:S(2)}) %collective-permute-start.6) | collective-permute-done | bytes 1056 | tf_op jit(solution)/shard_map/ppermute | solution.py:401
  44.5 11.0 %collective-permute-done.7 = f32[4,128]{1,0:T(4,128)S(1)} collective-permute-done((f32[4,128]{1,0:T(4,128)S(1)}, f32[4,128]{1,0:T(4,128)S(1)}, u32[]{:S(2)}, u32[]{:S(2)}) %collective-permute-start.7) | collective-permute-done | bytes 2080 | tf_op jit(solution)/shard_map/ppermute | solution.py:401
  59.3 18.6 %collective-permute-start.8 = (bf16[1536,256]{1,0:T(8,128)(2,1)}, bf16[1536,256]{1,0:T(8,128)(2,1)}, u32[]{:S(2)}, u32[]{:S(2)}) collective-permute-start(bf16[1536,256]{1,0:T(8,128)(2,1)} %get-tuple-element.24), channel_id=1, source_target_pairs={{0,1},{1,0},{3,2},{4,5},{5,4},{7,6},{8,9},{11,10},{12,13},{15,14},... | collective-permute-start | bytes 2359304 | tf_op jit(solution)/shard_map/ppermute | solution.py:294
  88.1 1.4 copy.55
  97.9 1.3 convert_reduce_fusion.4
  100.5 1.5 collective-permute-start.19
  102.9 64.3 %collective-permute-done.9 = bf16[1536,256]{1,0:T(8,128)(2,1)} collective-permute-done((bf16[1536,256]{1,0:T(8,128)(2,1)}, bf16[1536,256]{1,0:T(8,128)(2,1)}, u32[]{:S(2)}, u32[]{:S(2)}) %collective-permute-start.9) | collective-permute-done | bytes 786464 | tf_op jit(solution)/shard_map/ppermute | solution.py:294
  167.3 2.2 collective-permute-start.12
  169.5 2.3 collective-permute-start.14
  171.7 2.2 collective-permute-start.16
  173.9 1.6 collective-permute-start.21
  176.2 2.8 %select_reduce_fusion.3 = (s32[32,8]{1,0:T(8,128)S(1)}, s32[32,8]{1,0:T(8,128)S(1)}, s32[32,8]{1,0:T(8,128)S(1)}, s32[32,8]{1,0:T(8,128)}) fusion(s32[32,64]{1,0:T(8,128)S(1)} %broadcast_select_fusion, s32[32,64]{1,0:T(8,128)S(1)} %broadcast_add_fusion, s32[32,64]{1,0:T(8,128)S(1)} %get-tuple-element.65, s32[32,64]{1,0:T(8,128)S(1)} %bitcast.31, ...), kind=kLoop, calls=%fused_computation.3 | loop fusion | flops 162816 | bytes 45056 | tf_op jit(solution)/shard_map/reduce_sum | solution.py:355
  180.3 2.7 %concatenate.26.table = s32[331]{0:T(512)} concatenate(s32[1]{0:T(128)} %bitcast.6, s32[1]{0:T(128)} %bitcast.10, s32[1]{0:T(128)} %constant.32.clone.1, s32[1]{0:T(128)} %bitcast.11, s32[1]{0:T(128)} %bitcast.12, s32[1]{0:T(128)} %bitcast.13, s32[1]{0:T(128)} %bitcast.14, s32[1]{0:T(128)} %bitcast.15, s32[1]{0:T(128)} %bitcast.16, s32[1]{0:T(128)} %bitcast.17, s32[1]{0:T(128)} %bitcast.18, ...), dimensions={0} | concatenate | bytes 2648 | tf_op jit(solution)/shard_map/concatenate | solution.py:384
  183.1 1.5 select_reduce_fusion.18
  185.2 1.5 select_reduce_fusion.2
  186.7 2.6 %concatenate.27.table = s32[383]{0:T(512)} concatenate(s32[1]{0:T(128)} %bitcast.21, s32[1]{0:T(128)} %bitcast.23, s32[1]{0:T(128)} %constant.32.clone.1, s32[1]{0:T(128)} %bitcast.11, s32[1]{0:T(128)} %bitcast.12, s32[1]{0:T(128)} %bitcast.13, s32[1]{0:T(128)} %bitcast.14, s32[1]{0:T(128)} %bitcast.15, s32[1]{0:T(128)} %bitcast.16, s32[1]{0:T(128)} %bitcast.17, s32[1]{0:T(128)} %bitcast.18, ...), dimensions={0} | concatenate | bytes 3064 | tf_op jit(solution)/shard_map/concatenate | solution.py:384
  189.3 1.4 slice_reduce_fusion
  190.7 8.5 %collective-permute-done.16.refs_5_ = bf16[1536,256]{1,0:T(8,128)(2,1)} collective-permute-done((bf16[1536,256]{1,0:T(8,128)(2,1)}, bf16[1536,256]{1,0:T(8,128)(2,1)}, u32[]{:S(2)}, u32[]{:S(2)}) %collective-permute-start.16) | collective-permute-done | bytes 786464 | tf_op jit(solution)/shard_map/ppermute | solution.py:294
  199.2 20.6 %shard_map.78.refs_14_ = bf16[32,256,256]{2,1,0:T(8,128)(2,1)} custom-call(s32[383]{0:T(512)} %concatenate.27.table, bf16[8,3328,256]{2,1,0:T(8,128)(2,1)} %bitcast.27, bf16[3328,256]{1,0:T(8,128)(2,1)} %get-tuple-element.22.refs_0_, bf16[1792,256]{1,0:T(8,128)(2,1)} %copy-done.1, bf16[1536,256]{1,0:T(8,128)(2,1)} %collective-permute-done.8.refs_2_, ...), custom_call_target="tpu_custom_call" | custom-call | tf_op jit(solution)/shard_map/pallas_call | solution.py:264
  219.8 1.4 shard_map.79
  (138 shorter events, 39.6 us)
Async XLA Ops:
  7.2 192.0 %all-gather.3.cloned.1.call-start = ((), (), s32[]{:S(2)}) async-start(), calls=%async_computation | async-start | bytes 15335424 | tf_op jit(solution)/shard_map/all_gather | solution.py:426
  11.3 14.4 %collective-permute-start.2 = (f32[1,128]{1,0:T(1,128)}, f32[1,128]{1,0:T(1,128)S(1)}, u32[]{:S(2)}, u32[]{:S(2)}) collective-permute-start(f32[1,128]{1,0:T(1,128)} %get-tuple-element.18), channel_id=1, source_target_pairs={{0,3},{1,2},{2,1},{3,0},{4,7},{5,6},{6,5},{7,4},{8,11},{9,10},{10,... | collective-permute-start | bytes 1544 | tf_op jit(solution)/shard_map/ppermute | solution.py:285
  16.5 9.9 %collective-permute-start.1 = (f32[1,128]{1,0:T(1,128)}, f32[1,128]{1,0:T(1,128)S(1)}, u32[]{:S(2)}, u32[]{:S(2)}) collective-permute-start(f32[1,128]{1,0:T(1,128)} %get-tuple-element.18), channel_id=1, source_target_pairs={{0,2},{1,3},{2,0},{3,1},{4,6},{5,7},{6,4},{7,5},{8,10},{9,11},{10,... | collective-permute-start | bytes 1544 | tf_op jit(solution)/shard_map/ppermute | solution.py:285
  16.5 20.9 %collective-permute-start = (f32[1,128]{1,0:T(1,128)}, f32[1,128]{1,0:T(1,128)S(1)}, u32[]{:S(2)}, u32[]{:S(2)}) collective-permute-start(f32[1,128]{1,0:T(1,128)} %get-tuple-element.18), channel_id=1, source_target_pairs={{0,1},{1,0},{2,3},{3,2},{4,5},{5,4},{6,7},{7,6},{8,9},{9,8},{10,11... | collective-permute-start | bytes 1544 | tf_op jit(solution)/shard_map/ppermute | solution.py:285
  17.2 85.7 %collective-permute-start.15 = (bf16[1536,256]{1,0:T(8,128)(2,1)}, bf16[1536,256]{1,0:T(8,128)(2,1)}, u32[]{:S(2)}, u32[]{:S(2)}) collective-permute-start(bf16[1536,256]{1,0:T(8,128)(2,1)} %get-tuple-element.24), channel_id=1, source_target_pairs={{2,27},{6,31},{25,0},{29,4}} | collective-permute-start | bytes 2359304 | tf_op jit(solution)/shard_map/ppermute | solution.py:294
  18.5 84.4 %collective-permute-start.13 = (bf16[1536,256]{1,0:T(8,128)(2,1)}, bf16[1536,256]{1,0:T(8,128)(2,1)}, u32[]{:S(2)}, u32[]{:S(2)}) collective-permute-start(bf16[1536,256]{1,0:T(8,128)(2,1)} %get-tuple-element.24), channel_id=1, source_target_pairs={{10,27},{14,31},{17,0},{21,4}} | collective-permute-start | bytes 2359304 | tf_op jit(solution)/shard_map/ppermute | solution.py:294
  25.7 29.9 %collective-permute-start.4 = (bf16[1792,256]{1,0:T(8,128)(2,1)}, bf16[1792,256]{1,0:T(8,128)(2,1)S(1)}, u32[]{:S(2)}, u32[]{:S(2)}) collective-permute-start(bf16[1792,256]{1,0:T(8,128)(2,1)} %get-tuple-element.19), channel_id=1, source_target_pairs={{1,2},{2,1},{5,6},{6,5},{9,10},{10,9},{13,14},{14,13},{17,18},{18,... | collective-permute-start | bytes 2752520 | tf_op jit(solution)/shard_map/ppermute | solution.py:294
  26.4 30.3 %collective-permute-start.3 = (bf16[1792,256]{1,0:T(8,128)(2,1)}, bf16[1792,256]{1,0:T(8,128)(2,1)S(1)}, u32[]{:S(2)}, u32[]{:S(2)}) collective-permute-start(bf16[1792,256]{1,0:T(8,128)(2,1)} %get-tuple-element.19), channel_id=1, source_target_pairs={{0,1},{1,0},{2,3},{3,2},{4,5},{5,4},{6,7},{7,6},{8,9},{9,8},{10,11... | collective-permute-start | bytes 2752520 | tf_op jit(solution)/shard_map/ppermute | solution.py:294
  39.0 1.1 collective-permute-start.5
  40.2 3.6 %collective-permute-start.6 = (f32[2,128]{1,0:T(2,128)S(1)}, f32[2,128]{1,0:T(2,128)S(1)}, u32[]{:S(2)}, u32[]{:S(2)}) collective-permute-start(f32[2,128]{1,0:T(2,128)S(1)} %pad_maximum_fusion.3), channel_id=1, source_target_pairs={{0,8},{4,12},{8,0},{12,4},{16,24},{20,28},{24,16},{28,20},{1,9},{5... | collective-permute-start | bytes 3080 | tf_op jit(solution)/shard_map/ppermute | solution.py:401
  43.7 11.7 %collective-permute-start.7 = (f32[4,128]{1,0:T(4,128)S(1)}, f32[4,128]{1,0:T(4,128)S(1)}, u32[]{:S(2)}, u32[]{:S(2)}) collective-permute-start(f32[4,128]{1,0:T(4,128)S(1)} %pad_maximum_fusion.2), channel_id=1, source_target_pairs={{0,16},{4,20},{8,24},{12,28},{16,0},{20,4},{24,8},{28,12},{1,17},{... | collective-permute-start | bytes 6152 | tf_op jit(solution)/shard_map/ppermute | solution.py:401
  55.6 143.5 %copy-start = (bf16[1792,256]{1,0:T(8,128)(2,1)}, bf16[1792,256]{1,0:T(8,128)(2,1)S(1)}, u32[]{:S(2)}) copy-start(bf16[1792,256]{1,0:T(8,128)(2,1)S(1)} %collective-permute-done.4.refs_6_) | copy-start | bytes 2752516
  58.6 33.9 %collective-permute-start.10 = (bf16[1536,256]{1,0:T(8,128)(2,1)}, bf16[1536,256]{1,0:T(8,128)(2,1)S(1)}, u32[]{:S(2)}, u32[]{:S(2)}) collective-permute-start(bf16[1536,256]{1,0:T(8,128)(2,1)} %get-tuple-element.24), channel_id=1, source_target_pairs={{1,2},{2,1},{5,6},{6,5},{9,10},{10,9},{13,14},{14,13},{17,18},{18,... | collective-permute-start | bytes 2359304 | tf_op jit(solution)/shard_map/ppermute | solution.py:294
  59.3 39.9 %collective-permute-start.8 = (bf16[1536,256]{1,0:T(8,128)(2,1)}, bf16[1536,256]{1,0:T(8,128)(2,1)}, u32[]{:S(2)}, u32[]{:S(2)}) collective-permute-start(bf16[1536,256]{1,0:T(8,128)(2,1)} %get-tuple-element.24), channel_id=1, source_target_pairs={{0,1},{1,0},{3,2},{4,5},{5,4},{7,6},{8,9},{11,10},{12,13},{15,14},... | collective-permute-start | bytes 2359304 | tf_op jit(solution)/shard_map/ppermute | solution.py:294
  79.3 13.2 %collective-permute-start.17 = (bf16[1792,256]{1,0:T(8,128)(2,1)S(1)}, bf16[1792,256]{1,0:T(8,128)(2,1)S(1)}, u32[]{:S(2)}, u32[]{:S(2)}) collective-permute-start(bf16[1792,256]{1,0:T(8,128)(2,1)S(1)} %collective-permute-done.4.refs_6_), channel_id=1, source_target_pairs={{2,3},{6,7},{9,8},{10,11},{13,12},{14,15},{17,16},{18,19},{21,20},... | collective-permute-start | bytes 2752520 | tf_op jit(solution)/shard_map/ppermute | solution.py:294
  92.5 3.7 %collective-permute-start.18 = (bf16[1792,256]{1,0:T(8,128)(2,1)S(1)}, bf16[1792,256]{1,0:T(8,128)(2,1)S(1)}, u32[]{:S(2)}, u32[]{:S(2)}) collective-permute-start(bf16[1792,256]{1,0:T(8,128)(2,1)S(1)} %collective-permute-done.3.refs_1_), channel_id=1, source_target_pairs={{1,2},{2,1},{5,6},{6,5},{9,10},{10,9},{13,14},{14,13},{17,18},{18,... | collective-permute-start | bytes 2752520 | tf_op jit(solution)/shard_map/ppermute | solution.py:294
  94.7 5.8 %collective-permute-start.11 = (bf16[1536,256]{1,0:T(8,128)(2,1)S(1)}, bf16[1536,256]{1,0:T(8,128)(2,1)S(1)}, u32[]{:S(2)}, u32[]{:S(2)}) collective-permute-start(bf16[1536,256]{1,0:T(8,128)(2,1)S(1)} %collective-permute-done.10.refs_7_), channel_id=1, source_target_pairs={{2,3},{6,7},{9,8},{10,11},{13,12},{14,15},{17,16},{18,19},{21,20},... | collective-permute-start | bytes 2359304 | tf_op jit(solution)/shard_map/ppermute | solution.py:294
  97.2 76.7 %collective-permute-start.20 = (bf16[1792,256]{1,0:T(8,128)(2,1)S(1)}, bf16[1792,256]{1,0:T(8,128)(2,1)S(1)}, u32[]{:S(2)}, u32[]{:S(2)}) collective-permute-start(bf16[1792,256]{1,0:T(8,128)(2,1)S(1)} %collective-permute-done.18.refs_10_), channel_id=1, source_target_pairs={{2,3},{6,7},{9,8},{10,11},{13,12},{14,15},{17,16},{18,19},{21,20},... | collective-permute-start | bytes 2752520 | tf_op jit(solution)/shard_map/ppermute | solution.py:294
  99.2 68.0 %collective-permute-start.9 = (bf16[1536,256]{1,0:T(8,128)(2,1)}, bf16[1536,256]{1,0:T(8,128)(2,1)}, u32[]{:S(2)}, u32[]{:S(2)}) collective-permute-start(bf16[1536,256]{1,0:T(8,128)(2,1)} %get-tuple-element.24), channel_id=1, source_target_pairs={{9,0},{13,4},{18,27},{22,31}} | collective-permute-start | bytes 2359304 | tf_op jit(solution)/shard_map/ppermute | solution.py:294
  100.5 73.4 %collective-permute-start.19 = (bf16[1536,256]{1,0:T(8,128)(2,1)}, bf16[1536,256]{1,0:T(8,128)(2,1)}, u32[]{:S(2)}, u32[]{:S(2)}) collective-permute-start(bf16[1536,256]{1,0:T(8,128)(2,1)} %collective-permute-done.8.refs_2_), channel_id=1, source_target_pairs={{1,2},{2,1},{5,6},{6,5},{9,10},{10,9},{13,14},{14,13},{17,18},{18,... | collective-permute-start | bytes 2359304 | tf_op jit(solution)/shard_map/ppermute | solution.py:294
  167.3 23.4 %collective-permute-start.12 = (bf16[1536,256]{1,0:T(8,128)(2,1)}, bf16[1536,256]{1,0:T(8,128)(2,1)}, u32[]{:S(2)}, u32[]{:S(2)}) collective-permute-start(bf16[1536,256]{1,0:T(8,128)(2,1)} %collective-permute-done.9), channel_id=1, source_target_pairs={{0,8},{4,12},{27,19},{31,23}} | collective-permute-start | bytes 2359304 | tf_op jit(solution)/shard_map/ppermute | solution.py:294
  169.5 21.2 %collective-permute-start.14 = (bf16[1536,256]{1,0:T(8,128)(2,1)}, bf16[1536,256]{1,0:T(8,128)(2,1)}, u32[]{:S(2)}, u32[]{:S(2)}) collective-permute-start(bf16[1536,256]{1,0:T(8,128)(2,1)} %collective-permute-done.13), channel_id=1, source_target_pairs={{0,16},{4,20},{27,11},{31,15}} | collective-permute-start | bytes 2359304 | tf_op jit(solution)/shard_map/ppermute | solution.py:294
  171.7 27.4 %collective-permute-start.16 = (bf16[1536,256]{1,0:T(8,128)(2,1)}, bf16[1536,256]{1,0:T(8,128)(2,1)}, u32[]{:S(2)}, u32[]{:S(2)}) collective-permute-start(bf16[1536,256]{1,0:T(8,128)(2,1)} %collective-permute-done.15), channel_id=1, source_target_pairs={{0,24},{4,28},{27,3},{31,7}} | collective-permute-start | bytes 2359304 | tf_op jit(solution)/shard_map/ppermute | solution.py:294
  173.9 45.8 %collective-permute-start.21 = (bf16[1536,256]{1,0:T(8,128)(2,1)}, bf16[1536,256]{1,0:T(8,128)(2,1)}, u32[]{:S(2)}, u32[]{:S(2)}) collective-permute-start(bf16[1536,256]{1,0:T(8,128)(2,1)} %collective-permute-done.19.refs_11_), channel_id=1, source_target_pairs={{2,3},{6,7},{9,8},{10,11},{13,12},{14,15},{17,16},{18,19},{21,20},... | collective-permute-start | bytes 2359304 | tf_op jit(solution)/shard_map/ppermute | solution.py:294
  (7 other events, 433.2 us)
Sparse Core Ops, SparseCore 0:
  11.4 111.2 all-gather.2

commit v12 on v11

--- a/solution.py
+++ b/solution.py
@@ -285,48 +285,24 @@
     return lax.ppermute(array, "col", pairs)
 
 
-def send(array, moves):
+def gather_line(parts, facts):
+    first = [shift(part, [(0, 1), (1, 0), (2, 3), (3, 2)]) for part in parts]
+    middle = [shift(part, [(1, 2), (2, 1)]) for part in parts]
+    facts = gather_facts(facts, ("row",))
+    first[0], middle[0], facts = lax.optimization_barrier((first[0], middle[0], facts))
+    end_two = [shift(part, [(1, 0), (2, 3)]) for part in middle]
+    middle_two = [shift(part, [(1, 2), (2, 1)]) for part in first]
     pairs = []
-    for (q, c), (q_to, c_to) in list(moves):
-        for core in range(2):
-            pairs.append((4 * (2 * q + core) + c, 4 * (2 * q_to + core) + c_to))
-            pairs.append((4 * (7 - 2 * q - core) + 3 - c, 4 * (7 - 2 * q_to - core) + 3 - c_to))
-    return lax.ppermute(array, ("row", "col"), sorted(set(pairs)))
-
-
-def after(array, *others):
-    return lax.optimization_barrier((array, *others))[0]
-
-
-def gather_line(parts, facts):
-    part_a, part_b = parts
-    lines = range(4)
-    down = [((q, 3), (q, 2)) for q in lines]
-    inner = [((q, 2), (q, 1)) for q in lines]
-    ends = [((q, 1), (q, 0)) for q in lines]
-    first_a = send(part_a, down + ends)
-    middle_a = send(part_a, inner)
-    over = [send(part_b, [((q, 1), (0, 0))]) for q in (1, 2, 3)]
-    facts = gather_facts(facts, ("row",))
-    first_a, middle_a, part_b, facts = lax.optimization_barrier(
-        (first_a, middle_a, part_b, facts)
-    )
-    middle_b = send(part_b, inner)
-    first_b = send(part_b, down + ends[:1])
-    end_two_a = send(middle_a, ends[1:])
-    middle_two_a = send(after(first_a, middle_b, end_two_a), inner)
-    end_two_b = send(middle_b, ends[1:])
-    middle_two_b = send(after(first_b, middle_two_a, end_two_b), inner)
-    end_three_a = send(middle_two_a, ends[1:])
-    end_three_b = send(after(middle_two_b, end_three_a), ends[1:])
-    over = [after(array, end_two_b) for array in over]
+    for row in range(lax.axis_size("row")):
+        pairs += [(4 * row + 1, 4 * row)] * (row // 2 != 0)
+        pairs += [(4 * row + 2, 4 * row + 3)] * (row // 2 != 3)
+    end_three = [lax.ppermute(part, ("row", "col"), pairs) for part in middle_two]
     line = {
-        "first": (first_a, first_b),
-        "middle": (middle_a, middle_b),
-        "end_two": (end_two_a, end_two_b),
-        "middle_two": (middle_two_a, middle_two_b),
-        "end_three": (end_three_a, end_three_b),
-        "round": [send(over[q - 1], [((0, 0), (q, 0))]) for q in (1, 2, 3)],
+        "first": first,
+        "middle": middle,
+        "end_two": end_two,
+        "middle_two": middle_two,
+        "end_three": end_three,
     }
     return line, facts
 
@@ -489,22 +465,17 @@
         return purified.reshape(rows, kept, block, block), trace
 
     at_end = (col == 0) | (col == n_col - 1)
-    pair = row // 2
-    corner = at_end & (pair == col)
+    corner = at_end & (row // 2 == col)
     far = at_end & ~corner
-    from_corner = jnp.where(col == 0, pair, 3 - pair)
-    turn_row = jnp.where(col == 0, 4, 0)
-    wanted = [at_end | True, ~far, ~at_end, far, corner, turn_row]
-    wanted += [far & (from_corner == q) for q in (1, 2, 3)]
+    turn_row = 2 * (n_col - 1 - col)
+    wanted = [at_end | True, at_end, ~at_end, far, corner, turn_row]
     wanted = jnp.stack([value.astype(jnp.int32) for value in wanted])
-    always, not_far, inside, at_far, at_corner, turn_at = range(2, 8)
-    rounds = (8, 9, 10)
+    always, at_ends, inside, at_far, at_corner, turn_at = range(2, 8)
 
     entries = jnp.where(at_end, jnp.array([0, 1, 2, 3]), jnp.array([0, 1, 3, 2]))
     entries = entries.astype(jnp.int32)
-    early = straight(entries, (entries < 2) | ((entries == 2) & ~corner) | ~at_end)
-    from_plane, marks = turned(4, turn_row, 4, corner)
-    early = early + from_plane
+    from_plane, marks = turned(4, turn_row, 2, corner)
+    early = straight(entries, (entries < 3) | ~at_end) + from_plane
     late = straight(entries, (entries == 3) & far)
     meets = (jnp.repeat(late, kept, axis=0) > 0) & (right_of > 0)
     is_late = jnp.any(meets, axis=1)
@@ -522,17 +493,19 @@
         table, layout = make_table(
             left_of, right_of, owns, branch_flag, chosen, width, wanted, turn
         )
-        turn = (at_corner, turn_at, 4, 4) if before is None else None
-        n_entries = 8 if before is None else 4
+        turn = (at_corner, turn_at, 4, 2) if before is None else None
+        n_entries = 6 if before is None else 4
         return multiply(
             plane, list(arrays), tuple(loads), n_entries, layout, table, shape, turn, before
         )
 
-    add(line["first"][0], 1, 0, always)
-    add(line["first"][1], 1, 1, not_far)
-    for array, flag in zip(line["round"], rounds):
-        add(array, 1, 1, flag)
-    for name, entry, flag in (("middle", 2, inside), ("end_two", 2, at_far), ("middle_two", 3, inside)):
+    stages = (
+        ("first", 1, always),
+        ("middle", 2, inside),
+        ("end_two", 2, at_ends),
+        ("middle_two", 3, inside),
+    )
+    for name, entry, flag in stages:
         for which in range(2):
             add(line[name][which], entry, which, flag)
     purified = call(early, ~is_late)

time: 229 us -> 146 us (0.64)
  the two profiles are of different devices: /device:TPU:0 before, /device:TPU:4 now
where the time goes in v12:
time: 146 us; the launch traced here: 145 us
  waiting for transfers between devices  56.9 us (39%)
  starting transfers between devices  22.3 us (15%)
  other arithmetic  22.1 us (15%)
  Pallas kernels  19.3 us (13%)
  between operations  14.4 us (10%)
  local copies, waits for them, and re-layouts  10.3 us (7%)
    ppermute x2, waiting for transfers between devices, gather_line(): lax.ppermute(part, ('row', 'col'), pairs)  29.4 us
    ppermute x11, waiting for transfers between devices, shift(): return lax.ppermute(array, 'col', pairs)  21.1 us
    ppermute x11, starting transfers between devices, shift(): return lax.ppermute(array, 'col', pairs)  18.2 us
    pallas_call x2, Pallas kernels, multiply(): pl.pallas_call(functools.partial(multiply_kernel, loads, kept, layout, tu...  15.1 us
    ppermute x3, waiting for transfers between devices, gather_facts(): other = lax.ppermute(facts, axis, [(i, i ^ mask) for i in range(size)])  6.45 us
    concatenate x2, local copies, waits for them, and re-layouts, make_table(): return (jnp.concatenate(list(lists.values())), layout)  5.29 us
    pallas_call x1, Pallas kernels, pack(): pl.pallas_call(pack_kernel, out_shape=packed + [jax.ShapeDtypeStruct((1,...  4.25 us
    reduce_sum x1, other arithmetic, make_table(): rights = jnp.sum(jnp.where(pick, right_of[:, None, :] - 1, 0), axis=2)  3.59 us
  transfers between devices with their start and end apart: 17, of which 6 were waited for; matrix products, arithmetic and copies ran while one was open for 22% of the time, Pallas kernels for 6%

profile of v12, /device:TPU:4, one launch (start us, length us, event | category | flops | bytes accessed | tf_op | source)
XLA Modules:
  0.0 145.4 jit_solution(15024900449864045794)
XLA Ops:
  7.2 4.3 %shard_map.77 = (bf16[1792,256]{1,0:T(8,128)(2,1)}, bf16[1536,256]{1,0:T(8,128)(2,1)}, bf16[3328,256]{1,0:T(8,128)(2,1)}, f32[1,128]{1,0:T(1,128)}) custom-call(s32[2,8]{1,0:T(2,128)} %bitcast.37, s32[8]{0:T(128)} %flag_ref.1, s32[1]{0:T(128)} %bitcast.1.first_ref, bf16[16,256,256]{2,1,0:T(8,128)(2,1)} %bitcast.27), custom_call_target="tpu_custom_call" | custom-call | tf_op jit(solution)/shard_map/pallas_call | solution.py:83
  11.5 3.8 %collective-permute-start.2 = (f32[1,128]{1,0:T(1,128)}, f32[1,128]{1,0:T(1,128)S(1)}, u32[]{:S(2)}, u32[]{:S(2)}) collective-permute-start(f32[1,128]{1,0:T(1,128)} %get-tuple-element.11), channel_id=1, source_target_pairs={{0,3},{1,2},{2,1},{3,0},{4,7},{5,6},{6,5},{7,4},{8,11},{9,10},{10,... | collective-permute-start | bytes 1544 | tf_op jit(solution)/shard_map/ppermute | solution.py:285
  16.7 4.1 %collective-permute-start.8 = (bf16[1536,256]{1,0:T(8,128)(2,1)}, bf16[1536,256]{1,0:T(8,128)(2,1)}, u32[]{:S(2)}, u32[]{:S(2)}) collective-permute-start(bf16[1536,256]{1,0:T(8,128)(2,1)} %get-tuple-element.16), channel_id=1, source_target_pairs={{0,1},{1,0},{2,3},{3,2},{4,5},{5,4},{6,7},{7,6},{8,9},{9,8},{10,11... | collective-permute-start | bytes 2359304 | tf_op jit(solution)/shard_map/ppermute | solution.py:285
  25.2 3.4 %collective-permute-start.3 = (bf16[1792,256]{1,0:T(8,128)(2,1)}, bf16[1792,256]{1,0:T(8,128)(2,1)S(1)}, u32[]{:S(2)}, u32[]{:S(2)}) collective-permute-start(bf16[1792,256]{1,0:T(8,128)(2,1)} %get-tuple-element.12), channel_id=1, source_target_pairs={{0,1},{1,0},{2,3},{3,2},{4,5},{5,4},{6,7},{7,6},{8,9},{9,8},{10,11... | collective-permute-start | bytes 2752520 | tf_op jit(solution)/shard_map/ppermute | solution.py:285
  31.3 1.3 collective-permute-start.6
  32.8 2.1 %collective-permute-done.6 = f32[2,128]{1,0:T(2,128)S(1)} collective-permute-done((f32[2,128]{1,0:T(2,128)S(1)}, f32[2,128]{1,0:T(2,128)S(1)}, u32[]{:S(2)}, u32[]{:S(2)}) %collective-permute-start.6) | collective-permute-done | bytes 1056 | tf_op jit(solution)/shard_map/ppermute | solution.py:377
  35.2 3.3 %collective-permute-done.7 = f32[4,128]{1,0:T(4,128)S(1)} collective-permute-done((f32[4,128]{1,0:T(4,128)S(1)}, f32[4,128]{1,0:T(4,128)S(1)}, u32[]{:S(2)}, u32[]{:S(2)}) %collective-permute-start.7) | collective-permute-done | bytes 2080 | tf_op jit(solution)/shard_map/ppermute | solution.py:377
  38.7 1.3 collective-permute-start.11
  40.0 1.6 %collective-permute-start.13 = (bf16[1536,256]{1,0:T(8,128)(2,1)}, bf16[1536,256]{1,0:T(8,128)(2,1)}, u32[]{:S(2)}, u32[]{:S(2)}) collective-permute-start(bf16[1536,256]{1,0:T(8,128)(2,1)} %collective-permute-done.8.refs_2_), channel_id=1, source_target_pairs={{1,2},{2,1},{5,6},{6,5},{9,10},{10,9},{13,14},{14,13},{17,18},{18,... | collective-permute-start | bytes 2359304 | tf_op jit(solution)/shard_map/ppermute | solution.py:285
  41.6 17.5 %collective-permute-done.3.refs_1_ = bf16[1792,256]{1,0:T(8,128)(2,1)S(1)} collective-permute-done((bf16[1792,256]{1,0:T(8,128)(2,1)}, bf16[1792,256]{1,0:T(8,128)(2,1)S(1)}, u32[]{:S(2)}, u32[]{:S(2)}) %collective-permute-start.3) | collective-permute-done | bytes 917536 | tf_op jit(solution)/shard_map/ppermute | solution.py:285
  62.5 1.3 collective-permute-start.10
  70.7 1.3 collective-permute-start.14
  72.7 1.3 collective-permute-start.15
  74.7 3.6 %select_reduce_fusion.3 = (s32[32,8]{1,0:T(8,128)S(1)}, s32[32,8]{1,0:T(8,128)S(1)}, s32[32,8]{1,0:T(8,128)S(1)}, s32[32,8]{1,0:T(8,128)}) fusion(s32[32,64]{1,0:T(8,128)} %broadcast_select_fusion, s32[32,64]{1,0:T(8,128)} %broadcast_add_fusion, s32[32,64]{1,0:T(8,128)} %get-tuple-element.51, s32[32,64]{1,0:T(8,128)S(1)} %bitcast.28, s32[32,64]{1,0:T(8,128)S(1)} %bitcast.29), kind=kLoop, calls=%fused_computation.3 | loop fusion | flops 162816 | bytes 45056 | tf_op jit(solution)/shard_map/reduce_sum | solution.py:331
  78.3 1.5 %select_reduce_fusion.6 = (s32[104]{0:T(128)}, s32[104]{0:T(128)}) fusion(s32[32,8]{1,0:T(8,128)S(1)} %get-tuple-element.23, s32[32,8]{1,0:T(8,128)} %add_select_fusion.1, s32[32,8]{1,0:T(8,128)S(1)} %get-tuple-element.24), kind=kLoop, calls=%fused_computation.8 | loop fusion | flops 132912 | bytes 3904 | tf_op jit(solution)/shard_map/reduce_sum | solution.py:335
  80.3 2.6 %concatenate.26.table = s32[328]{0:T(512)} concatenate(s32[1]{0:T(128)} %bitcast.6, s32[1]{0:T(128)} %bitcast.10, s32[1]{0:T(128)} %constant.32.clone.1, s32[1]{0:T(128)} %bitcast.11, s32[1]{0:T(128)} %bitcast.12, s32[1]{0:T(128)} %bitcast.13, s32[1]{0:T(128)} %bitcast.14, s32[1]{0:T(128)} %bitcast.15, s32[32]{0:T(128)} %get-tuple-element.43, s32[4]{0:T(128)} %broadcast.382, ...), dimensions={0} | concatenate | bytes 2624 | tf_op jit(solution)/shard_map/concatenate | solution.py:360
  82.9 1.4 select_reduce_fusion.17
  85.0 1.4 select_reduce_fusion.2
  86.4 2.7 %concatenate.27.table = s32[354]{0:T(512)} concatenate(s32[1]{0:T(128)} %bitcast.18, s32[1]{0:T(128)} %bitcast.20, s32[1]{0:T(128)} %constant.32.clone.1, s32[1]{0:T(128)} %bitcast.11, s32[1]{0:T(128)} %bitcast.12, s32[1]{0:T(128)} %bitcast.13, s32[1]{0:T(128)} %bitcast.14, s32[1]{0:T(128)} %bitcast.15, s32[32]{0:T(128)} %get-tuple-element.38, s32[4]{0:T(128)} %broadcast.382, ...), dimensions={0} | concatenate | bytes 2832 | tf_op jit(solution)/shard_map/concatenate | solution.py:360
  89.1 1.3 slice_reduce_fusion
  90.4 3.6 %collective-permute-done.10.refs_5_ = bf16[1792,256]{1,0:T(8,128)(2,1)} collective-permute-done((bf16[1792,256]{1,0:T(8,128)(2,1)S(1)}, bf16[1792,256]{1,0:T(8,128)(2,1)}, u32[]{:S(2)}, u32[]{:S(2)}) %collective-permute-start.10) | collective-permute-done | bytes 917536 | tf_op jit(solution)/shard_map/ppermute | solution.py:285
  94.0 8.1 %shard_map.78.refs_11_ = bf16[32,256,256]{2,1,0:T(8,128)(2,1)} custom-call(s32[354]{0:T(512)} %concatenate.27.table, bf16[8,3328,256]{2,1,0:T(8,128)(2,1)} %bitcast.24, bf16[3328,256]{1,0:T(8,128)(2,1)} %get-tuple-element.14.refs_0_, bf16[1792,256]{1,0:T(8,128)(2,1)} %copy-done.1, bf16[1536,256]{1,0:T(8,128)(2,1)} %collective-permute-done.8.refs_2_, ...), custom_call_target="tpu_custom_call" | custom-call | tf_op jit(solution)/shard_map/pallas_call | solution.py:264
  102.2 29.4 %collective-permute-done.15.refs_10_ = bf16[1536,256]{1,0:T(8,128)(2,1)} collective-permute-done((bf16[1536,256]{1,0:T(8,128)(2,1)}, bf16[1536,256]{1,0:T(8,128)(2,1)}, u32[]{:S(2)}, u32[]{:S(2)}) %collective-permute-start.15) | collective-permute-done | bytes 786464 | tf_op jit(solution)/shard_map/ppermute | solution.py:299
  131.5 6.9 %shard_map.79 = bf16[32,256,256]{2,1,0:T(8,128)(2,1)} custom-call(s32[328]{0:T(512)} %concatenate.26.table, bf16[8,3328,256]{2,1,0:T(8,128)(2,1)} %bitcast.25, bf16[3328,256]{1,0:T(8,128)(2,1)} %get-tuple-element.14.refs_0_, bf16[1792,256]{1,0:T(8,128)(2,1)} %copy-done.1, ...), custom_call_target="tpu_custom_call", output_to_operand_aliasing={{}: (13, {})} | custom-call | tf_op jit(solution)/shard_map/pallas_call | solution.py:264
  (122 shorter events, 22.0 us)
Async XLA Ops:
  7.2 86.8 %all-gather.3.cloned.1.call-start = ((), (), s32[]{:S(2)}) async-start(), calls=%async_computation | async-start | bytes 15335424 | tf_op jit(solution)/shard_map/all_gather | solution.py:402
  11.5 13.0 %collective-permute-start.2 = (f32[1,128]{1,0:T(1,128)}, f32[1,128]{1,0:T(1,128)S(1)}, u32[]{:S(2)}, u32[]{:S(2)}) collective-permute-start(f32[1,128]{1,0:T(1,128)} %get-tuple-element.11), channel_id=1, source_target_pairs={{0,3},{1,2},{2,1},{3,0},{4,7},{5,6},{6,5},{7,4},{8,11},{9,10},{10,... | collective-permute-start | bytes 1544 | tf_op jit(solution)/shard_map/ppermute | solution.py:285
  15.3 9.9 %collective-permute-start.1 = (f32[1,128]{1,0:T(1,128)}, f32[1,128]{1,0:T(1,128)S(1)}, u32[]{:S(2)}, u32[]{:S(2)}) collective-permute-start(f32[1,128]{1,0:T(1,128)} %get-tuple-element.11), channel_id=1, source_target_pairs={{0,2},{1,3},{2,0},{3,1},{4,6},{5,7},{6,4},{7,5},{8,10},{9,11},{10,... | collective-permute-start | bytes 1544 | tf_op jit(solution)/shard_map/ppermute | solution.py:285
  15.3 13.3 %collective-permute-start = (f32[1,128]{1,0:T(1,128)}, f32[1,128]{1,0:T(1,128)S(1)}, u32[]{:S(2)}, u32[]{:S(2)}) collective-permute-start(f32[1,128]{1,0:T(1,128)} %get-tuple-element.11), channel_id=1, source_target_pairs={{0,1},{1,0},{2,3},{3,2},{4,5},{5,4},{6,7},{7,6},{8,9},{9,8},{10,11... | collective-permute-start | bytes 1544 | tf_op jit(solution)/shard_map/ppermute | solution.py:285
  16.0 22.7 %collective-permute-start.9 = (bf16[1536,256]{1,0:T(8,128)(2,1)}, bf16[1536,256]{1,0:T(8,128)(2,1)S(1)}, u32[]{:S(2)}, u32[]{:S(2)}) collective-permute-start(bf16[1536,256]{1,0:T(8,128)(2,1)} %get-tuple-element.16), channel_id=1, source_target_pairs={{1,2},{2,1},{5,6},{6,5},{9,10},{10,9},{13,14},{14,13},{17,18},{18,... | collective-permute-start | bytes 2359304 | tf_op jit(solution)/shard_map/ppermute | solution.py:285
  16.7 23.3 %collective-permute-start.8 = (bf16[1536,256]{1,0:T(8,128)(2,1)}, bf16[1536,256]{1,0:T(8,128)(2,1)}, u32[]{:S(2)}, u32[]{:S(2)}) collective-permute-start(bf16[1536,256]{1,0:T(8,128)(2,1)} %get-tuple-element.16), channel_id=1, source_target_pairs={{0,1},{1,0},{2,3},{3,2},{4,5},{5,4},{6,7},{7,6},{8,9},{9,8},{10,11... | collective-permute-start | bytes 2359304 | tf_op jit(solution)/shard_map/ppermute | solution.py:285
  21.8 39.9 %copy-start.6 = (s32[8]{0:T(128)}, s32[8]{0:T(128)S(1)}, u32[]{:S(2)}) copy-start(s32[8]{0:T(128)S(1)} %iota_add_fusion) | copy-start | bytes 100
  24.5 17.1 %collective-permute-start.4 = (bf16[1792,256]{1,0:T(8,128)(2,1)}, bf16[1792,256]{1,0:T(8,128)(2,1)S(1)}, u32[]{:S(2)}, u32[]{:S(2)}) collective-permute-start(bf16[1792,256]{1,0:T(8,128)(2,1)} %get-tuple-element.12), channel_id=1, source_target_pairs={{1,2},{2,1},{5,6},{6,5},{9,10},{10,9},{13,14},{14,13},{17,18},{18,... | collective-permute-start | bytes 2752520 | tf_op jit(solution)/shard_map/ppermute | solution.py:285
  25.2 33.9 %collective-permute-start.3 = (bf16[1792,256]{1,0:T(8,128)(2,1)}, bf16[1792,256]{1,0:T(8,128)(2,1)S(1)}, u32[]{:S(2)}, u32[]{:S(2)}) collective-permute-start(bf16[1792,256]{1,0:T(8,128)(2,1)} %get-tuple-element.12), channel_id=1, source_target_pairs={{0,1},{1,0},{2,3},{3,2},{4,5},{5,4},{6,7},{7,6},{8,9},{9,8},{10,11... | collective-permute-start | bytes 2752520 | tf_op jit(solution)/shard_map/ppermute | solution.py:285
  30.1 1.1 collective-permute-start.5
  31.3 3.6 %collective-permute-start.6 = (f32[2,128]{1,0:T(2,128)S(1)}, f32[2,128]{1,0:T(2,128)S(1)}, u32[]{:S(2)}, u32[]{:S(2)}) collective-permute-start(f32[2,128]{1,0:T(2,128)S(1)} %pad_maximum_fusion.3), channel_id=1, source_target_pairs={{0,8},{4,12},{8,0},{12,4},{16,24},{20,28},{24,16},{28,20},{1,9},{5... | collective-permute-start | bytes 3080 | tf_op jit(solution)/shard_map/ppermute | solution.py:377
  34.9 3.7 %collective-permute-start.7 = (f32[4,128]{1,0:T(4,128)S(1)}, f32[4,128]{1,0:T(4,128)S(1)}, u32[]{:S(2)}, u32[]{:S(2)}) collective-permute-start(f32[4,128]{1,0:T(4,128)S(1)} %pad_maximum_fusion.2), channel_id=1, source_target_pairs={{0,16},{4,20},{8,24},{12,28},{16,0},{20,4},{24,8},{28,12},{1,17},{... | collective-permute-start | bytes 6152 | tf_op jit(solution)/shard_map/ppermute | solution.py:377
  38.6 20.7 %copy-start.4 = (f32[8,128]{1,0:T(8,128)}, f32[8,128]{1,0:T(8,128)S(1)}, u32[]{:S(2)}) copy-start(f32[8,128]{1,0:T(8,128)S(1)} %select_reduce_fusion.14) | copy-start | bytes 12292
  38.6 55.4 %copy-start.3 = (bf16[1536,256]{1,0:T(8,128)(2,1)}, bf16[1536,256]{1,0:T(8,128)(2,1)S(1)}, u32[]{:S(2)}) copy-start(bf16[1536,256]{1,0:T(8,128)(2,1)S(1)} %collective-permute-done.9.refs_4_) | copy-start | bytes 2359300
  38.7 51.8 %collective-permute-start.11 = (bf16[1536,256]{1,0:T(8,128)(2,1)S(1)}, bf16[1536,256]{1,0:T(8,128)(2,1)}, u32[]{:S(2)}, u32[]{:S(2)}) collective-permute-start(bf16[1536,256]{1,0:T(8,128)(2,1)S(1)} %collective-permute-done.9.refs_4_), channel_id=1, source_target_pairs={{1,0},{2,3},{5,4},{6,7},{9,8},{10,11},{13,12},{14,15},{17,16},{18,... | collective-permute-start | bytes 2359304 | tf_op jit(solution)/shard_map/ppermute | solution.py:285
  40.0 32.7 %collective-permute-start.13 = (bf16[1536,256]{1,0:T(8,128)(2,1)}, bf16[1536,256]{1,0:T(8,128)(2,1)}, u32[]{:S(2)}, u32[]{:S(2)}) collective-permute-start(bf16[1536,256]{1,0:T(8,128)(2,1)} %collective-permute-done.8.refs_2_), channel_id=1, source_target_pairs={{1,2},{2,1},{5,6},{6,5},{9,10},{10,9},{13,14},{14,13},{17,18},{18,... | collective-permute-start | bytes 2359304 | tf_op jit(solution)/shard_map/ppermute | solution.py:285
  41.6 52.4 %copy-start = (bf16[1792,256]{1,0:T(8,128)(2,1)}, bf16[1792,256]{1,0:T(8,128)(2,1)S(1)}, u32[]{:S(2)}) copy-start(bf16[1792,256]{1,0:T(8,128)(2,1)S(1)} %collective-permute-done.4.refs_3_) | copy-start | bytes 2752516
  59.0 35.0 %copy-start.1 = (bf16[1792,256]{1,0:T(8,128)(2,1)}, bf16[1792,256]{1,0:T(8,128)(2,1)S(1)}, u32[]{:S(2)}) copy-start(bf16[1792,256]{1,0:T(8,128)(2,1)S(1)} %collective-permute-done.3.refs_1_) | copy-start | bytes 2752516
  59.7 2.0 %copy-start.5 = (s32[2,8,2]{1,2,0:T(2,128)}, s32[2,8,2]{1,2,0:T(2,128)S(1)}, u32[]{:S(2)}) copy-start(s32[2,8,2]{1,2,0:T(2,128)S(1)} %copy.59) | copy-start | bytes 388
  61.7 8.9 %collective-permute-start.12 = (bf16[1792,256]{1,0:T(8,128)(2,1)S(1)}, bf16[1792,256]{1,0:T(8,128)(2,1)S(1)}, u32[]{:S(2)}, u32[]{:S(2)}) collective-permute-start(bf16[1792,256]{1,0:T(8,128)(2,1)S(1)} %collective-permute-done.3.refs_1_), channel_id=1, source_target_pairs={{1,2},{2,1},{5,6},{6,5},{9,10},{10,9},{13,14},{14,13},{17,18},{18,... | collective-permute-start | bytes 2752520 | tf_op jit(solution)/shard_map/ppermute | solution.py:285
  62.5 31.5 %collective-permute-start.10 = (bf16[1792,256]{1,0:T(8,128)(2,1)S(1)}, bf16[1792,256]{1,0:T(8,128)(2,1)}, u32[]{:S(2)}, u32[]{:S(2)}) collective-permute-start(bf16[1792,256]{1,0:T(8,128)(2,1)S(1)} %collective-permute-done.4.refs_3_), channel_id=1, source_target_pairs={{1,0},{2,3},{5,4},{6,7},{9,8},{10,11},{13,12},{14,15},{17,16},{18,... | collective-permute-start | bytes 2752520 | tf_op jit(solution)/shard_map/ppermute | solution.py:285
  70.7 23.4 %copy-start.2 = (bf16[1792,256]{1,0:T(8,128)(2,1)}, bf16[1792,256]{1,0:T(8,128)(2,1)S(1)}, u32[]{:S(2)}) copy-start(bf16[1792,256]{1,0:T(8,128)(2,1)S(1)} %collective-permute-done.12.refs_7_) | copy-start | bytes 2752516
  70.7 60.9 %collective-permute-start.14 = (bf16[1792,256]{1,0:T(8,128)(2,1)S(1)}, bf16[1792,256]{1,0:T(8,128)(2,1)}, u32[]{:S(2)}, u32[]{:S(2)}) collective-permute-start(bf16[1792,256]{1,0:T(8,128)(2,1)S(1)} %collective-permute-done.12.refs_7_), channel_id=1, source_target_pairs={{2,3},{6,7},{9,8},{10,11},{13,12},{14,15},{17,16},{18,19},{21,20},... | collective-permute-start | bytes 2752520 | tf_op jit(solution)/shard_map/ppermute | solution.py:299
  72.7 58.8 %collective-permute-start.15 = (bf16[1536,256]{1,0:T(8,128)(2,1)}, bf16[1536,256]{1,0:T(8,128)(2,1)}, u32[]{:S(2)}, u32[]{:S(2)}) collective-permute-start(bf16[1536,256]{1,0:T(8,128)(2,1)} %collective-permute-done.13.refs_8_), channel_id=1, source_target_pairs={{2,3},{6,7},{9,8},{10,11},{13,12},{14,15},{17,16},{18,19},{21,20},... | collective-permute-start | bytes 2359304 | tf_op jit(solution)/shard_map/ppermute | solution.py:299
Sparse Core Ops, SparseCore 0:
  11.6 77.1 all-gather.2

commit v13 on v12

--- a/solution.py
+++ b/solution.py
@@ -289,14 +289,16 @@
     first = [shift(part, [(0, 1), (1, 0), (2, 3), (3, 2)]) for part in parts]
     middle = [shift(part, [(1, 2), (2, 1)]) for part in parts]
     facts = gather_facts(facts, ("row",))
-    first[0], middle[0], facts = lax.optimization_barrier((first[0], middle[0], facts))
+    middle[0], facts = lax.optimization_barrier((middle[0], facts))
     end_two = [shift(part, [(1, 0), (2, 3)]) for part in middle]
     middle_two = [shift(part, [(1, 2), (2, 1)]) for part in first]
     pairs = []
     for row in range(lax.axis_size("row")):
         pairs += [(4 * row + 1, 4 * row)] * (row // 2 != 0)
         pairs += [(4 * row + 2, 4 * row + 3)] * (row // 2 != 3)
-    end_three = [lax.ppermute(part, ("row", "col"), pairs) for part in middle_two]
+    small = lax.ppermute(middle_two[1], ("row", "col"), pairs)
+    large = lax.optimization_barrier((middle_two[0], small))[0]
+    end_three = [lax.ppermute(large, ("row", "col"), pairs), small]
     line = {
         "first": first,
         "middle": middle,

time: 146 us -> 156 us (1.068)
  the two profiles are of different devices: /device:TPU:4 before, /device:TPU:10 now
where the time goes in v13:
time: 156 us; the launch traced here: 155 us
  waiting for transfers between devices  55.1 us (35%)
  starting transfers between devices  30.7 us (20%)
  other arithmetic  23.8 us (15%)
  Pallas kernels  19.6 us (13%)
  between operations  14.4 us (9%)
  local copies, waits for them, and re-layouts  11.3 us (7%)
    ppermute x11, waiting for transfers between devices, shift(): return lax.ppermute(array, 'col', pairs)  33.4 us
    ppermute x11, starting transfers between devices, shift(): return lax.ppermute(array, 'col', pairs)  20.8 us
    ppermute x1, waiting for transfers between devices, gather_line(): small = lax.ppermute(middle_two[1], ('row', 'col'), pairs)  15.9 us
    pallas_call x2, Pallas kernels, multiply(): pl.pallas_call(functools.partial(multiply_kernel, loads, kept, layout, tu...  15.4 us
    ppermute x3, waiting for transfers between devices, gather_facts(): other = lax.ppermute(facts, axis, [(i, i ^ mask) for i in range(size)])  5.72 us
    concatenate x2, local copies, waits for them, and re-layouts, make_table(): return (jnp.concatenate(list(lists.values())), layout)  5.48 us
    ppermute x1, starting transfers between devices, gather_line(): end_three = [lax.ppermute(large, ('row', 'col'), pairs), small]  5.36 us
    pallas_call x1, Pallas kernels, pack(): pl.pallas_call(pack_kernel, out_shape=packed + [jax.ShapeDtypeStruct((1,...  4.22 us
  transfers between devices with their start and end apart: 17, of which 8 were waited for; matrix products, arithmetic and copies ran while one was open for 22% of the time, Pallas kernels for 9%

profile of v13, /device:TPU:10, one launch (start us, length us, event | category | flops | bytes accessed | tf_op | source)
XLA Modules:
  0.0 154.9 jit_solution(15274527977947124582)
XLA Ops:
  7.2 4.2 %shard_map.77 = (bf16[1792,256]{1,0:T(8,128)(2,1)}, bf16[1536,256]{1,0:T(8,128)(2,1)}, bf16[3328,256]{1,0:T(8,128)(2,1)}, f32[1,128]{1,0:T(1,128)}) custom-call(s32[2,8]{1,0:T(2,128)} %bitcast.37, s32[8]{0:T(128)} %flag_ref.1, s32[1]{0:T(128)} %bitcast.1.first_ref, bf16[16,256,256]{2,1,0:T(8,128)(2,1)} %bitcast.27), custom_call_target="tpu_custom_call" | custom-call | tf_op jit(solution)/shard_map/pallas_call | solution.py:83
  11.5 1.7 %collective-permute-start.2 = (f32[1,128]{1,0:T(1,128)}, f32[1,128]{1,0:T(1,128)S(1)}, u32[]{:S(2)}, u32[]{:S(2)}) collective-permute-start(f32[1,128]{1,0:T(1,128)} %get-tuple-element.11), channel_id=1, source_target_pairs={{0,3},{1,2},{2,1},{3,0},{4,7},{5,6},{6,5},{7,4},{8,11},{9,10},{10,... | collective-permute-start | bytes 1544 | tf_op jit(solution)/shard_map/ppermute | solution.py:285
  13.2 1.4 collective-permute-start.1
  15.4 3.4 %collective-permute-start.9 = (bf16[1536,256]{1,0:T(8,128)(2,1)}, bf16[1536,256]{1,0:T(8,128)(2,1)S(1)}, u32[]{:S(2)}, u32[]{:S(2)}) collective-permute-start(bf16[1536,256]{1,0:T(8,128)(2,1)} %get-tuple-element.15), channel_id=1, source_target_pairs={{1,2},{2,1},{5,6},{6,5},{9,10},{10,9},{13,14},{14,13},{17,18},{18,... | collective-permute-start | bytes 2359304 | tf_op jit(solution)/shard_map/ppermute | solution.py:285
  24.7 2.5 %collective-permute-start.3 = (bf16[1792,256]{1,0:T(8,128)(2,1)}, bf16[1792,256]{1,0:T(8,128)(2,1)S(1)}, u32[]{:S(2)}, u32[]{:S(2)}) collective-permute-start(bf16[1792,256]{1,0:T(8,128)(2,1)} %get-tuple-element.12), channel_id=1, source_target_pairs={{1,2},{2,1},{5,6},{6,5},{9,10},{10,9},{13,14},{14,13},{17,18},{18,... | collective-permute-start | bytes 2752520 | tf_op jit(solution)/shard_map/ppermute | solution.py:285
  30.8 2.7 %collective-permute-done.5 = f32[2,128]{1,0:T(2,128)S(1)} collective-permute-done((f32[2,128]{1,0:T(2,128)S(1)}, f32[2,128]{1,0:T(2,128)S(1)}, u32[]{:S(2)}, u32[]{:S(2)}) %collective-permute-start.5) | collective-permute-done | bytes 1056 | tf_op jit(solution)/shard_map/ppermute | solution.py:379
  33.5 1.6 %collective-permute-start.6 = (f32[4,128]{1,0:T(4,128)S(1)}, f32[4,128]{1,0:T(4,128)S(1)}, u32[]{:S(2)}, u32[]{:S(2)}) collective-permute-start(f32[4,128]{1,0:T(4,128)S(1)} %pad_maximum_fusion.2), channel_id=1, source_target_pairs={{0,16},{4,20},{8,24},{12,28},{16,0},{20,4},{24,8},{28,12},{1,17},{... | collective-permute-start | bytes 6152 | tf_op jit(solution)/shard_map/ppermute | solution.py:379
  35.2 2.0 %collective-permute-done.6 = f32[4,128]{1,0:T(4,128)S(1)} collective-permute-done((f32[4,128]{1,0:T(4,128)S(1)}, f32[4,128]{1,0:T(4,128)S(1)}, u32[]{:S(2)}, u32[]{:S(2)}) %collective-permute-start.6) | collective-permute-done | bytes 2080 | tf_op jit(solution)/shard_map/ppermute | solution.py:379
  38.0 2.2 %collective-permute-start.11 = (bf16[1536,256]{1,0:T(8,128)(2,1)S(1)}, bf16[1536,256]{1,0:T(8,128)(2,1)}, u32[]{:S(2)}, u32[]{:S(2)}) collective-permute-start(bf16[1536,256]{1,0:T(8,128)(2,1)S(1)} %collective-permute-done.9.refs_4_), channel_id=1, source_target_pairs={{1,0},{2,3},{5,4},{6,7},{9,8},{10,11},{13,12},{14,15},{17,16},{18,... | collective-permute-start | bytes 2359304 | tf_op jit(solution)/shard_map/ppermute | solution.py:285
  40.1 3.4 %collective-permute-start.13 = (bf16[1536,256]{1,0:T(8,128)(2,1)}, bf16[1536,256]{1,0:T(8,128)(2,1)}, u32[]{:S(2)}, u32[]{:S(2)}) collective-permute-start(bf16[1536,256]{1,0:T(8,128)(2,1)} %collective-permute-done.8.refs_2_), channel_id=1, source_target_pairs={{1,2},{2,1},{5,6},{6,5},{9,10},{10,9},{13,14},{14,13},{17,18},{18,... | collective-permute-start | bytes 2359304 | tf_op jit(solution)/shard_map/ppermute | solution.py:285
  43.5 14.1 %collective-permute-done.3.refs_3_ = bf16[1792,256]{1,0:T(8,128)(2,1)S(1)} collective-permute-done((bf16[1792,256]{1,0:T(8,128)(2,1)}, bf16[1792,256]{1,0:T(8,128)(2,1)S(1)}, u32[]{:S(2)}, u32[]{:S(2)}) %collective-permute-start.3) | collective-permute-done | bytes 917536 | tf_op jit(solution)/shard_map/ppermute | solution.py:285
  61.8 3.4 %collective-permute-start.12 = (bf16[1792,256]{1,0:T(8,128)(2,1)S(1)}, bf16[1792,256]{1,0:T(8,128)(2,1)}, u32[]{:S(2)}, u32[]{:S(2)}) collective-permute-start(bf16[1792,256]{1,0:T(8,128)(2,1)S(1)} %collective-permute-done.7.refs_1_), channel_id=1, source_target_pairs={{1,2},{2,1},{5,6},{6,5},{9,10},{10,9},{13,14},{14,13},{17,18},{18,... | collective-permute-start | bytes 2752520 | tf_op jit(solution)/shard_map/ppermute | solution.py:285
  69.6 5.0 %collective-permute-done.13.refs_8_ = bf16[1536,256]{1,0:T(8,128)(2,1)} collective-permute-done((bf16[1536,256]{1,0:T(8,128)(2,1)}, bf16[1536,256]{1,0:T(8,128)(2,1)}, u32[]{:S(2)}, u32[]{:S(2)}) %collective-permute-start.13) | collective-permute-done | bytes 786464 | tf_op jit(solution)/shard_map/ppermute | solution.py:285
  74.6 2.2 %collective-permute-start.14 = (bf16[1536,256]{1,0:T(8,128)(2,1)}, bf16[1536,256]{1,0:T(8,128)(2,1)}, u32[]{:S(2)}, u32[]{:S(2)}) collective-permute-start(bf16[1536,256]{1,0:T(8,128)(2,1)} %collective-permute-done.13.refs_8_), channel_id=1, source_target_pairs={{2,3},{6,7},{9,8},{10,11},{13,12},{14,15},{17,16},{18,19},{21,20},... | collective-permute-start | bytes 2359304 | tf_op jit(solution)/shard_map/ppermute | solution.py:299
  79.3 13.6 %collective-permute-done.12.refs_7_ = bf16[1792,256]{1,0:T(8,128)(2,1)} collective-permute-done((bf16[1792,256]{1,0:T(8,128)(2,1)S(1)}, bf16[1792,256]{1,0:T(8,128)(2,1)}, u32[]{:S(2)}, u32[]{:S(2)}) %collective-permute-start.12) | collective-permute-done | bytes 917536 | tf_op jit(solution)/shard_map/ppermute | solution.py:285
  92.9 15.9 %collective-permute-done.14.refs_10_ = bf16[1536,256]{1,0:T(8,128)(2,1)} collective-permute-done((bf16[1536,256]{1,0:T(8,128)(2,1)}, bf16[1536,256]{1,0:T(8,128)(2,1)}, u32[]{:S(2)}, u32[]{:S(2)}) %collective-permute-start.14) | collective-permute-done | bytes 786464 | tf_op jit(solution)/shard_map/ppermute | solution.py:299
  108.9 5.4 %collective-permute-start.15 = (bf16[1792,256]{1,0:T(8,128)(2,1)}, bf16[1792,256]{1,0:T(8,128)(2,1)}, u32[]{:S(2)}, u32[]{:S(2)}) collective-permute-start(bf16[1792,256]{1,0:T(8,128)(2,1)} %collective-permute-done.12.refs_7_), channel_id=1, source_target_pairs={{2,3},{6,7},{9,8},{10,11},{13,12},{14,15},{17,16},{18,19},{21,20},... | collective-permute-start | bytes 2752520 | tf_op jit(solution)/shard_map/ppermute | solution.py:301
  115.7 3.6 %select_reduce_fusion.3 = (s32[32,8]{1,0:T(8,128)S(1)}, s32[32,8]{1,0:T(8,128)S(1)}, s32[32,8]{1,0:T(8,128)S(1)}, s32[32,8]{1,0:T(8,128)}) fusion(s32[32,64]{1,0:T(8,128)} %broadcast_select_fusion, s32[32,64]{1,0:T(8,128)} %broadcast_add_fusion, s32[32,64]{1,0:T(8,128)} %get-tuple-element.51, s32[32,64]{1,0:T(8,128)S(1)} %bitcast.28, s32[32,64]{1,0:T(8,128)S(1)} %bitcast.29), kind=kLoop, calls=%fused_computation.3 | loop fusion | flops 162816 | bytes 45056 | tf_op jit(solution)/shard_map/reduce_sum | solution.py:333
  119.3 1.5 select_reduce_fusion.6
  121.3 2.7 %concatenate.26.table = s32[328]{0:T(512)} concatenate(s32[1]{0:T(128)} %bitcast.6, s32[1]{0:T(128)} %bitcast.10, s32[1]{0:T(128)} %constant.32.clone.1, s32[1]{0:T(128)} %bitcast.11, s32[1]{0:T(128)} %bitcast.12, s32[1]{0:T(128)} %bitcast.13, s32[1]{0:T(128)} %bitcast.14, s32[1]{0:T(128)} %bitcast.15, s32[32]{0:T(128)} %get-tuple-element.43, s32[4]{0:T(128)} %broadcast.382, ...), dimensions={0} | concatenate | bytes 2624 | tf_op jit(solution)/shard_map/concatenate | solution.py:362
  124.0 1.4 select_reduce_fusion.17
  126.1 1.4 select_reduce_fusion.2
  127.5 2.8 %concatenate.27.table = s32[354]{0:T(512)} concatenate(s32[1]{0:T(128)} %bitcast.18, s32[1]{0:T(128)} %bitcast.20, s32[1]{0:T(128)} %constant.32.clone.1, s32[1]{0:T(128)} %bitcast.11, s32[1]{0:T(128)} %bitcast.12, s32[1]{0:T(128)} %bitcast.13, s32[1]{0:T(128)} %bitcast.14, s32[1]{0:T(128)} %bitcast.15, s32[32]{0:T(128)} %get-tuple-element.38, s32[4]{0:T(128)} %broadcast.382, ...), dimensions={0} | concatenate | bytes 2832 | tf_op jit(solution)/shard_map/concatenate | solution.py:362
  132.6 14.0 %shard_map.78.refs_11_ = bf16[32,256,256]{2,1,0:T(8,128)(2,1)} custom-call(s32[354]{0:T(512)} %concatenate.27.table, bf16[8,3328,256]{2,1,0:T(8,128)(2,1)} %bitcast.24, bf16[3328,256]{1,0:T(8,128)(2,1)} %get-tuple-element.14.refs_0_, bf16[1792,256]{1,0:T(8,128)(2,1)} %copy-done, bf16[1536,256]{1,0:T(8,128)(2,1)} %collective-permute-done.8.refs_2_, ...), custom_call_target="tpu_custom_call" | custom-call | tf_op jit(solution)/shard_map/pallas_call | solution.py:264
  (122 shorter events, 28.5 us)
Async XLA Ops:
  7.2 124.5 %all-gather.3.cloned.1.call-start = ((), (), s32[]{:S(2)}) async-start(), calls=%async_computation | async-start | bytes 15335424 | tf_op jit(solution)/shard_map/all_gather | solution.py:404
  11.5 12.4 %collective-permute-start.2 = (f32[1,128]{1,0:T(1,128)}, f32[1,128]{1,0:T(1,128)S(1)}, u32[]{:S(2)}, u32[]{:S(2)}) collective-permute-start(f32[1,128]{1,0:T(1,128)} %get-tuple-element.11), channel_id=1, source_target_pairs={{0,3},{1,2},{2,1},{3,0},{4,7},{5,6},{6,5},{7,4},{8,11},{9,10},{10,... | collective-permute-start | bytes 1544 | tf_op jit(solution)/shard_map/ppermute | solution.py:285
  13.2 11.5 %collective-permute-start.1 = (f32[1,128]{1,0:T(1,128)}, f32[1,128]{1,0:T(1,128)S(1)}, u32[]{:S(2)}, u32[]{:S(2)}) collective-permute-start(f32[1,128]{1,0:T(1,128)} %get-tuple-element.11), channel_id=1, source_target_pairs={{0,2},{1,3},{2,0},{3,1},{4,6},{5,7},{6,4},{7,5},{8,10},{9,11},{10,... | collective-permute-start | bytes 1544 | tf_op jit(solution)/shard_map/ppermute | solution.py:285
  14.6 12.5 %collective-permute-start = (f32[1,128]{1,0:T(1,128)}, f32[1,128]{1,0:T(1,128)S(1)}, u32[]{:S(2)}, u32[]{:S(2)}) collective-permute-start(f32[1,128]{1,0:T(1,128)} %get-tuple-element.11), channel_id=1, source_target_pairs={{0,1},{1,0},{2,3},{3,2},{4,5},{5,4},{6,7},{7,6},{8,9},{9,8},{10,11... | collective-permute-start | bytes 1544 | tf_op jit(solution)/shard_map/ppermute | solution.py:285
  15.4 22.5 %collective-permute-start.9 = (bf16[1536,256]{1,0:T(8,128)(2,1)}, bf16[1536,256]{1,0:T(8,128)(2,1)S(1)}, u32[]{:S(2)}, u32[]{:S(2)}) collective-permute-start(bf16[1536,256]{1,0:T(8,128)(2,1)} %get-tuple-element.15), channel_id=1, source_target_pairs={{1,2},{2,1},{5,6},{6,5},{9,10},{10,9},{13,14},{14,13},{17,18},{18,... | collective-permute-start | bytes 2359304 | tf_op jit(solution)/shard_map/ppermute | solution.py:285
  18.8 21.4 %collective-permute-start.8 = (bf16[1536,256]{1,0:T(8,128)(2,1)}, bf16[1536,256]{1,0:T(8,128)(2,1)}, u32[]{:S(2)}, u32[]{:S(2)}) collective-permute-start(bf16[1536,256]{1,0:T(8,128)(2,1)} %get-tuple-element.15), channel_id=1, source_target_pairs={{0,1},{1,0},{2,3},{3,2},{4,5},{5,4},{6,7},{7,6},{8,9},{9,8},{10,11... | collective-permute-start | bytes 2359304 | tf_op jit(solution)/shard_map/ppermute | solution.py:285
  20.0 40.3 %copy-start.6 = (s32[8]{0:T(128)}, s32[8]{0:T(128)S(1)}, u32[]{:S(2)}) copy-start(s32[8]{0:T(128)S(1)} %iota_add_fusion) | copy-start | bytes 100
  23.9 37.8 %collective-permute-start.7 = (bf16[1792,256]{1,0:T(8,128)(2,1)}, bf16[1792,256]{1,0:T(8,128)(2,1)S(1)}, u32[]{:S(2)}, u32[]{:S(2)}) collective-permute-start(bf16[1792,256]{1,0:T(8,128)(2,1)} %get-tuple-element.12), channel_id=1, source_target_pairs={{0,1},{1,0},{2,3},{3,2},{4,5},{5,4},{6,7},{7,6},{8,9},{9,8},{10,11... | collective-permute-start | bytes 2752520 | tf_op jit(solution)/shard_map/ppermute | solution.py:285
  24.7 33.0 %collective-permute-start.3 = (bf16[1792,256]{1,0:T(8,128)(2,1)}, bf16[1792,256]{1,0:T(8,128)(2,1)S(1)}, u32[]{:S(2)}, u32[]{:S(2)}) collective-permute-start(bf16[1792,256]{1,0:T(8,128)(2,1)} %get-tuple-element.12), channel_id=1, source_target_pairs={{1,2},{2,1},{5,6},{6,5},{9,10},{10,9},{13,14},{14,13},{17,18},{18,... | collective-permute-start | bytes 2752520 | tf_op jit(solution)/shard_map/ppermute | solution.py:285
  28.8 1.1 collective-permute-start.4
  29.9 3.6 %collective-permute-start.5 = (f32[2,128]{1,0:T(2,128)S(1)}, f32[2,128]{1,0:T(2,128)S(1)}, u32[]{:S(2)}, u32[]{:S(2)}) collective-permute-start(f32[2,128]{1,0:T(2,128)S(1)} %pad_maximum_fusion.3), channel_id=1, source_target_pairs={{0,8},{4,12},{8,0},{12,4},{16,24},{20,28},{24,16},{28,20},{1,9},{5... | collective-permute-start | bytes 3080 | tf_op jit(solution)/shard_map/ppermute | solution.py:379
  33.5 3.7 %collective-permute-start.6 = (f32[4,128]{1,0:T(4,128)S(1)}, f32[4,128]{1,0:T(4,128)S(1)}, u32[]{:S(2)}, u32[]{:S(2)}) collective-permute-start(f32[4,128]{1,0:T(4,128)S(1)} %pad_maximum_fusion.2), channel_id=1, source_target_pairs={{0,16},{4,20},{8,24},{12,28},{16,0},{20,4},{24,8},{28,12},{1,17},{... | collective-permute-start | bytes 6152 | tf_op jit(solution)/shard_map/ppermute | solution.py:379
  37.3 20.6 %copy-start.4 = (f32[8,128]{1,0:T(8,128)}, f32[8,128]{1,0:T(8,128)S(1)}, u32[]{:S(2)}) copy-start(f32[8,128]{1,0:T(8,128)S(1)} %select_reduce_fusion.14) | copy-start | bytes 12292
  38.0 93.7 %copy-start.3 = (bf16[1536,256]{1,0:T(8,128)(2,1)}, bf16[1536,256]{1,0:T(8,128)(2,1)S(1)}, u32[]{:S(2)}) copy-start(bf16[1536,256]{1,0:T(8,128)(2,1)S(1)} %collective-permute-done.9.refs_4_) | copy-start | bytes 2359300
  38.0 93.7 %collective-permute-start.11 = (bf16[1536,256]{1,0:T(8,128)(2,1)S(1)}, bf16[1536,256]{1,0:T(8,128)(2,1)}, u32[]{:S(2)}, u32[]{:S(2)}) collective-permute-start(bf16[1536,256]{1,0:T(8,128)(2,1)S(1)} %collective-permute-done.9.refs_4_), channel_id=1, source_target_pairs={{1,0},{2,3},{5,4},{6,7},{9,8},{10,11},{13,12},{14,15},{17,16},{18,... | collective-permute-start | bytes 2359304 | tf_op jit(solution)/shard_map/ppermute | solution.py:285
  40.1 34.4 %collective-permute-start.13 = (bf16[1536,256]{1,0:T(8,128)(2,1)}, bf16[1536,256]{1,0:T(8,128)(2,1)}, u32[]{:S(2)}, u32[]{:S(2)}) collective-permute-start(bf16[1536,256]{1,0:T(8,128)(2,1)} %collective-permute-done.8.refs_2_), channel_id=1, source_target_pairs={{1,2},{2,1},{5,6},{6,5},{9,10},{10,9},{13,14},{14,13},{17,18},{18,... | collective-permute-start | bytes 2359304 | tf_op jit(solution)/shard_map/ppermute | solution.py:285
  57.6 74.1 %copy-start.1 = (bf16[1792,256]{1,0:T(8,128)(2,1)}, bf16[1792,256]{1,0:T(8,128)(2,1)S(1)}, u32[]{:S(2)}) copy-start(bf16[1792,256]{1,0:T(8,128)(2,1)S(1)} %collective-permute-done.3.refs_3_) | copy-start | bytes 2752516
  58.3 2.1 %copy-start.5 = (s32[2,8,2]{1,2,0:T(2,128)}, s32[2,8,2]{1,2,0:T(2,128)S(1)}, u32[]{:S(2)}) copy-start(s32[2,8,2]{1,2,0:T(2,128)S(1)} %copy.59) | copy-start | bytes 388
  60.4 71.3 %collective-permute-start.10 = (bf16[1792,256]{1,0:T(8,128)(2,1)S(1)}, bf16[1792,256]{1,0:T(8,128)(2,1)S(1)}, u32[]{:S(2)}, u32[]{:S(2)}) collective-permute-start(bf16[1792,256]{1,0:T(8,128)(2,1)S(1)} %collective-permute-done.3.refs_3_), channel_id=1, source_target_pairs={{1,0},{2,3},{5,4},{6,7},{9,8},{10,11},{13,12},{14,15},{17,16},{18,... | collective-permute-start | bytes 2752520 | tf_op jit(solution)/shard_map/ppermute | solution.py:285
  61.7 70.0 %copy-start = (bf16[1792,256]{1,0:T(8,128)(2,1)}, bf16[1792,256]{1,0:T(8,128)(2,1)S(1)}, u32[]{:S(2)}) copy-start(bf16[1792,256]{1,0:T(8,128)(2,1)S(1)} %collective-permute-done.7.refs_1_) | copy-start | bytes 2752516
  61.8 31.2 %collective-permute-start.12 = (bf16[1792,256]{1,0:T(8,128)(2,1)S(1)}, bf16[1792,256]{1,0:T(8,128)(2,1)}, u32[]{:S(2)}, u32[]{:S(2)}) collective-permute-start(bf16[1792,256]{1,0:T(8,128)(2,1)S(1)} %collective-permute-done.7.refs_1_), channel_id=1, source_target_pairs={{1,2},{2,1},{5,6},{6,5},{9,10},{10,9},{13,14},{14,13},{17,18},{18,... | collective-permute-start | bytes 2752520 | tf_op jit(solution)/shard_map/ppermute | solution.py:285
  74.6 34.3 %collective-permute-start.14 = (bf16[1536,256]{1,0:T(8,128)(2,1)}, bf16[1536,256]{1,0:T(8,128)(2,1)}, u32[]{:S(2)}, u32[]{:S(2)}) collective-permute-start(bf16[1536,256]{1,0:T(8,128)(2,1)} %collective-permute-done.13.refs_8_), channel_id=1, source_target_pairs={{2,3},{6,7},{9,8},{10,11},{13,12},{14,15},{17,16},{18,19},{21,20},... | collective-permute-start | bytes 2359304 | tf_op jit(solution)/shard_map/ppermute | solution.py:299
  108.9 37.8 %collective-permute-start.15 = (bf16[1792,256]{1,0:T(8,128)(2,1)}, bf16[1792,256]{1,0:T(8,128)(2,1)}, u32[]{:S(2)}, u32[]{:S(2)}) collective-permute-start(bf16[1792,256]{1,0:T(8,128)(2,1)} %collective-permute-done.12.refs_7_), channel_id=1, source_target_pairs={{2,3},{6,7},{9,8},{10,11},{13,12},{14,15},{17,16},{18,19},{21,20},... | collective-permute-start | bytes 2752520 | tf_op jit(solution)/shard_map/ppermute | solution.py:301
  131.7 0.9 copy-start.2
Sparse Core Ops, SparseCore 0:
  11.6 77.5 all-gather.2

commit v14 on v13

--- a/solution.py
+++ b/solution.py
@@ -285,28 +285,31 @@
     return lax.ppermute(array, "col", pairs)
 
 
-def gather_line(parts, facts):
+def start_line(parts, facts):
     first = [shift(part, [(0, 1), (1, 0), (2, 3), (3, 2)]) for part in parts]
     middle = [shift(part, [(1, 2), (2, 1)]) for part in parts]
     facts = gather_facts(facts, ("row",))
-    middle[0], facts = lax.optimization_barrier((middle[0], facts))
+    middle[1], facts = lax.optimization_barrier((middle[1], facts))
+    return first, middle, facts
+
+
+def relay_line(first, middle):
     end_two = [shift(part, [(1, 0), (2, 3)]) for part in middle]
     middle_two = [shift(part, [(1, 2), (2, 1)]) for part in first]
     pairs = []
     for row in range(lax.axis_size("row")):
         pairs += [(4 * row + 1, 4 * row)] * (row // 2 != 0)
         pairs += [(4 * row + 2, 4 * row + 3)] * (row // 2 != 3)
-    small = lax.ppermute(middle_two[1], ("row", "col"), pairs)
+    small = lax.optimization_barrier((middle_two[1], end_two[1]))[0]
+    small = lax.ppermute(small, ("row", "col"), pairs)
     large = lax.optimization_barrier((middle_two[0], small))[0]
-    end_three = [lax.ppermute(large, ("row", "col"), pairs), small]
-    line = {
+    return {
         "first": first,
         "middle": middle,
         "end_two": end_two,
         "middle_two": middle_two,
-        "end_three": end_three,
+        "end_three": (lax.ppermute(large, ("row", "col"), pairs), small),
     }
-    return line, facts
 
 
 def running_count(fill):
@@ -408,7 +411,7 @@
         line_cols = jnp.concatenate([facts, near, far_one, far_two])
         total = (facts + near) + (far_one + far_two)
         facts = jnp.where(jnp.arange(128) < count, facts, total)
-        line, facts = gather_line((part_a, part_b), facts)
+        first, middle, facts = start_line((part_a, part_b), facts)
         trace = jnp.sum(facts[:, count]).reshape(1)
     else:
         part_a, part_b, full, facts = pack(x_blocks, x_cols, branch_flag, row * rows)
@@ -482,6 +485,16 @@
     meets = (jnp.repeat(late, kept, axis=0) > 0) & (right_of > 0)
     is_late = jnp.any(meets, axis=1)
 
+    def table_of(left_of, chosen, turn=None):
+        return make_table(left_of, right_of, owns, branch_flag, chosen, width, wanted, turn)
+
+    early_table, early_layout = table_of(early, ~is_late, marks)
+    late_table, late_layout = table_of(early + late, is_late)
+    first[0], middle[0], early_table, late_table = lax.optimization_barrier(
+        (first[0], middle[0], early_table, late_table)
+    )
+    line = relay_line(first, middle)
+
     arrays = [full]
     loads = [(0, None, 0, 0, PACKED, always)]
     spans = ((0, SPLIT), (SPLIT, PACKED - SPLIT))
@@ -489,17 +502,6 @@
     def add(array, entry, which, wanted):
         loads.append((len(arrays), None, entry) + spans[which] + (wanted,))
         arrays.append(array)
-
-    def call(left_of, chosen, before=None):
-        turn = marks if before is None else None
-        table, layout = make_table(
-            left_of, right_of, owns, branch_flag, chosen, width, wanted, turn
-        )
-        turn = (at_corner, turn_at, 4, 2) if before is None else None
-        n_entries = 6 if before is None else 4
-        return multiply(
-            plane, list(arrays), tuple(loads), n_entries, layout, table, shape, turn, before
-        )
 
     stages = (
         ("first", 1, always),
@@ -510,11 +512,16 @@
     for name, entry, flag in stages:
         for which in range(2):
             add(line[name][which], entry, which, flag)
-    purified = call(early, ~is_late)
+    purified = multiply(
+        plane, list(arrays), tuple(loads), 6, early_layout, early_table, shape,
+        (at_corner, turn_at, 4, 2),
+    )
     for which in range(2):
         add(line["end_three"][which], 3, which, at_far)
     purified, trace = lax.optimization_barrier((purified, trace))
-    purified = call(early + late, is_late, purified)
+    purified = multiply(
+        plane, list(arrays), tuple(loads), 4, late_layout, late_table, shape, None, purified
+    )
     return purified.reshape(rows, kept, block, block), trace
 
 

time: 156 us -> 147 us (0.942)
  the two profiles are of different devices: /device:TPU:10 before, /device:TPU:2 now
where the time goes in v14:
time: 147 us
  waiting for transfers between devices  71.5 us (49%)
  starting transfers between devices  24.3 us (17%)
  Pallas kernels  19.1 us (13%)
  between operations  14.4 us (10%)
  other arithmetic  11 us (7%)
  local copies, waits for them, and re-layouts  6.53 us (4%)
    ppermute x11, waiting for transfers between devices, shift(): return lax.ppermute(array, 'col', pairs)  34.4 us
    ppermute x1, waiting for transfers between devices, relay_line(): small = lax.ppermute(small, ('row', 'col'), pairs)  23.9 us
    ppermute x11, starting transfers between devices, shift(): return lax.ppermute(array, 'col', pairs)  19.6 us
    pallas_call x2, Pallas kernels, multiply(): pl.pallas_call(functools.partial(multiply_kernel, loads, kept, layout, tu...  15.1 us
    ppermute x1, waiting for transfers between devices, relay_line(): lax.ppermute(large, ('row', 'col'), pairs)  7.27 us
    ppermute x3, waiting for transfers between devices, gather_facts(): other = lax.ppermute(facts, axis, [(i, i ^ mask) for i in range(size)])  5.91 us
    pallas_call x1, Pallas kernels, pack(): pl.pallas_call(pack_kernel, out_shape=packed + [jax.ShapeDtypeStruct((1,...  4 us
    concatenate x2, local copies, waits for them, and re-layouts, make_table(): return (jnp.concatenate(list(lists.values())), layout)  3.86 us
  transfers between devices with their start and end apart: 17, of which 8 were waited for; matrix products, arithmetic and copies ran while one was open for 12% of the time, Pallas kernels for 5%

profile of v14, /device:TPU:2, one launch (start us, length us, event | category | flops | bytes accessed | tf_op | source)
XLA Modules:
  0.0 147.0 jit_solution(3712575942653525196)
XLA Ops:
  7.2 4.0 %shard_map.77 = (bf16[1792,256]{1,0:T(8,128)(2,1)}, bf16[1536,256]{1,0:T(8,128)(2,1)}, bf16[3328,256]{1,0:T(8,128)(2,1)}, f32[1,128]{1,0:T(1,128)}) custom-call(s32[2,8]{1,0:T(2,128)} %bitcast.37, s32[8]{0:T(128)} %flag_ref.1, s32[1]{0:T(128)} %bitcast.1.first_ref, bf16[16,256,256]{2,1,0:T(8,128)(2,1)} %bitcast.27), custom_call_target="tpu_custom_call" | custom-call | tf_op jit(solution)/shard_map/pallas_call | solution.py:83
  11.3 4.0 %collective-permute-start.4 = (f32[1,128]{1,0:T(1,128)}, f32[1,128]{1,0:T(1,128)S(1)}, u32[]{:S(2)}, u32[]{:S(2)}) collective-permute-start(f32[1,128]{1,0:T(1,128)} %get-tuple-element.17), channel_id=1, source_target_pairs={{0,3},{1,2},{2,1},{3,0},{4,7},{5,6},{6,5},{7,4},{8,11},{9,10},{10,... | collective-permute-start | bytes 1544 | tf_op jit(solution)/shard_map/ppermute | solution.py:285
  15.9 1.4 collective-permute-start.9
  17.3 1.5 %collective-permute-start.5 = (bf16[1536,256]{1,0:T(8,128)(2,1)}, bf16[1536,256]{1,0:T(8,128)(2,1)}, u32[]{:S(2)}, u32[]{:S(2)}) collective-permute-start(bf16[1536,256]{1,0:T(8,128)(2,1)} %get-tuple-element.18), channel_id=1, source_target_pairs={{1,2},{2,1},{5,6},{6,5},{9,10},{10,9},{13,14},{14,13},{17,18},{18,... | collective-permute-start | bytes 2359304 | tf_op jit(solution)/shard_map/ppermute | solution.py:285
  22.8 6.5 %collective-permute-start = (bf16[1792,256]{1,0:T(8,128)(2,1)}, bf16[1792,256]{1,0:T(8,128)(2,1)S(1)}, u32[]{:S(2)}, u32[]{:S(2)}) collective-permute-start(bf16[1792,256]{1,0:T(8,128)(2,1)} %get-tuple-element.16), channel_id=1, source_target_pairs={{0,1},{1,0},{2,3},{3,2},{4,5},{5,4},{6,7},{7,6},{8,9},{9,8},{10,11... | collective-permute-start | bytes 2752520 | tf_op jit(solution)/shard_map/ppermute | solution.py:285
  30.9 1.0 collective-permute-done.6
  32.6 3.0 %collective-permute-done.7 = f32[2,128]{1,0:T(2,128)S(1)} collective-permute-done((f32[2,128]{1,0:T(2,128)S(1)}, f32[2,128]{1,0:T(2,128)S(1)}, u32[]{:S(2)}, u32[]{:S(2)}) %collective-permute-start.7) | collective-permute-done | bytes 1056 | tf_op jit(solution)/shard_map/ppermute | solution.py:382
  35.5 1.7 %collective-permute-start.8 = (f32[4,128]{1,0:T(4,128)S(1)}, f32[4,128]{1,0:T(4,128)S(1)}, u32[]{:S(2)}, u32[]{:S(2)}) collective-permute-start(f32[4,128]{1,0:T(4,128)S(1)} %pad_maximum_fusion.2), channel_id=1, source_target_pairs={{0,16},{4,20},{8,24},{12,28},{16,0},{20,4},{24,8},{28,12},{1,17},{... | collective-permute-start | bytes 6152 | tf_op jit(solution)/shard_map/ppermute | solution.py:382
  37.3 1.9 %collective-permute-done.8 = f32[4,128]{1,0:T(4,128)S(1)} collective-permute-done((f32[4,128]{1,0:T(4,128)S(1)}, f32[4,128]{1,0:T(4,128)S(1)}, u32[]{:S(2)}, u32[]{:S(2)}) %collective-permute-start.8) | collective-permute-done | bytes 2080 | tf_op jit(solution)/shard_map/ppermute | solution.py:382
  41.5 1.3 collective-permute-start.11
  42.8 1.6 %collective-permute-start.13 = (bf16[1536,256]{1,0:T(8,128)(2,1)S(1)}, bf16[1536,256]{1,0:T(8,128)(2,1)}, u32[]{:S(2)}, u32[]{:S(2)}) collective-permute-start(bf16[1536,256]{1,0:T(8,128)(2,1)S(1)} %collective-permute-done.9.refs_2_), channel_id=1, source_target_pairs={{1,2},{2,1},{5,6},{6,5},{9,10},{10,9},{13,14},{14,13},{17,18},{18,... | collective-permute-start | bytes 2359304 | tf_op jit(solution)/shard_map/ppermute | solution.py:285
  47.1 2.2 %select_reduce_fusion.3 = (s32[32,8]{1,0:T(8,128)S(1)}, s32[32,8]{1,0:T(8,128)S(1)}, s32[32,8]{1,0:T(8,128)S(1)}, s32[32,8]{1,0:T(8,128)S(1)}) fusion(s32[32,64]{1,0:T(8,128)S(1)} %broadcast_select_fusion, s32[32,64]{1,0:T(8,128)S(1)} %broadcast_add_fusion, s32[32,64]{1,0:T(8,128)S(1)} %get-tuple-element.61, s32[32,64]{1,0:T(8,128)S(1)} %bitcast.28, ...), kind=kLoop, calls=%fused_computation.3 | loop fusion | flops 162816 | bytes 45056 | tf_op jit(solution)/shard_map/reduce_sum | solution.py:336
  49.8 2.0 %concatenate.27.table = s32[328]{0:T(512)} concatenate(s32[1]{0:T(128)} %bitcast.17, s32[1]{0:T(128)} %bitcast.19, s32[1]{0:T(128)} %constant.32.clone.1, s32[1]{0:T(128)} %bitcast.11, s32[1]{0:T(128)} %bitcast.12, s32[1]{0:T(128)} %bitcast.13, s32[1]{0:T(128)} %bitcast.14, s32[1]{0:T(128)} %bitcast.15, s32[32]{0:T(128)S(1)} %get-tuple-element.48, s32[4]{0:T(128)S(1)} %broadcast.382, ...), dimensions={0} | concatenate | bytes 2624 | tf_op jit(solution)/shard_map/concatenate | solution.py:365
  52.2 1.9 %concatenate.26.table = s32[354]{0:T(512)} concatenate(s32[1]{0:T(128)} %bitcast.6, s32[1]{0:T(128)} %bitcast.10, s32[1]{0:T(128)} %constant.32.clone.1, s32[1]{0:T(128)} %bitcast.11, s32[1]{0:T(128)} %bitcast.12, s32[1]{0:T(128)} %bitcast.13, s32[1]{0:T(128)} %bitcast.14, s32[1]{0:T(128)} %bitcast.15, s32[32]{0:T(128)S(1)} %get-tuple-element.53, s32[4]{0:T(128)S(1)} %broadcast.382, ...), dimensions={0} | concatenate | bytes 2832 | tf_op jit(solution)/shard_map/concatenate | solution.py:365
  54.1 2.2 %collective-permute-done.refs_1_ = bf16[1792,256]{1,0:T(8,128)(2,1)S(1)} collective-permute-done((bf16[1792,256]{1,0:T(8,128)(2,1)}, bf16[1792,256]{1,0:T(8,128)(2,1)S(1)}, u32[]{:S(2)}, u32[]{:S(2)}) %collective-permute-start) | collective-permute-done | bytes 917536 | tf_op jit(solution)/shard_map/ppermute | solution.py:285
  57.0 14.5 %collective-permute-done.11.refs_6_ = bf16[1536,256]{1,0:T(8,128)(2,1)} collective-permute-done((bf16[1536,256]{1,0:T(8,128)(2,1)}, bf16[1536,256]{1,0:T(8,128)(2,1)}, u32[]{:S(2)}, u32[]{:S(2)}) %collective-permute-start.11) | collective-permute-done | bytes 786464 | tf_op jit(solution)/shard_map/ppermute | solution.py:285
  71.5 1.3 collective-permute-start.14
  72.8 1.3 collective-permute-start.10
  74.1 23.9 %collective-permute-done.14.refs_10_ = bf16[1536,256]{1,0:T(8,128)(2,1)} collective-permute-done((bf16[1536,256]{1,0:T(8,128)(2,1)}, bf16[1536,256]{1,0:T(8,128)(2,1)}, u32[]{:S(2)}, u32[]{:S(2)}) %collective-permute-start.14) | collective-permute-done | bytes 786464 | tf_op jit(solution)/shard_map/ppermute | solution.py:304
  98.0 1.3 collective-permute-start.15
  100.0 17.7 %collective-permute-done.10.refs_5_ = bf16[1792,256]{1,0:T(8,128)(2,1)} collective-permute-done((bf16[1792,256]{1,0:T(8,128)(2,1)S(1)}, bf16[1792,256]{1,0:T(8,128)(2,1)}, u32[]{:S(2)}, u32[]{:S(2)}) %collective-permute-start.10) | collective-permute-done | bytes 917536 | tf_op jit(solution)/shard_map/ppermute | solution.py:285
  117.7 7.6 %shard_map.78.refs_11_ = bf16[32,256,256]{2,1,0:T(8,128)(2,1)} custom-call(s32[354]{0:T(512)} %concatenate.26.table, bf16[8,3328,256]{2,1,0:T(8,128)(2,1)} %bitcast.24, bf16[3328,256]{1,0:T(8,128)(2,1)} %get-tuple-element.21.refs_0_, bf16[1792,256]{1,0:T(8,128)(2,1)} %copy-done.1, bf16[1536,256]{1,0:T(8,128)(2,1)} %copy-done.3, bf16[1792,256]{1,0:T(8,128)(2,1)} %copy-done, ...), custom_call_target="tpu_custom_call" | custom-call | tf_op jit(solution)/shard_map/pallas_call | solution.py:264
  125.3 7.3 %collective-permute-done.15.refs_9_ = bf16[1792,256]{1,0:T(8,128)(2,1)} collective-permute-done((bf16[1792,256]{1,0:T(8,128)(2,1)S(1)}, bf16[1792,256]{1,0:T(8,128)(2,1)}, u32[]{:S(2)}, u32[]{:S(2)}) %collective-permute-start.15) | collective-permute-done | bytes 917536 | tf_op jit(solution)/shard_map/ppermute | solution.py:311
  132.6 7.5 %shard_map.79 = bf16[32,256,256]{2,1,0:T(8,128)(2,1)} custom-call(s32[328]{0:T(512)} %concatenate.27.table, bf16[8,3328,256]{2,1,0:T(8,128)(2,1)} %bitcast.25, bf16[3328,256]{1,0:T(8,128)(2,1)} %get-tuple-element.21.refs_0_, bf16[1792,256]{1,0:T(8,128)(2,1)} %copy-done.1, bf16[1536,256]{1,0:T(8,128)(2,1)} %copy-done.3, ...), custom_call_target="tpu_custom_call", output_to_operand_aliasing={{}: (13, {})} | custom-call | tf_op jit(solution)/shard_map/pallas_call | solution.py:264
  (118 shorter events, 14.0 us)
Async XLA Ops:
  7.2 42.6 %copy-start.4 = (s32[8]{0:T(128)S(1)}, s32[8]{0:T(128)}, u32[]{:S(2)}) copy-start(s32[8]{0:T(128)} %flag_ref.1) | copy-start | bytes 100
  7.2 110.5 %all-gather.3.cloned.1.call-start = ((), (), s32[]{:S(2)}) async-start(), calls=%async_computation | async-start | bytes 15335424 | tf_op jit(solution)/shard_map/all_gather | solution.py:407
  11.3 10.8 %collective-permute-start.4 = (f32[1,128]{1,0:T(1,128)}, f32[1,128]{1,0:T(1,128)S(1)}, u32[]{:S(2)}, u32[]{:S(2)}) collective-permute-start(f32[1,128]{1,0:T(1,128)} %get-tuple-element.17), channel_id=1, source_target_pairs={{0,3},{1,2},{2,1},{3,0},{4,7},{5,6},{6,5},{7,4},{8,11},{9,10},{10,... | collective-permute-start | bytes 1544 | tf_op jit(solution)/shard_map/ppermute | solution.py:285
  15.3 7.5 %collective-permute-start.3 = (f32[1,128]{1,0:T(1,128)}, f32[1,128]{1,0:T(1,128)S(1)}, u32[]{:S(2)}, u32[]{:S(2)}) collective-permute-start(f32[1,128]{1,0:T(1,128)} %get-tuple-element.17), channel_id=1, source_target_pairs={{0,2},{1,3},{2,0},{3,1},{4,6},{5,7},{6,4},{7,5},{8,10},{9,11},{10,... | collective-permute-start | bytes 1544 | tf_op jit(solution)/shard_map/ppermute | solution.py:285
  15.3 14.0 %collective-permute-start.2 = (f32[1,128]{1,0:T(1,128)}, f32[1,128]{1,0:T(1,128)S(1)}, u32[]{:S(2)}, u32[]{:S(2)}) collective-permute-start(f32[1,128]{1,0:T(1,128)} %get-tuple-element.17), channel_id=1, source_target_pairs={{0,1},{1,0},{2,3},{3,2},{4,5},{5,4},{6,7},{7,6},{8,9},{9,8},{10,11... | collective-permute-start | bytes 1544 | tf_op jit(solution)/shard_map/ppermute | solution.py:285
  15.9 26.8 %collective-permute-start.9 = (bf16[1536,256]{1,0:T(8,128)(2,1)}, bf16[1536,256]{1,0:T(8,128)(2,1)S(1)}, u32[]{:S(2)}, u32[]{:S(2)}) collective-permute-start(bf16[1536,256]{1,0:T(8,128)(2,1)} %get-tuple-element.18), channel_id=1, source_target_pairs={{0,1},{1,0},{2,3},{3,2},{4,5},{5,4},{6,7},{7,6},{8,9},{9,8},{10,11... | collective-permute-start | bytes 2359304 | tf_op jit(solution)/shard_map/ppermute | solution.py:285
  17.3 22.0 %collective-permute-start.5 = (bf16[1536,256]{1,0:T(8,128)(2,1)}, bf16[1536,256]{1,0:T(8,128)(2,1)}, u32[]{:S(2)}, u32[]{:S(2)}) collective-permute-start(bf16[1536,256]{1,0:T(8,128)(2,1)} %get-tuple-element.18), channel_id=1, source_target_pairs={{1,2},{2,1},{5,6},{6,5},{9,10},{10,9},{13,14},{14,13},{17,18},{18,... | collective-permute-start | bytes 2359304 | tf_op jit(solution)/shard_map/ppermute | solution.py:285
  22.0 32.0 %collective-permute-start.1 = (bf16[1792,256]{1,0:T(8,128)(2,1)}, bf16[1792,256]{1,0:T(8,128)(2,1)S(1)}, u32[]{:S(2)}, u32[]{:S(2)}) collective-permute-start(bf16[1792,256]{1,0:T(8,128)(2,1)} %get-tuple-element.16), channel_id=1, source_target_pairs={{1,2},{2,1},{5,6},{6,5},{9,10},{10,9},{13,14},{14,13},{17,18},{18,... | collective-permute-start | bytes 2752520 | tf_op jit(solution)/shard_map/ppermute | solution.py:285
  22.8 33.5 %collective-permute-start = (bf16[1792,256]{1,0:T(8,128)(2,1)}, bf16[1792,256]{1,0:T(8,128)(2,1)S(1)}, u32[]{:S(2)}, u32[]{:S(2)}) collective-permute-start(bf16[1792,256]{1,0:T(8,128)(2,1)} %get-tuple-element.16), channel_id=1, source_target_pairs={{0,1},{1,0},{2,3},{3,2},{4,5},{5,4},{6,7},{7,6},{8,9},{9,8},{10,11... | collective-permute-start | bytes 2752520 | tf_op jit(solution)/shard_map/ppermute | solution.py:285
  30.8 1.1 collective-permute-start.6
  32.0 3.6 %collective-permute-start.7 = (f32[2,128]{1,0:T(2,128)S(1)}, f32[2,128]{1,0:T(2,128)S(1)}, u32[]{:S(2)}, u32[]{:S(2)}) collective-permute-start(f32[2,128]{1,0:T(2,128)S(1)} %pad_maximum_fusion.3), channel_id=1, source_target_pairs={{0,8},{4,12},{8,0},{12,4},{16,24},{20,28},{24,16},{28,20},{1,9},{5... | collective-permute-start | bytes 3080 | tf_op jit(solution)/shard_map/ppermute | solution.py:382
  35.5 3.7 %collective-permute-start.8 = (f32[4,128]{1,0:T(4,128)S(1)}, f32[4,128]{1,0:T(4,128)S(1)}, u32[]{:S(2)}, u32[]{:S(2)}) collective-permute-start(f32[4,128]{1,0:T(4,128)S(1)} %pad_maximum_fusion.2), channel_id=1, source_target_pairs={{0,16},{4,20},{8,24},{12,28},{16,0},{20,4},{24,8},{28,12},{1,17},{... | collective-permute-start | bytes 6152 | tf_op jit(solution)/shard_map/ppermute | solution.py:382
  41.5 30.0 %collective-permute-start.11 = (bf16[1536,256]{1,0:T(8,128)(2,1)}, bf16[1536,256]{1,0:T(8,128)(2,1)}, u32[]{:S(2)}, u32[]{:S(2)}) collective-permute-start(bf16[1536,256]{1,0:T(8,128)(2,1)} %collective-permute-done.5.refs_4_), channel_id=1, source_target_pairs={{1,0},{2,3},{5,4},{6,7},{9,8},{10,11},{13,12},{14,15},{17,16},{18,... | collective-permute-start | bytes 2359304 | tf_op jit(solution)/shard_map/ppermute | solution.py:285
  42.8 74.9 %copy-start.3 = (bf16[1536,256]{1,0:T(8,128)(2,1)}, bf16[1536,256]{1,0:T(8,128)(2,1)S(1)}, u32[]{:S(2)}) copy-start(bf16[1536,256]{1,0:T(8,128)(2,1)S(1)} %collective-permute-done.9.refs_2_) | copy-start | bytes 2359300
  42.8 14.2 %collective-permute-start.13 = (bf16[1536,256]{1,0:T(8,128)(2,1)S(1)}, bf16[1536,256]{1,0:T(8,128)(2,1)}, u32[]{:S(2)}, u32[]{:S(2)}) collective-permute-start(bf16[1536,256]{1,0:T(8,128)(2,1)S(1)} %collective-permute-done.9.refs_2_), channel_id=1, source_target_pairs={{1,2},{2,1},{5,6},{6,5},{9,10},{10,9},{13,14},{14,13},{17,18},{18,... | collective-permute-start | bytes 2359304 | tf_op jit(solution)/shard_map/ppermute | solution.py:285
  54.1 63.6 %copy-start = (bf16[1792,256]{1,0:T(8,128)(2,1)}, bf16[1792,256]{1,0:T(8,128)(2,1)S(1)}, u32[]{:S(2)}) copy-start(bf16[1792,256]{1,0:T(8,128)(2,1)S(1)} %collective-permute-done.1.refs_3_) | copy-start | bytes 2752516
  56.3 61.4 %copy-start.1 = (bf16[1792,256]{1,0:T(8,128)(2,1)}, bf16[1792,256]{1,0:T(8,128)(2,1)S(1)}, u32[]{:S(2)}) copy-start(bf16[1792,256]{1,0:T(8,128)(2,1)S(1)} %collective-permute-done.refs_1_) | copy-start | bytes 2752516
  56.3 17.8 %collective-permute-start.12 = (bf16[1792,256]{1,0:T(8,128)(2,1)S(1)}, bf16[1792,256]{1,0:T(8,128)(2,1)S(1)}, u32[]{:S(2)}, u32[]{:S(2)}) collective-permute-start(bf16[1792,256]{1,0:T(8,128)(2,1)S(1)} %collective-permute-done.refs_1_), channel_id=1, source_target_pairs={{1,2},{2,1},{5,6},{6,5},{9,10},{10,9},{13,14},{14,13},{17,18},{18,... | collective-permute-start | bytes 2752520 | tf_op jit(solution)/shard_map/ppermute | solution.py:285
  71.5 26.5 %collective-permute-start.14 = (bf16[1536,256]{1,0:T(8,128)(2,1)}, bf16[1536,256]{1,0:T(8,128)(2,1)}, u32[]{:S(2)}, u32[]{:S(2)}) collective-permute-start(bf16[1536,256]{1,0:T(8,128)(2,1)} %collective-permute-done.13.refs_8_), channel_id=1, source_target_pairs={{2,3},{6,7},{9,8},{10,11},{13,12},{14,15},{17,16},{18,19},{21,20},... | collective-permute-start | bytes 2359304 | tf_op jit(solution)/shard_map/ppermute | solution.py:304
  72.8 44.9 %collective-permute-start.10 = (bf16[1792,256]{1,0:T(8,128)(2,1)S(1)}, bf16[1792,256]{1,0:T(8,128)(2,1)}, u32[]{:S(2)}, u32[]{:S(2)}) collective-permute-start(bf16[1792,256]{1,0:T(8,128)(2,1)S(1)} %collective-permute-done.1.refs_3_), channel_id=1, source_target_pairs={{1,0},{2,3},{5,4},{6,7},{9,8},{10,11},{13,12},{14,15},{17,16},{18,... | collective-permute-start | bytes 2752520 | tf_op jit(solution)/shard_map/ppermute | solution.py:285
  74.1 43.6 %copy-start.2 = (bf16[1792,256]{1,0:T(8,128)(2,1)}, bf16[1792,256]{1,0:T(8,128)(2,1)S(1)}, u32[]{:S(2)}) copy-start(bf16[1792,256]{1,0:T(8,128)(2,1)S(1)} %collective-permute-done.12.refs_7_) | copy-start | bytes 2752516
  98.0 34.6 %collective-permute-start.15 = (bf16[1792,256]{1,0:T(8,128)(2,1)S(1)}, bf16[1792,256]{1,0:T(8,128)(2,1)}, u32[]{:S(2)}, u32[]{:S(2)}) collective-permute-start(bf16[1792,256]{1,0:T(8,128)(2,1)S(1)} %collective-permute-done.12.refs_7_), channel_id=1, source_target_pairs={{2,3},{6,7},{9,8},{10,11},{13,12},{14,15},{17,16},{18,19},{21,20},... | collective-permute-start | bytes 2752520 | tf_op jit(solution)/shard_map/ppermute | solution.py:311
Sparse Core Ops, SparseCore 0:
  11.4 78.2 all-gather.2

commit v15 on v14

--- a/solution.py
+++ b/solution.py
@@ -289,7 +289,7 @@
     first = [shift(part, [(0, 1), (1, 0), (2, 3), (3, 2)]) for part in parts]
     middle = [shift(part, [(1, 2), (2, 1)]) for part in parts]
     facts = gather_facts(facts, ("row",))
-    middle[1], facts = lax.optimization_barrier((middle[1], facts))
+    middle[0], facts = lax.optimization_barrier((middle[0], facts))
     return first, middle, facts
 
 
@@ -302,7 +302,7 @@
         pairs += [(4 * row + 2, 4 * row + 3)] * (row // 2 != 3)
     small = lax.optimization_barrier((middle_two[1], end_two[1]))[0]
     small = lax.ppermute(small, ("row", "col"), pairs)
-    large = lax.optimization_barrier((middle_two[0], small))[0]
+    large = lax.optimization_barrier((middle_two[0], small, end_two[0]))[0]
     return {
         "first": first,
         "middle": middle,
@@ -490,8 +490,8 @@
 
     early_table, early_layout = table_of(early, ~is_late, marks)
     late_table, late_layout = table_of(early + late, is_late)
-    first[0], middle[0], early_table, late_table = lax.optimization_barrier(
-        (first[0], middle[0], early_table, late_table)
+    first[0], early_table, late_table = lax.optimization_barrier(
+        (first[0], early_table, late_table)
     )
     line = relay_line(first, middle)
 

time: 147 us -> 148 us (level)
  waiting for transfers between devices: 71.5 us -> 63.8 us
  other arithmetic: 11 us -> 16.7 us
  local copies, waits for them, and re-layouts: 6.53 us -> 9.48 us
    ppermute x1, waiting for transfers between devices: 23.9 us -> 15.2 us  [relay_line(): small = lax.ppermute(small, ('row', 'col'), pairs)]
    ppermute x1, waiting for transfers between devices: 7.27 us -> 11.9 us  [relay_line(): lax.ppermute(large, ('row', 'col'), pairs)]
    ppermute x11, waiting for transfers between devices: 34.4 us -> 30.5 us  [shift(): return lax.ppermute(array, 'col', pairs)]
    reduce_sum x2, other arithmetic: 0.38 us -> 2.23 us  [make_table(): rights = jnp.sum(jnp.where(pick, rights, 0), axis=(1, 2))]
    reduce_sum x8, other arithmetic: 1.46 us -> 3.31 us  [running_count(): return jnp.sum(jnp.where(before, fill[..., :, None], 0), axis=-2)]
  transfers between devices with their start and end apart: 17 -> 17, of which waited for: 8 -> 7; matrix products, arithmetic and copies ran while one was open for 12% -> 18% of each run, Pallas kernels for 5% -> 6%
where the time goes in v15:
time: 148 us; the launch traced here: 147 us
  waiting for transfers between devices  63.8 us (43%)
  starting transfers between devices  23.3 us (16%)
  Pallas kernels  18.9 us (13%)
  other arithmetic  16.7 us (11%)
  between operations  14.4 us (10%)
  local copies, waits for them, and re-layouts  9.48 us (6%)
    ppermute x11, waiting for transfers between devices, shift(): return lax.ppermute(array, 'col', pairs)  30.5 us
    ppermute x11, starting transfers between devices, shift(): return lax.ppermute(array, 'col', pairs)  18.9 us
    ppermute x1, waiting for transfers between devices, relay_line(): small = lax.ppermute(small, ('row', 'col'), pairs)  15.2 us
    pallas_call x2, Pallas kernels, multiply(): pl.pallas_call(functools.partial(multiply_kernel, loads, kept, layout, tu...  14.5 us
    ppermute x1, waiting for transfers between devices, relay_line(): lax.ppermute(large, ('row', 'col'), pairs)  11.9 us
    ppermute x3, waiting for transfers between devices, gather_facts(): other = lax.ppermute(facts, axis, [(i, i ^ mask) for i in range(size)])  6.23 us
    concatenate x2, local copies, waits for them, and re-layouts, make_table(): return (jnp.concatenate(list(lists.values())), layout)  5.29 us
    pallas_call x1, Pallas kernels, pack(): pl.pallas_call(pack_kernel, out_shape=packed + [jax.ShapeDtypeStruct((1,...  4.34 us
  transfers between devices with their start and end apart: 17, of which 7 were waited for; matrix products, arithmetic and copies ran while one was open for 18% of the time, Pallas kernels for 6%

profile of v15, /device:TPU:2, one launch (start us, length us, event | category | flops | bytes accessed | tf_op | source)
XLA Modules:
  0.0 146.6 jit_solution(1530942513538390057)
XLA Ops:
  7.2 4.3 %shard_map.77 = (bf16[1792,256]{1,0:T(8,128)(2,1)}, bf16[1536,256]{1,0:T(8,128)(2,1)}, bf16[3328,256]{1,0:T(8,128)(2,1)}, f32[1,128]{1,0:T(1,128)}) custom-call(s32[2,8]{1,0:T(2,128)} %bitcast.37, s32[8]{0:T(128)} %flag_ref.1, s32[1]{0:T(128)} %bitcast.1.first_ref, bf16[16,256,256]{2,1,0:T(8,128)(2,1)} %bitcast.27), custom_call_target="tpu_custom_call" | custom-call | tf_op jit(solution)/shard_map/pallas_call | solution.py:83
  11.6 3.6 %collective-permute-start.3 = (f32[1,128]{1,0:T(1,128)}, f32[1,128]{1,0:T(1,128)S(1)}, u32[]{:S(2)}, u32[]{:S(2)}) collective-permute-start(f32[1,128]{1,0:T(1,128)} %get-tuple-element.16), channel_id=1, source_target_pairs={{0,3},{1,2},{2,1},{3,0},{4,7},{5,6},{6,5},{7,4},{8,11},{9,10},{10,... | collective-permute-start | bytes 1544 | tf_op jit(solution)/shard_map/ppermute | solution.py:285
  16.8 3.9 %collective-permute-start.8 = (bf16[1536,256]{1,0:T(8,128)(2,1)}, bf16[1536,256]{1,0:T(8,128)(2,1)}, u32[]{:S(2)}, u32[]{:S(2)}) collective-permute-start(bf16[1536,256]{1,0:T(8,128)(2,1)} %get-tuple-element.21), channel_id=1, source_target_pairs={{0,1},{1,0},{2,3},{3,2},{4,5},{5,4},{6,7},{7,6},{8,9},{9,8},{10,11... | collective-permute-start | bytes 2359304 | tf_op jit(solution)/shard_map/ppermute | solution.py:285
  25.1 3.4 %collective-permute-start = (bf16[1792,256]{1,0:T(8,128)(2,1)}, bf16[1792,256]{1,0:T(8,128)(2,1)S(1)}, u32[]{:S(2)}, u32[]{:S(2)}) collective-permute-start(bf16[1792,256]{1,0:T(8,128)(2,1)} %get-tuple-element.15), channel_id=1, source_target_pairs={{0,1},{1,0},{2,3},{3,2},{4,5},{5,4},{6,7},{7,6},{8,9},{9,8},{10,11... | collective-permute-start | bytes 2752520 | tf_op jit(solution)/shard_map/ppermute | solution.py:285
  31.7 3.0 %collective-permute-done.6 = f32[2,128]{1,0:T(2,128)S(1)} collective-permute-done((f32[2,128]{1,0:T(2,128)S(1)}, f32[2,128]{1,0:T(2,128)S(1)}, u32[]{:S(2)}, u32[]{:S(2)}) %collective-permute-start.6) | collective-permute-done | bytes 1056 | tf_op jit(solution)/shard_map/ppermute | solution.py:382
  34.7 1.4 collective-permute-start.7
  36.3 2.2 %collective-permute-done.7 = f32[4,128]{1,0:T(4,128)S(1)} collective-permute-done((f32[4,128]{1,0:T(4,128)S(1)}, f32[4,128]{1,0:T(4,128)S(1)}, u32[]{:S(2)}, u32[]{:S(2)}) %collective-permute-start.7) | collective-permute-done | bytes 2080 | tf_op jit(solution)/shard_map/ppermute | solution.py:382
  38.5 1.3 collective-permute-start.11
  39.9 1.6 %collective-permute-start.13 = (bf16[1536,256]{1,0:T(8,128)(2,1)}, bf16[1536,256]{1,0:T(8,128)(2,1)}, u32[]{:S(2)}, u32[]{:S(2)}) collective-permute-start(bf16[1536,256]{1,0:T(8,128)(2,1)} %collective-permute-done.8.refs_2_), channel_id=1, source_target_pairs={{1,2},{2,1},{5,6},{6,5},{9,10},{10,9},{13,14},{14,13},{17,18},{18,... | collective-permute-start | bytes 2359304 | tf_op jit(solution)/shard_map/ppermute | solution.py:285
  49.5 2.3 %select_reduce_fusion.3 = (s32[32,8]{1,0:T(8,128)S(1)}, s32[32,8]{1,0:T(8,128)S(1)}, s32[32,8]{1,0:T(8,128)}, s32[32,8]{1,0:T(8,128)S(1)}) fusion(s32[32,64]{1,0:T(8,128)S(1)} %broadcast_select_fusion, s32[32,64]{1,0:T(8,128)S(1)} %broadcast_add_fusion, s32[32,64]{1,0:T(8,128)S(1)} %get-tuple-element.59, s32[32,64]{1,0:T(8,128)S(1)} %bitcast.28, ...), kind=kLoop, calls=%fused_computation.3 | loop fusion | flops 162816 | bytes 45056 | tf_op jit(solution)/shard_map/reduce_sum | solution.py:336
  53.1 2.7 %concatenate.27.table = s32[328]{0:T(512)} concatenate(s32[1]{0:T(128)} %bitcast.17, s32[1]{0:T(128)} %bitcast.19, s32[1]{0:T(128)} %constant.32.clone.1, s32[1]{0:T(128)} %bitcast.11, s32[1]{0:T(128)} %bitcast.12, s32[1]{0:T(128)} %bitcast.13, s32[1]{0:T(128)} %bitcast.14, s32[1]{0:T(128)} %bitcast.15, s32[32]{0:T(128)} %get-tuple-element.46, s32[4]{0:T(128)} %broadcast.382, ...), dimensions={0} | concatenate | bytes 2624 | tf_op jit(solution)/shard_map/concatenate | solution.py:365
  55.7 1.5 select_reduce_fusion.21
  57.9 1.5 %select_reduce_fusion.6 = (s32[104]{0:T(128)}, s32[104]{0:T(128)}) fusion(s32[32,8]{1,0:T(8,128)S(1)} %get-tuple-element.31, s32[32,8]{1,0:T(8,128)S(1)} %add_select_fusion.1, s32[32,8]{1,0:T(8,128)} %get-tuple-element.32), kind=kLoop, calls=%fused_computation.8 | loop fusion | flops 132912 | bytes 3904 | tf_op jit(solution)/shard_map/reduce_sum | solution.py:340
  59.4 2.6 %concatenate.26.table = s32[354]{0:T(512)} concatenate(s32[1]{0:T(128)} %bitcast.6, s32[1]{0:T(128)} %bitcast.10, s32[1]{0:T(128)} %constant.32.clone.1, s32[1]{0:T(128)} %bitcast.11, s32[1]{0:T(128)} %bitcast.12, s32[1]{0:T(128)} %bitcast.13, s32[1]{0:T(128)} %bitcast.14, s32[1]{0:T(128)} %bitcast.15, s32[32]{0:T(128)} %get-tuple-element.51, s32[4]{0:T(128)} %broadcast.382, ...), dimensions={0} | concatenate | bytes 2832 | tf_op jit(solution)/shard_map/concatenate | solution.py:365
  62.0 1.6 %collective-permute-start.12 = (bf16[1792,256]{1,0:T(8,128)(2,1)S(1)}, bf16[1792,256]{1,0:T(8,128)(2,1)}, u32[]{:S(2)}, u32[]{:S(2)}) collective-permute-start(bf16[1792,256]{1,0:T(8,128)(2,1)S(1)} %collective-permute-done.refs_1_), channel_id=1, source_target_pairs={{1,2},{2,1},{5,6},{6,5},{9,10},{10,9},{13,14},{14,13},{17,18},{18,... | collective-permute-start | bytes 2752520 | tf_op jit(solution)/shard_map/ppermute | solution.py:285
  63.7 12.3 %collective-permute-done.11.refs_6_ = bf16[1536,256]{1,0:T(8,128)(2,1)} collective-permute-done((bf16[1536,256]{1,0:T(8,128)(2,1)S(1)}, bf16[1536,256]{1,0:T(8,128)(2,1)}, u32[]{:S(2)}, u32[]{:S(2)}) %collective-permute-start.11) | collective-permute-done | bytes 786464 | tf_op jit(solution)/shard_map/ppermute | solution.py:285
  75.9 1.3 collective-permute-start.14
  77.2 18.3 %collective-permute-done.10.refs_5_ = bf16[1792,256]{1,0:T(8,128)(2,1)S(1)} collective-permute-done((bf16[1792,256]{1,0:T(8,128)(2,1)S(1)}, bf16[1792,256]{1,0:T(8,128)(2,1)S(1)}, u32[]{:S(2)}, u32[]{:S(2)}) %collective-permute-start.10) | collective-permute-done | bytes 917536 | tf_op jit(solution)/shard_map/ppermute | solution.py:285
  95.5 15.2 %collective-permute-done.14.refs_10_ = bf16[1536,256]{1,0:T(8,128)(2,1)} collective-permute-done((bf16[1536,256]{1,0:T(8,128)(2,1)}, bf16[1536,256]{1,0:T(8,128)(2,1)}, u32[]{:S(2)}, u32[]{:S(2)}) %collective-permute-start.14) | collective-permute-done | bytes 786464 | tf_op jit(solution)/shard_map/ppermute | solution.py:304
  110.7 1.3 collective-permute-start.15
  112.0 1.4 slice_reduce_fusion
  113.3 8.3 %shard_map.78.refs_11_ = bf16[32,256,256]{2,1,0:T(8,128)(2,1)} custom-call(s32[354]{0:T(512)} %concatenate.26.table, bf16[8,3328,256]{2,1,0:T(8,128)(2,1)} %bitcast.24, bf16[3328,256]{1,0:T(8,128)(2,1)} %get-tuple-element.19.refs_0_, bf16[1792,256]{1,0:T(8,128)(2,1)} %copy-done.1, bf16[1536,256]{1,0:T(8,128)(2,1)} %collective-permute-done.8.refs_2_, ...), custom_call_target="tpu_custom_call" | custom-call | tf_op jit(solution)/shard_map/pallas_call | solution.py:264
  121.6 11.9 %collective-permute-done.15.refs_9_ = bf16[1792,256]{1,0:T(8,128)(2,1)} collective-permute-done((bf16[1792,256]{1,0:T(8,128)(2,1)}, bf16[1792,256]{1,0:T(8,128)(2,1)}, u32[]{:S(2)}, u32[]{:S(2)}) %collective-permute-start.15) | collective-permute-done | bytes 917536 | tf_op jit(solution)/shard_map/ppermute | solution.py:311
  133.5 6.3 %shard_map.79 = bf16[32,256,256]{2,1,0:T(8,128)(2,1)} custom-call(s32[328]{0:T(512)} %concatenate.27.table, bf16[8,3328,256]{2,1,0:T(8,128)(2,1)} %bitcast.25, bf16[3328,256]{1,0:T(8,128)(2,1)} %get-tuple-element.19.refs_0_, bf16[1792,256]{1,0:T(8,128)(2,1)} %copy-done.1, ...), custom_call_target="tpu_custom_call", output_to_operand_aliasing={{}: (13, {})} | custom-call | tf_op jit(solution)/shard_map/pallas_call | solution.py:264
  (118 shorter events, 19.4 us)
Async XLA Ops:
  7.2 106.2 %all-gather.3.cloned.1.call-start = ((), (), s32[]{:S(2)}) async-start(), calls=%async_computation | async-start | bytes 15335424 | tf_op jit(solution)/shard_map/all_gather | solution.py:407
  11.6 12.7 %collective-permute-start.3 = (f32[1,128]{1,0:T(1,128)}, f32[1,128]{1,0:T(1,128)S(1)}, u32[]{:S(2)}, u32[]{:S(2)}) collective-permute-start(f32[1,128]{1,0:T(1,128)} %get-tuple-element.16), channel_id=1, source_target_pairs={{0,3},{1,2},{2,1},{3,0},{4,7},{5,6},{6,5},{7,4},{8,11},{9,10},{10,... | collective-permute-start | bytes 1544 | tf_op jit(solution)/shard_map/ppermute | solution.py:285
  15.2 9.9 %collective-permute-start.2 = (f32[1,128]{1,0:T(1,128)}, f32[1,128]{1,0:T(1,128)S(1)}, u32[]{:S(2)}, u32[]{:S(2)}) collective-permute-start(f32[1,128]{1,0:T(1,128)} %get-tuple-element.16), channel_id=1, source_target_pairs={{0,2},{1,3},{2,0},{3,1},{4,6},{5,7},{6,4},{7,5},{8,10},{9,11},{10,... | collective-permute-start | bytes 1544 | tf_op jit(solution)/shard_map/ppermute | solution.py:285
  15.2 13.3 %collective-permute-start.1 = (f32[1,128]{1,0:T(1,128)}, f32[1,128]{1,0:T(1,128)S(1)}, u32[]{:S(2)}, u32[]{:S(2)}) collective-permute-start(f32[1,128]{1,0:T(1,128)} %get-tuple-element.16), channel_id=1, source_target_pairs={{0,1},{1,0},{2,3},{3,2},{4,5},{5,4},{6,7},{7,6},{8,9},{9,8},{10,11... | collective-permute-start | bytes 1544 | tf_op jit(solution)/shard_map/ppermute | solution.py:285
  16.0 22.5 %collective-permute-start.9 = (bf16[1536,256]{1,0:T(8,128)(2,1)}, bf16[1536,256]{1,0:T(8,128)(2,1)S(1)}, u32[]{:S(2)}, u32[]{:S(2)}) collective-permute-start(bf16[1536,256]{1,0:T(8,128)(2,1)} %get-tuple-element.21), channel_id=1, source_target_pairs={{1,2},{2,1},{5,6},{6,5},{9,10},{10,9},{13,14},{14,13},{17,18},{18,... | collective-permute-start | bytes 2359304 | tf_op jit(solution)/shard_map/ppermute | solution.py:285
  16.8 23.1 %collective-permute-start.8 = (bf16[1536,256]{1,0:T(8,128)(2,1)}, bf16[1536,256]{1,0:T(8,128)(2,1)}, u32[]{:S(2)}, u32[]{:S(2)}) collective-permute-start(bf16[1536,256]{1,0:T(8,128)(2,1)} %get-tuple-element.21), channel_id=1, source_target_pairs={{0,1},{1,0},{2,3},{3,2},{4,5},{5,4},{6,7},{7,6},{8,9},{9,8},{10,11... | collective-permute-start | bytes 2359304 | tf_op jit(solution)/shard_map/ppermute | solution.py:285
  24.3 17.1 %collective-permute-start.4 = (bf16[1792,256]{1,0:T(8,128)(2,1)}, bf16[1792,256]{1,0:T(8,128)(2,1)S(1)}, u32[]{:S(2)}, u32[]{:S(2)}) collective-permute-start(bf16[1792,256]{1,0:T(8,128)(2,1)} %get-tuple-element.15), channel_id=1, source_target_pairs={{1,2},{2,1},{5,6},{6,5},{9,10},{10,9},{13,14},{14,13},{17,18},{18,... | collective-permute-start | bytes 2752520 | tf_op jit(solution)/shard_map/ppermute | solution.py:285
  25.1 37.0 %collective-permute-start = (bf16[1792,256]{1,0:T(8,128)(2,1)}, bf16[1792,256]{1,0:T(8,128)(2,1)S(1)}, u32[]{:S(2)}, u32[]{:S(2)}) collective-permute-start(bf16[1792,256]{1,0:T(8,128)(2,1)} %get-tuple-element.15), channel_id=1, source_target_pairs={{0,1},{1,0},{2,3},{3,2},{4,5},{5,4},{6,7},{7,6},{8,9},{9,8},{10,11... | collective-permute-start | bytes 2752520 | tf_op jit(solution)/shard_map/ppermute | solution.py:285
  30.0 1.1 collective-permute-start.5
  31.2 3.6 %collective-permute-start.6 = (f32[2,128]{1,0:T(2,128)S(1)}, f32[2,128]{1,0:T(2,128)S(1)}, u32[]{:S(2)}, u32[]{:S(2)}) collective-permute-start(f32[2,128]{1,0:T(2,128)S(1)} %pad_maximum_fusion.3), channel_id=1, source_target_pairs={{0,8},{4,12},{8,0},{12,4},{16,24},{20,28},{24,16},{28,20},{1,9},{5... | collective-permute-start | bytes 3080 | tf_op jit(solution)/shard_map/ppermute | solution.py:382
  34.7 3.7 %collective-permute-start.7 = (f32[4,128]{1,0:T(4,128)S(1)}, f32[4,128]{1,0:T(4,128)S(1)}, u32[]{:S(2)}, u32[]{:S(2)}) collective-permute-start(f32[4,128]{1,0:T(4,128)S(1)} %pad_maximum_fusion.2), channel_id=1, source_target_pairs={{0,16},{4,20},{8,24},{12,28},{16,0},{20,4},{24,8},{28,12},{1,17},{... | collective-permute-start | bytes 6152 | tf_op jit(solution)/shard_map/ppermute | solution.py:382
  38.5 3.2 %copy-start.4 = (f32[8,128]{1,0:T(8,128)}, f32[8,128]{1,0:T(8,128)S(1)}, u32[]{:S(2)}) copy-start(f32[8,128]{1,0:T(8,128)S(1)} %select_reduce_fusion.14) | copy-start | bytes 12292
  38.5 74.8 %copy-start.3 = (bf16[1536,256]{1,0:T(8,128)(2,1)}, bf16[1536,256]{1,0:T(8,128)(2,1)S(1)}, u32[]{:S(2)}) copy-start(bf16[1536,256]{1,0:T(8,128)(2,1)S(1)} %collective-permute-done.9.refs_4_) | copy-start | bytes 2359300
  38.5 37.4 %collective-permute-start.11 = (bf16[1536,256]{1,0:T(8,128)(2,1)S(1)}, bf16[1536,256]{1,0:T(8,128)(2,1)}, u32[]{:S(2)}, u32[]{:S(2)}) collective-permute-start(bf16[1536,256]{1,0:T(8,128)(2,1)S(1)} %collective-permute-done.9.refs_4_), channel_id=1, source_target_pairs={{1,0},{2,3},{5,4},{6,7},{9,8},{10,11},{13,12},{14,15},{17,16},{18,... | collective-permute-start | bytes 2359304 | tf_op jit(solution)/shard_map/ppermute | solution.py:285
  39.9 36.1 %collective-permute-start.13 = (bf16[1536,256]{1,0:T(8,128)(2,1)}, bf16[1536,256]{1,0:T(8,128)(2,1)}, u32[]{:S(2)}, u32[]{:S(2)}) collective-permute-start(bf16[1536,256]{1,0:T(8,128)(2,1)} %collective-permute-done.8.refs_2_), channel_id=1, source_target_pairs={{1,2},{2,1},{5,6},{6,5},{9,10},{10,9},{13,14},{14,13},{17,18},{18,... | collective-permute-start | bytes 2359304 | tf_op jit(solution)/shard_map/ppermute | solution.py:285
  41.5 71.9 %copy-start = (bf16[1792,256]{1,0:T(8,128)(2,1)}, bf16[1792,256]{1,0:T(8,128)(2,1)S(1)}, u32[]{:S(2)}) copy-start(bf16[1792,256]{1,0:T(8,128)(2,1)S(1)} %collective-permute-done.4.refs_3_) | copy-start | bytes 2752516
  44.5 51.0 %collective-permute-start.10 = (bf16[1792,256]{1,0:T(8,128)(2,1)S(1)}, bf16[1792,256]{1,0:T(8,128)(2,1)S(1)}, u32[]{:S(2)}, u32[]{:S(2)}) collective-permute-start(bf16[1792,256]{1,0:T(8,128)(2,1)S(1)} %collective-permute-done.4.refs_3_), channel_id=1, source_target_pairs={{1,0},{2,3},{5,4},{6,7},{9,8},{10,11},{13,12},{14,15},{17,16},{18,... | collective-permute-start | bytes 2752520 | tf_op jit(solution)/shard_map/ppermute | solution.py:285
  62.0 51.3 %copy-start.1 = (bf16[1792,256]{1,0:T(8,128)(2,1)}, bf16[1792,256]{1,0:T(8,128)(2,1)S(1)}, u32[]{:S(2)}) copy-start(bf16[1792,256]{1,0:T(8,128)(2,1)S(1)} %collective-permute-done.refs_1_) | copy-start | bytes 2752516
  62.0 33.5 %collective-permute-start.12 = (bf16[1792,256]{1,0:T(8,128)(2,1)S(1)}, bf16[1792,256]{1,0:T(8,128)(2,1)}, u32[]{:S(2)}, u32[]{:S(2)}) collective-permute-start(bf16[1792,256]{1,0:T(8,128)(2,1)S(1)} %collective-permute-done.refs_1_), channel_id=1, source_target_pairs={{1,2},{2,1},{5,6},{6,5},{9,10},{10,9},{13,14},{14,13},{17,18},{18,... | collective-permute-start | bytes 2752520 | tf_op jit(solution)/shard_map/ppermute | solution.py:285
  75.9 34.8 %collective-permute-start.14 = (bf16[1536,256]{1,0:T(8,128)(2,1)}, bf16[1536,256]{1,0:T(8,128)(2,1)}, u32[]{:S(2)}, u32[]{:S(2)}) collective-permute-start(bf16[1536,256]{1,0:T(8,128)(2,1)} %collective-permute-done.13.refs_8_), channel_id=1, source_target_pairs={{2,3},{6,7},{9,8},{10,11},{13,12},{14,15},{17,16},{18,19},{21,20},... | collective-permute-start | bytes 2359304 | tf_op jit(solution)/shard_map/ppermute | solution.py:304
  95.5 17.9 %copy-start.2 = (bf16[1792,256]{1,0:T(8,128)(2,1)}, bf16[1792,256]{1,0:T(8,128)(2,1)S(1)}, u32[]{:S(2)}) copy-start(bf16[1792,256]{1,0:T(8,128)(2,1)S(1)} %collective-permute-done.10.refs_5_) | copy-start | bytes 2752516
  110.7 22.8 %collective-permute-start.15 = (bf16[1792,256]{1,0:T(8,128)(2,1)}, bf16[1792,256]{1,0:T(8,128)(2,1)}, u32[]{:S(2)}, u32[]{:S(2)}) collective-permute-start(bf16[1792,256]{1,0:T(8,128)(2,1)} %collective-permute-done.12.refs_7_), channel_id=1, source_target_pairs={{2,3},{6,7},{9,8},{10,11},{13,12},{14,15},{17,16},{18,19},{21,20},... | collective-permute-start | bytes 2752520 | tf_op jit(solution)/shard_map/ppermute | solution.py:311
Sparse Core Ops, SparseCore 0:
  11.7 77.5 all-gather.2
